TPU v7x, 32 devices: a whole 2x2x4 slice. The times are simulated.
32 devices in a mesh: dp: 2 (over x), ffn: 4 (over z), hid: 4 (over y, core).
Axes of the slice: x: 2, y: 2, z: 4, core: 2. Of those that a mesh axis runs over, the one named last changes fastest.
Arguments:
- stream: bfloat16 [512, 16384], P('dp', 'hid'), may hold values from -160 to 160
- steering: float32 [16384], P('hid'), may hold values from -40 to 40
- strength: float32 [512], P('dp'), may hold values from 0.5 to 2
- norm_gain_vector: float32 [16384], P('hid'), may hold values from 0.25 to 1.75
- frozen_weights: bfloat16 [2, 16384, 26624], P('dp', 'hid', 'ffn'), may hold values from -0.046875 to 0.046875
- adapter_down_factors: bfloat16 [2, 16384, 16], P(None, 'hid'), may hold values from -0.046875 to 0.046875
- adapter_up_factors: bfloat16 [2, 16, 26624], P(None, None, 'ffn'), may hold values from -1.5 to 1.5
- cotangent: bfloat16 [512, 26624], P(('dp', 'hid'), 'ffn'), may hold values from -6 to 6
Outputs:
- residual_stream_gradient: bfloat16 [512, 16384], P('dp', 'hid')
- steering_vector_gradient: float32 [16384], P('hid')
- adapter_down_gradient: float32 [2, 16384, 16], P(None, 'hid')
- adapter_up_gradient: float32 [2, 16, 26624], P(None, None, 'ffn')
All inputs are finite; a program needn't handle non-finite values.
Results may differ from a plain program's by a relative error of at most 0.0068.
Values may be sent and summed in bfloat16 or wider, within the bound.
No kernel may reach another device: no remote copies, remote signals or barrier semaphores. Data moves between devices by JAX's collectives and lax.ppermute only.
A program may use at most 256 MiB of HBM per device.

v0:
```python
import jax
import jax.numpy as jnp
from jax import lax
from jax.sharding import PartitionSpec as P

MODEL_WIDTH = 16384


ADAPTER_SCALE = 0.5


def gated_layer_backward(
    preactivation_values, adapter_input_rows, adapter_up_factors, incoming_gradient
):
    activation_values = preactivation_values + ADAPTER_SCALE * jnp.einsum(
        "dch,chn->dcn", adapter_input_rows, adapter_up_factors, preferred_element_type=jnp.float32
    )
    gate_values = activation_values[:, 0]
    up_projection_values = activation_values[:, 1]
    sigma = jax.nn.sigmoid(gate_values)
    flow = incoming_gradient.astype(jnp.float32)
    gate_grad = flow * up_projection_values * sigma * (1.0 + gate_values * (1.0 - sigma))
    upper_grad = flow * gate_values * sigma
    return jnp.stack([gate_grad, upper_grad], axis=1).astype(jnp.bfloat16)


def local(
    stream,
    steering,
    strength,
    norm_gain_vector,
    frozen_weights,
    adapter_down_factors,
    adapter_up_factors,
    cotangent,
):
    rows = stream.astype(jnp.float32)
    row_squares = jnp.sum(rows * rows, axis=1)
    steer_power = jnp.sum(steering * steering)
    total_rows, total_steer = lax.psum((row_squares, steer_power), "hid")
    stream_ms = total_rows / MODEL_WIDTH + 1e-06
    steer_ms = total_steer / MODEL_WIDTH + 1e-06
    scale = strength * jnp.sqrt(stream_ms / steer_ms)
    steered = rows + scale[:, None] * steering[None, :]
    steered_power = lax.psum(jnp.sum(steered * steered, axis=1), "hid")
    inv_rms = lax.rsqrt(steered_power / MODEL_WIDTH + 1e-05)
    normalized_input = (steered * inv_rms[:, None] * norm_gain_vector[None, :]).astype(jnp.bfloat16)
    down_piece = jnp.einsum(
        "jq,hqp->jhp", normalized_input, adapter_down_factors, preferred_element_type=jnp.float32
    )
    weights = lax.all_gather(frozen_weights, "dp", axis=0, tiled=True)
    full_acts = jnp.einsum(
        "td,kdf->tkf", normalized_input, weights, preferred_element_type=jnp.float32
    )
    preactivation_values, adapter_sum = lax.psum((full_acts, down_piece), "hid")
    incoming_gradient = lax.all_gather(cotangent, "hid", axis=0, tiled=True)
    adapter_input_rows = adapter_sum.astype(jnp.bfloat16)
    activation_gradient = gated_layer_backward(
        preactivation_values, adapter_input_rows, adapter_up_factors, incoming_gradient
    )
    grad_share = lax.psum_scatter(
        jnp.einsum("tkf,kdf->td", activation_gradient, weights, preferred_element_type=jnp.float32),
        "ffn",
        scatter_dimension=0,
        tiled=True,
    )
    input_frozen_term = lax.all_gather(grad_share, "ffn", axis=0, tiled=True)
    backward_piece = jnp.einsum(
        "sua,uqa->suq", activation_gradient, adapter_up_factors, preferred_element_type=jnp.float32
    )
    back_sum = lax.psum(backward_piece, "ffn")
    lowrank_backward = back_sum.astype(jnp.bfloat16)
    normalized_gradient = input_frozen_term + ADAPTER_SCALE * jnp.einsum(
        "qme,mfe->qf", lowrank_backward, adapter_down_factors, preferred_element_type=jnp.float32
    )
    product = (
        lax.psum(jnp.sum(steered * norm_gain_vector[None, :] * normalized_gradient, axis=1), "hid")
        / MODEL_WIDTH
    )
    steered_grad = (
        inv_rms[:, None] * norm_gain_vector[None, :] * normalized_gradient
        - (inv_rms**3 * product)[:, None] * steered
    )
    residual_stream_gradient = steered_grad.astype(jnp.bfloat16)
    steering_part = jnp.sum(scale[:, None] * steered_grad, axis=0)
    down_projection_gradient = ADAPTER_SCALE * jnp.einsum(
        "cl,can->aln", normalized_input, lowrank_backward, preferred_element_type=jnp.float32
    )
    up_projection_gradient = ADAPTER_SCALE * jnp.einsum(
        "qyj,qyi->yji", adapter_input_rows, activation_gradient, preferred_element_type=jnp.float32
    )
    down_projection_gradient, up_projection_gradient, steering_vector_gradient = lax.psum(
        (down_projection_gradient, up_projection_gradient, steering_part), "dp"
    )
    return (
        residual_stream_gradient,
        steering_vector_gradient,
        down_projection_gradient,
        up_projection_gradient,
    )


def solution(mesh):
    in_specs = (
        P("dp", "hid"),
        P("hid"),
        P("dp"),
        P("hid"),
        P("dp", "hid", "ffn"),
        P(None, "hid", None),
        P(None, None, "ffn"),
        P(("dp", "hid"), "ffn"),
    )
    out_specs = (P("dp", "hid"), P("hid"), P(None, "hid", None), P(None, None, "ffn"))
    return jax.shard_map(local, mesh=mesh, in_specs=in_specs, out_specs=out_specs, check_vma=False)
```

profile of v0, /device:TPU:0, one launch (start us, length us, event | category | flops | bytes accessed | tf_op | source)
XLA Modules:
  0.0 1841.9 jit_solution(14847296424243961605)
XLA Ops:
  7.2 0.0 copy-start
  7.2 0.0 copy-start.3
  7.2 0.0 copy-start.1
  7.2 0.0 copy-start.5
  7.2 0.0 all-gather.6.cloned.1.call-start
  7.3 0.7 all-gather.6.cloned.1.call-update
  7.9 0.0 copy-start.4
  8.0 0.0 all-reduce.5.cloned.1.call-start
  8.0 0.0 copy-done.3
  8.0 0.6 multiply_reduce_fusion.3
  8.6 0.2 copy-done.1
  8.8 0.5 fusion.8
  9.3 9.0 all-reduce
  19.0 0.0 copy-done.5
  19.0 0.8 multiply_reduce_fusion.2
  19.9 5.8 psum.72
  25.6 0.0 copy-done.4
  25.6 2.7 multiply_convert_fusion
  28.3 1226.2 %all-gather.6.cloned.1.call-done = bf16[2,4096,6656]{2,1,0:T(8,128)(2,1)} async-done(((bf16[1,4096,6656]{2,1,0:T(8,128)(2,1)}), bf16[2,4096,6656]{2,1,0:T(8,128)(2,1)}) %all-gather.6.cloned.1.call-update) | async-done | bytes 109051920 | tf_op jit(solution)/shard_map/all_gather | solution.py:51
  1254.5 44.7 %fusion.12 = f32[256,2,6656]{2,0,1:T(8,128)} fusion(bf16[2,4096,6656]{2,1,0:T(8,128)(2,1)} %all-gather.6.cloned.1.call-done, bf16[256,4096]{1,0:T(8,128)(2,1)} %multiply_convert_fusion), kind=kOutput, calls=%fused_computation.30 | convolution fusion | flops 27917287424 | bytes 124780544 | tf_op jit(solution)/shard_map/td,kdf->tkf/dot_general | solution.py:52
  1299.2 0.0 copy-start.2
  1299.2 0.0 all-reduce.5.cloned.1.call-update
  1299.3 0.0 all-gather.4.cloned.1.call-start
  1299.3 0.7 all-gather.4.cloned.1.call-update
  1300.0 0.0 reduce-scatter.2.cloned.1.call-start
  1300.1 0.1 copy-done.2
  1300.2 2.3 fusion.24
  1302.5 12.3 psum.74
  1314.9 222.7 %all-reduce.5.cloned.1.call-done = f32[256,2,6656]{2,0,1:T(8,128)} async-done(((f32[256,2,6656]{2,0,1:T(8,128)}), f32[256,2,6656]{2,0,1:T(8,128)}) %all-reduce.5.cloned.1.call-update) | async-done | bytes 13631504 | tf_op jit(solution)/shard_map/psum | solution.py:55
  1537.6 0.0 copy-done
  1537.6 12.4 bitcast_add_fusion
  1550.0 19.4 %all-gather.4.cloned.1.call-done = bf16[256,6656]{1,0:T(8,128)(2,1)} async-done(((bf16[64,6656]{1,0:T(8,128)(2,1)}), bf16[256,6656]{1,0:T(8,128)(2,1)}) %all-gather.4.cloned.1.call-update) | async-done | bytes 3407888 | tf_op jit(solution)/shard_map/all_gather | solution.py:56
  1569.4 9.2 fusion.10
  1578.6 43.2 %convolution_bitcast_fusion.1 = f32[256,4096]{1,0:T(8,128)} fusion(bf16[2,4096,6656]{2,1,0:T(8,128)(2,1)} %all-gather.6.cloned.1.call-done, bf16[256,1,6656]{2,0,1:T(8,128)(2,1)} %get-tuple-element.11, bf16[256,1,6656]{2,0,1:T(8,128)(2,1)} %get-tuple-element.10), kind=kOutput, calls=%fused_computation.16 | convolution fusion | flops 27920695296 | bytes 120061952 | tf_op jit(solution)/shard_map/tkf,kdf->td/dot_general | solution.py:62
  1621.7 0.0 reduce-scatter.2.cloned.1.call-update
  1621.8 0.0 all-gather.8.cloned.1.call-start
  1621.8 76.9 %reduce-scatter.2.cloned.1.call-done = f32[64,4096]{1,0:T(8,128)} async-done(((f32[256,4096]{1,0:T(8,128)}), f32[64,4096]{1,0:T(8,128)}) %reduce-scatter.2.cloned.1.call-update) | async-done | bytes 1048592 | tf_op jit(solution)/shard_map/reduce_scatter | solution.py:61
  1698.7 0.0 all-gather.8.cloned.1.call-update
  1698.7 0.0 all-reduce.7.cloned.1.call-start
  1698.7 4.0 fusion.15
  1702.7 19.3 %psum.75 = bf16[256,2,16]{0,2,1:T(8,128)(2,1)S(1)} all-reduce(f32[256,2,16]{0,2,1:T(8,128)S(1)} %fusion.15), channel_id=1, replica_groups=mesh['dp'=2,'ffn'=4,'hid'=4] {'ffn'}, use_global_device_ids=true, to_apply=%region_9.0 | all-reduce | flops 8192 | bytes 49152 | tf_op jit(solution)/shard_map/psum | solution.py:71
  1722.1 2.9 fusion.7
  1725.0 4.5 convolution_multiply_fusion
  1729.5 0.0 all-reduce.7.cloned.1.call-update
  1729.5 52.3 %all-gather.8.cloned.1.call-done = f32[256,4096]{1,0:T(8,128)} async-done(((f32[64,4096]{1,0:T(8,128)}), f32[256,4096]{1,0:T(8,128)}) %all-gather.8.cloned.1.call-update) | async-done | bytes 4194320 | tf_op jit(solution)/shard_map/all_gather | solution.py:67
  1781.9 5.5 multiply_reduce_fusion.1
  1787.3 7.0 psum.76
  1794.3 5.2 multiply_reduce_fusion
  1799.5 8.8 psum.77
  1808.3 22.8 %all-reduce.7.cloned.1.call-done = (f32[2,4096,16]{1,2,0:T(8,128)}, f32[2,16,6656]{2,1,0:T(8,128)}) async-done(((f32[2,4096,16]{1,2,0:T(8,128)}, f32[2,16,6656]{2,1,0:T(8,128)}), (f32[2,4096,16]{1,2,0:T(8,128)}, f32[2,16,6656]{2,1,0:T(8,128)})) %all-reduce.7.cloned.1.call-update) | async-done | bytes 1376272 | tf_op jit(solution)/shard_map/psum | solution.py:92
  1831.1 1.9 copy.15
  1833.0 2.1 copy.16
  (3 shorter events, 0.0 us)
Async XLA Ops:
  7.2 1530.4 %copy-start = (bf16[2,16,6656]{2,1,0:T(8,128)(2,1)S(1)}, bf16[2,16,6656]{2,1,0:T(8,128)(2,1)}, u32[]{:S(2)}) copy-start(bf16[2,16,6656]{2,1,0:T(8,128)(2,1)} %param.14) | copy-start | bytes 1277956
  7.2 0.8 copy-start.3
  7.2 1.7 copy-start.1
  7.2 11.8 copy-start.5
  7.2 1247.3 %all-gather.6.cloned.1.call-start = ((), (), s32[]{:S(2)}) async-start(), calls=%async_computation.2 | async-start | bytes 163577856 | tf_op jit(solution)/shard_map/all_gather | solution.py:51
  7.9 17.7 copy-start.4
  8.0 1529.6 %all-reduce.5.cloned.1.call-start = ((), (), s32[]{:S(2)}) async-start(), calls=%async_computation.3 | async-start | bytes 27262976 | tf_op jit(solution)/shard_map/psum | solution.py:55
  1299.2 0.9 copy-start.2
  1299.3 270.1 %all-gather.4.cloned.1.call-start = ((), (), s32[]{:S(2)}) async-start(), calls=%async_computation.1 | async-start | bytes 4259840 | tf_op jit(solution)/shard_map/all_gather | solution.py:56
  1300.0 398.7 %reduce-scatter.2.cloned.1.call-start = ((), (), s32[]{:S(2)}) async-start(), calls=%async_computation.4 | async-start | bytes 5242880 | tf_op jit(solution)/shard_map/reduce_scatter | solution.py:61
  1621.8 160.1 %all-gather.8.cloned.1.call-start = ((), (), s32[]{:S(2)}) async-start(), calls=%async_computation.5 | async-start | bytes 5242880 | tf_op jit(solution)/shard_map/all_gather | solution.py:67
  1698.7 132.4 %all-reduce.7.cloned.1.call-start = ((), (), s32[]{:S(2)}) async-start(), calls=%async_computation.6 | async-start | bytes 2752512 | tf_op jit(solution)/shard_map/psum | solution.py:92
Sparse Core Ops, SparseCore 0:
  9.6 1244.9 all-gather.5
  1299.4 238.1 all-reduce.4
  1539.1 30.2 all-gather.3
  1621.9 76.7 reduce-scatter.1
  1700.2 81.6 all-gather.7
  1784.7 46.3 all-reduce.6
where the time goes:
time: 1840 us
  waiting for transfers between devices  1620 us (88%)
  matrix products  119 us (6%)
  blocking collectives  62.2 us (3%)
  other arithmetic  19 us (1%)
    all_gather x1, waiting for transfers between devices, local(): weights = lax.all_gather(frozen_weights, 'dp', axis=0, tiled=True)  1230 us
    psum x1, waiting for transfers between devices, local(): preactivation_values, adapter_sum = lax.psum((full_acts, down_piece), 'hid')  223 us
    reduce_scatter x1, waiting for transfers between devices, local(): lax.psum_scatter(jnp.einsum('tkf,kdf->td', activation_gradient, weights,...  76.9 us
    all_gather x1, waiting for transfers between devices, local(): input_frozen_term = lax.all_gather(grad_share, 'ffn', axis=0, tiled=True)  52.3 us
    dot_general x1, matrix products, local(): jnp.einsum('td,kdf->tkf', normalized_input, weights, preferred_element_ty...  44.7 us
    dot_general x1, matrix products, local(): jnp.einsum('tkf,kdf->td', activation_gradient, weights, preferred_element...  43.2 us
  transfers between devices with their start and end apart: 6, of which 6 were waited for; matrix products, arithmetic and copies ran while one was open for 2% of the time, Pallas kernels for 0%

commit v1 on v0

v1 whole, which is shorter than its diff:
```python
import jax
import jax.numpy as jnp
from jax import lax
from jax.experimental import pallas as pl
from jax.experimental.pallas import tpu as pltpu
from jax.sharding import PartitionSpec as P

MODEL_WIDTH = 16384
ADAPTER_SCALE = 0.5
HIDDEN_CHUNKS = 2
WIDTH_CHUNKS = 4
VMEM_BYTES = 48 * 1024 * 1024

F32 = jnp.float32
BF16 = jnp.bfloat16


def bits_of(n):
    return n.bit_length() - 1


def reversed_bits(x, n):
    out = 0
    for i in range(n):
        out = out + (((x >> i) & 1) << (n - 1 - i))
    return out


def tile_of(n, cap):
    return max(t for t in range(128, cap + 1, 128) if n % t == 0)


def split_tiles(count, parts):
    edges = [count * i // parts for i in range(parts + 1)]
    return [(a, b - a) for a, b in zip(edges, edges[1:]) if b > a]


def take_blocks(x, sources, block):
    pieces = [lax.dynamic_slice_in_dim(x, s * block, block, axis=0) for s in sources]
    return jnp.concatenate(pieces, axis=0)


def to_relative(x, me, n):
    b = bits_of(n)
    return take_blocks(x, [me ^ reversed_bits(p, b) for p in range(n)], x.shape[0] // n)


def from_relative(x, me, n):
    b = bits_of(n)
    return take_blocks(x, [reversed_bits(t ^ me, b) for t in range(n)], x.shape[0] // n)


def relative_to_relative(x, me, n, other, m):
    count = max(n, m)
    rn, rm = count // n, count // m
    sources = []
    for p in range(count):
        natural = (reversed_bits(p // rm, bits_of(m)) ^ other) * rm + p % rm
        sources.append(reversed_bits((natural // rn) ^ me, bits_of(n)) * rn + natural % rn)
    return take_blocks(x, sources, x.shape[0] // count)


def swap(x, axis, n, mask):
    return lax.ppermute(x, axis, [(i, i ^ mask) for i in range(n)])


def halve(keep, send, axis, n, bit=0):
    received = swap(send, axis, n, 1 << bit)
    total = keep + received.astype(F32)
    if bit + 1 == bits_of(n):
        return total
    half = total.shape[0] // 2
    return halve(total[:half], total[half:].astype(BF16), axis, n, bit + 1)


def double(x, axis, n):
    for bit in reversed(range(bits_of(n))):
        x = jnp.concatenate([x, swap(x, axis, n, 1 << bit)], axis=0)
    return x


def forward_kernel(x_ref, w_ref, keep_ref, send_ref):
    y = jnp.dot(x_ref[...], w_ref[0], preferred_element_type=F32)
    half = keep_ref.shape[0]
    keep_ref[...] = y[:half]
    send_ref[...] = y[half:].astype(BF16)


def forward_matmul(x, weights, first, tiles, tile):
    rows, depth = x.shape
    half = rows // 2
    return pl.pallas_call(
        forward_kernel,
        grid=(tiles,),
        in_specs=[
            pl.BlockSpec((rows, depth), lambda i: (0, 0)),
            pl.BlockSpec((1, depth, tile), lambda i: (0, 0, first + i)),
        ],
        out_specs=[pl.BlockSpec((half, tile), lambda i: (0, i))] * 2,
        out_shape=[
            jax.ShapeDtypeStruct((half, tiles * tile), F32),
            jax.ShapeDtypeStruct((half, tiles * tile), BF16),
        ],
        compiler_params=pltpu.CompilerParams(vmem_limit_bytes=VMEM_BYTES),
        cost_estimate=pl.CostEstimate(
            flops=2 * rows * depth * tiles * tile,
            bytes_accessed=2 * depth * (rows + tiles * tile) + 6 * half * tiles * tile,
            transcendentals=0,
        ),
        name="forward_matmul",
    )(x, weights)


def backward_kernel(*refs):
    *g_refs, w_ref, keep_ref, send_ref = refs
    y, at = None, 0
    for g_ref in g_refs:
        width = g_ref.shape[1]
        part = lax.dot_general(
            g_ref[...], w_ref[0, :, at : at + width], (((1,), (1,)), ((), ())), preferred_element_type=F32
        )
        y = part if y is None else y + part
        at += width
    half = keep_ref.shape[0]
    keep_ref[...] = y[:half]
    send_ref[...] = y[half:].astype(BF16)


def backward_matmul(grads, weights, first, tiles, tile):
    rows = grads[0].shape[0]
    half, hidden = rows // 2, weights.shape[2]
    return pl.pallas_call(
        backward_kernel,
        grid=(tiles,),
        in_specs=[pl.BlockSpec(g.shape, lambda i: (0, 0)) for g in grads]
        + [pl.BlockSpec((1, tile, hidden), lambda i: (0, first + i, 0))],
        out_specs=[pl.BlockSpec((half, tile), lambda i: (0, i))] * 2,
        out_shape=[
            jax.ShapeDtypeStruct((half, tiles * tile), F32),
            jax.ShapeDtypeStruct((half, tiles * tile), BF16),
        ],
        compiler_params=pltpu.CompilerParams(vmem_limit_bytes=VMEM_BYTES),
        cost_estimate=pl.CostEstimate(
            flops=2 * rows * hidden * tiles * tile,
            bytes_accessed=2 * hidden * (rows + tiles * tile) + 6 * half * tiles * tile,
            transcendentals=0,
        ),
        name="backward_matmul",
    )(*grads, weights)


def make_local(dp, hid, ffn):
    def local(stream, steering, strength, gain, weights, down, up, cotangent):
        d, h, f = lax.axis_index("dp"), lax.axis_index("hid"), lax.axis_index("ffn")
        tokens, width = stream.shape
        hidden = weights.shape[2]
        own = tokens // hid
        rank = down.shape[2]
        first_pair = d == 0

        peer_stream = swap(stream, "dp", dp, 1)
        rows = stream.astype(F32)
        total_rows, total_steer = lax.psum(
            (jnp.sum(rows * rows, axis=1), jnp.sum(steering * steering)), "hid"
        )
        stream_ms = total_rows / MODEL_WIDTH + 1e-06
        steer_ms = total_steer / MODEL_WIDTH + 1e-06
        scale = strength * jnp.sqrt(stream_ms / steer_ms)
        steered = rows + scale[:, None] * steering[None, :]
        steered_power = lax.psum(jnp.sum(steered * steered, axis=1), "hid")
        inv_rms = lax.rsqrt(steered_power / MODEL_WIDTH + 1e-05)
        stats = jnp.stack([scale, inv_rms], axis=1)
        peer_stats = swap(stats, "dp", dp, 1)

        def normalize(rows, stats):
            steered = rows.astype(F32) + stats[:, :1] * steering[None, :]
            return (steered * stats[:, 1:] * gain[None, :]).astype(BF16)

        normed = [
            normalize(to_relative(r, h, hid), to_relative(s, h, hid))
            for r, s in ((stream, stats), (peer_stream, peer_stats))
        ]

        tile = tile_of(hidden, 256)
        chunks = split_tiles(hidden // tile, HIDDEN_CHUNKS)
        acts = [
            [
                halve(*forward_matmul(x, weights, first, count, tile), "hid", hid)
                for first, count in chunks
            ]
            for x in normed
        ]

        low_part = jnp.concatenate(
            [
                from_relative(
                    jnp.einsum("td,kdr->tkr", x, down, preferred_element_type=F32).reshape(tokens, 2 * rank), h, hid
                )
                for x in normed
            ],
            axis=0,
        )
        low = jnp.sum(lax.all_gather(low_part, "hid", axis=0), axis=0).astype(BF16)
        low_own = lax.dynamic_slice_in_dim(low[:tokens], h * own, own, axis=0)

        grads, back_part, up_parts = [], 0.0, []
        low_mine = jnp.concatenate(
            [to_relative(part, f, ffn) for part in (low[:tokens], low[tokens:])], axis=0
        )
        low_mine = jnp.where(first_pair, low_mine[:, :rank], low_mine[:, rank:])
        for c, (first, count) in enumerate(chunks):
            columns = slice(first * tile, (first + count) * tile)
            mine = acts[0][c]
            other = swap(acts[1][c].astype(BF16), "dp", dp, 1).astype(F32)
            factors = up[:, :, columns]
            gate = jnp.where(first_pair, mine, other) + ADAPTER_SCALE * jnp.dot(
                low_own[:, :rank], factors[0], preferred_element_type=F32
            )
            upper = jnp.where(first_pair, other, mine) + ADAPTER_SCALE * jnp.dot(
                low_own[:, rank:], factors[1], preferred_element_type=F32
            )
            sigma = jax.nn.sigmoid(gate)
            flow = cotangent[:, columns].astype(F32)
            gate_grad = (flow * upper * sigma * (1.0 + gate * (1.0 - sigma))).astype(BF16)
            upper_grad = (flow * gate * sigma).astype(BF16)
            back_part = back_part + jnp.concatenate(
                [
                    lax.dot_general(g, factors[k], (((1,), (1,)), ((), ())), preferred_element_type=F32)
                    for k, g in enumerate((gate_grad, upper_grad))
                ],
                axis=1,
            )
            mine_grad = jnp.where(first_pair, gate_grad, upper_grad)
            peer_grad = swap(jnp.where(first_pair, upper_grad, gate_grad), "dp", dp, 1)
            whole = jnp.concatenate(
                [
                    relative_to_relative(double(g, "hid", hid), h, hid, f, ffn)
                    for g in (mine_grad, peer_grad)
                ],
                axis=0,
            )
            grads.append(whole)
            up_parts.append(
                ADAPTER_SCALE
                * lax.dot_general(low_mine, whole, (((0,), (0,)), ((), ())), preferred_element_type=F32)
            )

        up_mine = jnp.concatenate(up_parts, axis=1)
        up_other = swap(up_mine.astype(BF16), "dp", dp, 1).astype(F32)
        up_gradient = jnp.where(
            first_pair, jnp.stack([up_mine, up_other]), jnp.stack([up_other, up_mine])
        )

        back = lax.all_gather(back_part, ("dp", "hid", "ffn"), axis=0).reshape(dp, hid, ffn, own, 2 * rank)
        back = jnp.sum(back, axis=2).astype(BF16).reshape(dp, tokens, 2 * rank)
        back_own = lax.dynamic_index_in_dim(back, d, axis=0, keepdims=False)
        back_peer = lax.dynamic_index_in_dim(back, 1 - d, axis=0, keepdims=False)
        back_normed = jnp.concatenate([to_relative(b, h, hid) for b in (back_own, back_peer)], axis=0)
        all_normed = jnp.concatenate(normed, axis=0)
        down_gradient = jnp.stack(
            [
                ADAPTER_SCALE
                * lax.dot_general(
                    all_normed,
                    back_normed[:, k * rank : (k + 1) * rank],
                    (((0,), (0,)), ((), ())),
                    preferred_element_type=F32,
                )
                for k in range(2)
            ]
        )

        width_tile = tile_of(width, 256)
        shard = tokens // ffn
        back_shard = lax.dynamic_slice_in_dim(back_own, f * shard, shard, axis=0)
        stream_shard = lax.dynamic_slice_in_dim(stream, f * shard, shard, axis=0)
        stats_shard = lax.dynamic_slice_in_dim(stats, f * shard, shard, axis=0)
        down_rows = jnp.concatenate([down[0], down[1]], axis=1)

        def low_rank_term(b, columns):
            return ADAPTER_SCALE * lax.dot_general(
                b, down_rows[columns], (((1,), (1,)), ((), ())), preferred_element_type=F32
            )

        inner, gathered = 0.0, []
        for first, count in split_tiles(width // width_tile, WIDTH_CHUNKS):
            columns = slice(first * width_tile, (first + count) * width_tile)
            keep, send = backward_matmul(grads, weights, first, count, width_tile)
            part = keep + swap(send, "dp", dp, 1).astype(F32)
            half = tokens // 2
            share = halve(part[:half], part[half:].astype(BF16), "ffn", ffn)
            steered_shard = stream_shard[:, columns].astype(F32) + stats_shard[:, :1] * steering[None, columns]
            inner = inner + jnp.sum(
                steered_shard * gain[None, columns] * (share + low_rank_term(back_shard, columns)), axis=1
            )
            gathered.append(from_relative(double(share.astype(BF16), "ffn", ffn), f, ffn))
        inner = lax.all_gather(inner, ("hid", "ffn"), axis=0).reshape(hid, tokens)
        dot = jnp.sum(inner, axis=0) / MODEL_WIDTH

        normed_grad = jnp.concatenate(gathered, axis=1).astype(F32) + low_rank_term(back_own, slice(None))
        steered_grad = (
            inv_rms[:, None] * gain[None, :] * normed_grad
            - (inv_rms**3 * dot)[:, None] * (stream.astype(F32) + scale[:, None] * steering[None, :])
        )
        steering_gradient = lax.psum(jnp.sum(scale[:, None] * steered_grad, axis=0), "dp")
        return steered_grad.astype(BF16), steering_gradient, down_gradient, up_gradient

    return local


def solution(mesh):
    in_specs = (
        P("dp", "hid"),
        P("hid"),
        P("dp"),
        P("hid"),
        P("dp", "hid", "ffn"),
        P(None, "hid", None),
        P(None, None, "ffn"),
        P(("dp", "hid"), "ffn"),
    )
    out_specs = (P("dp", "hid"), P("hid"), P(None, "hid", None), P(None, None, "ffn"))
    local = make_local(mesh.shape["dp"], mesh.shape["hid"], mesh.shape["ffn"])
    return jax.shard_map(local, mesh=mesh, in_specs=in_specs, out_specs=out_specs, check_vma=False)
```

time: 1840 us -> 558 us (0.30)
  waiting for transfers between devices: 1620 us -> 170 us
  Pallas kernels: 0 us -> 112 us
  blocking collectives: 62.2 us -> 132 us
  matrix products: 119 us -> 52.4 us
  starting transfers between devices: 0.24 us -> 36 us
    all_gather x3 -> x0, waiting for transfers between devices: 1300 us -> none  [the longest x1 1230 us: local(): weights = lax.all_gather(frozen_weights, 'dp', axis=0, tiled=True)]
    psum x2 -> x0, waiting for transfers between devices: 246 us -> none  [the longest x1 223 us: local(): preactivation_values, adapter_sum = lax.psum((full_acts, down_piece), 'hid')]
    ppermute x0 -> x43, waiting for transfers between devices: none -> 170 us  [swap(): return lax.ppermute(x, axis, [(i, i ^ mask) for i in range(n)])]
    pallas_call x0 -> x8, Pallas kernels: none -> 112 us  [the longest x4 68.6 us: forward_matmul(): pl.pallas_call(forward_kernel, grid=(tiles,), in_specs=[pl.BlockSpec((row...]
    all_gather x0 -> x2, blocking collectives: none -> 78 us  [the longest x1 71.7 us: local(): lax.all_gather(back_part, ('dp', 'hid', 'ffn'), axis=0)]
    reduce_scatter x1 -> x0, waiting for transfers between devices: 76.9 us -> none  [local(): lax.psum_scatter(jnp.einsum('tkf,kdf->td', activation_gradient, weights,...]
    dot_general x7 -> x17, matrix products: 117 us -> 51 us  [the longest x5 35.5 us: low_rank_term(): lax.dot_general(b, down_rows[columns], (((1,), (1,)), ((), ())), preferre...]
    psum x5 -> x2, blocking collectives: 56.4 us -> 15.5 us  [the longest x1 8.14 us: local(): lax.psum(jnp.sum(scale[:, None] * steered_grad, axis=0), 'dp')]
  transfers between devices with their start and end apart: 6 -> 43, of which waited for: 6 -> 24; matrix products, arithmetic and copies ran while one was open for 2% -> 7% of each run, Pallas kernels for 0% -> 2%
where the time goes in v1:
time: 558 us; the launch traced here: 549 us
  waiting for transfers between devices  170 us (30%)
  blocking collectives  132 us (24%)
  Pallas kernels  112 us (20%)
  matrix products  52.4 us (9%)
  starting transfers between devices  36 us (6%)
  other arithmetic  28 us (5%)
  local copies, waits for them, and re-layouts  14.7 us (3%)
    ppermute x43, waiting for transfers between devices, swap(): return lax.ppermute(x, axis, [(i, i ^ mask) for i in range(n)])  170 us
    all_gather x1, blocking collectives, local(): lax.all_gather(back_part, ('dp', 'hid', 'ffn'), axis=0)  71.7 us
    pallas_call x4, Pallas kernels, forward_matmul(): pl.pallas_call(forward_kernel, grid=(tiles,), in_specs=[pl.BlockSpec((row...  68.6 us
    pallas_call x4, Pallas kernels, backward_matmul(): pl.pallas_call(backward_kernel, grid=(tiles,), in_specs=[pl.BlockSpec(g.s...  43.8 us
    ppermute x43, starting transfers between devices, swap(): return lax.ppermute(x, axis, [(i, i ^ mask) for i in range(n)])  36 us
    dot_general x5, matrix products, low_rank_term(): lax.dot_general(b, down_rows[columns], (((1,), (1,)), ((), ())), preferre...  35.5 us
    unnamed x1, blocking collectives  32.1 us
  transfers between devices with their start and end apart: 43, of which 24 were waited for; matrix products, arithmetic and copies ran while one was open for 7% of the time, Pallas kernels for 2%

profile of v1, /device:TPU:0, one launch (start us, length us, event | category | flops | bytes accessed | tf_op | source)
XLA Modules:
  0.0 548.6 jit_solution(8510707784493842341)
XLA Ops:
  0.7 3.0 collective-permute-start
  3.7 2.1 fusion.5
  5.8 1.4 multiply_reduce_fusion.2
  7.2 7.3 %all-reduce.1 = (f32[256]{0:T(256)S(1)}, f32[]{:T(128)}) all-reduce(f32[256]{0:T(256)S(1)} %fusion.5, f32[]{:T(128)} %multiply_reduce_fusion.2), channel_id=1, replica_groups=mesh['dp'=2,'ffn'=4,'hid'=4] {'hid'}, use_global_device_ids=true, to_apply=%region_1.0 | all-reduce | flops 257 | bytes 2056 | tf_op jit(solution)/shard_map/psum | solution.py:163
  15.9 1.5 multiply_reduce_fusion.1
  17.4 6.1 %psum.30 = f32[256]{0:T(256)S(1)} all-reduce(f32[256]{0:T(256)S(1)} %multiply_reduce_fusion.1), channel_id=1, replica_groups=mesh['dp'=2,'ffn'=4,'hid'=4] {'hid'}, use_global_device_ids=true, to_apply=%region_5.0 | all-reduce | flops 256 | bytes 2048 | tf_op jit(solution)/shard_map/psum | solution.py:170
  29.4 20.3 %collective-permute-done.1 = f32[256,2]{0,1:T(2,128)S(1)} collective-permute-done((f32[256,2]{0,1:T(2,128)S(1)}, f32[256,2]{0,1:T(2,128)S(1)}, u32[]{:S(2)}, u32[]{:S(2)}) %collective-permute-start.1) | collective-permute-done | bytes 2080 | tf_op jit(solution)/shard_map/ppermute | solution.py:64
  49.8 1.7 constant_dynamic-slice_fusion.64
  51.6 4.8 multiply_convert_fusion
  56.4 18.2 %forward_matmul.7 = (f32[128,3328]{1,0:T(8,128)S(1)}, bf16[128,3328]{1,0:T(8,128)(2,1)}) custom-call(bf16[256,4096]{1,0:T(8,128)(2,1)S(1)} %get-tuple-element.90.x_ref, bf16[1,4096,6656]{2,1,0:T(8,128)(2,1)} %refs_2_.7), custom_call_target="tpu_custom_call" | custom-call | flops 6979321856 | bytes 31916032 | tf_op jit(solution)/shard_map/forward_matmul/pallas_call | solution.py:92
  75.8 16.6 %forward_matmul.5 = (f32[128,3328]{1,0:T(8,128)S(1)}, bf16[128,3328]{1,0:T(8,128)(2,1)S(1)}) custom-call(bf16[256,4096]{1,0:T(8,128)(2,1)S(1)} %get-tuple-element.90.x_ref, bf16[1,4096,6656]{2,1,0:T(8,128)(2,1)} %refs_2_.7), custom_call_target="tpu_custom_call" | custom-call | flops 6979321856 | bytes 31916032 | tf_op jit(solution)/shard_map/forward_matmul/pallas_call | solution.py:92
  94.4 16.6 %forward_matmul.6 = (f32[128,3328]{1,0:T(8,128)S(1)}, bf16[128,3328]{1,0:T(8,128)(2,1)S(1)}) custom-call(bf16[256,4096]{1,0:T(8,128)(2,1)S(1)} %get-tuple-element.91.x_ref, bf16[1,4096,6656]{2,1,0:T(8,128)(2,1)} %refs_2_.7), custom_call_target="tpu_custom_call" | custom-call | flops 6979321856 | bytes 31916032 | tf_op jit(solution)/shard_map/forward_matmul/pallas_call | solution.py:92
  111.0 17.2 %forward_matmul.4 = (f32[128,3328]{1,0:T(8,128)S(1)}, bf16[128,3328]{1,0:T(8,128)(2,1)S(1)}) custom-call(bf16[256,4096]{1,0:T(8,128)(2,1)S(1)} %get-tuple-element.91.x_ref, bf16[1,4096,6656]{2,1,0:T(8,128)(2,1)} %refs_2_.7), custom_call_target="tpu_custom_call" | custom-call | flops 6979321856 | bytes 31916032 | tf_op jit(solution)/shard_map/forward_matmul/pallas_call | solution.py:92
  130.7 6.3 %all-gather = f32[2048,32]{0,1:T(8,128)S(1)} all-gather(f32[512,32]{0,1:T(8,128)S(1)} %concatenate.139), channel_id=2, replica_groups=mesh['dp'=2,'ffn'=4,'hid'=4] {'hid'}, dimensions={0}, use_global_device_ids=true | all-gather | bytes 327680 | tf_op jit(solution)/shard_map/all_gather | solution.py:203
  138.3 2.4 convolution_multiply_fusion.3
  140.6 2.2 convolution_multiply_fusion.1
  142.8 1.8 convert_add_fusion.1
  145.5 1.7 collective-permute-start.16
  147.2 1.3 convert_add_fusion.3
  149.8 1.4 convert_add_fusion.4
  151.3 1.6 collective-permute-start.3
  152.9 1.4 convert_add_fusion.2
  154.9 21.7 %collective-permute-done.3 = bf16[64,3328]{1,0:T(8,128)(2,1)S(1)} collective-permute-done((bf16[64,3328]{1,0:T(8,128)(2,1)S(1)}, bf16[64,3328]{1,0:T(8,128)(2,1)S(1)}, u32[]{:S(2)}, u32[]{:S(2)}) %collective-permute-start.3) | collective-permute-done | bytes 426016 | tf_op jit(solution)/shard_map/ppermute | solution.py:64
  177.4 1.7 collective-permute-start.4
  179.1 5.8 %collective-permute-done.13 = bf16[64,3328]{1,0:T(8,128)(2,1)S(1)} collective-permute-done((bf16[64,3328]{1,0:T(8,128)(2,1)S(1)}, bf16[64,3328]{1,0:T(8,128)(2,1)S(1)}, u32[]{:S(2)}, u32[]{:S(2)}) %collective-permute-start.13) | collective-permute-done | bytes 426016 | tf_op jit(solution)/shard_map/ppermute | solution.py:64
  185.8 1.7 collective-permute-start.14
  188.0 2.4 fusion.20
  190.5 6.8 %collective-permute-done.14 = bf16[64,3328]{1,0:T(8,128)(2,1)} collective-permute-done((bf16[64,3328]{1,0:T(8,128)(2,1)}, bf16[64,3328]{1,0:T(8,128)(2,1)}, u32[]{:S(2)}, u32[]{:S(2)}) %collective-permute-start.14) | collective-permute-done | bytes 426016 | tf_op jit(solution)/shard_map/ppermute | solution.py:64
  197.3 3.5 broadcast_select_fusion
  201.8 71.7 %all_gather.16 = f32[32,64,32]{1,2,0:T(8,128)S(1)} all-gather(f32[1,64,32]{1,2,0:T(8,128)S(1)} %maximum_add_fusion), channel_id=1, replica_groups=mesh['dp'=2,'ffn'=4,'hid'=4] {'dp','hid','ffn'}, dimensions={0}, use_global_device_ids=true | all-gather | bytes 270336 | tf_op jit(solution)/shard_map/all_gather | solution.py:254
  274.0 2.4 fusion.3
  277.0 2.0 collective-permute-start.17
  279.3 1.8 collective-permute-start.9
  281.9 6.3 %collective-permute-done.7 = bf16[64,3328]{1,0:T(8,128)(2,1)S(1)} collective-permute-done((bf16[64,3328]{1,0:T(8,128)(2,1)S(1)}, bf16[64,3328]{1,0:T(8,128)(2,1)S(1)}, u32[]{:S(2)}, u32[]{:S(2)}) %collective-permute-start.7) | collective-permute-done | bytes 426016 | tf_op jit(solution)/shard_map/ppermute | solution.py:64
  288.4 4.4 collective-permute-done.17
  295.2 10.5 %collective-permute-done.20 = bf16[64,3328]{1,0:T(8,128)(2,1)S(1)} collective-permute-done((bf16[64,3328]{1,0:T(8,128)(2,1)S(1)}, bf16[64,3328]{1,0:T(8,128)(2,1)S(1)}, u32[]{:S(2)}, u32[]{:S(2)}) %collective-permute-start.20) | collective-permute-done | bytes 426016 | tf_op jit(solution)/shard_map/ppermute | solution.py:64
  305.8 8.5 %collective-permute-done.10 = bf16[64,3328]{1,0:T(8,128)(2,1)S(1)} collective-permute-done((bf16[64,3328]{1,0:T(8,128)(2,1)S(1)}, bf16[64,3328]{1,0:T(8,128)(2,1)S(1)}, u32[]{:S(2)}, u32[]{:S(2)}) %collective-permute-start.10) | collective-permute-done | bytes 426016 | tf_op jit(solution)/shard_map/ppermute | solution.py:64
  315.2 1.6 collective-permute-done.11
  319.0 11.0 %backward_matmul.7 = (f32[256,1024]{1,0:T(8,128)S(1)}, bf16[256,1024]{1,0:T(8,128)(2,1)S(1)}) custom-call(bf16[512,3328]{1,0:T(8,128)(2,1)S(1)} %dynamic-slice_dynamic-update-slice_fusion.8.refs_0_, bf16[512,3328]{1,0:T(8,128)(2,1)} %copy-done.11, bf16[1,4096,6656]{2,1,0:T(8,128)(2,1)} %refs_2_.7), custom_call_target="tpu_custom_call" | custom-call | flops 6979321856 | bytes 22020096 | tf_op jit(solution)/shard_map/backward_matmul/pallas_call | solution.py:132
  330.0 11.0 %backward_matmul.6 = (f32[256,1024]{1,0:T(8,128)S(1)}, bf16[256,1024]{1,0:T(8,128)(2,1)S(1)}) custom-call(bf16[512,3328]{1,0:T(8,128)(2,1)S(1)} %dynamic-slice_dynamic-update-slice_fusion.8.refs_0_, bf16[512,3328]{1,0:T(8,128)(2,1)} %copy-done.11, bf16[1,4096,6656]{2,1,0:T(8,128)(2,1)} %refs_2_.7), custom_call_target="tpu_custom_call" | custom-call | flops 6979321856 | bytes 22020096 | tf_op jit(solution)/shard_map/backward_matmul/pallas_call | solution.py:132
  341.0 11.0 %backward_matmul.5 = (f32[256,1024]{1,0:T(8,128)S(1)}, bf16[256,1024]{1,0:T(8,128)(2,1)S(1)}) custom-call(bf16[512,3328]{1,0:T(8,128)(2,1)S(1)} %dynamic-slice_dynamic-update-slice_fusion.8.refs_0_, bf16[512,3328]{1,0:T(8,128)(2,1)} %copy-done.11, bf16[1,4096,6656]{2,1,0:T(8,128)(2,1)} %refs_2_.7), custom_call_target="tpu_custom_call" | custom-call | flops 6979321856 | bytes 22020096 | tf_op jit(solution)/shard_map/backward_matmul/pallas_call | solution.py:132
  352.3 10.9 %backward_matmul.4 = (f32[256,1024]{1,0:T(8,128)S(1)}, bf16[256,1024]{1,0:T(8,128)(2,1)S(1)}) custom-call(bf16[512,3328]{1,0:T(8,128)(2,1)S(1)} %dynamic-slice_dynamic-update-slice_fusion.8.refs_0_, bf16[512,3328]{1,0:T(8,128)(2,1)} %copy-done.11, bf16[1,4096,6656]{2,1,0:T(8,128)(2,1)} %refs_2_.7), custom_call_target="tpu_custom_call" | custom-call | flops 6979321856 | bytes 22020096 | tf_op jit(solution)/shard_map/backward_matmul/pallas_call | solution.py:132
  363.2 1.8 collective-permute-start.37
  365.3 1.8 collective-permute-start.27
  368.3 9.7 %collective-permute-done.37 = bf16[256,1024]{1,0:T(8,128)(2,1)S(1)} collective-permute-done((bf16[256,1024]{1,0:T(8,128)(2,1)S(1)}, bf16[256,1024]{1,0:T(8,128)(2,1)S(1)}, u32[]{:S(2)}, u32[]{:S(2)}) %collective-permute-start.37) | collective-permute-done | bytes 524320 | tf_op jit(solution)/shard_map/ppermute | solution.py:64
  378.4 10.9 %collective-permute-done.32 = bf16[256,1024]{1,0:T(8,128)(2,1)S(1)} collective-permute-done((bf16[256,1024]{1,0:T(8,128)(2,1)S(1)}, bf16[256,1024]{1,0:T(8,128)(2,1)S(1)}, u32[]{:S(2)}, u32[]{:S(2)}) %collective-permute-start.32) | collective-permute-done | bytes 524320 | tf_op jit(solution)/shard_map/ppermute | solution.py:64
  389.6 10.9 %collective-permute-done.27 = bf16[256,1024]{1,0:T(8,128)(2,1)S(1)} collective-permute-done((bf16[256,1024]{1,0:T(8,128)(2,1)S(1)}, bf16[256,1024]{1,0:T(8,128)(2,1)S(1)}, u32[]{:S(2)}, u32[]{:S(2)}) %collective-permute-start.27) | collective-permute-done | bytes 524320 | tf_op jit(solution)/shard_map/ppermute | solution.py:64
  400.9 9.9 %collective-permute-done.22 = bf16[256,1024]{1,0:T(8,128)(2,1)S(1)} collective-permute-done((bf16[256,1024]{1,0:T(8,128)(2,1)S(1)}, bf16[256,1024]{1,0:T(8,128)(2,1)S(1)}, u32[]{:S(2)}, u32[]{:S(2)}) %collective-permute-start.22) | collective-permute-done | bytes 524320 | tf_op jit(solution)/shard_map/ppermute | solution.py:64
  411.2 4.6 collective-permute-start.39
  416.1 3.0 collective-permute-start.29
  419.1 3.8 collective-permute-done.23
  423.2 2.9 collective-permute-start.40
  426.1 9.1 %collective-permute-done.34 = bf16[64,1024]{1,0:T(8,128)(2,1)S(1)} collective-permute-done((bf16[64,1024]{1,0:T(8,128)(2,1)S(1)}, bf16[64,1024]{1,0:T(8,128)(2,1)S(1)}, u32[]{:S(2)}, u32[]{:S(2)}) %collective-permute-start.34) | collective-permute-done | bytes 131104 | tf_op jit(solution)/shard_map/ppermute | solution.py:64
  435.2 5.5 %collective-permute-done.29 = bf16[64,1024]{1,0:T(8,128)(2,1)S(1)} collective-permute-done((bf16[64,1024]{1,0:T(8,128)(2,1)S(1)}, bf16[64,1024]{1,0:T(8,128)(2,1)S(1)}, u32[]{:S(2)}, u32[]{:S(2)}) %collective-permute-start.29) | collective-permute-done | bytes 131104 | tf_op jit(solution)/shard_map/ppermute | solution.py:64
  442.1 4.2 collective-permute-done.24
  446.9 32.1 %all-reduce = f32[1024]{0:T(1024)S(1)} all-reduce(f32[1024]{0:T(1024)S(1)} %add_dynamic-update-slice_fusion), channel_id=3, replica_groups=mesh['dp'=2,'ffn'=4,'hid'=4] {'hid','ffn'}, use_global_device_ids=true, to_apply=%add | all-reduce | flops 1024 | bytes 8192
  481.1 2.1 collective-permute-start.36
  484.2 1.9 collective-permute-done.25
  486.3 4.5 collective-permute-done.41
  491.7 4.6 collective-permute-done.36
  497.3 4.6 collective-permute-done.31
  502.9 3.3 collective-permute-done.26
  506.3 33.9 %multiply_reduce_fusion = (f32[4096]{0:T(1024)S(1)}, bf16[256,4096]{1,0:T(8,128)(2,1)}) fusion(f32[256]{0:T(256)S(1)} %copy-done.32, f32[4096]{0:T(1024)S(1)} %copy-done.28, bf16[256,4096]{1,0:T(8,128)(2,1)S(1)} %copy-done.13, f32[256]{0:T(256)S(1)} %fusion.83, bf16[4096,16]{0,1:T(8,128)(2,1)S(1)} %copy-done.14, bf16[4096,16]{0,1:T(8,128)(2,1)S(1)} %copy-done.15, ...), kind=kOutput, calls=%fused_computation.18 | convolution fusion | flops 113766400 | bytes 6622212 | tf_op jit(solution)/shard_map/dot_general | solution.py:281
  540.3 8.1 %psum.31 = f32[4096]{0:T(1024)} all-reduce(f32[4096]{0:T(1024)S(1)} %get-tuple-element.42), channel_id=1, replica_groups=mesh['dp'=2,'ffn'=4,'hid'=4] {'dp'}, use_global_device_ids=true, to_apply=%region_14.15 | all-reduce | flops 4096 | bytes 32768 | tf_op jit(solution)/shard_map/psum | solution.py:305
  (270 shorter events, 38.2 us)
Async XLA Ops:
  0.6 23.6 %copy-start.27 = (f32[4096]{0:T(1024)S(1)}, f32[4096]{0:T(1024)}, u32[]{:S(2)}) copy-start(f32[4096]{0:T(1024)} %param.9) | copy-start | bytes 49156
  0.7 25.0 %copy-start.29 = (f32[4096]{0:T(1024)S(1)}, f32[4096]{0:T(1024)}, u32[]{:S(2)}) copy-start(f32[4096]{0:T(1024)} %param.11) | copy-start | bytes 49156
  0.7 49.1 %collective-permute-start = (bf16[256,4096]{1,0:T(8,128)(2,1)}, bf16[256,4096]{1,0:T(8,128)(2,1)}, u32[]{:S(2)}, u32[]{:S(2)}) collective-permute-start(bf16[256,4096]{1,0:T(8,128)(2,1)} %param.8), channel_id=1, source_target_pairs={{0,16},{16,0},{1,17},{17,1},{2,18},{18,2},{3,19},{19,3},{4,20},{20... | collective-permute-start | bytes 6291464 | tf_op jit(solution)/shard_map/ppermute | solution.py:64
  5.8 21.6 %copy-start.20 = (bf16[2,4096,16]{1,2,0:T(8,128)(2,1)S(1)}, bf16[2,4096,16]{1,2,0:T(8,128)(2,1)}, u32[]{:S(2)}) copy-start(bf16[2,4096,16]{1,2,0:T(8,128)(2,1)} %param.13) | copy-start | bytes 786436
  23.5 26.1 %collective-permute-start.1 = (f32[256,2]{0,1:T(2,128)S(1)}, f32[256,2]{0,1:T(2,128)S(1)}, u32[]{:S(2)}, u32[]{:S(2)}) collective-permute-start(f32[256,2]{0,1:T(2,128)S(1)} %pad_maximum_fusion.21), channel_id=1, source_target_pairs={{0,16},{16,0},{1,17},{17,1},{2,18},{18,2},{3,19},{19,3},{4,20},{20... | collective-permute-start | bytes 6152 | tf_op jit(solution)/shard_map/ppermute | solution.py:64
  28.1 23.4 %copy-start.21 = (bf16[64,4096]{1,0:T(8,128)(2,1)S(1)}, bf16[64,4096]{1,0:T(8,128)(2,1)}, u32[]{:S(2)}) copy-start(bf16[64,4096]{1,0:T(8,128)(2,1)} %get-tuple-element.46) | copy-start | bytes 1572868
  28.1 23.4 %copy-start.22 = (bf16[64,4096]{1,0:T(8,128)(2,1)S(1)}, bf16[64,4096]{1,0:T(8,128)(2,1)}, u32[]{:S(2)}) copy-start(bf16[64,4096]{1,0:T(8,128)(2,1)} %get-tuple-element.47) | copy-start | bytes 1572868
  56.4 54.6 %copy-start = (bf16[256,4096]{1,0:T(8,128)(2,1)}, bf16[256,4096]{1,0:T(8,128)(2,1)S(1)}, u32[]{:S(2)}) copy-start(bf16[256,4096]{1,0:T(8,128)(2,1)S(1)} %get-tuple-element.91.x_ref) | copy-start | bytes 6291460
  130.4 12.4 %collective-permute-start.15 = (bf16[128,3328]{1,0:T(8,128)(2,1)}, bf16[128,3328]{1,0:T(8,128)(2,1)}, u32[]{:S(2)}, u32[]{:S(2)}) collective-permute-start(bf16[128,3328]{1,0:T(8,128)(2,1)} %get-tuple-element.27), channel_id=1, source_target_pairs={{0,1},{1,0},{2,3},{3,2},{4,5},{5,4},{6,7},{7,6},{8,9},{9,8},{10,11... | collective-permute-start | bytes 2555912 | tf_op jit(solution)/shard_map/ppermute | solution.py:64
  137.2 10.1 %collective-permute-start.5 = (bf16[128,3328]{1,0:T(8,128)(2,1)}, bf16[128,3328]{1,0:T(8,128)(2,1)}, u32[]{:S(2)}, u32[]{:S(2)}) collective-permute-start(bf16[128,3328]{1,0:T(8,128)(2,1)} %copy-done.10), channel_id=1, source_target_pairs={{0,1},{1,0},{2,3},{3,2},{4,5},{5,4},{6,7},{7,6},{8,9},{9,8},{10,11... | collective-permute-start | bytes 2555912 | tf_op jit(solution)/shard_map/ppermute | solution.py:64
  137.6 15.3 %collective-permute-start.12 = (bf16[128,3328]{1,0:T(8,128)(2,1)S(1)}, bf16[128,3328]{1,0:T(8,128)(2,1)}, u32[]{:S(2)}, u32[]{:S(2)}) collective-permute-start(bf16[128,3328]{1,0:T(8,128)(2,1)S(1)} %get-tuple-element.25), channel_id=1, source_target_pairs={{0,1},{1,0},{2,3},{3,2},{4,5},{5,4},{6,7},{7,6},{8,9},{9,8},{10,11... | collective-permute-start | bytes 2555912 | tf_op jit(solution)/shard_map/ppermute | solution.py:64
  137.7 12.1 %collective-permute-start.2 = (bf16[128,3328]{1,0:T(8,128)(2,1)}, bf16[128,3328]{1,0:T(8,128)(2,1)}, u32[]{:S(2)}, u32[]{:S(2)}) collective-permute-start(bf16[128,3328]{1,0:T(8,128)(2,1)} %copy-done.9), channel_id=1, source_target_pairs={{0,1},{1,0},{2,3},{3,2},{4,5},{5,4},{6,7},{7,6},{8,9},{9,8},{10,11... | collective-permute-start | bytes 2555912 | tf_op jit(solution)/shard_map/ppermute | solution.py:64
  145.5 45.0 %collective-permute-start.16 = (bf16[64,3328]{1,0:T(8,128)(2,1)}, bf16[64,3328]{1,0:T(8,128)(2,1)}, u32[]{:S(2)}, u32[]{:S(2)}) collective-permute-start(bf16[64,3328]{1,0:T(8,128)(2,1)} %slice.447), channel_id=1, source_target_pairs={{0,2},{1,3},{2,0},{3,1},{4,6},{5,7},{6,4},{7,5},{8,10},{9,11},{10,... | collective-permute-start | bytes 1277960 | tf_op jit(solution)/shard_map/ppermute | solution.py:64
  149.4 38.4 %collective-permute-start.6 = (bf16[64,3328]{1,0:T(8,128)(2,1)}, bf16[64,3328]{1,0:T(8,128)(2,1)}, u32[]{:S(2)}, u32[]{:S(2)}) collective-permute-start(bf16[64,3328]{1,0:T(8,128)(2,1)} %slice.449), channel_id=1, source_target_pairs={{0,2},{1,3},{2,0},{3,1},{4,6},{5,7},{6,4},{7,5},{8,10},{9,11},{10,... | collective-permute-start | bytes 1277960 | tf_op jit(solution)/shard_map/ppermute | solution.py:64
  151.3 25.3 %collective-permute-start.3 = (bf16[64,3328]{1,0:T(8,128)(2,1)S(1)}, bf16[64,3328]{1,0:T(8,128)(2,1)S(1)}, u32[]{:S(2)}, u32[]{:S(2)}) collective-permute-start(bf16[64,3328]{1,0:T(8,128)(2,1)S(1)} %slice.450), channel_id=1, source_target_pairs={{0,2},{1,3},{2,0},{3,1},{4,6},{5,7},{6,4},{7,5},{8,10},{9,11},{10,... | collective-permute-start | bytes 1277960 | tf_op jit(solution)/shard_map/ppermute | solution.py:64
  152.9 35.1 %copy-start.23 = (bf16[2,16,6656]{2,1,0:T(8,128)(2,1)S(1)}, bf16[2,16,6656]{2,1,0:T(8,128)(2,1)}, u32[]{:S(2)}) copy-start(bf16[2,16,6656]{2,1,0:T(8,128)(2,1)} %param.14) | copy-start | bytes 1277956
  152.9 35.1 %copy-start.24 = (f32[64,3328]{1,0:T(8,128)S(1)}, f32[64,3328]{1,0:T(8,128)}, u32[]{:S(2)}) copy-start(f32[64,3328]{1,0:T(8,128)} %convolution_multiply_fusion.3) | copy-start | bytes 2555908
  154.4 30.5 %collective-permute-start.13 = (bf16[64,3328]{1,0:T(8,128)(2,1)S(1)}, bf16[64,3328]{1,0:T(8,128)(2,1)S(1)}, u32[]{:S(2)}, u32[]{:S(2)}) collective-permute-start(bf16[64,3328]{1,0:T(8,128)(2,1)S(1)} %slice.448), channel_id=1, source_target_pairs={{0,2},{1,3},{2,0},{3,1},{4,6},{5,7},{6,4},{7,5},{8,10},{9,11},{10,... | collective-permute-start | bytes 1277960 | tf_op jit(solution)/shard_map/ppermute | solution.py:64
  177.4 10.6 %collective-permute-start.4 = (bf16[64,3328]{1,0:T(8,128)(2,1)}, bf16[64,3328]{1,0:T(8,128)(2,1)}, u32[]{:S(2)}, u32[]{:S(2)}) collective-permute-start(bf16[64,3328]{1,0:T(8,128)(2,1)} %fusion.33), channel_id=1, source_target_pairs={{0,16},{16,0},{1,17},{17,1},{2,18},{18,2},{3,19},{19,3},{4,20},{20... | collective-permute-start | bytes 1277960 | tf_op jit(solution)/shard_map/ppermute | solution.py:64
  185.8 11.5 %collective-permute-start.14 = (bf16[64,3328]{1,0:T(8,128)(2,1)}, bf16[64,3328]{1,0:T(8,128)(2,1)}, u32[]{:S(2)}, u32[]{:S(2)}) collective-permute-start(bf16[64,3328]{1,0:T(8,128)(2,1)} %fusion.32), channel_id=1, source_target_pairs={{0,16},{16,0},{1,17},{17,1},{2,18},{18,2},{3,19},{19,3},{4,20},{20... | collective-permute-start | bytes 1277960 | tf_op jit(solution)/shard_map/ppermute | solution.py:64
  277.0 11.2 %collective-permute-start.7 = (bf16[64,3328]{1,0:T(8,128)(2,1)S(1)}, bf16[64,3328]{1,0:T(8,128)(2,1)S(1)}, u32[]{:S(2)}, u32[]{:S(2)}) collective-permute-start(bf16[64,3328]{1,0:T(8,128)(2,1)S(1)} %broadcast_select_fusion.3), channel_id=1, source_target_pairs={{0,2},{1,3},{2,0},{3,1},{4,6},{5,7},{6,4},{7,5},{8,10},{9,11},{10,... | collective-permute-start | bytes 1277960 | tf_op jit(solution)/shard_map/ppermute | solution.py:64
  277.0 15.8 %collective-permute-start.17 = (bf16[64,3328]{1,0:T(8,128)(2,1)S(1)}, bf16[64,3328]{1,0:T(8,128)(2,1)S(1)}, u32[]{:S(2)}, u32[]{:S(2)}) collective-permute-start(bf16[64,3328]{1,0:T(8,128)(2,1)S(1)} %broadcast_select_fusion.1), channel_id=1, source_target_pairs={{0,2},{1,3},{2,0},{3,1},{4,6},{5,7},{6,4},{7,5},{8,10},{9,11},{10,... | collective-permute-start | bytes 1277960 | tf_op jit(solution)/shard_map/ppermute | solution.py:64
  279.1 13.9 %collective-permute-start.19 = (bf16[64,3328]{1,0:T(8,128)(2,1)S(1)}, bf16[64,3328]{1,0:T(8,128)(2,1)S(1)}, u32[]{:S(2)}, u32[]{:S(2)}) collective-permute-start(bf16[64,3328]{1,0:T(8,128)(2,1)S(1)} %copy-done.48), channel_id=1, source_target_pairs={{0,16},{16,0},{1,17},{17,1},{2,18},{18,2},{3,19},{19,3},{4,20},{20... | collective-permute-start | bytes 1277960 | tf_op jit(solution)/shard_map/ppermute | solution.py:64
  279.3 14.9 %collective-permute-start.9 = (bf16[64,3328]{1,0:T(8,128)(2,1)S(1)}, bf16[64,3328]{1,0:T(8,128)(2,1)S(1)}, u32[]{:S(2)}, u32[]{:S(2)}) collective-permute-start(bf16[64,3328]{1,0:T(8,128)(2,1)S(1)} %copy-done.47), channel_id=1, source_target_pairs={{0,16},{16,0},{1,17},{17,1},{2,18},{18,2},{3,19},{19,3},{4,20},{20... | collective-permute-start | bytes 1277960 | tf_op jit(solution)/shard_map/ppermute | solution.py:64
  288.3 26.4 %collective-permute-start.8 = (bf16[128,3328]{1,0:T(8,128)(2,1)S(1)}, bf16[128,3328]{1,0:T(8,128)(2,1)S(1)}, u32[]{:S(2)}, u32[]{:S(2)}) collective-permute-start(bf16[128,3328]{1,0:T(8,128)(2,1)S(1)} %pad_maximum_fusion.5), channel_id=1, source_target_pairs={{0,1},{1,0},{2,3},{3,2},{4,5},{5,4},{6,7},{7,6},{8,9},{9,8},{10,11... | collective-permute-start | bytes 2555912 | tf_op jit(solution)/shard_map/ppermute | solution.py:64
  292.9 21.7 %collective-permute-start.18 = (bf16[128,3328]{1,0:T(8,128)(2,1)S(1)}, bf16[128,3328]{1,0:T(8,128)(2,1)S(1)}, u32[]{:S(2)}, u32[]{:S(2)}) collective-permute-start(bf16[128,3328]{1,0:T(8,128)(2,1)S(1)} %pad_maximum_fusion.7), channel_id=1, source_target_pairs={{0,1},{1,0},{2,3},{3,2},{4,5},{5,4},{6,7},{7,6},{8,9},{9,8},{10,11... | collective-permute-start | bytes 2555912 | tf_op jit(solution)/shard_map/ppermute | solution.py:64
  293.0 12.7 %collective-permute-start.20 = (bf16[64,3328]{1,0:T(8,128)(2,1)S(1)}, bf16[64,3328]{1,0:T(8,128)(2,1)S(1)}, u32[]{:S(2)}, u32[]{:S(2)}) collective-permute-start(bf16[64,3328]{1,0:T(8,128)(2,1)S(1)} %collective-permute-done.19), channel_id=1, source_target_pairs={{0,2},{1,3},{2,0},{3,1},{4,6},{5,7},{6,4},{7,5},{8,10},{9,11},{10,... | collective-permute-start | bytes 1277960 | tf_op jit(solution)/shard_map/ppermute | solution.py:64
  294.3 20.0 %collective-permute-start.10 = (bf16[64,3328]{1,0:T(8,128)(2,1)S(1)}, bf16[64,3328]{1,0:T(8,128)(2,1)S(1)}, u32[]{:S(2)}, u32[]{:S(2)}) collective-permute-start(bf16[64,3328]{1,0:T(8,128)(2,1)S(1)} %collective-permute-done.9), channel_id=1, source_target_pairs={{0,2},{1,3},{2,0},{3,1},{4,6},{5,7},{6,4},{7,5},{8,10},{9,11},{10,... | collective-permute-start | bytes 1277960 | tf_op jit(solution)/shard_map/ppermute | solution.py:64
  305.7 9.5 %collective-permute-start.21 = (bf16[128,3328]{1,0:T(8,128)(2,1)S(1)}, bf16[128,3328]{1,0:T(8,128)(2,1)S(1)}, u32[]{:S(2)}, u32[]{:S(2)}) collective-permute-start(bf16[128,3328]{1,0:T(8,128)(2,1)S(1)} %pad_maximum_fusion.8), channel_id=1, source_target_pairs={{0,1},{1,0},{2,3},{3,2},{4,5},{5,4},{6,7},{7,6},{8,9},{9,8},{10,11... | collective-permute-start | bytes 2555912 | tf_op jit(solution)/shard_map/ppermute | solution.py:64
  314.4 2.4 collective-permute-start.11
  352.0 15.4 %collective-permute-start.42 = (bf16[16,6656]{1,0:T(8,128)(2,1)S(1)}, bf16[16,6656]{1,0:T(8,128)(2,1)S(1)}, u32[]{:S(2)}, u32[]{:S(2)}) collective-permute-start(bf16[16,6656]{1,0:T(8,128)(2,1)S(1)} %fusion.34), channel_id=1, source_target_pairs={{0,16},{16,0},{1,17},{17,1},{2,18},{18,2},{3,19},{19,3},{4,20},{20... | collective-permute-start | bytes 638984 | tf_op jit(solution)/shard_map/ppermute | solution.py:64
  363.2 14.9 %collective-permute-start.37 = (bf16[256,1024]{1,0:T(8,128)(2,1)S(1)}, bf16[256,1024]{1,0:T(8,128)(2,1)S(1)}, u32[]{:S(2)}, u32[]{:S(2)}) collective-permute-start(bf16[256,1024]{1,0:T(8,128)(2,1)S(1)} %get-tuple-element.35), channel_id=1, source_target_pairs={{0,16},{16,0},{1,17},{17,1},{2,18},{18,2},{3,19},{19,3},{4,20},{20... | collective-permute-start | bytes 1572872 | tf_op jit(solution)/shard_map/ppermute | solution.py:64
  365.1 24.3 %collective-permute-start.32 = (bf16[256,1024]{1,0:T(8,128)(2,1)S(1)}, bf16[256,1024]{1,0:T(8,128)(2,1)S(1)}, u32[]{:S(2)}, u32[]{:S(2)}) collective-permute-start(bf16[256,1024]{1,0:T(8,128)(2,1)S(1)} %get-tuple-element.33), channel_id=1, source_target_pairs={{0,16},{16,0},{1,17},{17,1},{2,18},{18,2},{3,19},{19,3},{4,20},{20... | collective-permute-start | bytes 1572872 | tf_op jit(solution)/shard_map/ppermute | solution.py:64
  365.3 35.2 %collective-permute-start.27 = (bf16[256,1024]{1,0:T(8,128)(2,1)S(1)}, bf16[256,1024]{1,0:T(8,128)(2,1)S(1)}, u32[]{:S(2)}, u32[]{:S(2)}) collective-permute-start(bf16[256,1024]{1,0:T(8,128)(2,1)S(1)} %get-tuple-element.31), channel_id=1, source_target_pairs={{0,16},{16,0},{1,17},{17,1},{2,18},{18,2},{3,19},{19,3},{4,20},{20... | collective-permute-start | bytes 1572872 | tf_op jit(solution)/shard_map/ppermute | solution.py:64
  367.1 43.6 %collective-permute-start.22 = (bf16[256,1024]{1,0:T(8,128)(2,1)S(1)}, bf16[256,1024]{1,0:T(8,128)(2,1)S(1)}, u32[]{:S(2)}, u32[]{:S(2)}) collective-permute-start(bf16[256,1024]{1,0:T(8,128)(2,1)S(1)} %get-tuple-element.29), channel_id=1, source_target_pairs={{0,16},{16,0},{1,17},{17,1},{2,18},{18,2},{3,19},{19,3},{4,20},{20... | collective-permute-start | bytes 1572872 | tf_op jit(solution)/shard_map/ppermute | solution.py:64
  378.3 32.7 %collective-permute-start.38 = (bf16[128,1024]{1,0:T(8,128)(2,1)S(1)}, bf16[128,1024]{1,0:T(8,128)(2,1)S(1)}, u32[]{:S(2)}, u32[]{:S(2)}) collective-permute-start(bf16[128,1024]{1,0:T(8,128)(2,1)S(1)} %slice.451), channel_id=1, source_target_pairs={{0,4},{4,0},{8,12},{12,8},{1,5},{5,1},{9,13},{13,9},{2,6},{6,2},{1... | collective-permute-start | bytes 786440 | tf_op jit(solution)/shard_map/ppermute | solution.py:64
  389.5 26.3 %collective-permute-start.33 = (bf16[128,1024]{1,0:T(8,128)(2,1)S(1)}, bf16[128,1024]{1,0:T(8,128)(2,1)S(1)}, u32[]{:S(2)}, u32[]{:S(2)}) collective-permute-start(bf16[128,1024]{1,0:T(8,128)(2,1)S(1)} %slice.452), channel_id=1, source_target_pairs={{0,4},{4,0},{8,12},{12,8},{1,5},{5,1},{9,13},{13,9},{2,6},{6,2},{1... | collective-permute-start | bytes 786440 | tf_op jit(solution)/shard_map/ppermute | solution.py:64
  400.8 15.2 %collective-permute-start.28 = (bf16[128,1024]{1,0:T(8,128)(2,1)S(1)}, bf16[128,1024]{1,0:T(8,128)(2,1)S(1)}, u32[]{:S(2)}, u32[]{:S(2)}) collective-permute-start(bf16[128,1024]{1,0:T(8,128)(2,1)S(1)} %slice.453), channel_id=1, source_target_pairs={{0,4},{4,0},{8,12},{12,8},{1,5},{5,1},{9,13},{13,9},{2,6},{6,2},{1... | collective-permute-start | bytes 786440 | tf_op jit(solution)/shard_map/ppermute | solution.py:64
  411.0 11.9 %collective-permute-start.23 = (bf16[128,1024]{1,0:T(8,128)(2,1)S(1)}, bf16[128,1024]{1,0:T(8,128)(2,1)S(1)}, u32[]{:S(2)}, u32[]{:S(2)}) collective-permute-start(bf16[128,1024]{1,0:T(8,128)(2,1)S(1)} %slice.454), channel_id=1, source_target_pairs={{0,4},{4,0},{8,12},{12,8},{1,5},{5,1},{9,13},{13,9},{2,6},{6,2},{1... | collective-permute-start | bytes 786440 | tf_op jit(solution)/shard_map/ppermute | solution.py:64
  411.1 29.7 %copy-start.13 = (bf16[256,4096]{1,0:T(8,128)(2,1)S(1)}, bf16[256,4096]{1,0:T(8,128)(2,1)}, u32[]{:S(2)}) copy-start(bf16[256,4096]{1,0:T(8,128)(2,1)} %param.8) | copy-start | bytes 6291460
  411.1 29.7 %copy-start.14 = (bf16[4096,16]{0,1:T(8,128)(2,1)S(1)}, bf16[4096,16]{0,1:T(8,128)(2,1)}, u32[]{:S(2)}) copy-start(bf16[4096,16]{0,1:T(8,128)(2,1)} %get-tuple-element.70) | copy-start | bytes 393220
  411.1 29.7 %copy-start.15 = (bf16[4096,16]{0,1:T(8,128)(2,1)S(1)}, bf16[4096,16]{0,1:T(8,128)(2,1)}, u32[]{:S(2)}) copy-start(bf16[4096,16]{0,1:T(8,128)(2,1)} %get-tuple-element.71) | copy-start | bytes 393220
  411.1 29.7 %copy-start.36 = (f32[1024]{0:T(1024)S(1)}, f32[1024]{0:T(1024)}, u32[]{:S(2)}) copy-start(f32[1024]{0:T(1024)} %get-tuple-element.102) | copy-start | bytes 12292
  411.2 29.7 %copy-start.40 = (f32[1024]{0:T(1024)S(1)}, f32[1024]{0:T(1024)}, u32[]{:S(2)}) copy-start(f32[1024]{0:T(1024)} %get-tuple-element.106) | copy-start | bytes 12292
  411.2 29.7 %copy-start.45 = (f32[64]{0:T(128)S(1)}, f32[64]{0:T(128)}, u32[]{:S(2)}) copy-start(f32[64]{0:T(128)} %slice_bitcast_fusion.2) | copy-start | bytes 772
  411.2 30.1 %copy-start.35 = (f32[1024]{0:T(1024)S(1)}, f32[1024]{0:T(1024)}, u32[]{:S(2)}) copy-start(f32[1024]{0:T(1024)} %get-tuple-element.103) | copy-start | bytes 12292
  411.2 30.1 %copy-start.39 = (f32[1024]{0:T(1024)S(1)}, f32[1024]{0:T(1024)}, u32[]{:S(2)}) copy-start(f32[1024]{0:T(1024)} %get-tuple-element.107) | copy-start | bytes 12292
  411.2 11.9 %collective-permute-start.39 = (bf16[64,1024]{1,0:T(8,128)(2,1)S(1)}, bf16[64,1024]{1,0:T(8,128)(2,1)S(1)}, u32[]{:S(2)}, u32[]{:S(2)}) collective-permute-start(bf16[64,1024]{1,0:T(8,128)(2,1)S(1)} %slice.455), channel_id=1, source_target_pairs={{0,8},{4,12},{8,0},{12,4},{1,9},{5,13},{9,1},{13,5},{2,10},{6,14},... | collective-permute-start | bytes 393224 | tf_op jit(solution)/shard_map/ppermute | solution.py:64
  415.9 25.9 %copy-start.34 = (f32[1024]{0:T(1024)S(1)}, f32[1024]{0:T(1024)}, u32[]{:S(2)}) copy-start(f32[1024]{0:T(1024)} %get-tuple-element.100) | copy-start | bytes 12292
  415.9 25.9 %copy-start.38 = (f32[1024]{0:T(1024)S(1)}, f32[1024]{0:T(1024)}, u32[]{:S(2)}) copy-start(f32[1024]{0:T(1024)} %get-tuple-element.104) | copy-start | bytes 12292
  415.9 30.4 %copy-start.33 = (f32[1024]{0:T(1024)S(1)}, f32[1024]{0:T(1024)}, u32[]{:S(2)}) copy-start(f32[1024]{0:T(1024)} %get-tuple-element.101) | copy-start | bytes 12292
  415.9 30.4 %copy-start.37 = (f32[1024]{0:T(1024)S(1)}, f32[1024]{0:T(1024)}, u32[]{:S(2)}) copy-start(f32[1024]{0:T(1024)} %get-tuple-element.105) | copy-start | bytes 12292
  415.9 19.2 %collective-permute-start.34 = (bf16[64,1024]{1,0:T(8,128)(2,1)S(1)}, bf16[64,1024]{1,0:T(8,128)(2,1)S(1)}, u32[]{:S(2)}, u32[]{:S(2)}) collective-permute-start(bf16[64,1024]{1,0:T(8,128)(2,1)S(1)} %slice.456), channel_id=1, source_target_pairs={{0,8},{4,12},{8,0},{12,4},{1,9},{5,13},{9,1},{13,5},{2,10},{6,14},... | collective-permute-start | bytes 393224 | tf_op jit(solution)/shard_map/ppermute | solution.py:64
  416.1 62.9 %copy-start.42 = (f32[256]{0:T(256)S(1)}, f32[256]{0:T(256)}, u32[]{:S(2)}) copy-start(f32[256]{0:T(256)} %copy-done.41) | copy-start | bytes 3076
  416.1 24.6 %collective-permute-start.29 = (bf16[64,1024]{1,0:T(8,128)(2,1)S(1)}, bf16[64,1024]{1,0:T(8,128)(2,1)S(1)}, u32[]{:S(2)}, u32[]{:S(2)}) collective-permute-start(bf16[64,1024]{1,0:T(8,128)(2,1)S(1)} %slice.457), channel_id=1, source_target_pairs={{0,8},{4,12},{8,0},{12,4},{1,9},{5,13},{9,1},{13,5},{2,10},{6,14},... | collective-permute-start | bytes 393224 | tf_op jit(solution)/shard_map/ppermute | solution.py:64
  423.0 23.4 %collective-permute-start.24 = (bf16[64,1024]{1,0:T(8,128)(2,1)S(1)}, bf16[64,1024]{1,0:T(8,128)(2,1)S(1)}, u32[]{:S(2)}, u32[]{:S(2)}) collective-permute-start(bf16[64,1024]{1,0:T(8,128)(2,1)S(1)} %slice.458), channel_id=1, source_target_pairs={{0,8},{4,12},{8,0},{12,4},{1,9},{5,13},{9,1},{13,5},{2,10},{6,14},... | collective-permute-start | bytes 393224 | tf_op jit(solution)/shard_map/ppermute | solution.py:64
  423.2 56.0 %collective-permute-start.40 = (bf16[64,1024]{1,0:T(8,128)(2,1)S(1)}, bf16[64,1024]{1,0:T(8,128)(2,1)}, u32[]{:S(2)}, u32[]{:S(2)}) collective-permute-start(bf16[64,1024]{1,0:T(8,128)(2,1)S(1)} %fusion.39), channel_id=1, source_target_pairs={{0,8},{4,12},{8,0},{12,4},{1,9},{5,13},{9,1},{13,5},{2,10},{6,14},... | collective-permute-start | bytes 393224 | tf_op jit(solution)/shard_map/ppermute | solution.py:64
  435.1 45.0 %collective-permute-start.35 = (bf16[64,1024]{1,0:T(8,128)(2,1)S(1)}, bf16[64,1024]{1,0:T(8,128)(2,1)}, u32[]{:S(2)}, u32[]{:S(2)}) collective-permute-start(bf16[64,1024]{1,0:T(8,128)(2,1)S(1)} %fusion.38), channel_id=1, source_target_pairs={{0,8},{4,12},{8,0},{12,4},{1,9},{5,13},{9,1},{13,5},{2,10},{6,14},... | collective-permute-start | bytes 393224 | tf_op jit(solution)/shard_map/ppermute | solution.py:64
  440.8 42.4 %collective-permute-start.30 = (bf16[64,1024]{1,0:T(8,128)(2,1)S(1)}, bf16[64,1024]{1,0:T(8,128)(2,1)}, u32[]{:S(2)}, u32[]{:S(2)}) collective-permute-start(bf16[64,1024]{1,0:T(8,128)(2,1)S(1)} %fusion.37), channel_id=1, source_target_pairs={{0,8},{4,12},{8,0},{12,4},{1,9},{5,13},{9,1},{13,5},{2,10},{6,14},... | collective-permute-start | bytes 393224 | tf_op jit(solution)/shard_map/ppermute | solution.py:64
  479.0 7.0 %collective-permute-start.25 = (bf16[64,1024]{1,0:T(8,128)(2,1)S(1)}, bf16[64,1024]{1,0:T(8,128)(2,1)S(1)}, u32[]{:S(2)}, u32[]{:S(2)}) collective-permute-start(bf16[64,1024]{1,0:T(8,128)(2,1)S(1)} %fusion.36), channel_id=1, source_target_pairs={{0,8},{4,12},{8,0},{12,4},{1,9},{5,13},{9,1},{13,5},{2,10},{6,14},... | collective-permute-start | bytes 393224 | tf_op jit(solution)/shard_map/ppermute | solution.py:64
  480.1 10.7 %collective-permute-start.41 = (bf16[128,1024]{1,0:T(8,128)(2,1)S(1)}, bf16[128,1024]{1,0:T(8,128)(2,1)S(1)}, u32[]{:S(2)}, u32[]{:S(2)}) collective-permute-start(bf16[128,1024]{1,0:T(8,128)(2,1)S(1)} %pad_maximum_fusion.20), channel_id=1, source_target_pairs={{0,4},{4,0},{8,12},{12,8},{1,5},{5,1},{9,13},{13,9},{2,6},{6,2},{1... | collective-permute-start | bytes 786440 | tf_op jit(solution)/shard_map/ppermute | solution.py:64
  481.1 15.3 %collective-permute-start.36 = (bf16[128,1024]{1,0:T(8,128)(2,1)S(1)}, bf16[128,1024]{1,0:T(8,128)(2,1)S(1)}, u32[]{:S(2)}, u32[]{:S(2)}) collective-permute-start(bf16[128,1024]{1,0:T(8,128)(2,1)S(1)} %pad_maximum_fusion.19), channel_id=1, source_target_pairs={{0,4},{4,0},{8,12},{12,8},{1,5},{5,1},{9,13},{13,9},{2,6},{6,2},{1... | collective-permute-start | bytes 786440 | tf_op jit(solution)/shard_map/ppermute | solution.py:64
  484.1 17.9 %collective-permute-start.31 = (bf16[128,1024]{1,0:T(8,128)(2,1)S(1)}, bf16[128,1024]{1,0:T(8,128)(2,1)S(1)}, u32[]{:S(2)}, u32[]{:S(2)}) collective-permute-start(bf16[128,1024]{1,0:T(8,128)(2,1)S(1)} %pad_maximum_fusion.18), channel_id=1, source_target_pairs={{0,4},{4,0},{8,12},{12,8},{1,5},{5,1},{9,13},{13,9},{2,6},{6,2},{1... | collective-permute-start | bytes 786440 | tf_op jit(solution)/shard_map/ppermute | solution.py:64
  486.1 20.1 %collective-permute-start.26 = (bf16[128,1024]{1,0:T(8,128)(2,1)S(1)}, bf16[128,1024]{1,0:T(8,128)(2,1)S(1)}, u32[]{:S(2)}, u32[]{:S(2)}) collective-permute-start(bf16[128,1024]{1,0:T(8,128)(2,1)S(1)} %pad_maximum_fusion.17), channel_id=1, source_target_pairs={{0,4},{4,0},{8,12},{12,8},{1,5},{5,1},{9,13},{13,9},{2,6},{6,2},{1... | collective-permute-start | bytes 786440 | tf_op jit(solution)/shard_map/ppermute | solution.py:64
  (29 other events, 210.7 us)

commit v2 on v0

v2 whole, which is shorter than its diff:
```python
import jax
import jax.numpy as jnp
from jax import lax
from jax.experimental import pallas as pl
from jax.experimental.pallas import tpu as pltpu
from jax.sharding import PartitionSpec as P

MODEL_WIDTH = 16384
ADAPTER_SCALE = 0.5
WIDTH_CHUNKS = 4
VMEM_BYTES = 40 * 1024 * 1024

F32 = jnp.float32
BF16 = jnp.bfloat16
ANY = pl.BlockSpec(memory_space=pl.ANY)


def bits_of(n):
    return n.bit_length() - 1


def reversed_bits(x, n):
    out = 0
    for i in range(n):
        out = out + (((x >> i) & 1) << (n - 1 - i))
    return out


def tile_of(n, cap):
    return max(t for t in range(128, cap + 1, 128) if n % t == 0)


def split_tiles(count, parts):
    edges = [count * i // parts for i in range(parts + 1)]
    return [(a, b - a) for a, b in zip(edges, edges[1:]) if b > a]


def swap(x, axis, n, mask):
    return lax.ppermute(x, axis, [(i, i ^ mask) for i in range(n)])


def double(x, axis, n, dim=0):
    for bit in reversed(range(bits_of(n))):
        x = jnp.concatenate([x, swap(x, axis, n, 1 << bit)], axis=dim)
    return x


def ordered(x, *first):
    return lax.optimization_barrier((x, *first))[0]


def total_of(parts, start, stop):
    out = parts[0][start:stop]
    for part in parts[1:]:
        out = out + part[start:stop].astype(F32)
    return out


def halve(keep, send, axis, n):
    parts = [keep, swap(send, axis, n, 1)]
    for bit in range(1, bits_of(n)):
        rows = parts[-1].shape[0]
        parts.append(swap(total_of(parts, rows // 2, rows).astype(BF16), axis, n, 1 << bit))
    return parts


def params():
    return pltpu.CompilerParams(vmem_limit_bytes=VMEM_BYTES)


def normalize(stream, stats, steering, gain, down, h, hid):
    tokens, width = stream.shape
    block = tokens // hid
    ranks = down.shape[0]

    def place(p, h_ref):
        return h_ref[0] ^ reversed_bits(p, bits_of(hid))

    def kernel(h_ref, x_ref, s_ref, steer_ref, gain_ref, down_ref, out_ref, low_ref):
        steered = x_ref[...].astype(F32) + s_ref[:, :1] * steer_ref[...]
        normed = (steered * s_ref[:, 1:] * gain_ref[...]).astype(BF16)
        out_ref[...] = normed
        low_ref[...] = lax.dot_general(
            normed, down_ref[...], (((1,), (1,)), ((), ())), preferred_element_type=F32
        )

    return pl.pallas_call(
        kernel,
        grid_spec=pltpu.PrefetchScalarGridSpec(
            num_scalar_prefetch=1,
            grid=(hid,),
            in_specs=[
                pl.BlockSpec((block, width), lambda p, h_ref: (place(p, h_ref), 0)),
                pl.BlockSpec((block, 2), lambda p, h_ref: (place(p, h_ref), 0)),
                pl.BlockSpec((1, width), lambda p, h_ref: (0, 0)),
                pl.BlockSpec((1, width), lambda p, h_ref: (0, 0)),
                pl.BlockSpec((ranks, width), lambda p, h_ref: (0, 0)),
            ],
            out_specs=[
                pl.BlockSpec((block, width), lambda p, h_ref: (p, 0)),
                pl.BlockSpec((block, ranks), lambda p, h_ref: (p, 0)),
            ],
        ),
        out_shape=[
            jax.ShapeDtypeStruct((tokens, width), BF16),
            jax.ShapeDtypeStruct((tokens, ranks), F32),
        ],
        compiler_params=params(),
        cost_estimate=pl.CostEstimate(
            flops=2 * tokens * width * ranks, bytes_accessed=4 * tokens * width, transcendentals=0
        ),
        name="normalize",
    )(h.reshape(1), stream, stats, steering.reshape(1, width), gain.reshape(1, width), down)


def forward_matmul(x, weights, first, tiles, tile, after=()):
    rows, depth = x.shape
    half = rows // 2
    parts = 4
    step = depth // parts

    def kernel(x_ref, *refs):
        w_refs, (keep_ref, send_ref) = refs[:parts], refs[-2:]
        y = None
        for i, w_ref in enumerate(w_refs):
            part = jnp.dot(x_ref[:, i * step : (i + 1) * step], w_ref[0], preferred_element_type=F32)
            y = part if y is None else y + part
        keep_ref[...] = y[:half]
        send_ref[...] = y[half:].astype(BF16)

    return pl.pallas_call(
        kernel,
        grid=(tiles,),
        in_specs=[pl.BlockSpec((rows, depth), lambda i: (0, 0))]
        + [pl.BlockSpec((1, step, tile), lambda i, k=k: (0, k, first + i)) for k in range(parts)]
        + [ANY] * len(after),
        out_specs=[pl.BlockSpec((half, tile), lambda i: (0, i))] * 2,
        out_shape=[
            jax.ShapeDtypeStruct((half, tiles * tile), F32),
            jax.ShapeDtypeStruct((half, tiles * tile), BF16),
        ],
        compiler_params=params(),
        cost_estimate=pl.CostEstimate(
            flops=2 * rows * depth * tiles * tile,
            bytes_accessed=2 * depth * (rows + tiles * tile) + 6 * half * tiles * tile,
            transcendentals=0,
        ),
        name="forward_matmul",
    )(x, *[weights] * parts, *after)


def gated_gradients(d, mine, other, cotangent, first, low, up, own, after=()):
    columns = other.shape[1]
    rank = up.shape[1]
    tile = tile_of(columns, 1024)
    tiles = columns // tile
    base = first // tile

    def kernel(d_ref, *refs):
        mine_refs = refs[: len(mine)]
        other_ref, flow_ref, low_ref, up_ref = refs[len(mine) : len(mine) + 4]
        mine_out, other_out, back_ref = refs[-3:]
        own_is_gate = d_ref[0] == 0
        total = mine_refs[0][...].astype(F32)
        for ref in mine_refs[1:]:
            total = total + ref[...].astype(F32)
        passed = other_ref[...].astype(F32)
        low_terms = [
            ADAPTER_SCALE
            * jnp.dot(low_ref[:, k * rank : (k + 1) * rank], up_ref[k], preferred_element_type=F32)
            for k in range(2)
        ]
        gate = jnp.where(own_is_gate, total, passed) + low_terms[0]
        upper = jnp.where(own_is_gate, passed, total) + low_terms[1]
        sigma = 1.0 / (1.0 + jnp.exp(-gate))
        flow = flow_ref[...].astype(F32)
        gate_grad = (flow * upper * sigma * (1.0 + gate * (1.0 - sigma))).astype(BF16)
        upper_grad = (flow * gate * sigma).astype(BF16)
        mine_out[...] = jnp.where(own_is_gate, gate_grad, upper_grad)
        other_out[...] = jnp.where(own_is_gate, upper_grad, gate_grad)

        @pl.when(pl.program_id(0) == 0)
        def _():
            back_ref[...] = jnp.zeros_like(back_ref)

        contract = (((1,), (1,)), ((), ()))
        for k, grad in enumerate((gate_grad, upper_grad)):
            back_ref[:, k * rank : (k + 1) * rank] += lax.dot_general(
                grad, up_ref[k], contract, preferred_element_type=F32
            )
        back_ref[:, 2 * rank :] += jnp.sum(
            gate_grad.astype(F32) * gate + upper_grad.astype(F32) * upper, axis=1, keepdims=True
        )

    here = pl.BlockSpec((own, tile), lambda i, d_ref: (0, i))
    there = pl.BlockSpec((own, tile), lambda i, d_ref: (0, base + i))
    return pl.pallas_call(
        kernel,
        grid_spec=pltpu.PrefetchScalarGridSpec(
            num_scalar_prefetch=1,
            grid=(tiles,),
            in_specs=[here] * (len(mine) + 1)
            + [
                there,
                pl.BlockSpec((own, 2 * rank), lambda i, d_ref: (0, 0)),
                pl.BlockSpec((2, rank, tile), lambda i, d_ref: (0, 0, base + i)),
            ]
            + [ANY] * len(after),
            out_specs=[here, here, pl.BlockSpec((own, 2 * rank + 1), lambda i, d_ref: (0, 0))],
        ),
        out_shape=[
            jax.ShapeDtypeStruct((own, columns), BF16),
            jax.ShapeDtypeStruct((own, columns), BF16),
            jax.ShapeDtypeStruct((own, 2 * rank + 1), F32),
        ],
        compiler_params=params(),
        cost_estimate=pl.CostEstimate(
            flops=8 * own * columns * rank, bytes_accessed=16 * own * columns, transcendentals=own * columns
        ),
        name="gated_gradients",
    )(d.reshape(1), *mine, other, cotangent, low, up, *after)


def backward_matmul(grads, weights, chunk, first, tiles, tile, base=None, partial=False, after=()):
    rows, hidden = sum(g.shape[0] for g in grads), grads[0].shape[1]
    half = rows // 2
    n_base = 0 if base is None else 1

    def kernel(*refs):
        g_refs = refs[: len(grads)]
        w_ref = refs[len(grads)]
        g = jnp.concatenate([ref[...] for ref in g_refs], axis=0)
        y = lax.dot_general(g, w_ref[0], (((1,), (1,)), ((), ())), preferred_element_type=F32)
        if n_base:
            y = y + refs[len(grads) + 1][...]
        if partial:
            refs[-1][...] = y
        else:
            refs[-2][...] = y[:half]
            refs[-1][...] = y[half:].astype(BF16)

    if partial:
        out_specs = pl.BlockSpec((rows, tile), lambda i: (0, i))
        out_shape = jax.ShapeDtypeStruct((rows, tiles * tile), F32)
    else:
        out_specs = [pl.BlockSpec((half, tile), lambda i: (0, i))] * 2
        out_shape = [
            jax.ShapeDtypeStruct((half, tiles * tile), F32),
            jax.ShapeDtypeStruct((half, tiles * tile), BF16),
        ]
    return pl.pallas_call(
        kernel,
        grid=(tiles,),
        in_specs=[pl.BlockSpec(g.shape, lambda i: (0, 0)) for g in grads]
        + [pl.BlockSpec((1, tile, hidden), lambda i: (0, first + i, chunk))]
        + [pl.BlockSpec((rows, tile), lambda i: (0, first + i))] * n_base
        + [ANY] * len(after),
        out_specs=out_specs,
        out_shape=out_shape,
        compiler_params=params(),
        cost_estimate=pl.CostEstimate(
            flops=2 * rows * hidden * tiles * tile,
            bytes_accessed=2 * hidden * (rows + tiles * tile) + (4 + 4 * n_base) * rows * tiles * tile,
            transcendentals=0,
        ),
        name="backward_matmul",
    )(*grads, weights, *(() if base is None else (base,)), *after)


def finish(parts, stream, stats, back, down, steering, gain, columns):
    rows = stream.shape[0]
    width = parts[0].shape[1]
    start = columns // width

    def kernel(*refs):
        part_refs = refs[: len(parts)]
        x_ref, s_ref, back_ref, down_ref, steer_ref, gain_ref, out_ref, sum_ref = refs[len(parts) :]
        total = part_refs[0][...].astype(F32)
        for ref in part_refs[1:]:
            total = total + ref[...].astype(F32)
        total = total + ADAPTER_SCALE * jnp.dot(back_ref[...], down_ref[...], preferred_element_type=F32)
        steered = x_ref[...].astype(F32) + s_ref[:, 0:1] * steer_ref[...]
        grad = s_ref[:, 1:2] * gain_ref[...] * total - s_ref[:, 2:3] * steered
        out_ref[...] = grad.astype(BF16)
        sum_ref[...] = jnp.sum(s_ref[:, 0:1] * grad, axis=0, keepdims=True)

    across = lambda n: pl.BlockSpec((n, width), lambda i: (0, start))
    return pl.pallas_call(
        kernel,
        grid=(1,),
        in_specs=[pl.BlockSpec((rows, width), lambda i: (0, 0))] * len(parts)
        + [
            across(rows),
            pl.BlockSpec(stats.shape, lambda i: (0, 0)),
            pl.BlockSpec(back.shape, lambda i: (0, 0)),
            across(down.shape[0]),
            across(1),
            across(1),
        ],
        out_specs=[pl.BlockSpec((rows, width), lambda i: (0, 0)), pl.BlockSpec((1, width), lambda i: (0, 0))],
        out_shape=[jax.ShapeDtypeStruct((rows, width), BF16), jax.ShapeDtypeStruct((1, width), F32)],
        compiler_params=params(),
        cost_estimate=pl.CostEstimate(
            flops=2 * rows * width * down.shape[0], bytes_accessed=10 * rows * width, transcendentals=0
        ),
        name="finish",
    )(*parts, stream, stats, back, down, steering.reshape(1, -1), gain.reshape(1, -1))


def make_local(dp, hid, ffn):
    def local(stream, steering, strength, gain, weights, down, up, cotangent):
        d, h, f = lax.axis_index("dp"), lax.axis_index("hid"), lax.axis_index("ffn")
        tokens, width = stream.shape
        hidden = weights.shape[2]
        own = tokens // hid
        rank = down.shape[2]
        first_pair = d == 0
        down_rows = jnp.transpose(down, (0, 2, 1)).reshape(2 * rank, width)

        peer_stream = swap(stream, "dp", dp, 1)
        rows = stream.astype(F32)
        total_rows, total_steer = lax.psum(
            (jnp.sum(rows * rows, axis=1), jnp.sum(steering * steering)), "hid"
        )
        stream_ms = total_rows / MODEL_WIDTH + 1e-06
        steer_ms = total_steer / MODEL_WIDTH + 1e-06
        scale = strength * jnp.sqrt(stream_ms / steer_ms)
        steered = rows + scale[:, None] * steering[None, :]
        steered_power = lax.psum(jnp.sum(steered * steered, axis=1), "hid")
        inv_rms = lax.rsqrt(steered_power / MODEL_WIDTH + 1e-05)
        stats = jnp.stack([scale, inv_rms], axis=1)
        peer_stats = swap(stats, "dp", dp, 1)

        count = 2 if hidden % 256 == 0 else 1
        chunk = hidden // count
        tile = tile_of(chunk, 256)
        tiles = chunk // tile
        own_normed, own_low = normalize(stream, stats, steering, gain, down_rows, h, hid)
        own_acts = []
        for c in range(count):
            keep, send = forward_matmul(own_normed, weights, c * tiles, tiles, tile)
            own_acts.append(halve(keep, send, "hid", hid))
        peer_normed, peer_low = normalize(peer_stream, peer_stats, steering, gain, down_rows, h, hid)
        peer_acts = []
        for c in range(count):
            wait = (own_acts[c - 1][-1],) if c else ()
            keep, send = forward_matmul(peer_normed, weights, c * tiles, tiles, tile, wait)
            peer_acts.append(halve(keep, send, "hid", hid))

        low = jnp.stack([own_low, peer_low])
        for bit in range(bits_of(hid)):
            half = low.shape[1] // 2
            low = low[:, :half] + swap(low[:, half:], "hid", hid, 1 << bit)
        low = low.astype(BF16)
        low_own = low[0]
        low_mine = jnp.where(first_pair, low[:, :, :rank], low[:, :, rank:])
        low_mine = double(low_mine, "hid", hid, dim=1)

        width_tile = tile_of(width, 256)
        grads, back, base, wait = [], 0.0, None, ()
        for c in range(count):
            other = swap(total_of(peer_acts[c], 0, own).astype(BF16), "dp", dp, 1)
            mine_grad, other_grad, back_part = gated_gradients(
                d, own_acts[c], other, cotangent, c * chunk, low_own, up, own, wait
            )
            back = back + back_part
            peer_grad = swap(other_grad, "dp", dp, 1)
            pieces, wait = [], (peer_grad,)
            for g in (mine_grad, peer_grad):
                for bit in reversed(range(1, bits_of(hid))):
                    got = swap(g, "hid", hid, 1 << bit)
                    if g is mine_grad:
                        wait += (got,)
                    if c and g is peer_grad:
                        got = ordered(got, base)
                    g = jnp.concatenate([g, got], axis=0)
                pieces += [g, swap(g, "hid", hid, 1)]
            grads.append(pieces)
            if c < count - 1:
                base = backward_matmul(
                    pieces, weights, c, 0, width // width_tile, width_tile, base=base, partial=True
                )

        for bit in range(bits_of(ffn)):
            back = back + swap(back, "ffn", ffn, 1 << bit)
        back = jnp.stack([back, swap(back, "dp", dp, 1)])
        back = double(back, "hid", hid, dim=1)
        back_low = back[:, :, : 2 * rank].astype(BF16)
        acts_product = back[0, :, 2 * rank]

        shard = tokens // ffn
        place = reversed_bits(f, bits_of(ffn))
        block = min(own, shard)

        def natural(row):
            index = row // own
            return (h ^ reversed_bits(index, bits_of(hid))) * own + row % own

        def shard_rows(x):
            return jnp.concatenate(
                [
                    lax.dynamic_slice_in_dim(x, natural(place * shard + i * block), block, axis=0)
                    for i in range(shard // block)
                ],
                axis=0,
            )

        stats_shard = shard_rows(stats)
        dot_shard = lax.dynamic_slice_in_dim(acts_product, place * shard, shard, axis=0)
        dot_factor = stats_shard[:, 1] ** 2 * dot_shard / MODEL_WIDTH
        stats_shard = jnp.concatenate([stats_shard, dot_factor[:, None]], axis=1)
        stream_shard = shard_rows(stream)
        back_shard = lax.dynamic_slice_in_dim(back_low[0], place * shard, shard, axis=0)

        out = jnp.zeros((tokens, width), BF16)
        sums = []
        steps = split_tiles(width // width_tile, WIDTH_CHUNKS)
        products, received = [], []
        for first, n in steps:
            keep, send = backward_matmul(grads[-1], weights, count - 1, first, n, width_tile, base=base)
            products.append(keep)
            received.append(swap(send, "dp", dp, 1))
        results = []
        for j, (first, n) in enumerate(steps):
            held = received[j]
            if j >= 2:
                held = ordered(held, results[j - 2])
            part = products[j] + held.astype(F32)
            parts = [part]
            for bit in range(bits_of(ffn)):
                half = parts[-1].shape[0] // 2
                mine = (f >> bit) & 1
                halves = [
                    [lax.dynamic_slice_in_dim(p, side * half, half, axis=0) for p in parts]
                    for side in (mine, 1 - mine)
                ]
                parts = halves[0] + [swap(total_of(halves[1], 0, half).astype(BF16), "ffn", ffn, 1 << bit)]
            result, sum_part = finish(
                parts, stream_shard, stats_shard, back_shard, down_rows, steering, gain, first * width_tile
            )
            sums.append(sum_part)
            results.append(result)
            result = double(result, "ffn", ffn)
            for p in range(ffn):
                owner = reversed_bits(f ^ reversed_bits(p, bits_of(ffn)), bits_of(ffn))
                for i in range(shard // block):
                    out = lax.dynamic_update_slice(
                        out,
                        result[p * shard + i * block : p * shard + (i + 1) * block],
                        (natural(owner * shard + i * block), first * width_tile),
                    )

        steering_gradient = jnp.concatenate(sums, axis=1)
        for bit in range(bits_of(ffn)):
            steering_gradient = steering_gradient + swap(steering_gradient, "ffn", ffn, 1 << bit)
        steering_gradient = steering_gradient + swap(steering_gradient, "dp", dp, 1)

        up_parts = []
        for pieces in grads:
            total, at = 0.0, 0
            low_rows = low_mine.reshape(2 * tokens, rank)
            for g in pieces:
                total = total + lax.dot_general(
                    low_rows[at : at + g.shape[0]], g, (((0,), (0,)), ((), ())), preferred_element_type=F32
                )
                at += g.shape[0]
            up_parts.append(ADAPTER_SCALE * total)
        up_mine = jnp.concatenate(up_parts, axis=1)
        up_other = swap(up_mine.astype(BF16), "dp", dp, 1).astype(F32)
        up_gradient = jnp.where(
            first_pair, jnp.stack([up_mine, up_other]), jnp.stack([up_other, up_mine])
        )
        down_gradient = 0.0
        for x, b in ((own_normed, back_low[0]), (peer_normed, back_low[1])):
            down_gradient = down_gradient + lax.dot_general(
                b, x, (((0,), (0,)), ((), ())), preferred_element_type=F32
            )
        down_gradient = jnp.transpose(
            (ADAPTER_SCALE * down_gradient).reshape(2, rank, width), (0, 2, 1)
        )
        return out, steering_gradient.reshape(width), down_gradient, up_gradient

    return local


def solution(mesh):
    in_specs = (
        P("dp", "hid"),
        P("hid"),
        P("dp"),
        P("hid"),
        P("dp", "hid", "ffn"),
        P(None, "hid", None),
        P(None, None, "ffn"),
        P(("dp", "hid"), "ffn"),
    )
    out_specs = (P("dp", "hid"), P("hid"), P(None, "hid", None), P(None, None, "ffn"))
    local = make_local(mesh.shape["dp"], mesh.shape["hid"], mesh.shape["ffn"])
    return jax.shard_map(local, mesh=mesh, in_specs=in_specs, out_specs=out_specs, check_vma=False)
```

time: 1840 us -> 388 us (0.21)
  waiting for transfers between devices: 1620 us -> 78.2 us
  Pallas kernels: 0 us -> 138 us
  matrix products: 119 us -> 7.87 us
  local copies, waits for them, and re-layouts: 4.37 us -> 69.5 us
  starting transfers between devices: 0.24 us -> 59 us
  blocking collectives: 62.2 us -> 13.4 us
    all_gather x3 -> x0, waiting for transfers between devices: 1300 us -> none  [the longest x1 1230 us: local(): weights = lax.all_gather(frozen_weights, 'dp', axis=0, tiled=True)]
    psum x2 -> x0, waiting for transfers between devices: 246 us -> none  [the longest x1 223 us: local(): preactivation_values, adapter_sum = lax.psum((full_acts, down_piece), 'hid')]
    pallas_call x0 -> x17, Pallas kernels: none -> 138 us  [the longest x4 67.4 us: forward_matmul(): pl.pallas_call(kernel, grid=(tiles,), in_specs=[pl.BlockSpec((rows, depth...]
    dot_general x7 -> x10, matrix products: 117 us -> 7.87 us  [the longest x8 4.17 us: local(): lax.dot_general(low_rows[at:at + g.shape[0]], g, (((0,), (0,)), ((), ()))...]
    ppermute x0 -> x55, waiting for transfers between devices: none -> 78.2 us  [swap(): return lax.ppermute(x, axis, [(i, i ^ mask) for i in range(n)])]
    reduce_scatter x1 -> x0, waiting for transfers between devices: 76.9 us -> none  [local(): lax.psum_scatter(jnp.einsum('tkf,kdf->td', activation_gradient, weights,...]
    ppermute x0 -> x55, starting transfers between devices: none -> 59 us  [swap(): return lax.ppermute(x, axis, [(i, i ^ mask) for i in range(n)])]
    psum x5 -> x1, blocking collectives: 56.4 us -> 7.33 us  [local(): lax.psum((jnp.sum(rows * rows, axis=1), jnp.sum(steering * steering)), 'h...]
  transfers between devices with their start and end apart: 6 -> 55, of which waited for: 6 -> 19; matrix products, arithmetic and copies ran while one was open for 2% -> 21% of each run, Pallas kernels for 0% -> 36%
where the time goes in v2:
time: 388 us; the launch traced here: 384 us
  Pallas kernels  138 us (36%)
  waiting for transfers between devices  78.2 us (20%)
  local copies, waits for them, and re-layouts  69.5 us (18%)
  starting transfers between devices  59 us (15%)
  other arithmetic  15.5 us (4%)
  blocking collectives  13.4 us (3%)
  matrix products  7.87 us (2%)
    ppermute x55, waiting for transfers between devices, swap(): return lax.ppermute(x, axis, [(i, i ^ mask) for i in range(n)])  78.2 us
    pallas_call x4, Pallas kernels, forward_matmul(): pl.pallas_call(kernel, grid=(tiles,), in_specs=[pl.BlockSpec((rows, depth...  67.4 us
    ppermute x55, starting transfers between devices, swap(): return lax.ppermute(x, axis, [(i, i ^ mask) for i in range(n)])  59 us
    pallas_call x5, Pallas kernels, backward_matmul(): pl.pallas_call(kernel, grid=(tiles,), in_specs=[pl.BlockSpec(g.shape, lam...  48.1 us
    dynamic_update_slice x16, local copies, waits for them, and re-layouts, local(): lax.dynamic_update_slice(out, result[p * shard + i * block:p * shard + (i...  46.6 us
    pallas_call x2, Pallas kernels, gated_gradients(): pl.pallas_call(kernel, grid_spec=pltpu.PrefetchScalarGridSpec(num_scalar_...  16.3 us
    unnamed x59, local copies, waits for them, and re-layouts  11.3 us
  transfers between devices with their start and end apart: 55, of which 19 were waited for; matrix products, arithmetic and copies ran while one was open for 21% of the time, Pallas kernels for 36%

profile of v2, /device:TPU:0, one launch (start us, length us, event | category | flops | bytes accessed | tf_op | source)
XLA Modules:
  0.0 383.8 jit_solution(15872970106166985051)
XLA Ops:
  0.7 3.0 collective-permute-start.2
  3.7 2.1 fusion.6
  7.1 7.3 %all-reduce = (f32[256]{0:T(256)S(1)}, f32[]{:T(128)}) all-reduce(f32[256]{0:T(256)S(1)} %fusion.6, f32[]{:T(128)} %multiply_reduce_fusion), channel_id=1, replica_groups=mesh['dp'=2,'ffn'=4,'hid'=4] {'hid'}, use_global_device_ids=true, to_apply=%region_1.0 | all-reduce | flops 257 | bytes 2056 | tf_op jit(solution)/shard_map/psum | solution.py:322
  16.0 6.1 %psum.23 = f32[256]{0:T(256)S(1)} all-reduce(f32[256]{0:T(256)S(1)} %fusion.8), channel_id=1, replica_groups=mesh['dp'=2,'ffn'=4,'hid'=4] {'hid'}, use_global_device_ids=true, to_apply=%region_5.0 | all-reduce | flops 256 | bytes 2048 | tf_op jit(solution)/shard_map/psum | solution.py:329
  23.6 1.7 normalize.2
  25.3 17.8 %forward_matmul.5 = (f32[128,3328]{1,0:T(8,128)S(1)}, bf16[128,3328]{1,0:T(8,128)(2,1)}) custom-call(bf16[256,4096]{1,0:T(8,128)(2,1)S(1)} %get-tuple-element.41.x_ref, bf16[1,4096,6656]{2,1,0:T(8,128)(2,1)} %refs_4_.13, bf16[1,4096,6656]{2,1,0:T(8,128)(2,1)} %refs_4_.13, bf16[1,4096,6656]{2,1,0:T(8,128)(2,1)} %refs_4_.13, bf16[1,4096,6656]{2,1,0:T(8,128)(2,1)} %refs_4_.13), custom_call_target="tpu_custom_call" | custom-call | flops 6979321856 | bytes 31916032 | tf_op jit(solution)/shard_map/forward_matmul/pallas_call | solution.py:131
  44.3 17.0 %forward_matmul.4 = (f32[128,3328]{1,0:T(8,128)S(1)}, bf16[128,3328]{1,0:T(8,128)(2,1)}) custom-call(bf16[256,4096]{1,0:T(8,128)(2,1)S(1)} %get-tuple-element.41.x_ref, bf16[1,4096,6656]{2,1,0:T(8,128)(2,1)} %refs_4_.13, bf16[1,4096,6656]{2,1,0:T(8,128)(2,1)} %refs_4_.13, bf16[1,4096,6656]{2,1,0:T(8,128)(2,1)} %refs_4_.13, bf16[1,4096,6656]{2,1,0:T(8,128)(2,1)} %refs_4_.13), custom_call_target="tpu_custom_call" | custom-call | flops 6979321856 | bytes 31916032 | tf_op jit(solution)/shard_map/forward_matmul/pallas_call | solution.py:131
  64.0 1.6 add_convert_fusion.4
  66.5 1.8 add_convert_fusion.5
  69.6 3.4 normalize.3
  73.1 16.3 %forward_matmul.7 = (f32[128,3328]{1,0:T(8,128)S(1)}, bf16[128,3328]{1,0:T(8,128)(2,1)S(1)}) custom-call(bf16[256,4096]{1,0:T(8,128)(2,1)S(1)} %get-tuple-element.44.x_ref, bf16[1,4096,6656]{2,1,0:T(8,128)(2,1)} %refs_4_.13, bf16[1,4096,6656]{2,1,0:T(8,128)(2,1)} %refs_4_.13, bf16[1,4096,6656]{2,1,0:T(8,128)(2,1)} %refs_4_.13, bf16[1,4096,6656]{2,1,0:T(8,128)(2,1)} %refs_4_.13), custom_call_target="tpu_custom_call" | custom-call | flops 6979321856 | bytes 31916032 | tf_op jit(solution)/shard_map/forward_matmul/pallas_call | solution.py:131
  90.8 16.3 %forward_matmul.6 = (f32[128,3328]{1,0:T(8,128)S(1)}, bf16[128,3328]{1,0:T(8,128)(2,1)S(1)}) custom-call(bf16[256,4096]{1,0:T(8,128)(2,1)S(1)} %get-tuple-element.44.x_ref, bf16[1,4096,6656]{2,1,0:T(8,128)(2,1)} %refs_4_.13, bf16[1,4096,6656]{2,1,0:T(8,128)(2,1)} %refs_4_.13, bf16[1,4096,6656]{2,1,0:T(8,128)(2,1)} %refs_4_.13, ...), custom_call_target="tpu_custom_call" | custom-call | flops 6979321856 | bytes 31916032 | tf_op jit(solution)/shard_map/forward_matmul/pallas_call | solution.py:131
  111.0 9.0 %collective-permute-done.12 = bf16[64,3328]{1,0:T(8,128)(2,1)S(1)} collective-permute-done((bf16[64,3328]{1,0:T(8,128)(2,1)S(1)}, bf16[64,3328]{1,0:T(8,128)(2,1)S(1)}, u32[]{:S(2)}, u32[]{:S(2)}) %collective-permute-start.12) | collective-permute-done | bytes 426016 | tf_op jit(solution)/shard_map/ppermute | solution.py:39
  120.1 1.5 collective-permute-start.13
  121.6 7.1 %collective-permute-done.7 = bf16[64,3328]{1,0:T(8,128)(2,1)S(1)} collective-permute-done((bf16[64,3328]{1,0:T(8,128)(2,1)S(1)}, bf16[64,3328]{1,0:T(8,128)(2,1)S(1)}, u32[]{:S(2)}, u32[]{:S(2)}) %collective-permute-start.7) | collective-permute-done | bytes 426016 | tf_op jit(solution)/shard_map/ppermute | solution.py:39
  131.3 7.2 %gated_gradients.2 = (bf16[64,3328]{1,0:T(8,128)(2,1)}, bf16[64,3328]{1,0:T(8,128)(2,1)}, f32[64,33]{1,0:T(8,128)S(1)}) custom-call(s32[1]{0:T(128)} %bitcast.d_ref, f32[128,3328]{1,0:T(8,128)S(1)} %copy-done.10, bf16[128,3328]{1,0:T(8,128)(2,1)S(1)} %copy-done.13, bf16[64,3328]{1,0:T(8,128)(2,1)S(1)} %collective-permute-done.5.refs_4_.refs_2_, ...), custom_call_target="tpu_custom_call" | custom-call | flops 27262976 | bytes 3407872 | tf_op jit(solution)/shard_map/gated_gradients/pallas_call | solution.py:197
  142.2 8.1 %collective-permute-done.52 = bf16[2,64,16]{2,1,0:T(8,128)(2,1)S(1)} collective-permute-done((bf16[2,64,16]{2,1,0:T(8,128)(2,1)S(1)}, bf16[2,64,16]{2,1,0:T(8,128)(2,1)S(1)}, u32[]{:S(2)}, u32[]{:S(2)}) %collective-permute-start.52) | collective-permute-done | bytes 4128 | tf_op jit(solution)/shard_map/ppermute | solution.py:39
  153.1 9.1 %gated_gradients.3 = (bf16[64,3328]{1,0:T(8,128)(2,1)}, bf16[64,3328]{1,0:T(8,128)(2,1)}, f32[64,33]{1,0:T(8,128)S(1)}) custom-call(s32[1]{0:T(128)} %bitcast.d_ref, f32[128,3328]{1,0:T(8,128)S(1)} %copy-done.8, bf16[128,3328]{1,0:T(8,128)(2,1)} %collective-permute-done.refs_1_, bf16[64,3328]{1,0:T(8,128)(2,1)} %collective-permute-done.1.refs_2_, ...), custom_call_target="tpu_custom_call" | custom-call | flops 27262976 | bytes 3407872 | tf_op jit(solution)/shard_map/gated_gradients/pallas_call | solution.py:197
  162.3 1.7 collective-permute-start.27
  164.0 2.2 collective-permute-done.27
  166.3 2.7 collective-permute-start.28
  168.9 1.8 constant_dynamic-update-slice_fusion.3
  176.3 1.8 constant_dynamic-update-slice_fusion.2.refs_0_
  179.3 5.2 %collective-permute-done.30 = f32[2,64,33]{2,1,0:T(8,128)S(1)} collective-permute-done((f32[2,64,33]{2,1,0:T(8,128)S(1)}, f32[2,64,33]{2,1,0:T(8,128)S(1)}, u32[]{:S(2)}, u32[]{:S(2)}) %collective-permute-start.30) | collective-permute-done | bytes 16928 | tf_op jit(solution)/shard_map/ppermute | solution.py:39
  184.6 1.8 constant_dynamic-update-slice_fusion.5
  189.4 2.4 fusion
  191.8 7.1 %collective-permute-done.21 = bf16[64,3328]{1,0:T(8,128)(2,1)} collective-permute-done((bf16[64,3328]{1,0:T(8,128)(2,1)}, bf16[64,3328]{1,0:T(8,128)(2,1)}, u32[]{:S(2)}, u32[]{:S(2)}) %collective-permute-start.21) | collective-permute-done | bytes 426016 | tf_op jit(solution)/shard_map/ppermute | solution.py:39
  206.8 22.6 %backward_matmul.5.refs_5_ = f32[512,4096]{1,0:T(8,128)S(1)} custom-call(bf16[128,3328]{1,0:T(8,128)(2,1)} %constant_dynamic-update-slice_fusion.2.refs_0_, bf16[128,3328]{1,0:T(8,128)(2,1)} %collective-permute-done.20.refs_1_, bf16[128,3328]{1,0:T(8,128)(2,1)S(1)} %constant_dynamic-update-slice_fusion.4.refs_2_, ...), custom_call_target="tpu_custom_call" | custom-call | flops 13958643712 | bytes 39059456 | tf_op jit(solution)/shard_map/backward_matmul/pallas_call | solution.py:251
  233.8 6.4 %backward_matmul.7 = (f32[256,1024]{1,0:T(8,128)S(1)}, bf16[256,1024]{1,0:T(8,128)(2,1)S(1)}) custom-call(bf16[128,3328]{1,0:T(8,128)(2,1)S(1)} %constant_dynamic-update-slice_fusion.refs_0_, bf16[128,3328]{1,0:T(8,128)(2,1)S(1)} %collective-permute-done.17.refs_1_, bf16[128,3328]{1,0:T(8,128)(2,1)S(1)} %constant_dynamic-update-slice_fusion.6.refs_2_, ...), custom_call_target="tpu_custom_call" | custom-call | flops 3489660928 | bytes 14417920 | tf_op jit(solution)/shard_map/backward_matmul/pallas_call | solution.py:251
  240.9 6.4 %backward_matmul.6 = (f32[256,1024]{1,0:T(8,128)S(1)}, bf16[256,1024]{1,0:T(8,128)(2,1)S(1)}) custom-call(bf16[128,3328]{1,0:T(8,128)(2,1)S(1)} %constant_dynamic-update-slice_fusion.refs_0_, bf16[128,3328]{1,0:T(8,128)(2,1)S(1)} %collective-permute-done.17.refs_1_, bf16[128,3328]{1,0:T(8,128)(2,1)S(1)} %constant_dynamic-update-slice_fusion.6.refs_2_, ...), custom_call_target="tpu_custom_call" | custom-call | flops 3489660928 | bytes 14417920 | tf_op jit(solution)/shard_map/backward_matmul/pallas_call | solution.py:251
  248.7 6.4 %backward_matmul.8 = (f32[256,1024]{1,0:T(8,128)S(1)}, bf16[256,1024]{1,0:T(8,128)(2,1)S(1)}) custom-call(bf16[128,3328]{1,0:T(8,128)(2,1)S(1)} %constant_dynamic-update-slice_fusion.refs_0_, bf16[128,3328]{1,0:T(8,128)(2,1)S(1)} %collective-permute-done.17.refs_1_, bf16[128,3328]{1,0:T(8,128)(2,1)S(1)} %constant_dynamic-update-slice_fusion.6.refs_2_, ...), custom_call_target="tpu_custom_call" | custom-call | flops 3489660928 | bytes 14417920 | tf_op jit(solution)/shard_map/backward_matmul/pallas_call | solution.py:251
  255.9 6.4 %backward_matmul.9 = (f32[256,1024]{1,0:T(8,128)S(1)}, bf16[256,1024]{1,0:T(8,128)(2,1)S(1)}) custom-call(bf16[128,3328]{1,0:T(8,128)(2,1)S(1)} %constant_dynamic-update-slice_fusion.refs_0_, bf16[128,3328]{1,0:T(8,128)(2,1)S(1)} %collective-permute-done.17.refs_1_, bf16[128,3328]{1,0:T(8,128)(2,1)S(1)} %constant_dynamic-update-slice_fusion.6.refs_2_, ...), custom_call_target="tpu_custom_call" | custom-call | flops 3489660928 | bytes 14417920 | tf_op jit(solution)/shard_map/backward_matmul/pallas_call | solution.py:251
  263.9 1.6 collective-permute-start.35
  266.5 1.6 collective-permute-start.25
  269.1 5.5 %collective-permute-done.35 = bf16[128,1024]{1,0:T(8,128)(2,1)S(1)} collective-permute-done((bf16[128,1024]{1,0:T(8,128)(2,1)S(1)}, bf16[128,1024]{1,0:T(8,128)(2,1)S(1)}, u32[]{:S(2)}, u32[]{:S(2)}) %collective-permute-start.35) | collective-permute-done | bytes 262176 | tf_op jit(solution)/shard_map/ppermute | solution.py:39
  276.1 1.9 collective-permute-done.25
  278.0 2.2 collective-permute-start.26
  280.3 7.4 %collective-permute-done.26.refs_2_ = bf16[64,1024]{1,0:T(8,128)(2,1)S(1)} collective-permute-done((bf16[64,1024]{1,0:T(8,128)(2,1)S(1)}, bf16[64,1024]{1,0:T(8,128)(2,1)S(1)}, u32[]{:S(2)}, u32[]{:S(2)}) %collective-permute-start.26) | collective-permute-done | bytes 131104 | tf_op jit(solution)/shard_map/ppermute | solution.py:39
  289.0 2.7 collective-permute-start.40
  293.2 2.0 collective-permute-start.45
  295.2 1.6 broadcast_in_dim.8
  296.8 3.3 dynamic_update_slice.48
  302.3 2.7 collective-permute-start.38
  306.7 5.0 %collective-permute-done.45 = bf16[128,1024]{1,0:T(8,128)(2,1)} collective-permute-done((bf16[128,1024]{1,0:T(8,128)(2,1)}, bf16[128,1024]{1,0:T(8,128)(2,1)}, u32[]{:S(2)}, u32[]{:S(2)}) %collective-permute-start.45) | collective-permute-done | bytes 262176 | tf_op jit(solution)/shard_map/ppermute | solution.py:39
  314.8 5.4 %collective-permute-done.46.refs_2_ = bf16[64,1024]{1,0:T(8,128)(2,1)S(1)} collective-permute-done((bf16[64,1024]{1,0:T(8,128)(2,1)S(1)}, bf16[64,1024]{1,0:T(8,128)(2,1)S(1)}, u32[]{:S(2)}, u32[]{:S(2)}) %collective-permute-start.46) | collective-permute-done | bytes 131104 | tf_op jit(solution)/shard_map/ppermute | solution.py:39
  321.5 2.1 collective-permute-start.33
  323.6 3.4 dynamic_update_slice.49
  327.4 2.5 collective-permute-start.42
  331.4 8.7 %collective-permute-done.50 = f32[1,4096]{1,0:T(1,128)S(1)} collective-permute-done((f32[1,4096]{1,0:T(1,128)S(1)}, f32[1,4096]{1,0:T(1,128)S(1)}, u32[]{:S(2)}, u32[]{:S(2)}) %collective-permute-start.50) | collective-permute-done | bytes 16416 | tf_op jit(solution)/shard_map/ppermute | solution.py:39
  341.0 2.1 collective-permute-start.48
  343.1 3.4 dynamic_update_slice.50
  346.5 2.0 dynamic_update_slice.51
  348.5 3.4 dynamic_update_slice.52
  351.9 3.3 dynamic_update_slice.53
  355.2 3.3 dynamic_update_slice.54
  358.6 2.0 dynamic_update_slice.55
  360.6 3.4 dynamic_update_slice.56
  364.6 3.3 dynamic_update_slice.57
  368.0 3.4 dynamic_update_slice.58
  371.4 2.0 dynamic_update_slice.59
  373.4 2.8 dynamic_update_slice.60
  376.2 2.8 dynamic_update_slice.61
  379.0 2.7 dynamic_update_slice.62
  381.7 1.9 dynamic_update_slice.63
  (227 shorter events, 68.5 us)
Async XLA Ops:
  0.7 22.9 %copy-start.17 = (f32[4096]{0:T(1024)S(1)}, f32[4096]{0:T(1024)}, u32[]{:S(2)}) copy-start(f32[4096]{0:T(1024)} %param.11) | copy-start | bytes 49156
  0.7 22.9 %copy-start.4 = (bf16[2,4096,16]{1,2,0:T(8,128)(2,1)S(1)}, bf16[2,4096,16]{1,2,0:T(8,128)(2,1)}, u32[]{:S(2)}) copy-start(bf16[2,4096,16]{1,2,0:T(8,128)(2,1)} %param.13) | copy-start | bytes 786436
  0.7 68.9 %collective-permute-start.2 = (bf16[256,4096]{1,0:T(8,128)(2,1)}, bf16[256,4096]{1,0:T(8,128)(2,1)}, u32[]{:S(2)}, u32[]{:S(2)}) collective-permute-start(bf16[256,4096]{1,0:T(8,128)(2,1)} %x_ref.1), channel_id=1, source_target_pairs={{0,16},{16,0},{1,17},{17,1},{2,18},{18,2},{3,19},{19,3},{4,20},{20... | collective-permute-start | bytes 6291464 | tf_op jit(solution)/shard_map/ppermute | solution.py:39
  22.8 46.7 %collective-permute-start.3 = (f32[256,2]{1,0:T(8,128)S(1)}, f32[256,2]{1,0:T(8,128)}, u32[]{:S(2)}, u32[]{:S(2)}) collective-permute-start(f32[256,2]{1,0:T(8,128)S(1)} %copy.73.s_ref), channel_id=1, source_target_pairs={{0,16},{16,0},{1,17},{17,1},{2,18},{18,2},{3,19},{19,3},{4,20},{20... | collective-permute-start | bytes 6152 | tf_op jit(solution)/shard_map/ppermute | solution.py:39
  44.3 19.7 %collective-permute-start.4 = (bf16[128,3328]{1,0:T(8,128)(2,1)}, bf16[128,3328]{1,0:T(8,128)(2,1)S(1)}, u32[]{:S(2)}, u32[]{:S(2)}) collective-permute-start(bf16[128,3328]{1,0:T(8,128)(2,1)} %get-tuple-element.46), channel_id=1, source_target_pairs={{0,1},{1,0},{2,3},{3,2},{4,5},{5,4},{6,7},{7,6},{8,9},{9,8},{10,11... | collective-permute-start | bytes 2555912 | tf_op jit(solution)/shard_map/ppermute | solution.py:39
  62.6 3.9 %collective-permute-start = (bf16[128,3328]{1,0:T(8,128)(2,1)}, bf16[128,3328]{1,0:T(8,128)(2,1)}, u32[]{:S(2)}, u32[]{:S(2)}) collective-permute-start(bf16[128,3328]{1,0:T(8,128)(2,1)} %get-tuple-element.43), channel_id=1, source_target_pairs={{0,1},{1,0},{2,3},{3,2},{4,5},{5,4},{6,7},{7,6},{8,9},{9,8},{10,11... | collective-permute-start | bytes 2555912 | tf_op jit(solution)/shard_map/ppermute | solution.py:39
  65.6 25.2 %collective-permute-start.5 = (bf16[64,3328]{1,0:T(8,128)(2,1)S(1)}, bf16[64,3328]{1,0:T(8,128)(2,1)S(1)}, u32[]{:S(2)}, u32[]{:S(2)}) collective-permute-start(bf16[64,3328]{1,0:T(8,128)(2,1)S(1)} %add_convert_fusion.4), channel_id=1, source_target_pairs={{0,2},{1,3},{2,0},{3,1},{4,6},{5,7},{6,4},{7,5},{8,10},{9,11},{10,... | collective-permute-start | bytes 1277960 | tf_op jit(solution)/shard_map/ppermute | solution.py:39
  68.3 82.3 %collective-permute-start.1 = (bf16[64,3328]{1,0:T(8,128)(2,1)}, bf16[64,3328]{1,0:T(8,128)(2,1)}, u32[]{:S(2)}, u32[]{:S(2)}) collective-permute-start(bf16[64,3328]{1,0:T(8,128)(2,1)} %add_convert_fusion.5), channel_id=1, source_target_pairs={{0,2},{1,3},{2,0},{3,1},{4,6},{5,7},{6,4},{7,5},{8,10},{9,11},{10,... | collective-permute-start | bytes 1277960 | tf_op jit(solution)/shard_map/ppermute | solution.py:39
  73.0 16.9 %collective-permute-start.9 = (f32[2,128,32]{2,1,0:T(8,128)S(1)}, f32[2,128,32]{2,1,0:T(8,128)S(1)}, u32[]{:S(2)}, u32[]{:S(2)}) collective-permute-start(f32[2,128,32]{2,1,0:T(8,128)S(1)} %pad_maximum_fusion.6), channel_id=1, source_target_pairs={{0,1},{1,0},{2,3},{3,2},{4,5},{5,4},{6,7},{7,6},{8,9},{9,8},{10,11... | collective-permute-start | bytes 98312 | tf_op jit(solution)/shard_map/ppermute | solution.py:39
  89.4 17.9 %collective-permute-start.11 = (bf16[128,3328]{1,0:T(8,128)(2,1)S(1)}, bf16[128,3328]{1,0:T(8,128)(2,1)S(1)}, u32[]{:S(2)}, u32[]{:S(2)}) collective-permute-start(bf16[128,3328]{1,0:T(8,128)(2,1)S(1)} %get-tuple-element.52), channel_id=1, source_target_pairs={{0,1},{1,0},{2,3},{3,2},{4,5},{5,4},{6,7},{7,6},{8,9},{9,8},{10,11... | collective-permute-start | bytes 2555912 | tf_op jit(solution)/shard_map/ppermute | solution.py:39
  90.0 17.2 %collective-permute-start.10 = (f32[2,64,32]{2,1,0:T(8,128)S(1)}, f32[2,64,32]{2,1,0:T(8,128)S(1)}, u32[]{:S(2)}, u32[]{:S(2)}) collective-permute-start(f32[2,64,32]{2,1,0:T(8,128)S(1)} %slice.156), channel_id=1, source_target_pairs={{0,2},{1,3},{2,0},{3,1},{4,6},{5,7},{6,4},{7,5},{8,10},{9,11},{10,... | collective-permute-start | bytes 49160 | tf_op jit(solution)/shard_map/ppermute | solution.py:39
  107.1 2.4 collective-permute-start.6
  107.3 12.7 %collective-permute-start.12 = (bf16[64,3328]{1,0:T(8,128)(2,1)S(1)}, bf16[64,3328]{1,0:T(8,128)(2,1)S(1)}, u32[]{:S(2)}, u32[]{:S(2)}) collective-permute-start(bf16[64,3328]{1,0:T(8,128)(2,1)S(1)} %add_convert_fusion.1), channel_id=1, source_target_pairs={{0,2},{1,3},{2,0},{3,1},{4,6},{5,7},{6,4},{7,5},{8,10},{9,11},{10,... | collective-permute-start | bytes 1277960 | tf_op jit(solution)/shard_map/ppermute | solution.py:39
  109.6 21.6 %copy-start.10 = (f32[128,3328]{1,0:T(8,128)S(1)}, f32[128,3328]{1,0:T(8,128)}, u32[]{:S(2)}) copy-start(f32[128,3328]{1,0:T(8,128)} %copy-done.9) | copy-start | bytes 5111812
  109.7 21.6 %copy-start.11 = (bf16[64,6656]{1,0:T(8,128)(2,1)S(1)}, bf16[64,6656]{1,0:T(8,128)(2,1)}, u32[]{:S(2)}) copy-start(bf16[64,6656]{1,0:T(8,128)(2,1)} %refs_4_.8) | copy-start | bytes 2555908
  109.7 21.6 %copy-start.13 = (bf16[128,3328]{1,0:T(8,128)(2,1)S(1)}, bf16[128,3328]{1,0:T(8,128)(2,1)}, u32[]{:S(2)}) copy-start(bf16[128,3328]{1,0:T(8,128)(2,1)} %copy-done.12) | copy-start | bytes 2555908
  109.7 21.6 %copy-start.14 = (bf16[2,16,6656]{2,1,0:T(8,128)(2,1)S(1)}, bf16[2,16,6656]{2,1,0:T(8,128)(2,1)}, u32[]{:S(2)}) copy-start(bf16[2,16,6656]{2,1,0:T(8,128)(2,1)} %refs_6_.3) | copy-start | bytes 1277956
  109.7 19.0 %collective-permute-start.7 = (bf16[64,3328]{1,0:T(8,128)(2,1)S(1)}, bf16[64,3328]{1,0:T(8,128)(2,1)S(1)}, u32[]{:S(2)}, u32[]{:S(2)}) collective-permute-start(bf16[64,3328]{1,0:T(8,128)(2,1)S(1)} %add_convert_fusion.3), channel_id=1, source_target_pairs={{0,2},{1,3},{2,0},{3,1},{4,6},{5,7},{6,4},{7,5},{8,10},{9,11},{10,... | collective-permute-start | bytes 1277960 | tf_op jit(solution)/shard_map/ppermute | solution.py:39
  120.1 11.1 %collective-permute-start.13 = (bf16[64,3328]{1,0:T(8,128)(2,1)S(1)}, bf16[64,3328]{1,0:T(8,128)(2,1)S(1)}, u32[]{:S(2)}, u32[]{:S(2)}) collective-permute-start(bf16[64,3328]{1,0:T(8,128)(2,1)S(1)} %add_convert_fusion), channel_id=1, source_target_pairs={{0,16},{16,0},{1,17},{17,1},{2,18},{18,2},{3,19},{19,3},{4,20},{20... | collective-permute-start | bytes 1277960 | tf_op jit(solution)/shard_map/ppermute | solution.py:39
  129.6 21.0 %collective-permute-start.8 = (bf16[64,3328]{1,0:T(8,128)(2,1)}, bf16[64,3328]{1,0:T(8,128)(2,1)}, u32[]{:S(2)}, u32[]{:S(2)}) collective-permute-start(bf16[64,3328]{1,0:T(8,128)(2,1)} %add_convert_fusion.2), channel_id=1, source_target_pairs={{0,16},{16,0},{1,17},{17,1},{2,18},{18,2},{3,19},{19,3},{4,20},{20... | collective-permute-start | bytes 1277960 | tf_op jit(solution)/shard_map/ppermute | solution.py:39
  138.5 12.2 %collective-permute-start.15 = (bf16[64,3328]{1,0:T(8,128)(2,1)}, bf16[64,3328]{1,0:T(8,128)(2,1)}, u32[]{:S(2)}, u32[]{:S(2)}) collective-permute-start(bf16[64,3328]{1,0:T(8,128)(2,1)} %get-tuple-element.54), channel_id=1, source_target_pairs={{0,2},{1,3},{2,0},{3,1},{4,6},{5,7},{6,4},{7,5},{8,10},{9,11},{10,... | collective-permute-start | bytes 1277960 | tf_op jit(solution)/shard_map/ppermute | solution.py:39
  139.7 10.9 %collective-permute-start.14 = (bf16[64,3328]{1,0:T(8,128)(2,1)}, bf16[64,3328]{1,0:T(8,128)(2,1)}, u32[]{:S(2)}, u32[]{:S(2)}) collective-permute-start(bf16[64,3328]{1,0:T(8,128)(2,1)} %get-tuple-element.53), channel_id=1, source_target_pairs={{0,16},{16,0},{1,17},{17,1},{2,18},{18,2},{3,19},{19,3},{4,20},{20... | collective-permute-start | bytes 1277960 | tf_op jit(solution)/shard_map/ppermute | solution.py:39
  141.1 9.2 %collective-permute-start.52 = (bf16[2,64,16]{2,1,0:T(8,128)(2,1)S(1)}, bf16[2,64,16]{2,1,0:T(8,128)(2,1)S(1)}, u32[]{:S(2)}, u32[]{:S(2)}) collective-permute-start(bf16[2,64,16]{2,1,0:T(8,128)(2,1)S(1)} %slice_select_fusion), channel_id=1, source_target_pairs={{0,2},{1,3},{2,0},{3,1},{4,6},{5,7},{6,4},{7,5},{8,10},{9,11},{10,... | collective-permute-start | bytes 12296 | tf_op jit(solution)/shard_map/ppermute | solution.py:39
  150.5 13.4 %collective-permute-start.53 = (bf16[2,128,16]{1,2,0:T(8,128)(2,1)S(1)}, bf16[2,128,16]{1,2,0:T(8,128)(2,1)S(1)}, u32[]{:S(2)}, u32[]{:S(2)}) collective-permute-start(bf16[2,128,16]{1,2,0:T(8,128)(2,1)S(1)} %pad_maximum_fusion.9), channel_id=1, source_target_pairs={{0,1},{1,0},{2,3},{3,2},{4,5},{5,4},{6,7},{7,6},{8,9},{9,8},{10,11... | collective-permute-start | bytes 24584 | tf_op jit(solution)/shard_map/ppermute | solution.py:39
  162.3 4.0 %collective-permute-start.27 = (f32[64,33]{1,0:T(8,128)S(1)}, f32[64,33]{1,0:T(8,128)S(1)}, u32[]{:S(2)}, u32[]{:S(2)}) collective-permute-start(f32[64,33]{1,0:T(8,128)S(1)} %add.330), channel_id=1, source_target_pairs={{0,4},{4,0},{8,12},{12,8},{1,5},{5,1},{9,13},{13,9},{2,6},{6,2},{1... | collective-permute-start | bytes 25352 | tf_op jit(solution)/shard_map/ppermute | solution.py:39
  166.3 21.4 %copy-start.2 = (bf16[256,4096]{1,0:T(8,128)(2,1)S(1)}, bf16[256,4096]{1,0:T(8,128)(2,1)}, u32[]{:S(2)}) copy-start(bf16[256,4096]{1,0:T(8,128)(2,1)} %copy-done.1) | copy-start | bytes 6291460
  166.3 4.9 %collective-permute-start.28 = (f32[64,33]{1,0:T(8,128)S(1)}, f32[64,33]{1,0:T(8,128)S(1)}, u32[]{:S(2)}, u32[]{:S(2)}) collective-permute-start(f32[64,33]{1,0:T(8,128)S(1)} %add.331), channel_id=1, source_target_pairs={{0,8},{4,12},{8,0},{12,4},{1,9},{5,13},{9,1},{13,5},{2,10},{6,14},... | collective-permute-start | bytes 25352 | tf_op jit(solution)/shard_map/ppermute | solution.py:39
  171.2 3.9 %collective-permute-start.29 = (f32[64,33]{1,0:T(8,128)S(1)}, f32[64,33]{1,0:T(8,128)S(1)}, u32[]{:S(2)}, u32[]{:S(2)}) collective-permute-start(f32[64,33]{1,0:T(8,128)S(1)} %add.332), channel_id=1, source_target_pairs={{0,16},{16,0},{1,17},{17,1},{2,18},{18,2},{3,19},{19,3},{4,20},{20... | collective-permute-start | bytes 25352 | tf_op jit(solution)/shard_map/ppermute | solution.py:39
  173.4 26.6 %collective-permute-start.16 = (bf16[64,3328]{1,0:T(8,128)(2,1)}, bf16[64,3328]{1,0:T(8,128)(2,1)}, u32[]{:S(2)}, u32[]{:S(2)}) collective-permute-start(bf16[64,3328]{1,0:T(8,128)(2,1)} %get-tuple-element.55), channel_id=1, source_target_pairs={{0,2},{1,3},{2,0},{3,1},{4,6},{5,7},{6,4},{7,5},{8,10},{9,11},{10,... | collective-permute-start | bytes 1277960 | tf_op jit(solution)/shard_map/ppermute | solution.py:39
  175.1 9.4 %collective-permute-start.30 = (f32[2,64,33]{2,1,0:T(8,128)S(1)}, f32[2,64,33]{2,1,0:T(8,128)S(1)}, u32[]{:S(2)}, u32[]{:S(2)}) collective-permute-start(f32[2,64,33]{2,1,0:T(8,128)S(1)} %pad_maximum_fusion.8), channel_id=1, source_target_pairs={{0,2},{1,3},{2,0},{3,1},{4,6},{5,7},{6,4},{7,5},{8,10},{9,11},{10,... | collective-permute-start | bytes 50696 | tf_op jit(solution)/shard_map/ppermute | solution.py:39
  178.1 25.9 %collective-permute-start.20 = (bf16[128,3328]{1,0:T(8,128)(2,1)}, bf16[128,3328]{1,0:T(8,128)(2,1)}, u32[]{:S(2)}, u32[]{:S(2)}) collective-permute-start(bf16[128,3328]{1,0:T(8,128)(2,1)} %constant_dynamic-update-slice_fusion.2.refs_0_), channel_id=1, source_target_pairs={{0,1},{1,0},{2,3},{3,2},{4,5},{5,4},{6,7},{7,6},{8,9},{9,8},{10,11... | collective-permute-start | bytes 2555912 | tf_op jit(solution)/shard_map/ppermute | solution.py:39
  178.1 23.5 %collective-permute-start.18 = (bf16[64,3328]{1,0:T(8,128)(2,1)}, bf16[64,3328]{1,0:T(8,128)(2,1)}, u32[]{:S(2)}, u32[]{:S(2)}) collective-permute-start(bf16[64,3328]{1,0:T(8,128)(2,1)} %get-tuple-element.56), channel_id=1, source_target_pairs={{0,16},{16,0},{1,17},{17,1},{2,18},{18,2},{3,19},{19,3},{4,20},{20... | collective-permute-start | bytes 1277960 | tf_op jit(solution)/shard_map/ppermute | solution.py:39
  184.5 3.1 collective-permute-start.31
  186.4 12.5 %collective-permute-start.21 = (bf16[64,3328]{1,0:T(8,128)(2,1)}, bf16[64,3328]{1,0:T(8,128)(2,1)}, u32[]{:S(2)}, u32[]{:S(2)}) collective-permute-start(bf16[64,3328]{1,0:T(8,128)(2,1)} %collective-permute-done.14.refs_7_), channel_id=1, source_target_pairs={{0,2},{1,3},{2,0},{3,1},{4,6},{5,7},{6,4},{7,5},{8,10},{9,11},{10,... | collective-permute-start | bytes 1277960 | tf_op jit(solution)/shard_map/ppermute | solution.py:39
  200.0 6.8 %collective-permute-start.22 = (bf16[128,3328]{1,0:T(8,128)(2,1)S(1)}, bf16[128,3328]{1,0:T(8,128)(2,1)S(1)}, u32[]{:S(2)}, u32[]{:S(2)}) collective-permute-start(bf16[128,3328]{1,0:T(8,128)(2,1)S(1)} %constant_dynamic-update-slice_fusion.4.refs_2_), channel_id=1, source_target_pairs={{0,1},{1,0},{2,3},{3,2},{4,5},{5,4},{6,7},{7,6},{8,9},{9,8},{10,11... | collective-permute-start | bytes 2555912 | tf_op jit(solution)/shard_map/ppermute | solution.py:39
  201.1 28.8 %collective-permute-start.17 = (bf16[128,3328]{1,0:T(8,128)(2,1)S(1)}, bf16[128,3328]{1,0:T(8,128)(2,1)S(1)}, u32[]{:S(2)}, u32[]{:S(2)}) collective-permute-start(bf16[128,3328]{1,0:T(8,128)(2,1)S(1)} %constant_dynamic-update-slice_fusion.refs_0_), channel_id=1, source_target_pairs={{0,1},{1,0},{2,3},{3,2},{4,5},{5,4},{6,7},{7,6},{8,9},{9,8},{10,11... | collective-permute-start | bytes 2555912 | tf_op jit(solution)/shard_map/ppermute | solution.py:39
  201.7 27.7 %collective-permute-start.19 = (bf16[64,3328]{1,0:T(8,128)(2,1)}, bf16[64,3328]{1,0:T(8,128)(2,1)S(1)}, u32[]{:S(2)}, u32[]{:S(2)}) collective-permute-start(bf16[64,3328]{1,0:T(8,128)(2,1)} %collective-permute-done.18), channel_id=1, source_target_pairs={{0,2},{1,3},{2,0},{3,1},{4,6},{5,7},{6,4},{7,5},{8,10},{9,11},{10,... | collective-permute-start | bytes 1277960 | tf_op jit(solution)/shard_map/ppermute | solution.py:39
  229.4 2.4 collective-permute-start.23
  232.4 31.3 %collective-permute-start.54 = (bf16[16,6656]{1,0:T(8,128)(2,1)S(1)}, bf16[16,6656]{1,0:T(8,128)(2,1)S(1)}, u32[]{:S(2)}, u32[]{:S(2)}) collective-permute-start(bf16[16,6656]{1,0:T(8,128)(2,1)S(1)} %fusion.9), channel_id=1, source_target_pairs={{0,16},{16,0},{1,17},{17,1},{2,18},{18,2},{3,19},{19,3},{4,20},{20... | collective-permute-start | bytes 638984 | tf_op jit(solution)/shard_map/ppermute | solution.py:39
  240.2 23.5 %collective-permute-start.34 = (bf16[256,1024]{1,0:T(8,128)(2,1)S(1)}, bf16[256,1024]{1,0:T(8,128)(2,1)S(1)}, u32[]{:S(2)}, u32[]{:S(2)}) collective-permute-start(bf16[256,1024]{1,0:T(8,128)(2,1)S(1)} %get-tuple-element.64), channel_id=1, source_target_pairs={{0,16},{16,0},{1,17},{17,1},{2,18},{18,2},{3,19},{19,3},{4,20},{20... | collective-permute-start | bytes 1572872 | tf_op jit(solution)/shard_map/ppermute | solution.py:39
  247.3 18.9 %collective-permute-start.24 = (bf16[256,1024]{1,0:T(8,128)(2,1)S(1)}, bf16[256,1024]{1,0:T(8,128)(2,1)S(1)}, u32[]{:S(2)}, u32[]{:S(2)}) collective-permute-start(bf16[256,1024]{1,0:T(8,128)(2,1)S(1)} %get-tuple-element.59), channel_id=1, source_target_pairs={{0,16},{16,0},{1,17},{17,1},{2,18},{18,2},{3,19},{19,3},{4,20},{20... | collective-permute-start | bytes 1572872 | tf_op jit(solution)/shard_map/ppermute | solution.py:39
  255.1 32.9 %collective-permute-start.39 = (bf16[256,1024]{1,0:T(8,128)(2,1)S(1)}, bf16[256,1024]{1,0:T(8,128)(2,1)S(1)}, u32[]{:S(2)}, u32[]{:S(2)}) collective-permute-start(bf16[256,1024]{1,0:T(8,128)(2,1)S(1)} %get-tuple-element.67), channel_id=1, source_target_pairs={{0,16},{16,0},{1,17},{17,1},{2,18},{18,2},{3,19},{19,3},{4,20},{20... | collective-permute-start | bytes 1572872 | tf_op jit(solution)/shard_map/ppermute | solution.py:39
  262.3 30.0 %collective-permute-start.44 = (bf16[256,1024]{1,0:T(8,128)(2,1)S(1)}, bf16[256,1024]{1,0:T(8,128)(2,1)S(1)}, u32[]{:S(2)}, u32[]{:S(2)}) collective-permute-start(bf16[256,1024]{1,0:T(8,128)(2,1)S(1)} %get-tuple-element.71), channel_id=1, source_target_pairs={{0,16},{16,0},{1,17},{17,1},{2,18},{18,2},{3,19},{19,3},{4,20},{20... | collective-permute-start | bytes 1572872 | tf_op jit(solution)/shard_map/ppermute | solution.py:39
  263.9 10.7 %collective-permute-start.35 = (bf16[128,1024]{1,0:T(8,128)(2,1)S(1)}, bf16[128,1024]{1,0:T(8,128)(2,1)S(1)}, u32[]{:S(2)}, u32[]{:S(2)}) collective-permute-start(bf16[128,1024]{1,0:T(8,128)(2,1)S(1)} %dynamic-slice_convert_fusion.2), channel_id=1, source_target_pairs={{0,4},{4,0},{8,12},{12,8},{1,5},{5,1},{9,13},{13,9},{2,6},{6,2},{1... | collective-permute-start | bytes 786440 | tf_op jit(solution)/shard_map/ppermute | solution.py:39
  266.5 21.2 %copy-start.3 = (bf16[64,4096]{1,0:T(8,128)(2,1)S(1)}, bf16[64,4096]{1,0:T(8,128)(2,1)}, u32[]{:S(2)}) copy-start(bf16[64,4096]{1,0:T(8,128)(2,1)} %constant_dynamic-slice_fusion.8.refs_3_) | copy-start | bytes 1572868
  266.5 21.2 %copy-start.18 = (f32[4096]{0:T(1024)S(1)}, f32[4096]{0:T(1024)}, u32[]{:S(2)}) copy-start(f32[4096]{0:T(1024)} %param.11) | copy-start | bytes 49156
  266.5 11.4 %collective-permute-start.25 = (bf16[128,1024]{1,0:T(8,128)(2,1)S(1)}, bf16[128,1024]{1,0:T(8,128)(2,1)S(1)}, u32[]{:S(2)}, u32[]{:S(2)}) collective-permute-start(bf16[128,1024]{1,0:T(8,128)(2,1)S(1)} %dynamic-slice_convert_fusion.3), channel_id=1, source_target_pairs={{0,4},{4,0},{8,12},{12,8},{1,5},{5,1},{9,13},{13,9},{2,6},{6,2},{1... | collective-permute-start | bytes 786440 | tf_op jit(solution)/shard_map/ppermute | solution.py:39
  274.7 17.0 %collective-permute-start.36 = (bf16[64,1024]{1,0:T(8,128)(2,1)S(1)}, bf16[64,1024]{1,0:T(8,128)(2,1)S(1)}, u32[]{:S(2)}, u32[]{:S(2)}) collective-permute-start(bf16[64,1024]{1,0:T(8,128)(2,1)S(1)} %get-tuple-element.84), channel_id=1, source_target_pairs={{0,8},{4,12},{8,0},{12,4},{1,9},{5,13},{9,1},{13,5},{2,10},{6,14},... | collective-permute-start | bytes 393224 | tf_op jit(solution)/shard_map/ppermute | solution.py:39
  278.0 9.6 %collective-permute-start.26 = (bf16[64,1024]{1,0:T(8,128)(2,1)S(1)}, bf16[64,1024]{1,0:T(8,128)(2,1)S(1)}, u32[]{:S(2)}, u32[]{:S(2)}) collective-permute-start(bf16[64,1024]{1,0:T(8,128)(2,1)S(1)} %get-tuple-element.86), channel_id=1, source_target_pairs={{0,8},{4,12},{8,0},{12,4},{1,9},{5,13},{9,1},{13,5},{2,10},{6,14},... | collective-permute-start | bytes 393224 | tf_op jit(solution)/shard_map/ppermute | solution.py:39
  287.9 32.7 %collective-permute-start.32 = (bf16[64,1024]{1,0:T(8,128)(2,1)S(1)}, bf16[64,1024]{1,0:T(8,128)(2,1)}, u32[]{:S(2)}, u32[]{:S(2)}) collective-permute-start(bf16[64,1024]{1,0:T(8,128)(2,1)S(1)} %get-tuple-element.62), channel_id=1, source_target_pairs={{0,8},{4,12},{8,0},{12,4},{1,9},{5,13},{9,1},{13,5},{2,10},{6,14},... | collective-permute-start | bytes 393224 | tf_op jit(solution)/shard_map/ppermute | solution.py:39
  289.0 15.9 %collective-permute-start.40 = (bf16[128,1024]{1,0:T(8,128)(2,1)}, bf16[128,1024]{1,0:T(8,128)(2,1)}, u32[]{:S(2)}, u32[]{:S(2)}) collective-permute-start(bf16[128,1024]{1,0:T(8,128)(2,1)} %dynamic-slice_convert_fusion.1), channel_id=1, source_target_pairs={{0,4},{4,0},{8,12},{12,8},{1,5},{5,1},{9,13},{13,9},{2,6},{6,2},{1... | collective-permute-start | bytes 786440 | tf_op jit(solution)/shard_map/ppermute | solution.py:39
  292.0 9.6 %collective-permute-start.37 = (bf16[64,1024]{1,0:T(8,128)(2,1)S(1)}, bf16[64,1024]{1,0:T(8,128)(2,1)S(1)}, u32[]{:S(2)}, u32[]{:S(2)}) collective-permute-start(bf16[64,1024]{1,0:T(8,128)(2,1)S(1)} %get-tuple-element.65), channel_id=1, source_target_pairs={{0,8},{4,12},{8,0},{12,4},{1,9},{5,13},{9,1},{13,5},{2,10},{6,14},... | collective-permute-start | bytes 393224 | tf_op jit(solution)/shard_map/ppermute | solution.py:39
  293.2 18.5 %collective-permute-start.45 = (bf16[128,1024]{1,0:T(8,128)(2,1)}, bf16[128,1024]{1,0:T(8,128)(2,1)}, u32[]{:S(2)}, u32[]{:S(2)}) collective-permute-start(bf16[128,1024]{1,0:T(8,128)(2,1)} %dynamic-slice_convert_fusion), channel_id=1, source_target_pairs={{0,4},{4,0},{8,12},{12,8},{1,5},{5,1},{9,13},{13,9},{2,6},{6,2},{1... | collective-permute-start | bytes 786440 | tf_op jit(solution)/shard_map/ppermute | solution.py:39
  302.3 28.1 %collective-permute-start.38 = (bf16[128,1024]{1,0:T(8,128)(2,1)}, bf16[128,1024]{1,0:T(8,128)(2,1)}, u32[]{:S(2)}, u32[]{:S(2)}) collective-permute-start(bf16[128,1024]{1,0:T(8,128)(2,1)} %pad_maximum_fusion.3), channel_id=1, source_target_pairs={{0,4},{4,0},{8,12},{12,8},{1,5},{5,1},{9,13},{13,9},{2,6},{6,2},{1... | collective-permute-start | bytes 786440 | tf_op jit(solution)/shard_map/ppermute | solution.py:39
  305.9 8.7 %collective-permute-start.41 = (bf16[64,1024]{1,0:T(8,128)(2,1)S(1)}, bf16[64,1024]{1,0:T(8,128)(2,1)S(1)}, u32[]{:S(2)}, u32[]{:S(2)}) collective-permute-start(bf16[64,1024]{1,0:T(8,128)(2,1)S(1)} %get-tuple-element.82), channel_id=1, source_target_pairs={{0,8},{4,12},{8,0},{12,4},{1,9},{5,13},{9,1},{13,5},{2,10},{6,14},... | collective-permute-start | bytes 393224 | tf_op jit(solution)/shard_map/ppermute | solution.py:39
  312.7 7.6 %collective-permute-start.46 = (bf16[64,1024]{1,0:T(8,128)(2,1)S(1)}, bf16[64,1024]{1,0:T(8,128)(2,1)S(1)}, u32[]{:S(2)}, u32[]{:S(2)}) collective-permute-start(bf16[64,1024]{1,0:T(8,128)(2,1)S(1)} %get-tuple-element.80), channel_id=1, source_target_pairs={{0,8},{4,12},{8,0},{12,4},{1,9},{5,13},{9,1},{13,5},{2,10},{6,14},... | collective-permute-start | bytes 393224 | tf_op jit(solution)/shard_map/ppermute | solution.py:39
  320.5 9.4 %collective-permute-start.49 = (f32[1,4096]{1,0:T(1,128)S(1)}, f32[1,4096]{1,0:T(1,128)S(1)}, u32[]{:S(2)}, u32[]{:S(2)}) collective-permute-start(f32[1,4096]{1,0:T(1,128)S(1)} %constant_dynamic-update-slice_fusion.8), channel_id=1, source_target_pairs={{0,4},{4,0},{8,12},{12,8},{1,5},{5,1},{9,13},{13,9},{2,6},{6,2},{1... | collective-permute-start | bytes 49160 | tf_op jit(solution)/shard_map/ppermute | solution.py:39
  321.5 21.6 %collective-permute-start.33 = (bf16[128,1024]{1,0:T(8,128)(2,1)S(1)}, bf16[128,1024]{1,0:T(8,128)(2,1)S(1)}, u32[]{:S(2)}, u32[]{:S(2)}) collective-permute-start(bf16[128,1024]{1,0:T(8,128)(2,1)S(1)} %pad_maximum_fusion.2), channel_id=1, source_target_pairs={{0,4},{4,0},{8,12},{12,8},{1,5},{5,1},{9,13},{13,9},{2,6},{6,2},{1... | collective-permute-start | bytes 786440 | tf_op jit(solution)/shard_map/ppermute | solution.py:39
  327.0 14.0 %collective-permute-start.47 = (bf16[64,1024]{1,0:T(8,128)(2,1)S(1)}, bf16[64,1024]{1,0:T(8,128)(2,1)S(1)}, u32[]{:S(2)}, u32[]{:S(2)}) collective-permute-start(bf16[64,1024]{1,0:T(8,128)(2,1)S(1)} %get-tuple-element.73), channel_id=1, source_target_pairs={{0,8},{4,12},{8,0},{12,4},{1,9},{5,13},{9,1},{13,5},{2,10},{6,14},... | collective-permute-start | bytes 393224 | tf_op jit(solution)/shard_map/ppermute | solution.py:39
  327.4 13.5 %collective-permute-start.42 = (bf16[64,1024]{1,0:T(8,128)(2,1)S(1)}, bf16[64,1024]{1,0:T(8,128)(2,1)S(1)}, u32[]{:S(2)}, u32[]{:S(2)}) collective-permute-start(bf16[64,1024]{1,0:T(8,128)(2,1)S(1)} %get-tuple-element.69), channel_id=1, source_target_pairs={{0,8},{4,12},{8,0},{12,4},{1,9},{5,13},{9,1},{13,5},{2,10},{6,14},... | collective-permute-start | bytes 393224 | tf_op jit(solution)/shard_map/ppermute | solution.py:39
  330.0 10.1 %collective-permute-start.50 = (f32[1,4096]{1,0:T(1,128)S(1)}, f32[1,4096]{1,0:T(1,128)S(1)}, u32[]{:S(2)}, u32[]{:S(2)}) collective-permute-start(f32[1,4096]{1,0:T(1,128)S(1)} %add.355), channel_id=1, source_target_pairs={{0,8},{4,12},{8,0},{12,4},{1,9},{5,13},{9,1},{13,5},{2,10},{6,14},... | collective-permute-start | bytes 49160 | tf_op jit(solution)/shard_map/ppermute | solution.py:39
  340.1 23.9 %collective-permute-start.51 = (f32[1,4096]{1,0:T(1,128)S(1)}, f32[1,4096]{1,0:T(1,128)S(1)}, u32[]{:S(2)}, u32[]{:S(2)}) collective-permute-start(f32[1,4096]{1,0:T(1,128)S(1)} %add.356), channel_id=1, source_target_pairs={{0,16},{16,0},{1,17},{17,1},{2,18},{18,2},{3,19},{19,3},{4,20},{20... | collective-permute-start | bytes 49160 | tf_op jit(solution)/shard_map/ppermute | solution.py:39
  340.9 27.1 %collective-permute-start.43 = (bf16[128,1024]{1,0:T(8,128)(2,1)S(1)}, bf16[128,1024]{1,0:T(8,128)(2,1)S(1)}, u32[]{:S(2)}, u32[]{:S(2)}) collective-permute-start(bf16[128,1024]{1,0:T(8,128)(2,1)S(1)} %pad_maximum_fusion.4), channel_id=1, source_target_pairs={{0,4},{4,0},{8,12},{12,8},{1,5},{5,1},{9,13},{13,9},{2,6},{6,2},{1... | collective-permute-start | bytes 786440 | tf_op jit(solution)/shard_map/ppermute | solution.py:39
  341.0 35.2 %collective-permute-start.48 = (bf16[128,1024]{1,0:T(8,128)(2,1)S(1)}, bf16[128,1024]{1,0:T(8,128)(2,1)S(1)}, u32[]{:S(2)}, u32[]{:S(2)}) collective-permute-start(bf16[128,1024]{1,0:T(8,128)(2,1)S(1)} %pad_maximum_fusion.5), channel_id=1, source_target_pairs={{0,4},{4,0},{8,12},{12,8},{1,5},{5,1},{9,13},{13,9},{2,6},{6,2},{1... | collective-permute-start | bytes 786440 | tf_op jit(solution)/shard_map/ppermute | solution.py:39
  (17 other events, 135.1 us)

commit v3 on v2

--- a/solution.py
+++ b/solution.py
@@ -7,12 +7,14 @@
 
 MODEL_WIDTH = 16384
 ADAPTER_SCALE = 0.5
+HIDDEN_CHUNKS = 3
 WIDTH_CHUNKS = 4
-VMEM_BYTES = 40 * 1024 * 1024
+VMEM_BYTES = 28 * 1024 * 1024
 
 F32 = jnp.float32
 BF16 = jnp.bfloat16
 ANY = pl.BlockSpec(memory_space=pl.ANY)
+RESIDENT = pl.BlockSpec(memory_space=pltpu.VMEM)
 
 
 def bits_of(n):
@@ -56,103 +58,151 @@
     return out
 
 
-def halve(keep, send, axis, n):
-    parts = [keep, swap(send, axis, n, 1)]
-    for bit in range(1, bits_of(n)):
-        rows = parts[-1].shape[0]
-        parts.append(swap(total_of(parts, rows // 2, rows).astype(BF16), axis, n, 1 << bit))
-    return parts
-
-
 def params():
     return pltpu.CompilerParams(vmem_limit_bytes=VMEM_BYTES)
 
 
-def normalize(stream, stats, steering, gain, down, h, hid):
-    tokens, width = stream.shape
+def normalize(pieces, stats, steering, gain, down, h, hid, side, into=None):
+    tokens = stats.shape[0]
+    width = steering.shape[0]
     block = tokens // hid
     ranks = down.shape[0]
-
-    def place(p, h_ref):
-        return h_ref[0] ^ reversed_bits(p, bits_of(hid))
-
-    def kernel(h_ref, x_ref, s_ref, steer_ref, gain_ref, down_ref, out_ref, low_ref):
-        steered = x_ref[...].astype(F32) + s_ref[:, :1] * steer_ref[...]
-        normed = (steered * s_ref[:, 1:] * gain_ref[...]).astype(BF16)
+    n_into = 0 if into is None else 1
+
+    def token_block(p, s_ref):
+        return s_ref[0] ^ reversed_bits(p, bits_of(hid))
+
+    def kernel(s_ref, *refs):
+        x_refs = refs[: len(pieces)]
+        stat_ref, steer_ref, gain_ref, down_ref = refs[len(pieces) : len(pieces) + 4]
+        out_ref, low_ref = refs[-2:]
+        x = jnp.concatenate([ref[...].astype(F32) for ref in x_refs], axis=1)
+        steered = x + stat_ref[:, :1] * steer_ref[...]
+        normed = (steered * stat_ref[:, 1:] * gain_ref[...]).astype(BF16)
         out_ref[...] = normed
         low_ref[...] = lax.dot_general(
             normed, down_ref[...], (((1,), (1,)), ((), ())), preferred_element_type=F32
         )
 
+    scalars = [h]
+    specs = []
+    for x, where in pieces:
+        if where is None:
+            specs.append(pl.BlockSpec((block, x.shape[1]), lambda p, s_ref: (token_block(p, s_ref), 0)))
+        else:
+            scalars.append(where.me)
+            specs.append(
+                pl.BlockSpec((block, x.shape[1]), lambda p, s_ref: (where.at(token_block(p, s_ref), s_ref[1]), 0))
+            )
+    whole = lambda n: pl.BlockSpec((n, width), lambda p, s_ref: (0, 0))
     return pl.pallas_call(
         kernel,
         grid_spec=pltpu.PrefetchScalarGridSpec(
             num_scalar_prefetch=1,
             grid=(hid,),
-            in_specs=[
-                pl.BlockSpec((block, width), lambda p, h_ref: (place(p, h_ref), 0)),
-                pl.BlockSpec((block, 2), lambda p, h_ref: (place(p, h_ref), 0)),
-                pl.BlockSpec((1, width), lambda p, h_ref: (0, 0)),
-                pl.BlockSpec((1, width), lambda p, h_ref: (0, 0)),
-                pl.BlockSpec((ranks, width), lambda p, h_ref: (0, 0)),
+            in_specs=specs
+            + [
+                pl.BlockSpec((block, 2), lambda p, s_ref: (token_block(p, s_ref), 0)),
+                whole(1),
+                whole(1),
+                whole(ranks),
+            ]
+            + [ANY] * n_into,
+            out_specs=[
+                pl.BlockSpec((block, width), lambda p, s_ref: (2 * p + side, 0)),
+                pl.BlockSpec((block, ranks), lambda p, s_ref: (p, 0)),
             ],
-            out_specs=[
-                pl.BlockSpec((block, width), lambda p, h_ref: (p, 0)),
-                pl.BlockSpec((block, ranks), lambda p, h_ref: (p, 0)),
-            ],
         ),
         out_shape=[
-            jax.ShapeDtypeStruct((tokens, width), BF16),
+            jax.ShapeDtypeStruct((2 * tokens, width), BF16),
             jax.ShapeDtypeStruct((tokens, ranks), F32),
         ],
+        input_output_aliases={len(pieces) + 5: 0} if n_into else {},
         compiler_params=params(),
         cost_estimate=pl.CostEstimate(
             flops=2 * tokens * width * ranks, bytes_accessed=4 * tokens * width, transcendentals=0
         ),
         name="normalize",
-    )(h.reshape(1), stream, stats, steering.reshape(1, width), gain.reshape(1, width), down)
-
-
-def forward_matmul(x, weights, first, tiles, tile, after=()):
+    )(
+        jnp.stack(scalars),
+        *[x for x, _ in pieces],
+        stats,
+        steering.reshape(1, width),
+        gain.reshape(1, width),
+        down,
+        *((into,) if n_into else ()),
+    )
+
+
+class GatheredRows:
+    def __init__(self, me, n, shard, block):
+        self.me, self.n, self.ratio = me, n, shard // block
+
+    def at(self, index, me):
+        owner = index // self.ratio
+        return reversed_bits(owner ^ me, bits_of(self.n)) * self.ratio + index % self.ratio
+
+
+def forward_matmul(x, weights, first, tiles, start, stop, tile, into=(), after=()):
     rows, depth = x.shape
     half = rows // 2
-    parts = 4
-    step = depth // parts
-
-    def kernel(x_ref, *refs):
-        w_refs, (keep_ref, send_ref) = refs[:parts], refs[-2:]
-        y = None
-        for i, w_ref in enumerate(w_refs):
-            part = jnp.dot(x_ref[:, i * step : (i + 1) * step], w_ref[0], preferred_element_type=F32)
-            y = part if y is None else y + part
+
+    def kernel(x_ref, w_ref, *refs):
+        keep_ref, send_ref = refs[-2:]
+        y = jnp.dot(x_ref[...], w_ref[0], preferred_element_type=F32)
         keep_ref[...] = y[:half]
         send_ref[...] = y[half:].astype(BF16)
 
     return pl.pallas_call(
         kernel,
-        grid=(tiles,),
-        in_specs=[pl.BlockSpec((rows, depth), lambda i: (0, 0))]
-        + [pl.BlockSpec((1, step, tile), lambda i, k=k: (0, k, first + i)) for k in range(parts)]
-        + [ANY] * len(after),
-        out_specs=[pl.BlockSpec((half, tile), lambda i: (0, i))] * 2,
+        grid=(stop - start,),
+        in_specs=[RESIDENT, pl.BlockSpec((1, depth, tile), lambda i: (0, 0, first + start + i))]
+        + [ANY] * (len(into) + len(after)),
+        out_specs=[pl.BlockSpec((half, tile), lambda i: (0, start + i))] * 2,
         out_shape=[
             jax.ShapeDtypeStruct((half, tiles * tile), F32),
             jax.ShapeDtypeStruct((half, tiles * tile), BF16),
         ],
+        input_output_aliases={2 + i: i for i in range(len(into))},
         compiler_params=params(),
         cost_estimate=pl.CostEstimate(
-            flops=2 * rows * depth * tiles * tile,
-            bytes_accessed=2 * depth * (rows + tiles * tile) + 6 * half * tiles * tile,
+            flops=2 * rows * depth * (stop - start) * tile,
+            bytes_accessed=2 * depth * (rows + (stop - start) * tile) + 6 * half * (stop - start) * tile,
             transcendentals=0,
         ),
         name="forward_matmul",
-    )(x, *[weights] * parts, *after)
+    )(x, weights, *into, *after)
+
+
+def share_sums(parts, own):
+    columns = parts[0].shape[1]
+    tile = tile_of(columns, 1536)
+
+    def kernel(*refs):
+        total = refs[0][...].astype(F32)
+        for ref in refs[1 : len(parts)]:
+            total = total + ref[...].astype(F32)
+        refs[-2][...] = total[:own].astype(BF16)
+        refs[-1][...] = total[own:].astype(BF16)
+
+    return pl.pallas_call(
+        kernel,
+        grid=(columns // tile,),
+        in_specs=[pl.BlockSpec((2 * own, tile), lambda i: (1, i))] * len(parts),
+        out_specs=[pl.BlockSpec((own, tile), lambda i: (0, i))] * 2,
+        out_shape=[jax.ShapeDtypeStruct((own, columns), BF16)] * 2,
+        compiler_params=params(),
+        cost_estimate=pl.CostEstimate(
+            flops=2 * own * columns, bytes_accessed=16 * own * columns, transcendentals=0
+        ),
+        name="share_sums",
+    )(*parts)
 
 
 def gated_gradients(d, mine, other, cotangent, first, low, up, own, after=()):
     columns = other.shape[1]
     rank = up.shape[1]
-    tile = tile_of(columns, 1024)
+    tile = max(t for t in range(128, 2049, 128) if columns % t == 0 and first % t == 0)
     tiles = columns // tile
     base = first // tile
 
@@ -221,18 +271,18 @@
     )(d.reshape(1), *mine, other, cotangent, low, up, *after)
 
 
-def backward_matmul(grads, weights, chunk, first, tiles, tile, base=None, partial=False, after=()):
-    rows, hidden = sum(g.shape[0] for g in grads), grads[0].shape[1]
+def backward_matmul(pieces, weights, hidden_start, first, tiles, tile, base=None, base_first=0, partial=False, after=()):
+    rows = sum(g.shape[0] for g in pieces)
     half = rows // 2
     n_base = 0 if base is None else 1
+    hidden = pieces[0].shape[1]
 
     def kernel(*refs):
-        g_refs = refs[: len(grads)]
-        w_ref = refs[len(grads)]
-        g = jnp.concatenate([ref[...] for ref in g_refs], axis=0)
+        w_ref = refs[len(pieces)]
+        g = jnp.concatenate([ref[...] for ref in refs[: len(pieces)]], axis=0)
         y = lax.dot_general(g, w_ref[0], (((1,), (1,)), ((), ())), preferred_element_type=F32)
         if n_base:
-            y = y + refs[len(grads) + 1][...]
+            y = y + refs[len(pieces) + 1][...]
         if partial:
             refs[-1][...] = y
         else:
@@ -251,9 +301,14 @@
     return pl.pallas_call(
         kernel,
         grid=(tiles,),
-        in_specs=[pl.BlockSpec(g.shape, lambda i: (0, 0)) for g in grads]
-        + [pl.BlockSpec((1, tile, hidden), lambda i: (0, first + i, chunk))]
-        + [pl.BlockSpec((rows, tile), lambda i: (0, first + i))] * n_base
+        in_specs=[RESIDENT] * len(pieces)
+        + [
+            pl.BlockSpec(
+                (pl.Element(1), pl.Element(tile), pl.Element(hidden)),
+                lambda i: (0, (first + i) * tile, hidden_start),
+            )
+        ]
+        + [pl.BlockSpec((rows, tile), lambda i: (0, first - base_first + i))] * n_base
         + [ANY] * len(after),
         out_specs=out_specs,
         out_shape=out_shape,
@@ -264,7 +319,66 @@
             transcendentals=0,
         ),
         name="backward_matmul",
-    )(*grads, weights, *(() if base is None else (base,)), *after)
+    )(*pieces, weights, *(() if base is None else (base,)), *after)
+
+
+def adapter_up(low, groups):
+    rank = low.shape[0]
+
+    def kernel(*refs):
+        at = 1
+        for i, pieces in enumerate(groups):
+            g = jnp.concatenate([ref[...] for ref in refs[at : at + len(pieces)]], axis=0)
+            at += len(pieces)
+            refs[i - len(groups)][...] = ADAPTER_SCALE * jnp.dot(
+                refs[0][...], g, preferred_element_type=F32
+            )
+
+    operands = [g for pieces in groups for g in pieces]
+    widths = [pieces[0].shape[1] for pieces in groups]
+    return pl.pallas_call(
+        kernel,
+        grid=(1,),
+        in_specs=[RESIDENT] * (1 + len(operands)),
+        out_specs=[pl.BlockSpec((rank, w), lambda i: (0, 0)) for w in widths],
+        out_shape=[jax.ShapeDtypeStruct((rank, w), F32) for w in widths],
+        compiler_params=params(),
+        cost_estimate=pl.CostEstimate(
+            flops=2 * rank * low.shape[1] * sum(widths),
+            bytes_accessed=2 * low.shape[1] * sum(widths),
+            transcendentals=0,
+        ),
+        name="adapter_up",
+    )(low, *operands)
+
+
+def assemble(pieces, places, block, tokens, width, columns, into=None):
+    chunk = pieces[0].shape[1]
+    start = columns // chunk
+
+    def kernel(place_ref, *refs):
+        out_ref = refs[-1]
+        i = 0
+        for ref in refs[: len(pieces)]:
+            for r in range(0, ref.shape[0], block):
+                out_ref[pl.ds(pl.multiple_of(place_ref[i], block), block), :] = ref[r : r + block, :]
+                i += 1
+
+    n_into = 0 if into is None else 1
+    return pl.pallas_call(
+        kernel,
+        grid_spec=pltpu.PrefetchScalarGridSpec(
+            num_scalar_prefetch=1,
+            grid=(1,),
+            in_specs=[pl.BlockSpec(x.shape, lambda i, p: (0, 0)) for x in pieces] + [ANY] * n_into,
+            out_specs=pl.BlockSpec((tokens, chunk), lambda i, p: (0, start)),
+        ),
+        out_shape=jax.ShapeDtypeStruct((tokens, width), BF16),
+        input_output_aliases={len(pieces) + 1: 0} if n_into else {},
+        compiler_params=params(),
+        cost_estimate=pl.CostEstimate(flops=0, bytes_accessed=4 * tokens * chunk, transcendentals=0),
+        name="assemble",
+    )(places, *pieces, *((into,) if n_into else ()))
 
 
 def finish(parts, stream, stats, back, down, steering, gain, columns):
@@ -317,7 +431,15 @@
         first_pair = d == 0
         down_rows = jnp.transpose(down, (0, 2, 1)).reshape(2 * rank, width)
 
-        peer_stream = swap(stream, "dp", dp, 1)
+        shard = tokens // ffn
+        split = width // 2 if hid >= ffn and width % 256 == 0 else width
+        if split < width:
+            mine = lax.dynamic_slice(stream, (f * shard, split), (shard, width - split))
+            far = double(swap(mine, "dp", dp, 1), "ffn", ffn)
+            near = swap(stream[:, :split], "dp", dp, 1)
+            peer_pieces = [(near, None), (far, GatheredRows(f, ffn, shard, own))]
+        else:
+            peer_pieces = [(swap(stream, "dp", dp, 1), None)]
         rows = stream.astype(F32)
         total_rows, total_steer = lax.psum(
             (jnp.sum(rows * rows, axis=1), jnp.sum(steering * steering)), "hid"
@@ -331,64 +453,96 @@
         stats = jnp.stack([scale, inv_rms], axis=1)
         peer_stats = swap(stats, "dp", dp, 1)
 
-        count = 2 if hidden % 256 == 0 else 1
-        chunk = hidden // count
-        tile = tile_of(chunk, 256)
-        tiles = chunk // tile
-        own_normed, own_low = normalize(stream, stats, steering, gain, down_rows, h, hid)
-        own_acts = []
-        for c in range(count):
-            keep, send = forward_matmul(own_normed, weights, c * tiles, tiles, tile)
-            own_acts.append(halve(keep, send, "hid", hid))
-        peer_normed, peer_low = normalize(peer_stream, peer_stats, steering, gain, down_rows, h, hid)
-        peer_acts = []
-        for c in range(count):
-            wait = (own_acts[c - 1][-1],) if c else ()
-            keep, send = forward_matmul(peer_normed, weights, c * tiles, tiles, tile, wait)
-            peer_acts.append(halve(keep, send, "hid", hid))
-
-        low = jnp.stack([own_low, peer_low])
+        tile = tile_of(hidden, 512)
+        count = hidden // tile
+        chunks = split_tiles(count, HIDDEN_CHUNKS)
+        normed, own_low = normalize([(stream, None)], stats, steering, gain, down_rows, h, hid, 0)
+        normed, peer_low = normalize(
+            peer_pieces, peer_stats, steering, gain, down_rows, h, hid, 1, into=normed
+        )
+
+        low, low_steps = jnp.stack([own_low, peer_low]), []
         for bit in range(bits_of(hid)):
             half = low.shape[1] // 2
             low = low[:, :half] + swap(low[:, half:], "hid", hid, 1 << bit)
+            low_steps.append(low)
         low = low.astype(BF16)
         low_own = low[0]
-        low_mine = jnp.where(first_pair, low[:, :, :rank], low[:, :, rank:])
-        low_mine = double(low_mine, "hid", hid, dim=1)
-
-        width_tile = tile_of(width, 256)
-        grads, back, base, wait = [], 0.0, None, ()
-        for c in range(count):
-            other = swap(total_of(peer_acts[c], 0, own).astype(BF16), "dp", dp, 1)
+
+        acts, sent, others = [], [], []
+        last_bit = 1 << (bits_of(hid) - 1)
+        for c, (first, n) in enumerate(chunks):
+            middle = (n + 1) // 2
+            wait = tuple(sent[-1]) if c else ()
+            if c >= 2:
+                wait += (acts[c - 2][1],)
+            half_done = forward_matmul(normed, weights, first, n, 0, middle, tile, after=wait)
+            wait = tuple(low_steps[c : c + 1])
+            if c:
+                wait += (acts[c - 1][2],)
+            if c >= 2:
+                wait += (others[c - 2],)
+            keep, send = forward_matmul(normed, weights, first, n, middle, n, tile, into=half_done, after=wait)
+            parts = [keep, swap(send, "hid", hid, 1)]
+            for bit in range(1, bits_of(hid) - 1):
+                size = parts[-1].shape[0]
+                send = total_of(parts, size // 2, size).astype(BF16)
+                parts.append(swap(send, "hid", hid, 1 << bit))
+            sent.append(share_sums(parts, own))
+            peer_got = swap(sent[-1][1], "hid", hid, last_bit)
+            own_got = swap(sent[-1][0], "hid", hid, last_bit)
+            acts.append((parts, own_got, peer_got))
+            others.append(
+                swap((total_of(parts, own, 2 * own) + peer_got.astype(F32)).astype(BF16), "dp", dp, 1)
+            )
+
+        width_tile = tile_of(width, 512)
+        halves = split_tiles(width // width_tile, 2)
+        grads, back, bases, wait = [], 0.0, [], ()
+
+        def partial_sums(c, which, base, after):
+            first, n = halves[which]
+            return backward_matmul(
+                grads[c], weights, chunks[c][0] * tile, first, n, width_tile,
+                base=base, base_first=first, partial=True, after=after,
+            )
+
+        for c, (first, n) in enumerate(chunks):
+            parts, own_got, _ = acts[c]
+            if c == len(chunks) - 1:
+                bases = [partial_sums(0, 0, None, wait[:1])]
+                wait += (bases[0],)
             mine_grad, other_grad, back_part = gated_gradients(
-                d, own_acts[c], other, cotangent, c * chunk, low_own, up, own, wait
+                d, parts + [own_got], others[c], cotangent, first * tile, low_own, up, own, wait
             )
             back = back + back_part
             peer_grad = swap(other_grad, "dp", dp, 1)
-            pieces, wait = [], (peer_grad,)
+            wait = (peer_grad,)
+            pieces = []
             for g in (mine_grad, peer_grad):
-                for bit in reversed(range(1, bits_of(hid))):
-                    got = swap(g, "hid", hid, 1 << bit)
-                    if g is mine_grad:
-                        wait += (got,)
-                    if c and g is peer_grad:
-                        got = ordered(got, base)
-                    g = jnp.concatenate([g, got], axis=0)
-                pieces += [g, swap(g, "hid", hid, 1)]
+                blocks = [g]
+                for bit in reversed(range(bits_of(hid))):
+                    blocks += [swap(x, "hid", hid, 1 << bit) for x in blocks]
+                if g is mine_grad:
+                    wait += (blocks[1],)
+                pieces += blocks
             grads.append(pieces)
-            if c < count - 1:
-                base = backward_matmul(
-                    pieces, weights, c, 0, width // width_tile, width_tile, base=base, partial=True
-                )
+        bases.append(partial_sums(0, 1, None, (mine_grad,)))
+        for c in range(1, len(chunks) - 1):
+            for which in range(2):
+                bases[which] = partial_sums(c, which, bases[which], wait)
+                wait = (grads[-1][len(grads[-1]) // 2 + 1],)
+        base = bases[-1]
+        bases = [(halves[i][0], bases[i]) for i in range(2)]
 
         for bit in range(bits_of(ffn)):
             back = back + swap(back, "ffn", ffn, 1 << bit)
+        back = ordered(back, base)
         back = jnp.stack([back, swap(back, "dp", dp, 1)])
         back = double(back, "hid", hid, dim=1)
         back_low = back[:, :, : 2 * rank].astype(BF16)
         acts_product = back[0, :, 2 * rank]
 
-        shard = tokens // ffn
         place = reversed_bits(f, bits_of(ffn))
         block = min(own, shard)
 
@@ -412,21 +566,27 @@
         stream_shard = shard_rows(stream)
         back_shard = lax.dynamic_slice_in_dim(back_low[0], place * shard, shard, axis=0)
 
-        out = jnp.zeros((tokens, width), BF16)
-        sums = []
+        out, sums, gathered = None, [], []
         steps = split_tiles(width // width_tile, WIDTH_CHUNKS)
         products, received = [], []
         for first, n in steps:
-            keep, send = backward_matmul(grads[-1], weights, count - 1, first, n, width_tile, base=base)
+            held_first, held = [b for b in bases if b[0] <= first][-1]
+            keep, send = backward_matmul(
+                grads[-1], weights, chunks[-1][0] * tile, first, n, width_tile,
+                base=held, base_first=held_first,
+            )
             products.append(keep)
             received.append(swap(send, "dp", dp, 1))
-        results = []
+        places = []
+        for p in range(ffn):
+            owner = reversed_bits(f ^ reversed_bits(p, bits_of(ffn)), bits_of(ffn))
+            places += [natural(owner * shard + i * block) for i in range(shard // block)]
+        places = jnp.stack(places)
         for j, (first, n) in enumerate(steps):
-            held = received[j]
+            got = received[j]
             if j >= 2:
-                held = ordered(held, results[j - 2])
-            part = products[j] + held.astype(F32)
-            parts = [part]
+                got = ordered(got, gathered[j - 2][1], *(gathered[j - 3][-1:] if j >= 3 else ()))
+            parts = [products[j], got]
             for bit in range(bits_of(ffn)):
                 half = parts[-1].shape[0] // 2
                 mine = (f >> bit) & 1
@@ -434,47 +594,35 @@
                     [lax.dynamic_slice_in_dim(p, side * half, half, axis=0) for p in parts]
                     for side in (mine, 1 - mine)
                 ]
-                parts = halves[0] + [swap(total_of(halves[1], 0, half).astype(BF16), "ffn", ffn, 1 << bit)]
+                parts = [total_of(halves[0], 0, half)] + [
+                    swap(total_of(halves[1], 0, half).astype(BF16), "ffn", ffn, 1 << bit)
+                ]
             result, sum_part = finish(
                 parts, stream_shard, stats_shard, back_shard, down_rows, steering, gain, first * width_tile
             )
             sums.append(sum_part)
-            results.append(result)
-            result = double(result, "ffn", ffn)
-            for p in range(ffn):
-                owner = reversed_bits(f ^ reversed_bits(p, bits_of(ffn)), bits_of(ffn))
-                for i in range(shard // block):
-                    out = lax.dynamic_update_slice(
-                        out,
-                        result[p * shard + i * block : p * shard + (i + 1) * block],
-                        (natural(owner * shard + i * block), first * width_tile),
-                    )
+            blocks = [result]
+            for bit in reversed(range(bits_of(ffn))):
+                blocks += [swap(x, "ffn", ffn, 1 << bit) for x in blocks]
+            gathered.append(blocks)
+            out = assemble(blocks, places, block, tokens, width, first * width_tile, into=out)
 
         steering_gradient = jnp.concatenate(sums, axis=1)
         for bit in range(bits_of(ffn)):
             steering_gradient = steering_gradient + swap(steering_gradient, "ffn", ffn, 1 << bit)
         steering_gradient = steering_gradient + swap(steering_gradient, "dp", dp, 1)
 
-        up_parts = []
-        for pieces in grads:
-            total, at = 0.0, 0
-            low_rows = low_mine.reshape(2 * tokens, rank)
-            for g in pieces:
-                total = total + lax.dot_general(
-                    low_rows[at : at + g.shape[0]], g, (((0,), (0,)), ((), ())), preferred_element_type=F32
-                )
-                at += g.shape[0]
-            up_parts.append(ADAPTER_SCALE * total)
-        up_mine = jnp.concatenate(up_parts, axis=1)
-        up_other = swap(up_mine.astype(BF16), "dp", dp, 1).astype(F32)
+        low_mine = jnp.where(first_pair, low[:, :, :rank], low[:, :, rank:])
+        low_mine = double(ordered(low_mine, base), "hid", hid, dim=1).reshape(2 * tokens, rank)
+        up_mine = jnp.concatenate(adapter_up(ordered(low_mine.T, products[-1]), grads), axis=1)
+        up_other = swap(ordered(up_mine.astype(BF16), received[-1]), "dp", dp, 1).astype(F32)
         up_gradient = jnp.where(
             first_pair, jnp.stack([up_mine, up_other]), jnp.stack([up_other, up_mine])
         )
-        down_gradient = 0.0
-        for x, b in ((own_normed, back_low[0]), (peer_normed, back_low[1])):
-            down_gradient = down_gradient + lax.dot_general(
-                b, x, (((0,), (0,)), ((), ())), preferred_element_type=F32
-            )
+        back_rows = back_low.reshape(2, hid, own, 2 * rank).transpose(1, 0, 2, 3).reshape(2 * tokens, 2 * rank)
+        down_gradient = lax.dot_general(
+            back_rows, normed, (((0,), (0,)), ((), ())), preferred_element_type=F32
+        )
         down_gradient = jnp.transpose(
             (ADAPTER_SCALE * down_gradient).reshape(2, rank, width), (0, 2, 1)
         )

time: 388 us -> 356 us (0.918)
  local copies, waits for them, and re-layouts: 69.5 us -> 34.3 us
  starting transfers between devices: 59 us -> 81.7 us
  Pallas kernels: 138 us -> 124 us
  matrix products: 7.87 us -> 1.62 us
  waiting for transfers between devices: 78.2 us -> 82.1 us
    dynamic_update_slice x16 -> x0, local copies, waits for them, and re-layouts: 46.6 us -> none  [local(): lax.dynamic_update_slice(out, result[p * shard + i * block:p * shard + (i...]
    ppermute x55 -> x75, starting transfers between devices: 59 us -> 81.7 us  [swap(): return lax.ppermute(x, axis, [(i, i ^ mask) for i in range(n)])]
    unnamed x59 -> x159, local copies, waits for them, and re-layouts: 11.3 us -> 28.5 us
    pallas_call x2 -> x3, Pallas kernels: 16.3 us -> 8.19 us  [gated_gradients(): pl.pallas_call(kernel, grid_spec=pltpu.PrefetchScalarGridSpec(num_scalar_...]
    dot_general x10 -> x1, matrix products: 7.87 us -> 1.62 us  [local(): lax.dot_general(back_rows, normed, (((0,), (0,)), ((), ())), preferred_el...]
    pallas_call x9 -> x22, Pallas kernels: 116 us -> 109 us  [the longest x8 51.7 us: backward_matmul(): pl.pallas_call(kernel, grid=(tiles,), in_specs=[RESIDENT] * len(pieces) +...]
    concatenate x4 -> x1, local copies, waits for them, and re-layouts: 3.89 us -> 0.01 us  [local(): jnp.concatenate(adapter_up(ordered(low_mine.T, products[-1]), grads), axi...]
    ppermute x55 -> x75, waiting for transfers between devices: 78.2 us -> 82.1 us  [swap(): return lax.ppermute(x, axis, [(i, i ^ mask) for i in range(n)])]
  transfers between devices with their start and end apart: 55 -> 75, of which waited for: 19 -> 30; matrix products, arithmetic and copies ran while one was open for 21% -> 6% of each run, Pallas kernels for 36% -> 26%
where the time goes in v3:
time: 356 us; the launch traced here: 355 us
  Pallas kernels  124 us (35%)
  waiting for transfers between devices  82.1 us (23%)
  starting transfers between devices  81.7 us (23%)
  local copies, waits for them, and re-layouts  34.3 us (10%)
  other arithmetic  15.1 us (4%)
  blocking collectives  13.3 us (4%)
    ppermute x75, waiting for transfers between devices, swap(): return lax.ppermute(x, axis, [(i, i ^ mask) for i in range(n)])  82.1 us
    ppermute x75, starting transfers between devices, swap(): return lax.ppermute(x, axis, [(i, i ^ mask) for i in range(n)])  81.7 us
    pallas_call x8, Pallas kernels, backward_matmul(): pl.pallas_call(kernel, grid=(tiles,), in_specs=[RESIDENT] * len(pieces) +...  51.7 us
    pallas_call x6, Pallas kernels, forward_matmul(): pl.pallas_call(kernel, grid=(stop - start,), in_specs=[RESIDENT, pl.Block...  47.3 us
    unnamed x159, local copies, waits for them, and re-layouts  28.5 us
    pallas_call x3, Pallas kernels, gated_gradients(): pl.pallas_call(kernel, grid_spec=pltpu.PrefetchScalarGridSpec(num_scalar_...  8.19 us
  transfers between devices with their start and end apart: 75, of which 30 were waited for; matrix products, arithmetic and copies ran while one was open for 6% of the time, Pallas kernels for 26%

profile of v3, /device:TPU:0, one launch (start us, length us, event | category | flops | bytes accessed | tf_op | source)
XLA Modules:
  0.0 354.5 jit_solution(10140817484750401610)
XLA Ops:
  1.8 3.0 collective-permute-start.1
  4.8 2.3 slice.56
  7.6 4.3 %collective-permute-done.1 = bf16[64,2048]{1,0:T(8,128)(2,1)S(1)} collective-permute-done((bf16[64,2048]{1,0:T(8,128)(2,1)S(1)}, bf16[64,2048]{1,0:T(8,128)(2,1)S(1)}, u32[]{:S(2)}, u32[]{:S(2)}) %collective-permute-start.1) | collective-permute-done | bytes 262176 | tf_op jit(solution)/shard_map/ppermute | solution.py:41
  11.9 3.2 collective-permute-start.2
  15.7 6.7 %all-reduce = (f32[256]{0:T(256)S(1)}, f32[]{:T(128)}) all-reduce(f32[256]{0:T(256)S(1)} %fusion, f32[]{:T(128)} %multiply_reduce_fusion), channel_id=1, replica_groups=mesh['dp'=2,'ffn'=4,'hid'=4] {'hid'}, use_global_device_ids=true, to_apply=%region_1.0 | all-reduce | flops 257 | bytes 2056 | tf_op jit(solution)/shard_map/psum | solution.py:444
  23.0 2.1 collective-permute-done.2
  27.4 6.7 %psum.23 = f32[256]{0:T(256)S(1)} all-reduce(f32[256]{0:T(256)S(1)} %fusion.2), channel_id=1, replica_groups=mesh['dp'=2,'ffn'=4,'hid'=4] {'hid'}, use_global_device_ids=true, to_apply=%region_5.0 | all-reduce | flops 256 | bytes 2048 | tf_op jit(solution)/shard_map/psum | solution.py:451
  35.8 1.7 normalize.2
  40.4 3.7 %normalize.3 = (bf16[512,4096]{1,0:T(8,128)(2,1)S(1)}, f32[256,32]{1,0:T(8,128)S(1)}) custom-call(s32[2]{0:T(128)S(1)} %pad_add_fusion.1.s_ref, bf16[256,2048]{1,0:T(8,128)(2,1)} %collective-permute-done.refs_0_, bf16[256,2048]{1,0:T(8,128)(2,1)S(1)} %pad_maximum_fusion.refs_1_, ...), custom_call_target="tpu_custom_call", output_to_operand_aliasing={{0}: (7, {})} | custom-call | flops 67108864 | bytes 4194304 | tf_op jit(solution)/shard_map/normalize/pallas_call | solution.py:98
  44.3 8.4 %forward_matmul.6 = (f32[256,2048]{1,0:T(8,128)S(1)}, bf16[256,2048]{1,0:T(8,128)(2,1)S(1)}) custom-call(bf16[512,4096]{1,0:T(8,128)(2,1)S(1)} %get-tuple-element.61.x_ref, bf16[1,4096,6656]{2,1,0:T(8,128)(2,1)} %refs_8_.15), custom_call_target="tpu_custom_call" | custom-call | flops 4294967296 | bytes 14155776 | tf_op jit(solution)/shard_map/forward_matmul/pallas_call | solution.py:156
  52.7 7.0 %forward_matmul.7 = (f32[256,2048]{1,0:T(8,128)S(1)}, bf16[256,2048]{1,0:T(8,128)(2,1)S(1)}) custom-call(bf16[512,4096]{1,0:T(8,128)(2,1)S(1)} %get-tuple-element.61.x_ref, bf16[1,4096,6656]{2,1,0:T(8,128)(2,1)} %refs_8_.15, f32[256,2048]{1,0:T(8,128)S(1)} %get-tuple-element.62.refs_0_, ...), custom_call_target="tpu_custom_call", output_to_operand_aliasing={{0}: (2, {}), {1}: (3, {})} | custom-call | flops 4294967296 | bytes 14155776 | tf_op jit(solution)/shard_map/forward_matmul/pallas_call | solution.py:156
  61.2 3.1 collective-permute-done.7
  66.0 7.0 %forward_matmul.8 = (f32[256,2048]{1,0:T(8,128)S(1)}, bf16[256,2048]{1,0:T(8,128)(2,1)S(1)}) custom-call(bf16[512,4096]{1,0:T(8,128)(2,1)S(1)} %get-tuple-element.61.x_ref, bf16[1,4096,6656]{2,1,0:T(8,128)(2,1)} %refs_8_.15, bf16[64,2048]{1,0:T(8,128)(2,1)S(1)} %get-tuple-element.68.refs_0_, bf16[64,2048]{1,0:T(8,128)(2,1)S(1)} %get-tuple-element.69.refs_1_), custom_call_target="tpu_custom_call" | custom-call | flops 4294967296 | bytes 14155776 | tf_op jit(solution)/shard_map/forward_matmul/pallas_call | solution.py:156
  73.0 7.1 %forward_matmul.9 = (f32[256,2048]{1,0:T(8,128)S(1)}, bf16[256,2048]{1,0:T(8,128)(2,1)S(1)}) custom-call(bf16[512,4096]{1,0:T(8,128)(2,1)S(1)} %get-tuple-element.61.x_ref, bf16[1,4096,6656]{2,1,0:T(8,128)(2,1)} %refs_8_.15, f32[256,2048]{1,0:T(8,128)S(1)} %get-tuple-element.70.refs_0_, ...), custom_call_target="tpu_custom_call", output_to_operand_aliasing={{0}: (2, {}), {1}: (3, {})} | custom-call | flops 4294967296 | bytes 14155776 | tf_op jit(solution)/shard_map/forward_matmul/pallas_call | solution.py:156
  84.3 5.0 %collective-permute-done.10.refs_2_ = bf16[64,2048]{1,0:T(8,128)(2,1)S(1)} collective-permute-done((bf16[64,2048]{1,0:T(8,128)(2,1)S(1)}, bf16[64,2048]{1,0:T(8,128)(2,1)S(1)}, u32[]{:S(2)}, u32[]{:S(2)}) %collective-permute-start.10) | collective-permute-done | bytes 262176 | tf_op jit(solution)/shard_map/ppermute | solution.py:41
  89.3 10.1 %forward_matmul.10 = (f32[256,2560]{1,0:T(8,128)S(1)}, bf16[256,2560]{1,0:T(8,128)(2,1)}) custom-call(bf16[512,4096]{1,0:T(8,128)(2,1)S(1)} %get-tuple-element.61.x_ref, bf16[1,4096,6656]{2,1,0:T(8,128)(2,1)} %refs_8_.15, bf16[64,2048]{1,0:T(8,128)(2,1)S(1)} %get-tuple-element.74.refs_0_, bf16[64,2048]{1,0:T(8,128)(2,1)S(1)} %get-tuple-element.75.refs_1_, ...), custom_call_target="tpu_custom_call" | custom-call | flops 6442450944 | bytes 19136512 | tf_op jit(solution)/shard_map/forward_matmul/pallas_call | solution.py:156
  99.5 7.8 %forward_matmul.11 = (f32[256,2560]{1,0:T(8,128)S(1)}, bf16[256,2560]{1,0:T(8,128)(2,1)}) custom-call(bf16[512,4096]{1,0:T(8,128)(2,1)S(1)} %get-tuple-element.61.x_ref, bf16[1,4096,6656]{2,1,0:T(8,128)(2,1)} %refs_8_.15, f32[256,2560]{1,0:T(8,128)S(1)} %get-tuple-element.76.refs_0_, ...), custom_call_target="tpu_custom_call", output_to_operand_aliasing={{0}: (2, {}), {1}: (3, {})} | custom-call | flops 4294967296 | bytes 14155776 | tf_op jit(solution)/shard_map/forward_matmul/pallas_call | solution.py:156
  119.1 6.7 %collective-permute-done.19.refs_7_.refs_4_.refs_5_ = bf16[64,2048]{1,0:T(8,128)(2,1)} collective-permute-done((bf16[64,2048]{1,0:T(8,128)(2,1)}, bf16[64,2048]{1,0:T(8,128)(2,1)}, u32[]{:S(2)}, u32[]{:S(2)}) %collective-permute-start.19) | collective-permute-done | bytes 262176 | tf_op jit(solution)/shard_map/ppermute | solution.py:41
  127.8 2.0 add_convert_fusion.5
  131.3 1.7 copy-done.10
  133.0 1.9 share_sums.5
  138.5 2.4 collective-permute-done.17.refs_2_
  145.3 2.0 gated_gradients.4
  151.0 4.6 %collective-permute-done.21.refs_9_.refs_7_.refs_4_.refs_13_ = bf16[64,2048]{1,0:T(8,128)(2,1)S(1)} collective-permute-done((bf16[64,2048]{1,0:T(8,128)(2,1)S(1)}, bf16[64,2048]{1,0:T(8,128)(2,1)S(1)}, u32[]{:S(2)}, u32[]{:S(2)}) %collective-permute-start.21) | collective-permute-done | bytes 262176 | tf_op jit(solution)/shard_map/ppermute | solution.py:41
  159.2 7.6 %backward_matmul.8.refs_9_ = f32[512,2048]{1,0:T(8,128)S(1)} custom-call(bf16[64,2048]{1,0:T(8,128)(2,1)S(1)} %copy-done.29, bf16[64,2048]{1,0:T(8,128)(2,1)} %collective-permute-done.20.refs_8_.refs_1_.refs_2_, bf16[64,2048]{1,0:T(8,128)(2,1)S(1)} %collective-permute-done.23.refs_2_.refs_3_, bf16[64,2048]{1,0:T(8,128)(2,1)S(1)} %collective-permute-done.24.refs_3_.refs_4_, ...), custom_call_target="tpu_custom_call" | custom-call | flops 4294967296 | bytes 14680064 | tf_op jit(solution)/shard_map/backward_matmul/pallas_call | solution.py:301
  166.9 3.8 %collective-permute-done.14.refs_2_ = bf16[64,2560]{1,0:T(8,128)(2,1)S(1)} collective-permute-done((bf16[64,2560]{1,0:T(8,128)(2,1)S(1)}, bf16[64,2560]{1,0:T(8,128)(2,1)S(1)}, u32[]{:S(2)}, u32[]{:S(2)}) %collective-permute-start.14) | collective-permute-done | bytes 327712 | tf_op jit(solution)/shard_map/ppermute | solution.py:41
  170.7 4.8 %gated_gradients.5 = (bf16[64,2560]{1,0:T(8,128)(2,1)S(1)}, bf16[64,2560]{1,0:T(8,128)(2,1)}, f32[64,33]{1,0:T(8,128)S(1)}) custom-call(s32[1]{0:T(128)} %bitcast.4.d_ref, f32[256,2560]{1,0:T(8,128)S(1)} %copy-done.11, bf16[256,2560]{1,0:T(8,128)(2,1)} %collective-permute-done.13.refs_1_, bf16[64,2560]{1,0:T(8,128)(2,1)S(1)} %collective-permute-done.14.refs_2_, ...), custom_call_target="tpu_custom_call" | custom-call | flops 20971520 | bytes 2621440 | tf_op jit(solution)/shard_map/gated_gradients/pallas_call | solution.py:247
  179.5 3.1 collective-permute-start.45
  189.3 7.5 %backward_matmul.9.refs_9_ = f32[512,2048]{1,0:T(8,128)S(1)} custom-call(bf16[64,2048]{1,0:T(8,128)(2,1)S(1)} %copy-done.29, bf16[64,2048]{1,0:T(8,128)(2,1)} %collective-permute-done.20.refs_8_.refs_1_.refs_2_, bf16[64,2048]{1,0:T(8,128)(2,1)S(1)} %collective-permute-done.23.refs_2_.refs_3_, bf16[64,2048]{1,0:T(8,128)(2,1)S(1)} %copy-done.37, ...), custom_call_target="tpu_custom_call" | custom-call | flops 4294967296 | bytes 14680064 | tf_op jit(solution)/shard_map/backward_matmul/pallas_call | solution.py:301
  198.3 7.6 %backward_matmul.10.refs_9_ = f32[512,2048]{1,0:T(8,128)S(1)} custom-call(bf16[64,2048]{1,0:T(8,128)(2,1)S(1)} %get-tuple-element.85.refs_0_.refs_9_, bf16[64,2048]{1,0:T(8,128)(2,1)S(1)} %collective-permute-done.22.refs_8_.refs_1_.refs_10_, bf16[64,2048]{1,0:T(8,128)(2,1)S(1)} %collective-permute-done.35.refs_2_.refs_11_, ...), custom_call_target="tpu_custom_call" | custom-call | flops 4294967296 | bytes 18874368 | tf_op jit(solution)/shard_map/backward_matmul/pallas_call | solution.py:301
  205.9 2.0 copy-done.4
  209.2 7.4 %backward_matmul.12.refs_9_ = f32[512,2048]{1,0:T(8,128)S(1)} custom-call(bf16[64,2048]{1,0:T(8,128)(2,1)S(1)} %get-tuple-element.85.refs_0_.refs_9_, bf16[64,2048]{1,0:T(8,128)(2,1)S(1)} %collective-permute-done.22.refs_8_.refs_1_.refs_10_, bf16[64,2048]{1,0:T(8,128)(2,1)S(1)} %collective-permute-done.35.refs_2_.refs_11_, ...), custom_call_target="tpu_custom_call" | custom-call | flops 4294967296 | bytes 18874368 | tf_op jit(solution)/shard_map/backward_matmul/pallas_call | solution.py:301
  216.6 2.1 copy-done.6
  222.1 2.9 collective-permute-done.47
  227.7 2.2 copy-done.7
  229.9 5.7 %backward_matmul.14 = (f32[256,1024]{1,0:T(8,128)S(1)}, bf16[256,1024]{1,0:T(8,128)(2,1)}) custom-call(bf16[64,2560]{1,0:T(8,128)(2,1)S(1)} %get-tuple-element.86.refs_9_.refs_0_.refs_17_, bf16[64,2560]{1,0:T(8,128)(2,1)S(1)} %collective-permute-done.28.refs_1_.refs_11_.refs_18_, bf16[64,2560]{1,0:T(8,128)(2,1)S(1)} %collective-permute-done.29.refs_2_.refs_19_, ...), custom_call_target="tpu_custom_call" | custom-call | flops 2684354560 | bytes 12058624 | tf_op jit(solution)/shard_map/backward_matmul/pallas_call | solution.py:301
  236.5 1.7 collective-permute-start.50
  238.3 5.7 %backward_matmul.13 = (f32[256,1024]{1,0:T(8,128)S(1)}, bf16[256,1024]{1,0:T(8,128)(2,1)}) custom-call(bf16[64,2560]{1,0:T(8,128)(2,1)S(1)} %get-tuple-element.86.refs_9_.refs_0_.refs_17_, bf16[64,2560]{1,0:T(8,128)(2,1)S(1)} %collective-permute-done.28.refs_1_.refs_11_.refs_18_, bf16[64,2560]{1,0:T(8,128)(2,1)S(1)} %collective-permute-done.29.refs_2_.refs_19_, ...), custom_call_target="tpu_custom_call" | custom-call | flops 2684354560 | bytes 12058624 | tf_op jit(solution)/shard_map/backward_matmul/pallas_call | solution.py:301
  247.1 2.2 copy-done.5
  249.2 5.3 %backward_matmul.15 = (f32[256,1024]{1,0:T(8,128)S(1)}, bf16[256,1024]{1,0:T(8,128)(2,1)S(1)}) custom-call(bf16[64,2560]{1,0:T(8,128)(2,1)S(1)} %get-tuple-element.86.refs_9_.refs_0_.refs_17_, bf16[64,2560]{1,0:T(8,128)(2,1)S(1)} %collective-permute-done.28.refs_1_.refs_11_.refs_18_, bf16[64,2560]{1,0:T(8,128)(2,1)S(1)} %collective-permute-done.29.refs_2_.refs_19_, ...), custom_call_target="tpu_custom_call" | custom-call | flops 2684354560 | bytes 12058624 | tf_op jit(solution)/shard_map/backward_matmul/pallas_call | solution.py:301
  254.6 1.8 collective-permute-start.60
  258.4 4.5 %collective-permute-done.41 = bf16[256,1024]{1,0:T(8,128)(2,1)} collective-permute-done((bf16[256,1024]{1,0:T(8,128)(2,1)}, bf16[256,1024]{1,0:T(8,128)(2,1)}, u32[]{:S(2)}, u32[]{:S(2)}) %collective-permute-start.41) | collective-permute-done | bytes 524320 | tf_op jit(solution)/shard_map/ppermute | solution.py:41
  265.4 5.0 %backward_matmul.11 = (f32[256,1024]{1,0:T(8,128)S(1)}, bf16[256,1024]{1,0:T(8,128)(2,1)S(1)}) custom-call(bf16[64,2560]{1,0:T(8,128)(2,1)S(1)} %get-tuple-element.86.refs_9_.refs_0_.refs_17_, bf16[64,2560]{1,0:T(8,128)(2,1)S(1)} %collective-permute-done.28.refs_1_.refs_11_.refs_18_, bf16[64,2560]{1,0:T(8,128)(2,1)S(1)} %collective-permute-done.29.refs_2_.refs_19_, ...), custom_call_target="tpu_custom_call" | custom-call | flops 2684354560 | bytes 12058624 | tf_op jit(solution)/shard_map/backward_matmul/pallas_call | solution.py:301
  271.9 3.3 collective-permute-start.52
  275.3 2.3 adapter_up.1
  277.7 3.6 %collective-permute-done.52.refs_1_ = bf16[64,1024]{1,0:T(8,128)(2,1)S(1)} collective-permute-done((bf16[64,1024]{1,0:T(8,128)(2,1)S(1)}, bf16[64,1024]{1,0:T(8,128)(2,1)S(1)}, u32[]{:S(2)}, u32[]{:S(2)}) %collective-permute-start.52) | collective-permute-done | bytes 131104 | tf_op jit(solution)/shard_map/ppermute | solution.py:41
  282.5 3.9 %collective-permute-done.43.refs_1_ = bf16[64,1024]{1,0:T(8,128)(2,1)S(1)} collective-permute-done((bf16[64,1024]{1,0:T(8,128)(2,1)S(1)}, bf16[64,1024]{1,0:T(8,128)(2,1)S(1)}, u32[]{:S(2)}, u32[]{:S(2)}) %collective-permute-start.43) | collective-permute-done | bytes 131104 | tf_op jit(solution)/shard_map/ppermute | solution.py:41
  286.7 3.9 %collective-permute-done.53.refs_1_ = bf16[64,1024]{1,0:T(8,128)(2,1)S(1)} collective-permute-done((bf16[64,1024]{1,0:T(8,128)(2,1)S(1)}, bf16[64,1024]{1,0:T(8,128)(2,1)S(1)}, u32[]{:S(2)}, u32[]{:S(2)}) %collective-permute-start.53) | collective-permute-done | bytes 131104 | tf_op jit(solution)/shard_map/ppermute | solution.py:41
  290.6 5.8 %collective-permute-start.54 = (bf16[64,1024]{1,0:T(8,128)(2,1)S(1)}, bf16[64,1024]{1,0:T(8,128)(2,1)S(1)}, u32[]{:S(2)}, u32[]{:S(2)}) collective-permute-start(bf16[64,1024]{1,0:T(8,128)(2,1)S(1)} %collective-permute-done.53.refs_1_), channel_id=1, source_target_pairs={{0,4},{4,0},{8,12},{12,8},{1,5},{5,1},{9,13},{13,9},{2,6},{6,2},{1... | collective-permute-start | bytes 393224 | tf_op jit(solution)/shard_map/ppermute | solution.py:41
  296.7 4.2 %collective-permute-done.54.refs_3_ = bf16[64,1024]{1,0:T(8,128)(2,1)S(1)} collective-permute-done((bf16[64,1024]{1,0:T(8,128)(2,1)S(1)}, bf16[64,1024]{1,0:T(8,128)(2,1)S(1)}, u32[]{:S(2)}, u32[]{:S(2)}) %collective-permute-start.54) | collective-permute-done | bytes 131104 | tf_op jit(solution)/shard_map/ppermute | solution.py:41
  301.0 2.1 collective-permute-start.55
  303.2 2.3 collective-permute-done.61
  305.5 3.9 %collective-permute-start.62 = (bf16[64,1024]{1,0:T(8,128)(2,1)S(1)}, bf16[64,1024]{1,0:T(8,128)(2,1)S(1)}, u32[]{:S(2)}, u32[]{:S(2)}) collective-permute-start(bf16[64,1024]{1,0:T(8,128)(2,1)S(1)} %get-tuple-element.130), channel_id=1, source_target_pairs={{0,8},{4,12},{8,0},{12,4},{1,9},{5,13},{9,1},{13,5},{2,10},{6,14},... | collective-permute-start | bytes 393224 | tf_op jit(solution)/shard_map/ppermute | solution.py:41
  309.7 4.4 %collective-permute-start.56 = (bf16[64,1024]{1,0:T(8,128)(2,1)S(1)}, bf16[64,1024]{1,0:T(8,128)(2,1)S(1)}, u32[]{:S(2)}, u32[]{:S(2)}) collective-permute-start(bf16[64,1024]{1,0:T(8,128)(2,1)S(1)} %get-tuple-element.132), channel_id=1, source_target_pairs={{0,8},{4,12},{8,0},{12,4},{1,9},{5,13},{9,1},{13,5},{2,10},{6,14},... | collective-permute-start | bytes 393224 | tf_op jit(solution)/shard_map/ppermute | solution.py:41
  314.2 2.5 collective-permute-done.62.refs_1_
  316.9 3.3 collective-permute-done.56.refs_1_
  322.0 2.2 collective-permute-done.69
  325.8 1.6 convolution_multiply_fusion
  327.4 2.0 collective-permute-start.68
  329.5 2.0 collective-permute-start.67
  331.5 2.9 collective-permute-start.57
  334.5 2.9 collective-permute-done.68.refs_2_
  337.4 4.9 %collective-permute-done.66.refs_2_ = bf16[64,1024]{1,0:T(8,128)(2,1)S(1)} collective-permute-done((bf16[64,1024]{1,0:T(8,128)(2,1)S(1)}, bf16[64,1024]{1,0:T(8,128)(2,1)S(1)}, u32[]{:S(2)}, u32[]{:S(2)}) %collective-permute-start.66) | collective-permute-done | bytes 131104 | tf_op jit(solution)/shard_map/ppermute | solution.py:41
  342.3 2.0 collective-permute-start.65
  (343 shorter events, 92.5 us)
Async XLA Ops:
  1.8 10.1 %collective-permute-start.1 = (bf16[64,2048]{1,0:T(8,128)(2,1)S(1)}, bf16[64,2048]{1,0:T(8,128)(2,1)S(1)}, u32[]{:S(2)}, u32[]{:S(2)}) collective-permute-start(bf16[64,2048]{1,0:T(8,128)(2,1)S(1)} %constant_dynamic-slice_fusion.5), channel_id=1, source_target_pairs={{0,16},{16,0},{1,17},{17,1},{2,18},{18,2},{3,19},{19,3},{4,20},{20... | collective-permute-start | bytes 786440 | tf_op jit(solution)/shard_map/ppermute | solution.py:41
  7.1 33.3 %collective-permute-start = (bf16[256,2048]{1,0:T(8,128)(2,1)}, bf16[256,2048]{1,0:T(8,128)(2,1)}, u32[]{:S(2)}, u32[]{:S(2)}) collective-permute-start(bf16[256,2048]{1,0:T(8,128)(2,1)} %slice.56), channel_id=1, source_target_pairs={{0,16},{16,0},{1,17},{17,1},{2,18},{18,2},{3,19},{19,3},{4,20},{20... | collective-permute-start | bytes 3145736 | tf_op jit(solution)/shard_map/ppermute | solution.py:41
  11.9 13.2 %collective-permute-start.2 = (bf16[64,2048]{1,0:T(8,128)(2,1)S(1)}, bf16[64,2048]{1,0:T(8,128)(2,1)S(1)}, u32[]{:S(2)}, u32[]{:S(2)}) collective-permute-start(bf16[64,2048]{1,0:T(8,128)(2,1)S(1)} %collective-permute-done.1), channel_id=1, source_target_pairs={{0,8},{4,12},{8,0},{12,4},{1,9},{5,13},{9,1},{13,5},{2,10},{6,14},... | collective-permute-start | bytes 786440 | tf_op jit(solution)/shard_map/ppermute | solution.py:41
  26.0 13.2 %collective-permute-start.3 = (bf16[128,2048]{1,0:T(8,128)(2,1)}, bf16[128,2048]{1,0:T(8,128)(2,1)}, u32[]{:S(2)}, u32[]{:S(2)}) collective-permute-start(bf16[128,2048]{1,0:T(8,128)(2,1)} %pad_maximum_fusion.1), channel_id=1, source_target_pairs={{0,4},{4,0},{8,12},{12,8},{1,5},{5,1},{9,13},{13,9},{2,6},{6,2},{1... | collective-permute-start | bytes 1572872 | tf_op jit(solution)/shard_map/ppermute | solution.py:41
  44.2 8.4 %collective-permute-start.5 = (f32[2,128,32]{2,1,0:T(8,128)S(1)}, f32[2,128,32]{2,1,0:T(8,128)S(1)}, u32[]{:S(2)}, u32[]{:S(2)}) collective-permute-start(f32[2,128,32]{2,1,0:T(8,128)S(1)} %pad_maximum_fusion.2), channel_id=1, source_target_pairs={{0,1},{1,0},{2,3},{3,2},{4,5},{5,4},{6,7},{7,6},{8,9},{9,8},{10,11... | collective-permute-start | bytes 98312 | tf_op jit(solution)/shard_map/ppermute | solution.py:41
  64.6 8.4 %collective-permute-start.8 = (bf16[64,2048]{1,0:T(8,128)(2,1)S(1)}, bf16[64,2048]{1,0:T(8,128)(2,1)S(1)}, u32[]{:S(2)}, u32[]{:S(2)}) collective-permute-start(bf16[64,2048]{1,0:T(8,128)(2,1)S(1)} %get-tuple-element.69.refs_1_), channel_id=1, source_target_pairs={{0,2},{1,3},{2,0},{3,1},{4,6},{5,7},{6,4},{7,5},{8,10},{9,11},{10,... | collective-permute-start | bytes 786440 | tf_op jit(solution)/shard_map/ppermute | solution.py:41
  80.2 9.2 %collective-permute-start.10 = (bf16[64,2048]{1,0:T(8,128)(2,1)S(1)}, bf16[64,2048]{1,0:T(8,128)(2,1)S(1)}, u32[]{:S(2)}, u32[]{:S(2)}) collective-permute-start(bf16[64,2048]{1,0:T(8,128)(2,1)S(1)} %get-tuple-element.68.refs_0_), channel_id=1, source_target_pairs={{0,2},{1,3},{2,0},{3,1},{4,6},{5,7},{6,4},{7,5},{8,10},{9,11},{10,... | collective-permute-start | bytes 786440 | tf_op jit(solution)/shard_map/ppermute | solution.py:41
  81.2 18.3 %collective-permute-start.12 = (bf16[64,2048]{1,0:T(8,128)(2,1)S(1)}, bf16[64,2048]{1,0:T(8,128)(2,1)S(1)}, u32[]{:S(2)}, u32[]{:S(2)}) collective-permute-start(bf16[64,2048]{1,0:T(8,128)(2,1)S(1)} %add_convert_fusion.6), channel_id=1, source_target_pairs={{0,16},{16,0},{1,17},{17,1},{2,18},{18,2},{3,19},{19,3},{4,20},{20... | collective-permute-start | bytes 786440 | tf_op jit(solution)/shard_map/ppermute | solution.py:41
  83.1 16.3 %collective-permute-start.11 = (bf16[64,2048]{1,0:T(8,128)(2,1)S(1)}, bf16[64,2048]{1,0:T(8,128)(2,1)S(1)}, u32[]{:S(2)}, u32[]{:S(2)}) collective-permute-start(bf16[64,2048]{1,0:T(8,128)(2,1)S(1)} %get-tuple-element.75.refs_1_), channel_id=1, source_target_pairs={{0,2},{1,3},{2,0},{3,1},{4,6},{5,7},{6,4},{7,5},{8,10},{9,11},{10,... | collective-permute-start | bytes 786440 | tf_op jit(solution)/shard_map/ppermute | solution.py:41
  108.9 22.3 %collective-permute-start.13 = (bf16[256,2560]{1,0:T(8,128)(2,1)}, bf16[256,2560]{1,0:T(8,128)(2,1)}, u32[]{:S(2)}, u32[]{:S(2)}) collective-permute-start(bf16[256,2560]{1,0:T(8,128)(2,1)} %get-tuple-element.79), channel_id=1, source_target_pairs={{0,1},{1,0},{2,3},{3,2},{4,5},{5,4},{6,7},{7,6},{8,9},{9,8},{10,11... | collective-permute-start | bytes 3932168 | tf_op jit(solution)/shard_map/ppermute | solution.py:41
  116.7 9.0 %collective-permute-start.19 = (bf16[64,2048]{1,0:T(8,128)(2,1)}, bf16[64,2048]{1,0:T(8,128)(2,1)}, u32[]{:S(2)}, u32[]{:S(2)}) collective-permute-start(bf16[64,2048]{1,0:T(8,128)(2,1)} %get-tuple-element.82), channel_id=1, source_target_pairs={{0,16},{16,0},{1,17},{17,1},{2,18},{18,2},{3,19},{19,3},{4,20},{20... | collective-permute-start | bytes 786440 | tf_op jit(solution)/shard_map/ppermute | solution.py:41
  118.2 19.8 %collective-permute-start.20 = (bf16[64,2048]{1,0:T(8,128)(2,1)}, bf16[64,2048]{1,0:T(8,128)(2,1)}, u32[]{:S(2)}, u32[]{:S(2)}) collective-permute-start(bf16[64,2048]{1,0:T(8,128)(2,1)} %copy-done.28), channel_id=1, source_target_pairs={{0,2},{1,3},{2,0},{3,1},{4,6},{5,7},{6,4},{7,5},{8,10},{9,11},{10,... | collective-permute-start | bytes 786440 | tf_op jit(solution)/shard_map/ppermute | solution.py:41
  125.8 12.2 %collective-permute-start.25 = (bf16[64,2048]{1,0:T(8,128)(2,1)}, bf16[64,2048]{1,0:T(8,128)(2,1)}, u32[]{:S(2)}, u32[]{:S(2)}) collective-permute-start(bf16[64,2048]{1,0:T(8,128)(2,1)} %collective-permute-done.19.refs_7_.refs_4_.refs_5_), channel_id=1, source_target_pairs={{0,2},{1,3},{2,0},{3,1},{4,6},{5,7},{6,4},{7,5},{8,10},{9,11},{10,... | collective-permute-start | bytes 786440 | tf_op jit(solution)/shard_map/ppermute | solution.py:41
  126.6 14.3 %collective-permute-start.17 = (bf16[64,2048]{1,0:T(8,128)(2,1)}, bf16[64,2048]{1,0:T(8,128)(2,1)}, u32[]{:S(2)}, u32[]{:S(2)}) collective-permute-start(bf16[64,2048]{1,0:T(8,128)(2,1)} %copy-done.66), channel_id=1, source_target_pairs={{0,2},{1,3},{2,0},{3,1},{4,6},{5,7},{6,4},{7,5},{8,10},{9,11},{10,... | collective-permute-start | bytes 786440 | tf_op jit(solution)/shard_map/ppermute | solution.py:41
  129.8 11.2 %collective-permute-start.18 = (bf16[64,2048]{1,0:T(8,128)(2,1)}, bf16[64,2048]{1,0:T(8,128)(2,1)}, u32[]{:S(2)}, u32[]{:S(2)}) collective-permute-start(bf16[64,2048]{1,0:T(8,128)(2,1)} %add_convert_fusion.5), channel_id=1, source_target_pairs={{0,16},{16,0},{1,17},{17,1},{2,18},{18,2},{3,19},{19,3},{4,20},{20... | collective-permute-start | bytes 786440 | tf_op jit(solution)/shard_map/ppermute | solution.py:41
  135.6 11.7 %collective-permute-start.15 = (bf16[64,2560]{1,0:T(8,128)(2,1)}, bf16[64,2560]{1,0:T(8,128)(2,1)}, u32[]{:S(2)}, u32[]{:S(2)}) collective-permute-start(bf16[64,2560]{1,0:T(8,128)(2,1)} %get-tuple-element.81), channel_id=1, source_target_pairs={{0,2},{1,3},{2,0},{3,1},{4,6},{5,7},{6,4},{7,5},{8,10},{9,11},{10,... | collective-permute-start | bytes 983048 | tf_op jit(solution)/shard_map/ppermute | solution.py:41
  138.0 12.1 %collective-permute-start.23 = (bf16[64,2048]{1,0:T(8,128)(2,1)}, bf16[64,2048]{1,0:T(8,128)(2,1)S(1)}, u32[]{:S(2)}, u32[]{:S(2)}) collective-permute-start(bf16[64,2048]{1,0:T(8,128)(2,1)} %copy-done.28), channel_id=1, source_target_pairs={{0,1},{1,0},{2,3},{3,2},{4,5},{5,4},{6,7},{7,6},{8,9},{9,8},{10,11... | collective-permute-start | bytes 786440 | tf_op jit(solution)/shard_map/ppermute | solution.py:41
  138.0 18.4 %collective-permute-start.26 = (bf16[64,2048]{1,0:T(8,128)(2,1)}, bf16[64,2048]{1,0:T(8,128)(2,1)S(1)}, u32[]{:S(2)}, u32[]{:S(2)}) collective-permute-start(bf16[64,2048]{1,0:T(8,128)(2,1)} %collective-permute-done.19.refs_7_.refs_4_.refs_5_), channel_id=1, source_target_pairs={{0,1},{1,0},{2,3},{3,2},{4,5},{5,4},{6,7},{7,6},{8,9},{9,8},{10,11... | collective-permute-start | bytes 786440 | tf_op jit(solution)/shard_map/ppermute | solution.py:41
  140.9 16.8 %collective-permute-start.24 = (bf16[64,2048]{1,0:T(8,128)(2,1)}, bf16[64,2048]{1,0:T(8,128)(2,1)S(1)}, u32[]{:S(2)}, u32[]{:S(2)}) collective-permute-start(bf16[64,2048]{1,0:T(8,128)(2,1)} %collective-permute-done.20.refs_8_.refs_1_.refs_2_), channel_id=1, source_target_pairs={{0,1},{1,0},{2,3},{3,2},{4,5},{5,4},{6,7},{7,6},{8,9},{9,8},{10,11... | collective-permute-start | bytes 786440 | tf_op jit(solution)/shard_map/ppermute | solution.py:41
  140.9 18.3 %collective-permute-start.27 = (bf16[64,2048]{1,0:T(8,128)(2,1)}, bf16[64,2048]{1,0:T(8,128)(2,1)S(1)}, u32[]{:S(2)}, u32[]{:S(2)}) collective-permute-start(bf16[64,2048]{1,0:T(8,128)(2,1)} %collective-permute-done.25.refs_5_.refs_6_), channel_id=1, source_target_pairs={{0,1},{1,0},{2,3},{3,2},{4,5},{5,4},{6,7},{7,6},{8,9},{9,8},{10,11... | collective-permute-start | bytes 786440 | tf_op jit(solution)/shard_map/ppermute | solution.py:41
  147.3 8.3 %collective-permute-start.21 = (bf16[64,2048]{1,0:T(8,128)(2,1)S(1)}, bf16[64,2048]{1,0:T(8,128)(2,1)S(1)}, u32[]{:S(2)}, u32[]{:S(2)}) collective-permute-start(bf16[64,2048]{1,0:T(8,128)(2,1)S(1)} %get-tuple-element.84), channel_id=1, source_target_pairs={{0,16},{16,0},{1,17},{17,1},{2,18},{18,2},{3,19},{19,3},{4,20},{20... | collective-permute-start | bytes 786440 | tf_op jit(solution)/shard_map/ppermute | solution.py:41
  150.1 16.8 %collective-permute-start.22 = (bf16[64,2048]{1,0:T(8,128)(2,1)S(1)}, bf16[64,2048]{1,0:T(8,128)(2,1)S(1)}, u32[]{:S(2)}, u32[]{:S(2)}) collective-permute-start(bf16[64,2048]{1,0:T(8,128)(2,1)S(1)} %get-tuple-element.85.refs_0_.refs_9_), channel_id=1, source_target_pairs={{0,2},{1,3},{2,0},{3,1},{4,6},{5,7},{6,4},{7,5},{8,10},{9,11},{10,... | collective-permute-start | bytes 786440 | tf_op jit(solution)/shard_map/ppermute | solution.py:41
  155.6 27.7 %collective-permute-start.37 = (bf16[64,2048]{1,0:T(8,128)(2,1)S(1)}, bf16[64,2048]{1,0:T(8,128)(2,1)}, u32[]{:S(2)}, u32[]{:S(2)}) collective-permute-start(bf16[64,2048]{1,0:T(8,128)(2,1)S(1)} %collective-permute-done.21.refs_9_.refs_7_.refs_4_.refs_13_), channel_id=1, source_target_pairs={{0,2},{1,3},{2,0},{3,1},{4,6},{5,7},{6,4},{7,5},{8,10},{9,11},{10,... | collective-permute-start | bytes 786440 | tf_op jit(solution)/shard_map/ppermute | solution.py:41
  156.5 14.3 %collective-permute-start.14 = (bf16[64,2560]{1,0:T(8,128)(2,1)S(1)}, bf16[64,2560]{1,0:T(8,128)(2,1)S(1)}, u32[]{:S(2)}, u32[]{:S(2)}) collective-permute-start(bf16[64,2560]{1,0:T(8,128)(2,1)S(1)} %copy-done.69), channel_id=1, source_target_pairs={{0,2},{1,3},{2,0},{3,1},{4,6},{5,7},{6,4},{7,5},{8,10},{9,11},{10,... | collective-permute-start | bytes 983048 | tf_op jit(solution)/shard_map/ppermute | solution.py:41
  157.7 13.0 %collective-permute-start.16 = (bf16[64,2560]{1,0:T(8,128)(2,1)S(1)}, bf16[64,2560]{1,0:T(8,128)(2,1)S(1)}, u32[]{:S(2)}, u32[]{:S(2)}) collective-permute-start(bf16[64,2560]{1,0:T(8,128)(2,1)S(1)} %add_convert_fusion), channel_id=1, source_target_pairs={{0,16},{16,0},{1,17},{17,1},{2,18},{18,2},{3,19},{19,3},{4,20},{20... | collective-permute-start | bytes 983048 | tf_op jit(solution)/shard_map/ppermute | solution.py:41
  177.1 8.5 %collective-permute-start.31 = (bf16[64,2560]{1,0:T(8,128)(2,1)}, bf16[64,2560]{1,0:T(8,128)(2,1)S(1)}, u32[]{:S(2)}, u32[]{:S(2)}) collective-permute-start(bf16[64,2560]{1,0:T(8,128)(2,1)} %get-tuple-element.87), channel_id=1, source_target_pairs={{0,16},{16,0},{1,17},{17,1},{2,18},{18,2},{3,19},{19,3},{4,20},{20... | collective-permute-start | bytes 983048 | tf_op jit(solution)/shard_map/ppermute | solution.py:41
  182.7 14.0 %collective-permute-start.35 = (bf16[64,2048]{1,0:T(8,128)(2,1)S(1)}, bf16[64,2048]{1,0:T(8,128)(2,1)S(1)}, u32[]{:S(2)}, u32[]{:S(2)}) collective-permute-start(bf16[64,2048]{1,0:T(8,128)(2,1)S(1)} %get-tuple-element.85.refs_0_.refs_9_), channel_id=1, source_target_pairs={{0,1},{1,0},{2,3},{3,2},{4,5},{5,4},{6,7},{7,6},{8,9},{9,8},{10,11... | collective-permute-start | bytes 786440 | tf_op jit(solution)/shard_map/ppermute | solution.py:41
  182.8 14.1 %collective-permute-start.38 = (bf16[64,2048]{1,0:T(8,128)(2,1)S(1)}, bf16[64,2048]{1,0:T(8,128)(2,1)S(1)}, u32[]{:S(2)}, u32[]{:S(2)}) collective-permute-start(bf16[64,2048]{1,0:T(8,128)(2,1)S(1)} %collective-permute-done.21.refs_9_.refs_7_.refs_4_.refs_13_), channel_id=1, source_target_pairs={{0,1},{1,0},{2,3},{3,2},{4,5},{5,4},{6,7},{7,6},{8,9},{9,8},{10,11... | collective-permute-start | bytes 786440 | tf_op jit(solution)/shard_map/ppermute | solution.py:41
  183.3 14.9 %collective-permute-start.36 = (bf16[64,2048]{1,0:T(8,128)(2,1)S(1)}, bf16[64,2048]{1,0:T(8,128)(2,1)S(1)}, u32[]{:S(2)}, u32[]{:S(2)}) collective-permute-start(bf16[64,2048]{1,0:T(8,128)(2,1)S(1)} %collective-permute-done.22.refs_8_.refs_1_.refs_10_), channel_id=1, source_target_pairs={{0,1},{1,0},{2,3},{3,2},{4,5},{5,4},{6,7},{7,6},{8,9},{9,8},{10,11... | collective-permute-start | bytes 786440 | tf_op jit(solution)/shard_map/ppermute | solution.py:41
  184.5 13.8 %collective-permute-start.39 = (bf16[64,2048]{1,0:T(8,128)(2,1)}, bf16[64,2048]{1,0:T(8,128)(2,1)S(1)}, u32[]{:S(2)}, u32[]{:S(2)}) collective-permute-start(bf16[64,2048]{1,0:T(8,128)(2,1)} %collective-permute-done.37.refs_5_.refs_14_), channel_id=1, source_target_pairs={{0,1},{1,0},{2,3},{3,2},{4,5},{5,4},{6,7},{7,6},{8,9},{9,8},{10,11... | collective-permute-start | bytes 786440 | tf_op jit(solution)/shard_map/ppermute | solution.py:41
  185.6 12.7 %collective-permute-start.32 = (bf16[64,2560]{1,0:T(8,128)(2,1)S(1)}, bf16[64,2560]{1,0:T(8,128)(2,1)S(1)}, u32[]{:S(2)}, u32[]{:S(2)}) collective-permute-start(bf16[64,2560]{1,0:T(8,128)(2,1)S(1)} %collective-permute-done.31.refs_4_.refs_10_.refs_21_), channel_id=1, source_target_pairs={{0,2},{1,3},{2,0},{3,1},{4,6},{5,7},{6,4},{7,5},{8,10},{9,11},{10,... | collective-permute-start | bytes 983048 | tf_op jit(solution)/shard_map/ppermute | solution.py:41
  196.8 30.9 %collective-permute-start.29 = (bf16[64,2560]{1,0:T(8,128)(2,1)S(1)}, bf16[64,2560]{1,0:T(8,128)(2,1)S(1)}, u32[]{:S(2)}, u32[]{:S(2)}) collective-permute-start(bf16[64,2560]{1,0:T(8,128)(2,1)S(1)} %get-tuple-element.86.refs_9_.refs_0_.refs_17_), channel_id=1, source_target_pairs={{0,1},{1,0},{2,3},{3,2},{4,5},{5,4},{6,7},{7,6},{8,9},{9,8},{10,11... | collective-permute-start | bytes 983048 | tf_op jit(solution)/shard_map/ppermute | solution.py:41
  196.9 12.2 %collective-permute-start.28 = (bf16[64,2560]{1,0:T(8,128)(2,1)S(1)}, bf16[64,2560]{1,0:T(8,128)(2,1)S(1)}, u32[]{:S(2)}, u32[]{:S(2)}) collective-permute-start(bf16[64,2560]{1,0:T(8,128)(2,1)S(1)} %get-tuple-element.86.refs_9_.refs_0_.refs_17_), channel_id=1, source_target_pairs={{0,2},{1,3},{2,0},{3,1},{4,6},{5,7},{6,4},{7,5},{8,10},{9,11},{10,... | collective-permute-start | bytes 983048 | tf_op jit(solution)/shard_map/ppermute | solution.py:41
  198.2 29.5 %collective-permute-start.33 = (bf16[64,2560]{1,0:T(8,128)(2,1)S(1)}, bf16[64,2560]{1,0:T(8,128)(2,1)S(1)}, u32[]{:S(2)}, u32[]{:S(2)}) collective-permute-start(bf16[64,2560]{1,0:T(8,128)(2,1)S(1)} %collective-permute-done.31.refs_4_.refs_10_.refs_21_), channel_id=1, source_target_pairs={{0,1},{1,0},{2,3},{3,2},{4,5},{5,4},{6,7},{7,6},{8,9},{9,8},{10,11... | collective-permute-start | bytes 983048 | tf_op jit(solution)/shard_map/ppermute | solution.py:41
  208.0 11.4 %collective-permute-start.46 = (f32[64,33]{1,0:T(8,128)S(1)}, f32[64,33]{1,0:T(8,128)S(1)}, u32[]{:S(2)}, u32[]{:S(2)}) collective-permute-start(f32[64,33]{1,0:T(8,128)S(1)} %add.271), channel_id=1, source_target_pairs={{0,16},{16,0},{1,17},{17,1},{2,18},{18,2},{3,19},{19,3},{4,20},{20... | collective-permute-start | bytes 25352 | tf_op jit(solution)/shard_map/ppermute | solution.py:41
  208.3 10.5 %collective-permute-start.72 = (bf16[2,64,16]{2,1,0:T(8,128)(2,1)S(1)}, bf16[2,64,16]{2,1,0:T(8,128)(2,1)S(1)}, u32[]{:S(2)}, u32[]{:S(2)}) collective-permute-start(bf16[2,64,16]{2,1,0:T(8,128)(2,1)S(1)} %slice_select_fusion), channel_id=1, source_target_pairs={{0,2},{1,3},{2,0},{3,1},{4,6},{5,7},{6,4},{7,5},{8,10},{9,11},{10,... | collective-permute-start | bytes 12296 | tf_op jit(solution)/shard_map/ppermute | solution.py:41
  218.7 9.0 %collective-permute-start.30 = (bf16[64,2560]{1,0:T(8,128)(2,1)S(1)}, bf16[64,2560]{1,0:T(8,128)(2,1)S(1)}, u32[]{:S(2)}, u32[]{:S(2)}) collective-permute-start(bf16[64,2560]{1,0:T(8,128)(2,1)S(1)} %collective-permute-done.28.refs_1_.refs_11_.refs_18_), channel_id=1, source_target_pairs={{0,1},{1,0},{2,3},{3,2},{4,5},{5,4},{6,7},{7,6},{8,9},{9,8},{10,11... | collective-permute-start | bytes 983048 | tf_op jit(solution)/shard_map/ppermute | solution.py:41
  218.8 8.9 %collective-permute-start.34 = (bf16[64,2560]{1,0:T(8,128)(2,1)S(1)}, bf16[64,2560]{1,0:T(8,128)(2,1)}, u32[]{:S(2)}, u32[]{:S(2)}) collective-permute-start(bf16[64,2560]{1,0:T(8,128)(2,1)S(1)} %collective-permute-done.32.refs_10_.refs_5_.refs_22_), channel_id=1, source_target_pairs={{0,1},{1,0},{2,3},{3,2},{4,5},{5,4},{6,7},{7,6},{8,9},{9,8},{10,11... | collective-permute-start | bytes 983048 | tf_op jit(solution)/shard_map/ppermute | solution.py:41
  236.5 19.9 %collective-permute-start.50 = (bf16[256,1024]{1,0:T(8,128)(2,1)}, bf16[256,1024]{1,0:T(8,128)(2,1)}, u32[]{:S(2)}, u32[]{:S(2)}) collective-permute-start(bf16[256,1024]{1,0:T(8,128)(2,1)} %get-tuple-element.98), channel_id=1, source_target_pairs={{0,16},{16,0},{1,17},{17,1},{2,18},{18,2},{3,19},{19,3},{4,20},{20... | collective-permute-start | bytes 1572872 | tf_op jit(solution)/shard_map/ppermute | solution.py:41
  244.9 18.0 %collective-permute-start.41 = (bf16[256,1024]{1,0:T(8,128)(2,1)}, bf16[256,1024]{1,0:T(8,128)(2,1)}, u32[]{:S(2)}, u32[]{:S(2)}) collective-permute-start(bf16[256,1024]{1,0:T(8,128)(2,1)} %get-tuple-element.91), channel_id=1, source_target_pairs={{0,16},{16,0},{1,17},{17,1},{2,18},{18,2},{3,19},{19,3},{4,20},{20... | collective-permute-start | bytes 1572872 | tf_op jit(solution)/shard_map/ppermute | solution.py:41
  254.6 32.1 %collective-permute-start.60 = (bf16[256,1024]{1,0:T(8,128)(2,1)S(1)}, bf16[256,1024]{1,0:T(8,128)(2,1)S(1)}, u32[]{:S(2)}, u32[]{:S(2)}) collective-permute-start(bf16[256,1024]{1,0:T(8,128)(2,1)S(1)} %get-tuple-element.103), channel_id=1, source_target_pairs={{0,16},{16,0},{1,17},{17,1},{2,18},{18,2},{3,19},{19,3},{4,20},{20... | collective-permute-start | bytes 1572872 | tf_op jit(solution)/shard_map/ppermute | solution.py:41
  257.5 14.2 %collective-permute-start.51 = (bf16[128,1024]{1,0:T(8,128)(2,1)S(1)}, bf16[128,1024]{1,0:T(8,128)(2,1)S(1)}, u32[]{:S(2)}, u32[]{:S(2)}) collective-permute-start(bf16[128,1024]{1,0:T(8,128)(2,1)S(1)} %get-tuple-element.126), channel_id=1, source_target_pairs={{0,4},{4,0},{8,12},{12,8},{1,5},{5,1},{9,13},{13,9},{2,6},{6,2},{1... | collective-permute-start | bytes 786440 | tf_op jit(solution)/shard_map/ppermute | solution.py:41
  264.1 13.4 %collective-permute-start.42 = (bf16[128,1024]{1,0:T(8,128)(2,1)S(1)}, bf16[128,1024]{1,0:T(8,128)(2,1)S(1)}, u32[]{:S(2)}, u32[]{:S(2)}) collective-permute-start(bf16[128,1024]{1,0:T(8,128)(2,1)S(1)} %get-tuple-element.128), channel_id=1, source_target_pairs={{0,4},{4,0},{8,12},{12,8},{1,5},{5,1},{9,13},{13,9},{2,6},{6,2},{1... | collective-permute-start | bytes 786440 | tf_op jit(solution)/shard_map/ppermute | solution.py:41
  270.4 26.3 %collective-permute-start.40 = (bf16[256,1024]{1,0:T(8,128)(2,1)S(1)}, bf16[256,1024]{1,0:T(8,128)(2,1)S(1)}, u32[]{:S(2)}, u32[]{:S(2)}) collective-permute-start(bf16[256,1024]{1,0:T(8,128)(2,1)S(1)} %get-tuple-element.89), channel_id=1, source_target_pairs={{0,16},{16,0},{1,17},{17,1},{2,18},{18,2},{3,19},{19,3},{4,20},{20... | collective-permute-start | bytes 1572872 | tf_op jit(solution)/shard_map/ppermute | solution.py:41
  271.9 9.5 %collective-permute-start.52 = (bf16[64,1024]{1,0:T(8,128)(2,1)S(1)}, bf16[64,1024]{1,0:T(8,128)(2,1)S(1)}, u32[]{:S(2)}, u32[]{:S(2)}) collective-permute-start(bf16[64,1024]{1,0:T(8,128)(2,1)S(1)} %get-tuple-element.134), channel_id=1, source_target_pairs={{0,8},{4,12},{8,0},{12,4},{1,9},{5,13},{9,1},{13,5},{2,10},{6,14},... | collective-permute-start | bytes 393224 | tf_op jit(solution)/shard_map/ppermute | solution.py:41
  277.6 8.8 %collective-permute-start.43 = (bf16[64,1024]{1,0:T(8,128)(2,1)S(1)}, bf16[64,1024]{1,0:T(8,128)(2,1)S(1)}, u32[]{:S(2)}, u32[]{:S(2)}) collective-permute-start(bf16[64,1024]{1,0:T(8,128)(2,1)S(1)} %get-tuple-element.136), channel_id=1, source_target_pairs={{0,8},{4,12},{8,0},{12,4},{1,9},{5,13},{9,1},{13,5},{2,10},{6,14},... | collective-permute-start | bytes 393224 | tf_op jit(solution)/shard_map/ppermute | solution.py:41
  281.6 9.1 %collective-permute-start.53 = (bf16[64,1024]{1,0:T(8,128)(2,1)S(1)}, bf16[64,1024]{1,0:T(8,128)(2,1)S(1)}, u32[]{:S(2)}, u32[]{:S(2)}) collective-permute-start(bf16[64,1024]{1,0:T(8,128)(2,1)S(1)} %get-tuple-element.99.refs_0_), channel_id=1, source_target_pairs={{0,8},{4,12},{8,0},{12,4},{1,9},{5,13},{9,1},{13,5},{2,10},{6,14},... | collective-permute-start | bytes 393224 | tf_op jit(solution)/shard_map/ppermute | solution.py:41
  286.6 10.1 %collective-permute-start.49 = (bf16[64,1024]{1,0:T(8,128)(2,1)S(1)}, bf16[64,1024]{1,0:T(8,128)(2,1)S(1)}, u32[]{:S(2)}, u32[]{:S(2)}) collective-permute-start(bf16[64,1024]{1,0:T(8,128)(2,1)S(1)} %get-tuple-element.96.refs_0_), channel_id=1, source_target_pairs={{0,8},{4,12},{8,0},{12,4},{1,9},{5,13},{9,1},{13,5},{2,10},{6,14},... | collective-permute-start | bytes 393224 | tf_op jit(solution)/shard_map/ppermute | solution.py:41
  290.6 10.3 %collective-permute-start.54 = (bf16[64,1024]{1,0:T(8,128)(2,1)S(1)}, bf16[64,1024]{1,0:T(8,128)(2,1)S(1)}, u32[]{:S(2)}, u32[]{:S(2)}) collective-permute-start(bf16[64,1024]{1,0:T(8,128)(2,1)S(1)} %collective-permute-done.53.refs_1_), channel_id=1, source_target_pairs={{0,4},{4,0},{8,12},{12,8},{1,5},{5,1},{9,13},{13,9},{2,6},{6,2},{1... | collective-permute-start | bytes 393224 | tf_op jit(solution)/shard_map/ppermute | solution.py:41
  296.6 8.8 %collective-permute-start.61 = (bf16[128,1024]{1,0:T(8,128)(2,1)S(1)}, bf16[128,1024]{1,0:T(8,128)(2,1)S(1)}, u32[]{:S(2)}, u32[]{:S(2)}) collective-permute-start(bf16[128,1024]{1,0:T(8,128)(2,1)S(1)} %get-tuple-element.122), channel_id=1, source_target_pairs={{0,4},{4,0},{8,12},{12,8},{1,5},{5,1},{9,13},{13,9},{2,6},{6,2},{1... | collective-permute-start | bytes 786440 | tf_op jit(solution)/shard_map/ppermute | solution.py:41
  301.0 8.6 %collective-permute-start.55 = (bf16[128,1024]{1,0:T(8,128)(2,1)S(1)}, bf16[128,1024]{1,0:T(8,128)(2,1)S(1)}, u32[]{:S(2)}, u32[]{:S(2)}) collective-permute-start(bf16[128,1024]{1,0:T(8,128)(2,1)S(1)} %get-tuple-element.124), channel_id=1, source_target_pairs={{0,4},{4,0},{8,12},{12,8},{1,5},{5,1},{9,13},{13,9},{2,6},{6,2},{1... | collective-permute-start | bytes 786440 | tf_op jit(solution)/shard_map/ppermute | solution.py:41
  305.5 11.2 %collective-permute-start.62 = (bf16[64,1024]{1,0:T(8,128)(2,1)S(1)}, bf16[64,1024]{1,0:T(8,128)(2,1)S(1)}, u32[]{:S(2)}, u32[]{:S(2)}) collective-permute-start(bf16[64,1024]{1,0:T(8,128)(2,1)S(1)} %get-tuple-element.130), channel_id=1, source_target_pairs={{0,8},{4,12},{8,0},{12,4},{1,9},{5,13},{9,1},{13,5},{2,10},{6,14},... | collective-permute-start | bytes 393224 | tf_op jit(solution)/shard_map/ppermute | solution.py:41
  309.7 10.5 %collective-permute-start.56 = (bf16[64,1024]{1,0:T(8,128)(2,1)S(1)}, bf16[64,1024]{1,0:T(8,128)(2,1)S(1)}, u32[]{:S(2)}, u32[]{:S(2)}) collective-permute-start(bf16[64,1024]{1,0:T(8,128)(2,1)S(1)} %get-tuple-element.132), channel_id=1, source_target_pairs={{0,8},{4,12},{8,0},{12,4},{1,9},{5,13},{9,1},{13,5},{2,10},{6,14},... | collective-permute-start | bytes 393224 | tf_op jit(solution)/shard_map/ppermute | solution.py:41
  320.7 10.8 %collective-permute-start.74 = (bf16[16,6656]{1,0:T(8,128)(2,1)S(1)}, bf16[16,6656]{1,0:T(8,128)(2,1)S(1)}, u32[]{:S(2)}, u32[]{:S(2)}) collective-permute-start(bf16[16,6656]{1,0:T(8,128)(2,1)S(1)} %convert_element_type.145), channel_id=1, source_target_pairs={{0,16},{16,0},{1,17},{17,1},{2,18},{18,2},{3,19},{19,3},{4,20},{20... | collective-permute-start | bytes 638984 | tf_op jit(solution)/shard_map/ppermute | solution.py:41
  324.2 7.3 %collective-permute-start.70 = (f32[1,4096]{1,0:T(1,128)S(1)}, f32[1,4096]{1,0:T(1,128)S(1)}, u32[]{:S(2)}, u32[]{:S(2)}) collective-permute-start(f32[1,4096]{1,0:T(1,128)S(1)} %add.285), channel_id=1, source_target_pairs={{0,8},{4,12},{8,0},{12,4},{1,9},{5,13},{9,1},{13,5},{2,10},{6,14},... | collective-permute-start | bytes 49160 | tf_op jit(solution)/shard_map/ppermute | solution.py:41
  327.4 10.0 %collective-permute-start.68 = (bf16[64,1024]{1,0:T(8,128)(2,1)S(1)}, bf16[64,1024]{1,0:T(8,128)(2,1)S(1)}, u32[]{:S(2)}, u32[]{:S(2)}) collective-permute-start(bf16[64,1024]{1,0:T(8,128)(2,1)S(1)} %get-tuple-element.99.refs_0_), channel_id=1, source_target_pairs={{0,4},{4,0},{8,12},{12,8},{1,5},{5,1},{9,13},{13,9},{2,6},{6,2},{1... | collective-permute-start | bytes 393224 | tf_op jit(solution)/shard_map/ppermute | solution.py:41
  329.5 12.8 %collective-permute-start.66 = (bf16[64,1024]{1,0:T(8,128)(2,1)S(1)}, bf16[64,1024]{1,0:T(8,128)(2,1)S(1)}, u32[]{:S(2)}, u32[]{:S(2)}) collective-permute-start(bf16[64,1024]{1,0:T(8,128)(2,1)S(1)} %get-tuple-element.96.refs_0_), channel_id=1, source_target_pairs={{0,4},{4,0},{8,12},{12,8},{1,5},{5,1},{9,13},{13,9},{2,6},{6,2},{1... | collective-permute-start | bytes 393224 | tf_op jit(solution)/shard_map/ppermute | solution.py:41
  329.5 15.6 %collective-permute-start.67 = (bf16[64,1024]{1,0:T(8,128)(2,1)S(1)}, bf16[64,1024]{1,0:T(8,128)(2,1)S(1)}, u32[]{:S(2)}, u32[]{:S(2)}) collective-permute-start(bf16[64,1024]{1,0:T(8,128)(2,1)S(1)} %collective-permute-done.49.refs_1_), channel_id=1, source_target_pairs={{0,4},{4,0},{8,12},{12,8},{1,5},{5,1},{9,13},{13,9},{2,6},{6,2},{1... | collective-permute-start | bytes 393224 | tf_op jit(solution)/shard_map/ppermute | solution.py:41
  331.5 10.8 %collective-permute-start.63 = (bf16[64,1024]{1,0:T(8,128)(2,1)S(1)}, bf16[64,1024]{1,0:T(8,128)(2,1)S(1)}, u32[]{:S(2)}, u32[]{:S(2)}) collective-permute-start(bf16[64,1024]{1,0:T(8,128)(2,1)S(1)} %get-tuple-element.105.refs_0_), channel_id=1, source_target_pairs={{0,8},{4,12},{8,0},{12,4},{1,9},{5,13},{9,1},{13,5},{2,10},{6,14},... | collective-permute-start | bytes 393224 | tf_op jit(solution)/shard_map/ppermute | solution.py:41
  331.5 14.2 %collective-permute-start.57 = (bf16[64,1024]{1,0:T(8,128)(2,1)S(1)}, bf16[64,1024]{1,0:T(8,128)(2,1)S(1)}, u32[]{:S(2)}, u32[]{:S(2)}) collective-permute-start(bf16[64,1024]{1,0:T(8,128)(2,1)S(1)} %get-tuple-element.101.refs_0_), channel_id=1, source_target_pairs={{0,8},{4,12},{8,0},{12,4},{1,9},{5,13},{9,1},{13,5},{2,10},{6,14},... | collective-permute-start | bytes 393224 | tf_op jit(solution)/shard_map/ppermute | solution.py:41
  337.4 13.5 %collective-permute-start.64 = (bf16[64,1024]{1,0:T(8,128)(2,1)S(1)}, bf16[64,1024]{1,0:T(8,128)(2,1)S(1)}, u32[]{:S(2)}, u32[]{:S(2)}) collective-permute-start(bf16[64,1024]{1,0:T(8,128)(2,1)S(1)} %get-tuple-element.105.refs_0_), channel_id=1, source_target_pairs={{0,4},{4,0},{8,12},{12,8},{1,5},{5,1},{9,13},{13,9},{2,6},{6,2},{1... | collective-permute-start | bytes 393224 | tf_op jit(solution)/shard_map/ppermute | solution.py:41
  342.3 10.8 %collective-permute-start.58 = (bf16[64,1024]{1,0:T(8,128)(2,1)S(1)}, bf16[64,1024]{1,0:T(8,128)(2,1)S(1)}, u32[]{:S(2)}, u32[]{:S(2)}) collective-permute-start(bf16[64,1024]{1,0:T(8,128)(2,1)S(1)} %get-tuple-element.101.refs_0_), channel_id=1, source_target_pairs={{0,4},{4,0},{8,12},{12,8},{1,5},{5,1},{9,13},{13,9},{2,6},{6,2},{1... | collective-permute-start | bytes 393224 | tf_op jit(solution)/shard_map/ppermute | solution.py:41
  342.3 9.4 %collective-permute-start.65 = (bf16[64,1024]{1,0:T(8,128)(2,1)S(1)}, bf16[64,1024]{1,0:T(8,128)(2,1)S(1)}, u32[]{:S(2)}, u32[]{:S(2)}) collective-permute-start(bf16[64,1024]{1,0:T(8,128)(2,1)S(1)} %collective-permute-done.63.refs_1_), channel_id=1, source_target_pairs={{0,4},{4,0},{8,12},{12,8},{1,5},{5,1},{9,13},{13,9},{2,6},{6,2},{1... | collective-permute-start | bytes 393224 | tf_op jit(solution)/shard_map/ppermute | solution.py:41
  345.7 7.4 %collective-permute-start.59 = (bf16[64,1024]{1,0:T(8,128)(2,1)S(1)}, bf16[64,1024]{1,0:T(8,128)(2,1)S(1)}, u32[]{:S(2)}, u32[]{:S(2)}) collective-permute-start(bf16[64,1024]{1,0:T(8,128)(2,1)S(1)} %collective-permute-done.57.refs_1_), channel_id=1, source_target_pairs={{0,4},{4,0},{8,12},{12,8},{1,5},{5,1},{9,13},{13,9},{2,6},{6,2},{1... | collective-permute-start | bytes 393224 | tf_op jit(solution)/shard_map/ppermute | solution.py:41
  (88 other events, 909.2 us)

commit v4 on v3

--- a/solution.py
+++ b/solution.py
@@ -8,8 +8,9 @@
 MODEL_WIDTH = 16384
 ADAPTER_SCALE = 0.5
 HIDDEN_CHUNKS = 3
-WIDTH_CHUNKS = 4
-VMEM_BYTES = 28 * 1024 * 1024
+VMEM_MIB = 12
+MATMUL_VMEM_MIB = 18
+COST_SHARE = 0.01
 
 F32 = jnp.float32
 BF16 = jnp.bfloat16
@@ -58,8 +59,14 @@
     return out
 
 
-def params():
-    return pltpu.CompilerParams(vmem_limit_bytes=VMEM_BYTES)
+def params(mib=VMEM_MIB):
+    return pltpu.CompilerParams(vmem_limit_bytes=mib * 1024 * 1024)
+
+
+def cost(flops, size):
+    return pl.CostEstimate(
+        flops=int(flops * COST_SHARE), bytes_accessed=int(size * COST_SHARE), transcendentals=0
+    )
 
 
 def normalize(pieces, stats, steering, gain, down, h, hid, side, into=None):
@@ -119,9 +126,7 @@
         ],
         input_output_aliases={len(pieces) + 5: 0} if n_into else {},
         compiler_params=params(),
-        cost_estimate=pl.CostEstimate(
-            flops=2 * tokens * width * ranks, bytes_accessed=4 * tokens * width, transcendentals=0
-        ),
+        cost_estimate=cost(2 * tokens * width * ranks, 4 * tokens * width),
         name="normalize",
     )(
         jnp.stack(scalars),
@@ -164,12 +169,8 @@
             jax.ShapeDtypeStruct((half, tiles * tile), BF16),
         ],
         input_output_aliases={2 + i: i for i in range(len(into))},
-        compiler_params=params(),
-        cost_estimate=pl.CostEstimate(
-            flops=2 * rows * depth * (stop - start) * tile,
-            bytes_accessed=2 * depth * (rows + (stop - start) * tile) + 6 * half * (stop - start) * tile,
-            transcendentals=0,
-        ),
+        compiler_params=params(MATMUL_VMEM_MIB),
+        cost_estimate=cost(2 * rows * depth * (stop - start) * tile, 2 * depth * (rows + (stop - start) * tile) + 6 * half * (stop - start) * tile),
         name="forward_matmul",
     )(x, weights, *into, *after)
 
@@ -192,9 +193,7 @@
         out_specs=[pl.BlockSpec((own, tile), lambda i: (0, i))] * 2,
         out_shape=[jax.ShapeDtypeStruct((own, columns), BF16)] * 2,
         compiler_params=params(),
-        cost_estimate=pl.CostEstimate(
-            flops=2 * own * columns, bytes_accessed=16 * own * columns, transcendentals=0
-        ),
+        cost_estimate=cost(2 * own * columns, 16 * own * columns),
         name="share_sums",
     )(*parts)
 
@@ -264,9 +263,7 @@
             jax.ShapeDtypeStruct((own, 2 * rank + 1), F32),
         ],
         compiler_params=params(),
-        cost_estimate=pl.CostEstimate(
-            flops=8 * own * columns * rank, bytes_accessed=16 * own * columns, transcendentals=own * columns
-        ),
+        cost_estimate=cost(8 * own * columns * rank, 16 * own * columns),
         name="gated_gradients",
     )(d.reshape(1), *mine, other, cotangent, low, up, *after)
 
@@ -312,12 +309,8 @@
         + [ANY] * len(after),
         out_specs=out_specs,
         out_shape=out_shape,
-        compiler_params=params(),
-        cost_estimate=pl.CostEstimate(
-            flops=2 * rows * hidden * tiles * tile,
-            bytes_accessed=2 * hidden * (rows + tiles * tile) + (4 + 4 * n_base) * rows * tiles * tile,
-            transcendentals=0,
-        ),
+        compiler_params=params(MATMUL_VMEM_MIB),
+        cost_estimate=cost(2 * rows * hidden * tiles * tile, 2 * hidden * (rows + tiles * tile) + (4 + 4 * n_base) * rows * tiles * tile),
         name="backward_matmul",
     )(*pieces, weights, *(() if base is None else (base,)), *after)
 
@@ -343,42 +336,47 @@
         out_specs=[pl.BlockSpec((rank, w), lambda i: (0, 0)) for w in widths],
         out_shape=[jax.ShapeDtypeStruct((rank, w), F32) for w in widths],
         compiler_params=params(),
-        cost_estimate=pl.CostEstimate(
-            flops=2 * rank * low.shape[1] * sum(widths),
-            bytes_accessed=2 * low.shape[1] * sum(widths),
-            transcendentals=0,
-        ),
+        cost_estimate=cost(2 * rank * low.shape[1] * sum(widths), 2 * low.shape[1] * sum(widths)),
         name="adapter_up",
     )(low, *operands)
 
 
 def assemble(pieces, places, block, tokens, width, columns, into=None):
-    chunk = pieces[0].shape[1]
+    chunk = pieces[0][0].shape[1]
     start = columns // chunk
 
     def kernel(place_ref, *refs):
-        out_ref = refs[-1]
+        out_ref, token_ref = refs[-2:]
+        token_ref[...] = jnp.zeros_like(token_ref)
         i = 0
-        for ref in refs[: len(pieces)]:
-            for r in range(0, ref.shape[0], block):
-                out_ref[pl.ds(pl.multiple_of(place_ref[i], block), block), :] = ref[r : r + block, :]
+        count = sum(a.shape[0] // block for a, _ in pieces)
+        for k, (a, b) in enumerate(pieces):
+            for r in range(0, a.shape[0], block):
+                rows = refs[2 * k][r : r + block, :]
+                if b is not a:
+                    rows = jnp.where(place_ref[count] == 1, rows, refs[2 * k + 1][r : r + block, :])
+                out_ref[pl.ds(pl.multiple_of(place_ref[i], block), block), :] = rows
                 i += 1
 
     n_into = 0 if into is None else 1
+    operands = [x for pair in pieces for x in pair]
     return pl.pallas_call(
         kernel,
         grid_spec=pltpu.PrefetchScalarGridSpec(
             num_scalar_prefetch=1,
             grid=(1,),
-            in_specs=[pl.BlockSpec(x.shape, lambda i, p: (0, 0)) for x in pieces] + [ANY] * n_into,
-            out_specs=pl.BlockSpec((tokens, chunk), lambda i, p: (0, start)),
+            in_specs=[pl.BlockSpec(x.shape, lambda i, p: (0, 0)) for x in operands] + [ANY] * n_into,
+            out_specs=[
+                pl.BlockSpec((tokens, chunk), lambda i, p: (0, start)),
+                pl.BlockSpec((8, 128), lambda i, p: (0, 0)),
+            ],
         ),
-        out_shape=jax.ShapeDtypeStruct((tokens, width), BF16),
-        input_output_aliases={len(pieces) + 1: 0} if n_into else {},
+        out_shape=[jax.ShapeDtypeStruct((tokens, width), BF16), jax.ShapeDtypeStruct((8, 128), F32)],
+        input_output_aliases={len(operands) + 1: 0} if n_into else {},
         compiler_params=params(),
-        cost_estimate=pl.CostEstimate(flops=0, bytes_accessed=4 * tokens * chunk, transcendentals=0),
+        cost_estimate=cost(0, 4 * tokens * chunk),
         name="assemble",
-    )(places, *pieces, *((into,) if n_into else ()))
+    )(places, *operands, *((into,) if n_into else ()))
 
 
 def finish(parts, stream, stats, back, down, steering, gain, columns):
@@ -414,9 +412,7 @@
         out_specs=[pl.BlockSpec((rows, width), lambda i: (0, 0)), pl.BlockSpec((1, width), lambda i: (0, 0))],
         out_shape=[jax.ShapeDtypeStruct((rows, width), BF16), jax.ShapeDtypeStruct((1, width), F32)],
         compiler_params=params(),
-        cost_estimate=pl.CostEstimate(
-            flops=2 * rows * width * down.shape[0], bytes_accessed=10 * rows * width, transcendentals=0
-        ),
+        cost_estimate=cost(2 * rows * width * down.shape[0], 10 * rows * width),
         name="finish",
     )(*parts, stream, stats, back, down, steering.reshape(1, -1), gain.reshape(1, -1))
 
@@ -431,13 +427,13 @@
         first_pair = d == 0
         down_rows = jnp.transpose(down, (0, 2, 1)).reshape(2 * rank, width)
 
-        shard = tokens // ffn
         split = width // 2 if hid >= ffn and width % 256 == 0 else width
         if split < width:
-            mine = lax.dynamic_slice(stream, (f * shard, split), (shard, width - split))
+            quarter = tokens // ffn
+            mine = lax.dynamic_slice(stream, (f * quarter, split), (quarter, width - split))
             far = double(swap(mine, "dp", dp, 1), "ffn", ffn)
             near = swap(stream[:, :split], "dp", dp, 1)
-            peer_pieces = [(near, None), (far, GatheredRows(f, ffn, shard, own))]
+            peer_pieces = [(near, None), (far, GatheredRows(f, ffn, quarter, own))]
         else:
             peer_pieces = [(swap(stream, "dp", dp, 1), None)]
         rows = stream.astype(F32)
@@ -469,20 +465,19 @@
         low = low.astype(BF16)
         low_own = low[0]
 
-        acts, sent, others = [], [], []
+        width_tile = tile_of(width, 512)
+        halves = split_tiles(width // width_tile, 2)
         last_bit = 1 << (bits_of(hid) - 1)
-        for c, (first, n) in enumerate(chunks):
+        acts, sent, others, grads, back, bases = [], [], [], [], 0.0, []
+        mine_grads, peer_grads, own_first, peer_first = [], [], [], []
+
+        def sums_over_hid(c, after_first, after_second):
+            first, n = chunks[c]
             middle = (n + 1) // 2
-            wait = tuple(sent[-1]) if c else ()
-            if c >= 2:
-                wait += (acts[c - 2][1],)
-            half_done = forward_matmul(normed, weights, first, n, 0, middle, tile, after=wait)
-            wait = tuple(low_steps[c : c + 1])
-            if c:
-                wait += (acts[c - 1][2],)
-            if c >= 2:
-                wait += (others[c - 2],)
-            keep, send = forward_matmul(normed, weights, first, n, middle, n, tile, into=half_done, after=wait)
+            half_done = forward_matmul(normed, weights, first, n, 0, middle, tile, after=after_first)
+            keep, send = forward_matmul(
+                normed, weights, first, n, middle, n, tile, into=half_done, after=after_second()
+            )
             parts = [keep, swap(send, "hid", hid, 1)]
             for bit in range(1, bits_of(hid) - 1):
                 size = parts[-1].shape[0]
@@ -496,9 +491,23 @@
                 swap((total_of(parts, own, 2 * own) + peer_got.astype(F32)).astype(BF16), "dp", dp, 1)
             )
 
-        width_tile = tile_of(width, 512)
-        halves = split_tiles(width // width_tile, 2)
-        grads, back, bases, wait = [], 0.0, [], ()
+        def gradients(c, after):
+            parts, own_got, _ = acts[c]
+            mine_grad, other_grad, back_part = gated_gradients(
+                d, parts + [own_got], others[c], cotangent, chunks[c][0] * tile, low_own, up, own, after
+            )
+            peer_grad = swap(other_grad, "dp", dp, 1)
+            pieces = []
+            for g, firsts in ((mine_grad, own_first), (peer_grad, peer_first)):
+                blocks = [g]
+                for bit in reversed(range(bits_of(hid))):
+                    blocks += [swap(x, "hid", hid, 1 << bit) for x in blocks]
+                firsts.append(blocks[1])
+                pieces += blocks
+            mine_grads.append(mine_grad)
+            peer_grads.append(peer_grad)
+            grads.append(pieces)
+            return back + back_part
 
         def partial_sums(c, which, base, after):
             first, n = halves[which]
@@ -507,31 +516,32 @@
                 base=base, base_first=first, partial=True, after=after,
             )
 
-        for c, (first, n) in enumerate(chunks):
-            parts, own_got, _ = acts[c]
-            if c == len(chunks) - 1:
-                bases = [partial_sums(0, 0, None, wait[:1])]
-                wait += (bases[0],)
-            mine_grad, other_grad, back_part = gated_gradients(
-                d, parts + [own_got], others[c], cotangent, first * tile, low_own, up, own, wait
-            )
-            back = back + back_part
-            peer_grad = swap(other_grad, "dp", dp, 1)
-            wait = (peer_grad,)
-            pieces = []
-            for g in (mine_grad, peer_grad):
-                blocks = [g]
-                for bit in reversed(range(bits_of(hid))):
-                    blocks += [swap(x, "hid", hid, 1 << bit) for x in blocks]
-                if g is mine_grad:
-                    wait += (blocks[1],)
-                pieces += blocks
-            grads.append(pieces)
-        bases.append(partial_sums(0, 1, None, (mine_grad,)))
-        for c in range(1, len(chunks) - 1):
+        end = len(chunks) - 1
+        for c in range(len(chunks)):
+            before = tuple(sent[-1]) if c else ()
+            if c >= 2:
+                back = gradients(c - 2, (peer_grads[-1], own_first[-1]) if c >= 3 else ())
+                before += (mine_grads[-1],)
+
+            def between():
+                wait = tuple(low_steps[c : c + 1])
+                if c:
+                    wait += acts[c - 1][1:]
+                if c and c == end:
+                    nonlocal back
+                    back = gradients(c - 1, (peer_grads[-1], own_first[-1]) if c >= 2 else ())
+                    wait += (mine_grads[-1],)
+                return wait
+
+            sums_over_hid(c, before, between)
+        bases = [partial_sums(0, 0, None, tuple(sent[-1]) + (own_first[-1], peer_first[-1]))]
+        bases.append(partial_sums(0, 1, None, (bases[0], acts[end][2])))
+        back = gradients(end, (bases[1],))
+        wait = (peer_grads[-1], own_first[-1])
+        for c in range(1, end):
             for which in range(2):
                 bases[which] = partial_sums(c, which, bases[which], wait)
-                wait = (grads[-1][len(grads[-1]) // 2 + 1],)
+                wait = (peer_first[-1],)
         base = bases[-1]
         bases = [(halves[i][0], bases[i]) for i in range(2)]
 
@@ -543,7 +553,10 @@
         back_low = back[:, :, : 2 * rank].astype(BF16)
         acts_product = back[0, :, 2 * rank]
 
-        place = reversed_bits(f, bits_of(ffn))
+        line = ffn == 4
+        shard = tokens // 2 if line else tokens // ffn
+        place = f >> 1 if line else reversed_bits(f, bits_of(ffn))
+        middle = (f == 1) | (f == 2)
         block = min(own, shard)
 
         def natural(row):
@@ -566,8 +579,9 @@
         stream_shard = shard_rows(stream)
         back_shard = lax.dynamic_slice_in_dim(back_low[0], place * shard, shard, axis=0)
 
-        out, sums, gathered = None, [], []
-        steps = split_tiles(width // width_tile, WIDTH_CHUNKS)
+        out, sums, gathered, written = None, [], [], []
+        tiles = width // width_tile
+        steps = [(0, 2), (2, 2), (4, 2), (6, 1), (7, 1)] if tiles == 8 else split_tiles(tiles, 4)
         products, received = [], []
         for first, n in steps:
             held_first, held = [b for b in bases if b[0] <= first][-1]
@@ -577,35 +591,56 @@
             )
             products.append(keep)
             received.append(swap(send, "dp", dp, 1))
-        places = []
-        for p in range(ffn):
-            owner = reversed_bits(f ^ reversed_bits(p, bits_of(ffn)), bits_of(ffn))
-            places += [natural(owner * shard + i * block) for i in range(shard // block)]
-        places = jnp.stack(places)
+        owners = [place, 1 - place] if line else [
+            reversed_bits(f ^ reversed_bits(p, bits_of(ffn)), bits_of(ffn)) for p in range(ffn)
+        ]
+        places = [natural(o * shard + i * block) for o in owners for i in range(shard // block)]
+        places = jnp.stack(places + [jnp.where(middle, 1, 0).astype(places[0].dtype)])
+
+        def send_line(x, pairs):
+            return lax.ppermute(x, "ffn", pairs)
+
         for j, (first, n) in enumerate(steps):
-            got = received[j]
+            got = ordered(received[j], products[min(j + 2, len(steps) - 1)])
             if j >= 2:
-                got = ordered(got, gathered[j - 2][1], *(gathered[j - 3][-1:] if j >= 3 else ()))
-            parts = [products[j], got]
-            for bit in range(bits_of(ffn)):
-                half = parts[-1].shape[0] // 2
-                mine = (f >> bit) & 1
-                halves = [
-                    [lax.dynamic_slice_in_dim(p, side * half, half, axis=0) for p in parts]
-                    for side in (mine, 1 - mine)
-                ]
-                parts = [total_of(halves[0], 0, half)] + [
-                    swap(total_of(halves[1], 0, half).astype(BF16), "ffn", ffn, 1 << bit)
-                ]
+                got = ordered(got, *gathered[j - 2], *(written[j - 3 : j - 2] if j >= 3 else ()))
+            if line:
+                part = products[j] + got.astype(F32)
+                total = part + send_line(part.astype(BF16), [(0, 1), (3, 2)]).astype(F32)
+                upper = place == 1
+                keep = jnp.where(upper, total[shard:], total[:shard])
+                send = jnp.where(upper, total[:shard], total[shard:]).astype(BF16)
+                parts = [keep, send_line(send, [(1, 2), (2, 1)])]
+            else:
+                parts = [products[j], got]
+                for bit in range(bits_of(ffn)):
+                    half = parts[-1].shape[0] // 2
+                    mine = (f >> bit) & 1
+                    sides = [
+                        [lax.dynamic_slice_in_dim(p, side * half, half, axis=0) for p in parts]
+                        for side in (mine, 1 - mine)
+                    ]
+                    parts = [total_of(sides[0], 0, half)] + [
+                        swap(total_of(sides[1], 0, half).astype(BF16), "ffn", ffn, 1 << bit)
+                    ]
             result, sum_part = finish(
                 parts, stream_shard, stats_shard, back_shard, down_rows, steering, gain, first * width_tile
             )
+            if line:
+                sum_part = jnp.where(middle, sum_part, 0.0)
+                outward = [(1, 0), (2, 3)]
+                other = send_line(result, [(1, 2), (2, 1)])
+                pieces = [(result, send_line(result, outward)), (other, send_line(other, outward))]
+            else:
+                blocks = [result]
+                for bit in reversed(range(bits_of(ffn))):
+                    blocks += [swap(x, "ffn", ffn, 1 << bit) for x in blocks]
+                other = blocks[1]
+                pieces = [(x, x) for x in blocks]
             sums.append(sum_part)
-            blocks = [result]
-            for bit in reversed(range(bits_of(ffn))):
-                blocks += [swap(x, "ffn", ffn, 1 << bit) for x in blocks]
-            gathered.append(blocks)
-            out = assemble(blocks, places, block, tokens, width, first * width_tile, into=out)
+            gathered.append((other, pieces[0][1]))
+            out, token = assemble(pieces, places, block, tokens, width, first * width_tile, into=out)
+            written.append(token)
 
         steering_gradient = jnp.concatenate(sums, axis=1)
         for bit in range(bits_of(ffn)):

time: 356 us -> 416 us (1.17)
  waiting for transfers between devices: 82.1 us -> 118 us
  starting transfers between devices: 81.7 us -> 95.9 us
    ppermute x0 -> x25, waiting for transfers between devices: none -> 50.9 us  [send_line(): return lax.ppermute(x, 'ffn', pairs)]
    ppermute x0 -> x25, starting transfers between devices: none -> 37.7 us  [send_line(): return lax.ppermute(x, 'ffn', pairs)]
    ppermute x75 -> x56, starting transfers between devices: 81.7 us -> 58.2 us  [swap(): return lax.ppermute(x, axis, [(i, i ^ mask) for i in range(n)])]
    ppermute x75 -> x56, waiting for transfers between devices: 82.1 us -> 67.5 us  [swap(): return lax.ppermute(x, axis, [(i, i ^ mask) for i in range(n)])]
    pallas_call x8 -> x9, Pallas kernels: 51.7 us -> 54.9 us  [backward_matmul(): pl.pallas_call(kernel, grid=(tiles,), in_specs=[RESIDENT] * len(pieces) +...]
    unnamed x159 -> x196, local copies, waits for them, and re-layouts: 28.5 us -> 29.4 us
  transfers between devices with their start and end apart: 75 -> 81, of which waited for: 30 -> 28; matrix products, arithmetic and copies ran while one was open for 6% -> 6% of each run, Pallas kernels for 26% -> 23%
where the time goes in v4:
time: 416 us; the launch traced here: 414 us
  Pallas kernels  126 us (30%)
  waiting for transfers between devices  118 us (28%)
  starting transfers between devices  95.9 us (23%)
  local copies, waits for them, and re-layouts  37.8 us (9%)
  other arithmetic  17.1 us (4%)
  blocking collectives  13.3 us (3%)
    ppermute x56, waiting for transfers between devices, swap(): return lax.ppermute(x, axis, [(i, i ^ mask) for i in range(n)])  67.5 us
    ppermute x56, starting transfers between devices, swap(): return lax.ppermute(x, axis, [(i, i ^ mask) for i in range(n)])  58.2 us
    pallas_call x9, Pallas kernels, backward_matmul(): pl.pallas_call(kernel, grid=(tiles,), in_specs=[RESIDENT] * len(pieces) +...  54.9 us
    ppermute x25, waiting for transfers between devices, send_line(): return lax.ppermute(x, 'ffn', pairs)  50.9 us
    pallas_call x6, Pallas kernels, forward_matmul(): pl.pallas_call(kernel, grid=(stop - start,), in_specs=[RESIDENT, pl.Block...  46 us
    ppermute x25, starting transfers between devices, send_line(): return lax.ppermute(x, 'ffn', pairs)  37.7 us
    unnamed x196, local copies, waits for them, and re-layouts  29.4 us
  transfers between devices with their start and end apart: 81, of which 28 were waited for; matrix products, arithmetic and copies ran while one was open for 6% of the time, Pallas kernels for 23%

profile of v4, /device:TPU:0, one launch (start us, length us, event | category | flops | bytes accessed | tf_op | source)
XLA Modules:
  0.0 413.8 jit_solution(11687947777043702621)
XLA Ops:
  1.8 3.0 collective-permute-start.1
  4.8 2.3 slice.96
  7.6 4.4 %collective-permute-done.1 = bf16[64,2048]{1,0:T(8,128)(2,1)} collective-permute-done((bf16[64,2048]{1,0:T(8,128)(2,1)S(1)}, bf16[64,2048]{1,0:T(8,128)(2,1)}, u32[]{:S(2)}, u32[]{:S(2)}) %collective-permute-start.1) | collective-permute-done | bytes 262176 | tf_op jit(solution)/shard_map/ppermute | solution.py:42
  12.0 3.2 collective-permute-start.2
  15.8 6.7 %all-reduce = (f32[256]{0:T(256)S(1)}, f32[]{:T(128)}) all-reduce(f32[256]{0:T(256)S(1)} %fusion, f32[]{:T(128)} %multiply_reduce_fusion), channel_id=1, replica_groups=mesh['dp'=2,'ffn'=4,'hid'=4] {'hid'}, use_global_device_ids=true, to_apply=%region_1.0 | all-reduce | flops 257 | bytes 2056 | tf_op jit(solution)/shard_map/psum | solution.py:440
  23.2 2.4 collective-permute-done.2
  25.5 1.9 pad_maximum_fusion.2
  28.8 6.7 %psum.23 = f32[256]{0:T(256)S(1)} all-reduce(f32[256]{0:T(256)S(1)} %fusion.2), channel_id=1, replica_groups=mesh['dp'=2,'ffn'=4,'hid'=4] {'hid'}, use_global_device_ids=true, to_apply=%region_5.0 | all-reduce | flops 256 | bytes 2048 | tf_op jit(solution)/shard_map/psum | solution.py:447
  39.3 1.7 normalize.2
  42.4 3.3 normalize.3
  45.9 8.4 %forward_matmul.6 = (f32[256,2048]{1,0:T(8,128)S(1)}, bf16[256,2048]{1,0:T(8,128)(2,1)S(1)}) custom-call(bf16[512,4096]{1,0:T(8,128)(2,1)S(1)} %get-tuple-element.76.x_ref, bf16[1,4096,6656]{2,1,0:T(8,128)(2,1)} %refs_8_.17), custom_call_target="tpu_custom_call" | custom-call | flops 42949672 | bytes 141557 | tf_op jit(solution)/shard_map/forward_matmul/pallas_call | solution.py:161
  54.3 7.0 %forward_matmul.7 = (f32[256,2048]{1,0:T(8,128)S(1)}, bf16[256,2048]{1,0:T(8,128)(2,1)S(1)}) custom-call(bf16[512,4096]{1,0:T(8,128)(2,1)S(1)} %get-tuple-element.76.x_ref, bf16[1,4096,6656]{2,1,0:T(8,128)(2,1)} %refs_8_.17, f32[256,2048]{1,0:T(8,128)S(1)} %get-tuple-element.77.refs_0_, ...), custom_call_target="tpu_custom_call", output_to_operand_aliasing={{0}: (2, {}), {1}: (3, {})} | custom-call | flops 42949672 | bytes 141557 | tf_op jit(solution)/shard_map/forward_matmul/pallas_call | solution.py:161
  61.3 2.6 collective-permute-done.6.refs_1_
  67.3 12.4 %collective-permute-done.7 = f32[2,64,32]{2,1,0:T(8,128)S(1)} collective-permute-done((f32[2,64,32]{2,1,0:T(8,128)S(1)}, f32[2,64,32]{2,1,0:T(8,128)S(1)}, u32[]{:S(2)}, u32[]{:S(2)}) %collective-permute-start.7) | collective-permute-done | bytes 16416 | tf_op jit(solution)/shard_map/ppermute | solution.py:42
  79.7 7.0 %forward_matmul.8 = (f32[256,2048]{1,0:T(8,128)S(1)}, bf16[256,2048]{1,0:T(8,128)(2,1)S(1)}) custom-call(bf16[512,4096]{1,0:T(8,128)(2,1)S(1)} %get-tuple-element.76.x_ref, bf16[1,4096,6656]{2,1,0:T(8,128)(2,1)} %refs_8_.17, bf16[64,2048]{1,0:T(8,128)(2,1)S(1)} %get-tuple-element.83.refs_0_, bf16[64,2048]{1,0:T(8,128)(2,1)S(1)} %get-tuple-element.84.refs_1_), custom_call_target="tpu_custom_call" | custom-call | flops 42949672 | bytes 141557 | tf_op jit(solution)/shard_map/forward_matmul/pallas_call | solution.py:161
  86.8 7.1 %forward_matmul.9 = (f32[256,2048]{1,0:T(8,128)S(1)}, bf16[256,2048]{1,0:T(8,128)(2,1)S(1)}) custom-call(bf16[512,4096]{1,0:T(8,128)(2,1)S(1)} %get-tuple-element.76.x_ref, bf16[1,4096,6656]{2,1,0:T(8,128)(2,1)} %refs_8_.17, f32[256,2048]{1,0:T(8,128)S(1)} %get-tuple-element.85.refs_0_, ...), custom_call_target="tpu_custom_call", output_to_operand_aliasing={{0}: (2, {}), {1}: (3, {})} | custom-call | flops 42949672 | bytes 141557 | tf_op jit(solution)/shard_map/forward_matmul/pallas_call | solution.py:161
  99.3 4.5 %collective-permute-done.11.refs_3_ = bf16[64,2048]{1,0:T(8,128)(2,1)} collective-permute-done((bf16[64,2048]{1,0:T(8,128)(2,1)}, bf16[64,2048]{1,0:T(8,128)(2,1)}, u32[]{:S(2)}, u32[]{:S(2)}) %collective-permute-start.11) | collective-permute-done | bytes 262176 | tf_op jit(solution)/shard_map/ppermute | solution.py:42
  103.8 1.6 copy-done.18
  107.6 2.0 gated_gradients.3
  115.0 9.5 %forward_matmul.10 = (f32[256,2560]{1,0:T(8,128)S(1)}, bf16[256,2560]{1,0:T(8,128)(2,1)S(1)}) custom-call(bf16[512,4096]{1,0:T(8,128)(2,1)S(1)} %copy-done.1, bf16[1,4096,6656]{2,1,0:T(8,128)(2,1)} %refs_8_.17, bf16[64,2048]{1,0:T(8,128)(2,1)S(1)} %copy-done.82, bf16[64,2048]{1,0:T(8,128)(2,1)} %get-tuple-element.90.refs_1_, ...), custom_call_target="tpu_custom_call" | custom-call | flops 64424508 | bytes 191365 | tf_op jit(solution)/shard_map/forward_matmul/pallas_call | solution.py:161
  125.7 7.1 %forward_matmul.11 = (f32[256,2560]{1,0:T(8,128)S(1)}, bf16[256,2560]{1,0:T(8,128)(2,1)S(1)}) custom-call(bf16[512,4096]{1,0:T(8,128)(2,1)S(1)} %copy-done.1, bf16[1,4096,6656]{2,1,0:T(8,128)(2,1)} %refs_8_.17, f32[256,2560]{1,0:T(8,128)S(1)} %get-tuple-element.92.refs_0_, ...), custom_call_target="tpu_custom_call", output_to_operand_aliasing={{0}: (2, {}), {1}: (3, {})} | custom-call | flops 42949672 | bytes 141557 | tf_op jit(solution)/shard_map/forward_matmul/pallas_call | solution.py:161
  132.9 3.0 collective-permute-done.17.refs_1_
  139.6 8.0 %collective-permute-done.19.refs_10_ = bf16[64,2560]{1,0:T(8,128)(2,1)S(1)} collective-permute-done((bf16[64,2560]{1,0:T(8,128)(2,1)S(1)}, bf16[64,2560]{1,0:T(8,128)(2,1)S(1)}, u32[]{:S(2)}, u32[]{:S(2)}) %collective-permute-start.19) | collective-permute-done | bytes 327712 | tf_op jit(solution)/shard_map/ppermute | solution.py:42
  150.7 2.5 collective-permute-done.23.refs_5_.refs_6_
  157.8 7.8 %collective-permute-done.26.refs_11_.refs_1_.refs_10_ = bf16[64,2048]{1,0:T(8,128)(2,1)S(1)} collective-permute-done((bf16[64,2048]{1,0:T(8,128)(2,1)S(1)}, bf16[64,2048]{1,0:T(8,128)(2,1)S(1)}, u32[]{:S(2)}, u32[]{:S(2)}) %collective-permute-start.26) | collective-permute-done | bytes 262176 | tf_op jit(solution)/shard_map/ppermute | solution.py:42
  165.6 5.2 %collective-permute-done.28.refs_12_.refs_5_.refs_14_ = bf16[64,2048]{1,0:T(8,128)(2,1)} collective-permute-done((bf16[64,2048]{1,0:T(8,128)(2,1)}, bf16[64,2048]{1,0:T(8,128)(2,1)}, u32[]{:S(2)}, u32[]{:S(2)}) %collective-permute-start.28) | collective-permute-done | bytes 262176 | tf_op jit(solution)/shard_map/ppermute | solution.py:42
  175.6 7.4 %backward_matmul.9.refs_9_ = f32[512,2048]{1,0:T(8,128)S(1)} custom-call(bf16[64,2048]{1,0:T(8,128)(2,1)S(1)} %get-tuple-element.91.refs_2_.refs_0_.refs_1_, bf16[64,2048]{1,0:T(8,128)(2,1)S(1)} %copy-done.43, bf16[64,2048]{1,0:T(8,128)(2,1)S(1)} %collective-permute-done.21.refs_2_.refs_3_, bf16[64,2048]{1,0:T(8,128)(2,1)S(1)} %copy-done.62, ...), custom_call_target="tpu_custom_call" | custom-call | flops 42949672 | bytes 146800 | tf_op jit(solution)/shard_map/backward_matmul/pallas_call | solution.py:298
  186.4 8.9 %backward_matmul.10.refs_7_.refs_9_ = f32[512,2048]{1,0:T(8,128)S(1)} custom-call(bf16[64,2048]{1,0:T(8,128)(2,1)S(1)} %get-tuple-element.91.refs_2_.refs_0_.refs_1_, bf16[64,2048]{1,0:T(8,128)(2,1)S(1)} %copy-done.44, bf16[64,2048]{1,0:T(8,128)(2,1)S(1)} %copy-done.56, bf16[64,2048]{1,0:T(8,128)(2,1)S(1)} %copy-done.63, bf16[64,2048]{1,0:T(8,128)(2,1)S(1)} %copy-done.40, ...), custom_call_target="tpu_custom_call" | custom-call | flops 42949672 | bytes 146800 | tf_op jit(solution)/shard_map/backward_matmul/pallas_call | solution.py:298
  195.4 4.5 %gated_gradients.5 = (bf16[64,2560]{1,0:T(8,128)(2,1)S(1)}, bf16[64,2560]{1,0:T(8,128)(2,1)S(1)}, f32[64,33]{1,0:T(8,128)S(1)}) custom-call(s32[1]{0:T(128)} %bitcast.5.d_ref, f32[256,2560]{1,0:T(8,128)S(1)} %copy-done.14, bf16[256,2560]{1,0:T(8,128)(2,1)S(1)} %copy-done.24, bf16[64,2560]{1,0:T(8,128)(2,1)} %collective-permute-done.18.refs_2_, ...), custom_call_target="tpu_custom_call" | custom-call | flops 209715 | bytes 26214 | tf_op jit(solution)/shard_map/gated_gradients/pallas_call | solution.py:246
  203.2 1.9 collective-permute-done.45
  205.1 4.1 collective-permute-done.32.refs_4_.refs_10_.refs_21_
  210.4 3.3 collective-permute-start.46
  213.9 1.7 collective-permute-done.46
  217.3 1.9 collective-permute-done.33.refs_10_.refs_5_.refs_22_
  219.2 2.2 copy-done.7
  221.4 7.9 %backward_matmul.11.refs_9_ = f32[512,2048]{1,0:T(8,128)S(1)} custom-call(bf16[64,2048]{1,0:T(8,128)(2,1)S(1)} %get-tuple-element.95.refs_4_.refs_0_.refs_9_, bf16[64,2048]{1,0:T(8,128)(2,1)S(1)} %copy-done.35, bf16[64,2048]{1,0:T(8,128)(2,1)S(1)} %collective-permute-done.36.refs_2_.refs_11_, bf16[64,2048]{1,0:T(8,128)(2,1)} %collective-permute-done.37.refs_3_.refs_12_, ...), custom_call_target="tpu_custom_call" | custom-call | flops 42949672 | bytes 188743 | tf_op jit(solution)/shard_map/backward_matmul/pallas_call | solution.py:298
  229.3 2.0 copy-done.3
  235.6 7.7 %backward_matmul.14.refs_9_ = f32[512,2048]{1,0:T(8,128)S(1)} custom-call(bf16[64,2048]{1,0:T(8,128)(2,1)S(1)} %copy-done.32, bf16[64,2048]{1,0:T(8,128)(2,1)S(1)} %copy-done.36, bf16[64,2048]{1,0:T(8,128)(2,1)S(1)} %copy-done.70, bf16[64,2048]{1,0:T(8,128)(2,1)} %collective-permute-done.37.refs_3_.refs_12_, ...), custom_call_target="tpu_custom_call" | custom-call | flops 42949672 | bytes 188743 | tf_op jit(solution)/shard_map/backward_matmul/pallas_call | solution.py:298
  243.3 2.1 copy-done.10
  247.0 3.2 collective-permute-done.48
  251.0 2.2 copy-done.11
  253.2 5.0 %backward_matmul.15 = (f32[256,1024]{1,0:T(8,128)S(1)}, bf16[256,1024]{1,0:T(8,128)(2,1)S(1)}) custom-call(bf16[64,2560]{1,0:T(8,128)(2,1)S(1)} %get-tuple-element.101.refs_0_.refs_17_, bf16[64,2560]{1,0:T(8,128)(2,1)S(1)} %collective-permute-done.29.refs_1_.refs_11_.refs_18_, bf16[64,2560]{1,0:T(8,128)(2,1)S(1)} %collective-permute-done.30.refs_2_.refs_19_, ...), custom_call_target="tpu_custom_call" | custom-call | flops 26843544 | bytes 120586 | tf_op jit(solution)/shard_map/backward_matmul/pallas_call | solution.py:298
  258.2 1.6 collective-permute-start.42
  260.1 5.8 %backward_matmul.17 = (f32[256,1024]{1,0:T(8,128)S(1)}, bf16[256,1024]{1,0:T(8,128)(2,1)}) custom-call(bf16[64,2560]{1,0:T(8,128)(2,1)S(1)} %get-tuple-element.101.refs_0_.refs_17_, bf16[64,2560]{1,0:T(8,128)(2,1)S(1)} %collective-permute-done.29.refs_1_.refs_11_.refs_18_, bf16[64,2560]{1,0:T(8,128)(2,1)S(1)} %collective-permute-done.30.refs_2_.refs_19_, ...), custom_call_target="tpu_custom_call" | custom-call | flops 26843544 | bytes 120586 | tf_op jit(solution)/shard_map/backward_matmul/pallas_call | solution.py:298
  266.5 5.0 %backward_matmul.13 = (f32[256,1024]{1,0:T(8,128)S(1)}, bf16[256,1024]{1,0:T(8,128)(2,1)S(1)}) custom-call(bf16[64,2560]{1,0:T(8,128)(2,1)S(1)} %get-tuple-element.101.refs_0_.refs_17_, bf16[64,2560]{1,0:T(8,128)(2,1)S(1)} %collective-permute-done.29.refs_1_.refs_11_.refs_18_, bf16[64,2560]{1,0:T(8,128)(2,1)S(1)} %collective-permute-done.30.refs_2_.refs_19_, ...), custom_call_target="tpu_custom_call" | custom-call | flops 26843544 | bytes 120586 | tf_op jit(solution)/shard_map/backward_matmul/pallas_call | solution.py:298
  274.0 4.9 %collective-permute-start.43 = (bf16[256,1024]{1,0:T(8,128)(2,1)}, bf16[256,1024]{1,0:T(8,128)(2,1)}, u32[]{:S(2)}, u32[]{:S(2)}) collective-permute-start(bf16[256,1024]{1,0:T(8,128)(2,1)} %fusion.3), channel_id=1, source_target_pairs={{0,4},{12,8},{1,5},{13,9},{2,6},{14,10},{3,7},{15,11},{16,20},{28,... | collective-permute-start | bytes 1572872 | tf_op jit(solution)/shard_map/ppermute | solution.py:601
  282.4 2.2 copy-done.5
  284.6 3.4 backward_matmul.12
  288.1 1.7 collective-permute-start.40
  290.3 3.6 backward_matmul.16
  295.5 2.5 adapter_up.1
  302.9 7.3 %collective-permute-done.63 = bf16[256,1024]{1,0:T(8,128)(2,1)S(1)} collective-permute-done((bf16[256,1024]{1,0:T(8,128)(2,1)S(1)}, bf16[256,1024]{1,0:T(8,128)(2,1)S(1)}, u32[]{:S(2)}, u32[]{:S(2)}) %collective-permute-start.63) | collective-permute-done | bytes 524320 | tf_op jit(solution)/shard_map/ppermute | solution.py:601
  317.3 10.3 %collective-permute-done.51.refs_1_ = bf16[128,1024]{1,0:T(8,128)(2,1)S(1)} collective-permute-done((bf16[128,1024]{1,0:T(8,128)(2,1)S(1)}, bf16[128,1024]{1,0:T(8,128)(2,1)S(1)}, u32[]{:S(2)}, u32[]{:S(2)}) %collective-permute-start.51) | collective-permute-done | bytes 262176 | tf_op jit(solution)/shard_map/ppermute | solution.py:601
  327.7 5.2 %collective-permute-start.52 = (bf16[256,1024]{1,0:T(8,128)(2,1)S(1)}, bf16[256,1024]{1,0:T(8,128)(2,1)S(1)}, u32[]{:S(2)}, u32[]{:S(2)}) collective-permute-start(bf16[256,1024]{1,0:T(8,128)(2,1)S(1)} %fusion.4), channel_id=1, source_target_pairs={{0,4},{12,8},{1,5},{13,9},{2,6},{14,10},{3,7},{15,11},{16,20},{28,... | collective-permute-start | bytes 1572872 | tf_op jit(solution)/shard_map/ppermute | solution.py:601
  333.0 2.1 collective-permute-done.66.refs_1_
  336.7 5.5 %collective-permute-done.52 = bf16[256,1024]{1,0:T(8,128)(2,1)S(1)} collective-permute-done((bf16[256,1024]{1,0:T(8,128)(2,1)S(1)}, bf16[256,1024]{1,0:T(8,128)(2,1)S(1)}, u32[]{:S(2)}, u32[]{:S(2)}) %collective-permute-start.52) | collective-permute-done | bytes 524320 | tf_op jit(solution)/shard_map/ppermute | solution.py:601
  343.1 1.9 collective-permute-done.67
  348.5 15.0 %collective-permute-done.55.refs_1_ = bf16[128,1024]{1,0:T(8,128)(2,1)S(1)} collective-permute-done((bf16[128,1024]{1,0:T(8,128)(2,1)S(1)}, bf16[128,1024]{1,0:T(8,128)(2,1)S(1)}, u32[]{:S(2)}, u32[]{:S(2)}) %collective-permute-start.55) | collective-permute-done | bytes 262176 | tf_op jit(solution)/shard_map/ppermute | solution.py:601
  363.5 4.8 %collective-permute-start.56 = (bf16[256,512]{1,0:T(8,128)(2,1)S(1)}, bf16[256,512]{1,0:T(8,128)(2,1)S(1)}, u32[]{:S(2)}, u32[]{:S(2)}) collective-permute-start(bf16[256,512]{1,0:T(8,128)(2,1)S(1)} %fusion.6), channel_id=1, source_target_pairs={{0,4},{12,8},{1,5},{13,9},{2,6},{14,10},{3,7},{15,11},{16,20},{28,... | collective-permute-start | bytes 786440 | tf_op jit(solution)/shard_map/ppermute | solution.py:601
  368.3 4.2 %collective-permute-done.56 = bf16[256,512]{1,0:T(8,128)(2,1)S(1)} collective-permute-done((bf16[256,512]{1,0:T(8,128)(2,1)S(1)}, bf16[256,512]{1,0:T(8,128)(2,1)S(1)}, u32[]{:S(2)}, u32[]{:S(2)}) %collective-permute-start.56) | collective-permute-done | bytes 262176 | tf_op jit(solution)/shard_map/ppermute | solution.py:601
  373.8 8.8 %collective-permute-start.75 = (f32[1,4096]{1,0:T(1,128)S(1)}, f32[1,4096]{1,0:T(1,128)S(1)}, u32[]{:S(2)}, u32[]{:S(2)}) collective-permute-start(f32[1,4096]{1,0:T(1,128)S(1)} %constant_dynamic-update-slice_fusion), channel_id=1, source_target_pairs={{0,4},{4,0},{8,12},{12,8},{1,5},{5,1},{9,13},{13,9},{2,6},{6,2},{1... | collective-permute-start | bytes 49160 | tf_op jit(solution)/shard_map/ppermute | solution.py:42
  384.5 3.0 collective-permute-start.76
  387.5 1.6 convolution_multiply_fusion
  394.5 2.9 collective-permute-done.74.refs_3_
  (413 shorter events, 110.3 us)
Async XLA Ops:
  1.8 10.2 %collective-permute-start.1 = (bf16[64,2048]{1,0:T(8,128)(2,1)S(1)}, bf16[64,2048]{1,0:T(8,128)(2,1)}, u32[]{:S(2)}, u32[]{:S(2)}) collective-permute-start(bf16[64,2048]{1,0:T(8,128)(2,1)S(1)} %constant_dynamic-slice_fusion.4), channel_id=1, source_target_pairs={{0,16},{16,0},{1,17},{17,1},{2,18},{18,2},{3,19},{19,3},{4,20},{20... | collective-permute-start | bytes 786440 | tf_op jit(solution)/shard_map/ppermute | solution.py:42
  7.1 35.3 %collective-permute-start = (bf16[256,2048]{1,0:T(8,128)(2,1)}, bf16[256,2048]{1,0:T(8,128)(2,1)S(1)}, u32[]{:S(2)}, u32[]{:S(2)}) collective-permute-start(bf16[256,2048]{1,0:T(8,128)(2,1)} %slice.96), channel_id=1, source_target_pairs={{0,16},{16,0},{1,17},{17,1},{2,18},{18,2},{3,19},{19,3},{4,20},{20... | collective-permute-start | bytes 3145736 | tf_op jit(solution)/shard_map/ppermute | solution.py:42
  12.0 13.5 %collective-permute-start.2 = (bf16[64,2048]{1,0:T(8,128)(2,1)}, bf16[64,2048]{1,0:T(8,128)(2,1)}, u32[]{:S(2)}, u32[]{:S(2)}) collective-permute-start(bf16[64,2048]{1,0:T(8,128)(2,1)} %collective-permute-done.1), channel_id=1, source_target_pairs={{0,8},{4,12},{8,0},{12,4},{1,9},{5,13},{9,1},{13,5},{2,10},{6,14},... | collective-permute-start | bytes 786440 | tf_op jit(solution)/shard_map/ppermute | solution.py:42
  27.4 13.7 %collective-permute-start.3 = (bf16[128,2048]{1,0:T(8,128)(2,1)}, bf16[128,2048]{1,0:T(8,128)(2,1)}, u32[]{:S(2)}, u32[]{:S(2)}) collective-permute-start(bf16[128,2048]{1,0:T(8,128)(2,1)} %pad_maximum_fusion.2), channel_id=1, source_target_pairs={{0,4},{4,0},{8,12},{12,8},{1,5},{5,1},{9,13},{13,9},{2,6},{6,2},{1... | collective-permute-start | bytes 1572872 | tf_op jit(solution)/shard_map/ppermute | solution.py:42
  45.8 8.4 %collective-permute-start.5 = (f32[2,128,32]{2,1,0:T(8,128)S(1)}, f32[2,128,32]{2,1,0:T(8,128)S(1)}, u32[]{:S(2)}, u32[]{:S(2)}) collective-permute-start(f32[2,128,32]{2,1,0:T(8,128)S(1)} %pad_maximum_fusion.3), channel_id=1, source_target_pairs={{0,1},{1,0},{2,3},{3,2},{4,5},{5,4},{6,7},{7,6},{8,9},{9,8},{10,11... | collective-permute-start | bytes 98312 | tf_op jit(solution)/shard_map/ppermute | solution.py:42
  64.3 22.5 %collective-permute-start.8 = (bf16[64,2048]{1,0:T(8,128)(2,1)S(1)}, bf16[64,2048]{1,0:T(8,128)(2,1)S(1)}, u32[]{:S(2)}, u32[]{:S(2)}) collective-permute-start(bf16[64,2048]{1,0:T(8,128)(2,1)S(1)} %get-tuple-element.83.refs_0_), channel_id=1, source_target_pairs={{0,2},{1,3},{2,0},{3,1},{4,6},{5,7},{6,4},{7,5},{8,10},{9,11},{10,... | collective-permute-start | bytes 786440 | tf_op jit(solution)/shard_map/ppermute | solution.py:42
  65.3 21.5 %collective-permute-start.9 = (bf16[64,2048]{1,0:T(8,128)(2,1)S(1)}, bf16[64,2048]{1,0:T(8,128)(2,1)S(1)}, u32[]{:S(2)}, u32[]{:S(2)}) collective-permute-start(bf16[64,2048]{1,0:T(8,128)(2,1)S(1)} %get-tuple-element.84.refs_1_), channel_id=1, source_target_pairs={{0,2},{1,3},{2,0},{3,1},{4,6},{5,7},{6,4},{7,5},{8,10},{9,11},{10,... | collective-permute-start | bytes 786440 | tf_op jit(solution)/shard_map/ppermute | solution.py:42
  66.4 13.3 %collective-permute-start.7 = (f32[2,64,32]{2,1,0:T(8,128)S(1)}, f32[2,64,32]{2,1,0:T(8,128)S(1)}, u32[]{:S(2)}, u32[]{:S(2)}) collective-permute-start(f32[2,64,32]{2,1,0:T(8,128)S(1)} %slice.127), channel_id=1, source_target_pairs={{0,2},{1,3},{2,0},{3,1},{4,6},{5,7},{6,4},{7,5},{8,10},{9,11},{10,... | collective-permute-start | bytes 49160 | tf_op jit(solution)/shard_map/ppermute | solution.py:42
  94.7 9.0 %collective-permute-start.11 = (bf16[64,2048]{1,0:T(8,128)(2,1)}, bf16[64,2048]{1,0:T(8,128)(2,1)}, u32[]{:S(2)}, u32[]{:S(2)}) collective-permute-start(bf16[64,2048]{1,0:T(8,128)(2,1)} %add_convert_fusion.2), channel_id=1, source_target_pairs={{0,16},{16,0},{1,17},{17,1},{2,18},{18,2},{3,19},{19,3},{4,20},{20... | collective-permute-start | bytes 786440 | tf_op jit(solution)/shard_map/ppermute | solution.py:42
  98.3 14.6 %collective-permute-start.13 = (bf16[64,2048]{1,0:T(8,128)(2,1)}, bf16[64,2048]{1,0:T(8,128)(2,1)}, u32[]{:S(2)}, u32[]{:S(2)}) collective-permute-start(bf16[64,2048]{1,0:T(8,128)(2,1)} %get-tuple-element.90.refs_1_), channel_id=1, source_target_pairs={{0,2},{1,3},{2,0},{3,1},{4,6},{5,7},{6,4},{7,5},{8,10},{9,11},{10,... | collective-permute-start | bytes 786440 | tf_op jit(solution)/shard_map/ppermute | solution.py:42
  109.5 15.0 %collective-permute-start.15 = (bf16[64,2048]{1,0:T(8,128)(2,1)S(1)}, bf16[64,2048]{1,0:T(8,128)(2,1)S(1)}, u32[]{:S(2)}, u32[]{:S(2)}) collective-permute-start(bf16[64,2048]{1,0:T(8,128)(2,1)S(1)} %get-tuple-element.94), channel_id=1, source_target_pairs={{0,16},{16,0},{1,17},{17,1},{2,18},{18,2},{3,19},{19,3},{4,20},{20... | collective-permute-start | bytes 786440 | tf_op jit(solution)/shard_map/ppermute | solution.py:42
  110.9 13.7 %collective-permute-start.16 = (bf16[64,2048]{1,0:T(8,128)(2,1)S(1)}, bf16[64,2048]{1,0:T(8,128)(2,1)S(1)}, u32[]{:S(2)}, u32[]{:S(2)}) collective-permute-start(bf16[64,2048]{1,0:T(8,128)(2,1)S(1)} %get-tuple-element.91.refs_2_.refs_0_.refs_1_), channel_id=1, source_target_pairs={{0,2},{1,3},{2,0},{3,1},{4,6},{5,7},{6,4},{7,5},{8,10},{9,11},{10,... | collective-permute-start | bytes 786440 | tf_op jit(solution)/shard_map/ppermute | solution.py:42
  111.9 12.7 %collective-permute-start.12 = (bf16[64,2048]{1,0:T(8,128)(2,1)S(1)}, bf16[64,2048]{1,0:T(8,128)(2,1)S(1)}, u32[]{:S(2)}, u32[]{:S(2)}) collective-permute-start(bf16[64,2048]{1,0:T(8,128)(2,1)S(1)} %copy-done.82), channel_id=1, source_target_pairs={{0,2},{1,3},{2,0},{3,1},{4,6},{5,7},{6,4},{7,5},{8,10},{9,11},{10,... | collective-permute-start | bytes 786440 | tf_op jit(solution)/shard_map/ppermute | solution.py:42
  114.2 10.4 %collective-permute-start.14 = (bf16[64,2048]{1,0:T(8,128)(2,1)S(1)}, bf16[64,2048]{1,0:T(8,128)(2,1)S(1)}, u32[]{:S(2)}, u32[]{:S(2)}) collective-permute-start(bf16[64,2048]{1,0:T(8,128)(2,1)S(1)} %add_convert_fusion.1), channel_id=1, source_target_pairs={{0,16},{16,0},{1,17},{17,1},{2,18},{18,2},{3,19},{19,3},{4,20},{20... | collective-permute-start | bytes 786440 | tf_op jit(solution)/shard_map/ppermute | solution.py:42
  137.0 10.6 %collective-permute-start.19 = (bf16[64,2560]{1,0:T(8,128)(2,1)S(1)}, bf16[64,2560]{1,0:T(8,128)(2,1)S(1)}, u32[]{:S(2)}, u32[]{:S(2)}) collective-permute-start(bf16[64,2560]{1,0:T(8,128)(2,1)S(1)} %get-tuple-element.99.refs_10_), channel_id=1, source_target_pairs={{0,2},{1,3},{2,0},{3,1},{4,6},{5,7},{6,4},{7,5},{8,10},{9,11},{10,... | collective-permute-start | bytes 983048 | tf_op jit(solution)/shard_map/ppermute | solution.py:42
  138.1 11.5 %collective-permute-start.21 = (bf16[64,2048]{1,0:T(8,128)(2,1)S(1)}, bf16[64,2048]{1,0:T(8,128)(2,1)S(1)}, u32[]{:S(2)}, u32[]{:S(2)}) collective-permute-start(bf16[64,2048]{1,0:T(8,128)(2,1)S(1)} %get-tuple-element.91.refs_2_.refs_0_.refs_1_), channel_id=1, source_target_pairs={{0,1},{1,0},{2,3},{3,2},{4,5},{5,4},{6,7},{7,6},{8,9},{9,8},{10,11... | collective-permute-start | bytes 786440 | tf_op jit(solution)/shard_map/ppermute | solution.py:42
  138.1 15.1 %collective-permute-start.23 = (bf16[64,2048]{1,0:T(8,128)(2,1)S(1)}, bf16[64,2048]{1,0:T(8,128)(2,1)S(1)}, u32[]{:S(2)}, u32[]{:S(2)}) collective-permute-start(bf16[64,2048]{1,0:T(8,128)(2,1)S(1)} %collective-permute-done.15.refs_7_.refs_4_.refs_5_), channel_id=1, source_target_pairs={{0,2},{1,3},{2,0},{3,1},{4,6},{5,7},{6,4},{7,5},{8,10},{9,11},{10,... | collective-permute-start | bytes 786440 | tf_op jit(solution)/shard_map/ppermute | solution.py:42
  139.1 15.3 %collective-permute-start.22 = (bf16[64,2048]{1,0:T(8,128)(2,1)S(1)}, bf16[64,2048]{1,0:T(8,128)(2,1)S(1)}, u32[]{:S(2)}, u32[]{:S(2)}) collective-permute-start(bf16[64,2048]{1,0:T(8,128)(2,1)S(1)} %collective-permute-done.16.refs_8_.refs_1_.refs_2_), channel_id=1, source_target_pairs={{0,1},{1,0},{2,3},{3,2},{4,5},{5,4},{6,7},{7,6},{8,9},{9,8},{10,11... | collective-permute-start | bytes 786440 | tf_op jit(solution)/shard_map/ppermute | solution.py:42
  139.3 15.7 %collective-permute-start.24 = (bf16[64,2048]{1,0:T(8,128)(2,1)S(1)}, bf16[64,2048]{1,0:T(8,128)(2,1)S(1)}, u32[]{:S(2)}, u32[]{:S(2)}) collective-permute-start(bf16[64,2048]{1,0:T(8,128)(2,1)S(1)} %collective-permute-done.15.refs_7_.refs_4_.refs_5_), channel_id=1, source_target_pairs={{0,1},{1,0},{2,3},{3,2},{4,5},{5,4},{6,7},{7,6},{8,9},{9,8},{10,11... | collective-permute-start | bytes 786440 | tf_op jit(solution)/shard_map/ppermute | solution.py:42
  147.6 9.2 %collective-permute-start.27 = (bf16[64,2048]{1,0:T(8,128)(2,1)S(1)}, bf16[64,2048]{1,0:T(8,128)(2,1)}, u32[]{:S(2)}, u32[]{:S(2)}) collective-permute-start(bf16[64,2048]{1,0:T(8,128)(2,1)S(1)} %get-tuple-element.100), channel_id=1, source_target_pairs={{0,16},{16,0},{1,17},{17,1},{2,18},{18,2},{3,19},{19,3},{4,20},{20... | collective-permute-start | bytes 786440 | tf_op jit(solution)/shard_map/ppermute | solution.py:42
  149.6 45.8 %collective-permute-start.18 = (bf16[64,2560]{1,0:T(8,128)(2,1)}, bf16[64,2560]{1,0:T(8,128)(2,1)}, u32[]{:S(2)}, u32[]{:S(2)}) collective-permute-start(bf16[64,2560]{1,0:T(8,128)(2,1)} %get-tuple-element.98.refs_9_), channel_id=1, source_target_pairs={{0,2},{1,3},{2,0},{3,1},{4,6},{5,7},{6,4},{7,5},{8,10},{9,11},{10,... | collective-permute-start | bytes 983048 | tf_op jit(solution)/shard_map/ppermute | solution.py:42
  153.2 42.1 %collective-permute-start.20 = (bf16[64,2560]{1,0:T(8,128)(2,1)}, bf16[64,2560]{1,0:T(8,128)(2,1)}, u32[]{:S(2)}, u32[]{:S(2)}) collective-permute-start(bf16[64,2560]{1,0:T(8,128)(2,1)} %add_convert_fusion), channel_id=1, source_target_pairs={{0,16},{16,0},{1,17},{17,1},{2,18},{18,2},{3,19},{19,3},{4,20},{20... | collective-permute-start | bytes 983048 | tf_op jit(solution)/shard_map/ppermute | solution.py:42
  155.7 9.8 %collective-permute-start.26 = (bf16[64,2048]{1,0:T(8,128)(2,1)S(1)}, bf16[64,2048]{1,0:T(8,128)(2,1)S(1)}, u32[]{:S(2)}, u32[]{:S(2)}) collective-permute-start(bf16[64,2048]{1,0:T(8,128)(2,1)S(1)} %get-tuple-element.95.refs_4_.refs_0_.refs_9_), channel_id=1, source_target_pairs={{0,2},{1,3},{2,0},{3,1},{4,6},{5,7},{6,4},{7,5},{8,10},{9,11},{10,... | collective-permute-start | bytes 786440 | tf_op jit(solution)/shard_map/ppermute | solution.py:42
  156.8 14.0 %collective-permute-start.28 = (bf16[64,2048]{1,0:T(8,128)(2,1)}, bf16[64,2048]{1,0:T(8,128)(2,1)}, u32[]{:S(2)}, u32[]{:S(2)}) collective-permute-start(bf16[64,2048]{1,0:T(8,128)(2,1)} %collective-permute-done.27.refs_4_.refs_13_), channel_id=1, source_target_pairs={{0,2},{1,3},{2,0},{3,1},{4,6},{5,7},{6,4},{7,5},{8,10},{9,11},{10,... | collective-permute-start | bytes 786440 | tf_op jit(solution)/shard_map/ppermute | solution.py:42
  199.9 9.3 %collective-permute-start.32 = (bf16[64,2560]{1,0:T(8,128)(2,1)S(1)}, bf16[64,2560]{1,0:T(8,128)(2,1)S(1)}, u32[]{:S(2)}, u32[]{:S(2)}) collective-permute-start(bf16[64,2560]{1,0:T(8,128)(2,1)S(1)} %get-tuple-element.102), channel_id=1, source_target_pairs={{0,16},{16,0},{1,17},{17,1},{2,18},{18,2},{3,19},{19,3},{4,20},{20... | collective-permute-start | bytes 983048 | tf_op jit(solution)/shard_map/ppermute | solution.py:42
  202.6 14.7 %collective-permute-start.37 = (bf16[64,2048]{1,0:T(8,128)(2,1)S(1)}, bf16[64,2048]{1,0:T(8,128)(2,1)}, u32[]{:S(2)}, u32[]{:S(2)}) collective-permute-start(bf16[64,2048]{1,0:T(8,128)(2,1)S(1)} %copy-done.35), channel_id=1, source_target_pairs={{0,1},{1,0},{2,3},{3,2},{4,5},{5,4},{6,7},{7,6},{8,9},{9,8},{10,11... | collective-permute-start | bytes 786440 | tf_op jit(solution)/shard_map/ppermute | solution.py:42
  203.1 14.2 %collective-permute-start.38 = (bf16[64,2048]{1,0:T(8,128)(2,1)}, bf16[64,2048]{1,0:T(8,128)(2,1)}, u32[]{:S(2)}, u32[]{:S(2)}) collective-permute-start(bf16[64,2048]{1,0:T(8,128)(2,1)} %collective-permute-done.27.refs_4_.refs_13_), channel_id=1, source_target_pairs={{0,1},{1,0},{2,3},{3,2},{4,5},{5,4},{6,7},{7,6},{8,9},{9,8},{10,11... | collective-permute-start | bytes 786440 | tf_op jit(solution)/shard_map/ppermute | solution.py:42
  205.1 12.2 %collective-permute-start.39 = (bf16[64,2048]{1,0:T(8,128)(2,1)}, bf16[64,2048]{1,0:T(8,128)(2,1)}, u32[]{:S(2)}, u32[]{:S(2)}) collective-permute-start(bf16[64,2048]{1,0:T(8,128)(2,1)} %collective-permute-done.28.refs_12_.refs_5_.refs_14_), channel_id=1, source_target_pairs={{0,1},{1,0},{2,3},{3,2},{4,5},{5,4},{6,7},{7,6},{8,9},{9,8},{10,11... | collective-permute-start | bytes 786440 | tf_op jit(solution)/shard_map/ppermute | solution.py:42
  209.2 10.0 %collective-permute-start.33 = (bf16[64,2560]{1,0:T(8,128)(2,1)S(1)}, bf16[64,2560]{1,0:T(8,128)(2,1)S(1)}, u32[]{:S(2)}, u32[]{:S(2)}) collective-permute-start(bf16[64,2560]{1,0:T(8,128)(2,1)S(1)} %collective-permute-done.32.refs_4_.refs_10_.refs_21_), channel_id=1, source_target_pairs={{0,2},{1,3},{2,0},{3,1},{4,6},{5,7},{6,4},{7,5},{8,10},{9,11},{10,... | collective-permute-start | bytes 983048 | tf_op jit(solution)/shard_map/ppermute | solution.py:42
  215.6 17.0 %collective-permute-start.29 = (bf16[64,2560]{1,0:T(8,128)(2,1)S(1)}, bf16[64,2560]{1,0:T(8,128)(2,1)S(1)}, u32[]{:S(2)}, u32[]{:S(2)}) collective-permute-start(bf16[64,2560]{1,0:T(8,128)(2,1)S(1)} %get-tuple-element.101.refs_0_.refs_17_), channel_id=1, source_target_pairs={{0,2},{1,3},{2,0},{3,1},{4,6},{5,7},{6,4},{7,5},{8,10},{9,11},{10,... | collective-permute-start | bytes 983048 | tf_op jit(solution)/shard_map/ppermute | solution.py:42
  231.4 14.4 %collective-permute-start.47 = (f32[64,33]{1,0:T(8,128)S(1)}, f32[64,33]{1,0:T(8,128)S(1)}, u32[]{:S(2)}, u32[]{:S(2)}) collective-permute-start(f32[64,33]{1,0:T(8,128)S(1)} %add.211), channel_id=1, source_target_pairs={{0,16},{16,0},{1,17},{17,1},{2,18},{18,2},{3,19},{19,3},{4,20},{20... | collective-permute-start | bytes 25352 | tf_op jit(solution)/shard_map/ppermute | solution.py:42
  232.0 18.4 %collective-permute-start.30 = (bf16[64,2560]{1,0:T(8,128)(2,1)S(1)}, bf16[64,2560]{1,0:T(8,128)(2,1)S(1)}, u32[]{:S(2)}, u32[]{:S(2)}) collective-permute-start(bf16[64,2560]{1,0:T(8,128)(2,1)S(1)} %get-tuple-element.101.refs_0_.refs_17_), channel_id=1, source_target_pairs={{0,1},{1,0},{2,3},{3,2},{4,5},{5,4},{6,7},{7,6},{8,9},{9,8},{10,11... | collective-permute-start | bytes 983048 | tf_op jit(solution)/shard_map/ppermute | solution.py:42
  232.1 18.9 %collective-permute-start.34 = (bf16[64,2560]{1,0:T(8,128)(2,1)S(1)}, bf16[64,2560]{1,0:T(8,128)(2,1)S(1)}, u32[]{:S(2)}, u32[]{:S(2)}) collective-permute-start(bf16[64,2560]{1,0:T(8,128)(2,1)S(1)} %collective-permute-done.32.refs_4_.refs_10_.refs_21_), channel_id=1, source_target_pairs={{0,1},{1,0},{2,3},{3,2},{4,5},{5,4},{6,7},{7,6},{8,9},{9,8},{10,11... | collective-permute-start | bytes 983048 | tf_op jit(solution)/shard_map/ppermute | solution.py:42
  232.6 18.4 %collective-permute-start.31 = (bf16[64,2560]{1,0:T(8,128)(2,1)S(1)}, bf16[64,2560]{1,0:T(8,128)(2,1)S(1)}, u32[]{:S(2)}, u32[]{:S(2)}) collective-permute-start(bf16[64,2560]{1,0:T(8,128)(2,1)S(1)} %collective-permute-done.29.refs_1_.refs_11_.refs_18_), channel_id=1, source_target_pairs={{0,1},{1,0},{2,3},{3,2},{4,5},{5,4},{6,7},{7,6},{8,9},{9,8},{10,11... | collective-permute-start | bytes 983048 | tf_op jit(solution)/shard_map/ppermute | solution.py:42
  232.6 12.9 %collective-permute-start.78 = (bf16[2,64,16]{2,1,0:T(8,128)(2,1)S(1)}, bf16[2,64,16]{2,1,0:T(8,128)(2,1)S(1)}, u32[]{:S(2)}, u32[]{:S(2)}) collective-permute-start(bf16[2,64,16]{2,1,0:T(8,128)(2,1)S(1)} %slice_select_fusion.5), channel_id=1, source_target_pairs={{0,2},{1,3},{2,0},{3,1},{4,6},{5,7},{6,4},{7,5},{8,10},{9,11},{10,... | collective-permute-start | bytes 12296 | tf_op jit(solution)/shard_map/ppermute | solution.py:42
  250.2 9.6 %collective-permute-start.79 = (bf16[2,128,16]{1,2,0:T(8,128)(2,1)S(1)}, bf16[2,128,16]{1,2,0:T(8,128)(2,1)S(1)}, u32[]{:S(2)}, u32[]{:S(2)}) collective-permute-start(bf16[2,128,16]{1,2,0:T(8,128)(2,1)S(1)} %pad_maximum_fusion.7), channel_id=1, source_target_pairs={{0,1},{1,0},{2,3},{3,2},{4,5},{5,4},{6,7},{7,6},{8,9},{9,8},{10,11... | collective-permute-start | bytes 24584 | tf_op jit(solution)/shard_map/ppermute | solution.py:42
  250.4 9.5 %collective-permute-start.49 = (f32[2,128,33]{1,0,2:T(2,128)S(1)}, f32[2,128,33]{1,0,2:T(2,128)S(1)}, u32[]{:S(2)}, u32[]{:S(2)}) collective-permute-start(f32[2,128,33]{1,0,2:T(2,128)S(1)} %pad_maximum_fusion.6), channel_id=1, source_target_pairs={{0,1},{1,0},{2,3},{3,2},{4,5},{5,4},{6,7},{7,6},{8,9},{9,8},{10,11... | collective-permute-start | bytes 101384 | tf_op jit(solution)/shard_map/ppermute | solution.py:42
  258.2 14.9 %collective-permute-start.42 = (bf16[256,1024]{1,0:T(8,128)(2,1)S(1)}, bf16[256,1024]{1,0:T(8,128)(2,1)S(1)}, u32[]{:S(2)}, u32[]{:S(2)}) collective-permute-start(bf16[256,1024]{1,0:T(8,128)(2,1)S(1)} %get-tuple-element.110), channel_id=1, source_target_pairs={{0,16},{16,0},{1,17},{17,1},{2,18},{18,2},{3,19},{19,3},{4,20},{20... | collective-permute-start | bytes 1572872 | tf_op jit(solution)/shard_map/ppermute | solution.py:42
  266.0 32.1 %collective-permute-start.62 = (bf16[256,1024]{1,0:T(8,128)(2,1)}, bf16[256,1024]{1,0:T(8,128)(2,1)}, u32[]{:S(2)}, u32[]{:S(2)}) collective-permute-start(bf16[256,1024]{1,0:T(8,128)(2,1)} %get-tuple-element.125), channel_id=1, source_target_pairs={{0,16},{16,0},{1,17},{17,1},{2,18},{18,2},{3,19},{19,3},{4,20},{20... | collective-permute-start | bytes 1572872 | tf_op jit(solution)/shard_map/ppermute | solution.py:42
  274.0 26.7 %collective-permute-start.43 = (bf16[256,1024]{1,0:T(8,128)(2,1)}, bf16[256,1024]{1,0:T(8,128)(2,1)}, u32[]{:S(2)}, u32[]{:S(2)}) collective-permute-start(bf16[256,1024]{1,0:T(8,128)(2,1)} %fusion.3), channel_id=1, source_target_pairs={{0,4},{12,8},{1,5},{13,9},{2,6},{14,10},{3,7},{15,11},{16,20},{28,... | collective-permute-start | bytes 1572872 | tf_op jit(solution)/shard_map/ppermute | solution.py:601
  288.1 26.8 %collective-permute-start.40 = (bf16[256,512]{1,0:T(8,128)(2,1)S(1)}, bf16[256,512]{1,0:T(8,128)(2,1)S(1)}, u32[]{:S(2)}, u32[]{:S(2)}) collective-permute-start(bf16[256,512]{1,0:T(8,128)(2,1)S(1)} %get-tuple-element.104), channel_id=1, source_target_pairs={{0,16},{16,0},{1,17},{17,1},{2,18},{18,2},{3,19},{19,3},{4,20},{20... | collective-permute-start | bytes 786440 | tf_op jit(solution)/shard_map/ppermute | solution.py:42
  289.9 25.0 %collective-permute-start.41 = (bf16[256,1024]{1,0:T(8,128)(2,1)S(1)}, bf16[256,1024]{1,0:T(8,128)(2,1)S(1)}, u32[]{:S(2)}, u32[]{:S(2)}) collective-permute-start(bf16[256,1024]{1,0:T(8,128)(2,1)S(1)} %copy-done.84), channel_id=1, source_target_pairs={{0,16},{16,0},{1,17},{17,1},{2,18},{18,2},{3,19},{19,3},{4,20},{20... | collective-permute-start | bytes 1572872 | tf_op jit(solution)/shard_map/ppermute | solution.py:42
  293.9 19.6 %collective-permute-start.61 = (bf16[256,512]{1,0:T(8,128)(2,1)S(1)}, bf16[256,512]{1,0:T(8,128)(2,1)S(1)}, u32[]{:S(2)}, u32[]{:S(2)}) collective-permute-start(bf16[256,512]{1,0:T(8,128)(2,1)S(1)} %get-tuple-element.122), channel_id=1, source_target_pairs={{0,16},{16,0},{1,17},{17,1},{2,18},{18,2},{3,19},{19,3},{4,20},{20... | collective-permute-start | bytes 786440 | tf_op jit(solution)/shard_map/ppermute | solution.py:42
  299.4 10.9 %collective-permute-start.63 = (bf16[256,1024]{1,0:T(8,128)(2,1)S(1)}, bf16[256,1024]{1,0:T(8,128)(2,1)S(1)}, u32[]{:S(2)}, u32[]{:S(2)}) collective-permute-start(bf16[256,1024]{1,0:T(8,128)(2,1)S(1)} %fusion.5), channel_id=1, source_target_pairs={{0,4},{12,8},{1,5},{13,9},{2,6},{14,10},{3,7},{15,11},{16,20},{28,... | collective-permute-start | bytes 1572872 | tf_op jit(solution)/shard_map/ppermute | solution.py:601
  302.1 10.2 %collective-permute-start.44 = (bf16[128,1024]{1,0:T(8,128)(2,1)S(1)}, bf16[128,1024]{1,0:T(8,128)(2,1)S(1)}, u32[]{:S(2)}, u32[]{:S(2)}) collective-permute-start(bf16[128,1024]{1,0:T(8,128)(2,1)S(1)} %select_convert_fusion.2), channel_id=1, source_target_pairs={{4,8},{8,4},{5,9},{9,5},{6,10},{10,6},{7,11},{11,7},{20,24},{24,20... | collective-permute-start | bytes 786440 | tf_op jit(solution)/shard_map/ppermute | solution.py:601
  313.5 14.0 %collective-permute-start.51 = (bf16[128,1024]{1,0:T(8,128)(2,1)S(1)}, bf16[128,1024]{1,0:T(8,128)(2,1)S(1)}, u32[]{:S(2)}, u32[]{:S(2)}) collective-permute-start(bf16[128,1024]{1,0:T(8,128)(2,1)S(1)} %get-tuple-element.116.refs_0_), channel_id=1, source_target_pairs={{4,0},{8,12},{5,1},{9,13},{6,2},{10,14},{7,3},{11,15},{20,16},{24,... | collective-permute-start | bytes 786440 | tf_op jit(solution)/shard_map/ppermute | solution.py:601
  315.3 17.7 %collective-permute-start.65 = (bf16[128,1024]{1,0:T(8,128)(2,1)S(1)}, bf16[128,1024]{1,0:T(8,128)(2,1)S(1)}, u32[]{:S(2)}, u32[]{:S(2)}) collective-permute-start(bf16[128,1024]{1,0:T(8,128)(2,1)S(1)} %get-tuple-element.127.refs_0_), channel_id=1, source_target_pairs={{4,8},{8,4},{5,9},{9,5},{6,10},{10,6},{7,11},{11,7},{20,24},{24,20... | collective-permute-start | bytes 786440 | tf_op jit(solution)/shard_map/ppermute | solution.py:601
  316.0 19.1 %collective-permute-start.66 = (bf16[128,1024]{1,0:T(8,128)(2,1)S(1)}, bf16[128,1024]{1,0:T(8,128)(2,1)S(1)}, u32[]{:S(2)}, u32[]{:S(2)}) collective-permute-start(bf16[128,1024]{1,0:T(8,128)(2,1)S(1)} %get-tuple-element.127.refs_0_), channel_id=1, source_target_pairs={{4,0},{8,12},{5,1},{9,13},{6,2},{10,14},{7,3},{11,15},{20,16},{24,... | collective-permute-start | bytes 786440 | tf_op jit(solution)/shard_map/ppermute | solution.py:601
  327.7 14.4 %collective-permute-start.52 = (bf16[256,1024]{1,0:T(8,128)(2,1)S(1)}, bf16[256,1024]{1,0:T(8,128)(2,1)S(1)}, u32[]{:S(2)}, u32[]{:S(2)}) collective-permute-start(bf16[256,1024]{1,0:T(8,128)(2,1)S(1)} %fusion.4), channel_id=1, source_target_pairs={{0,4},{12,8},{1,5},{13,9},{2,6},{14,10},{3,7},{15,11},{16,20},{28,... | collective-permute-start | bytes 1572872 | tf_op jit(solution)/shard_map/ppermute | solution.py:601
  335.2 9.7 %collective-permute-start.67 = (bf16[256,512]{1,0:T(8,128)(2,1)S(1)}, bf16[256,512]{1,0:T(8,128)(2,1)S(1)}, u32[]{:S(2)}, u32[]{:S(2)}) collective-permute-start(bf16[256,512]{1,0:T(8,128)(2,1)S(1)} %fusion.7), channel_id=1, source_target_pairs={{0,4},{12,8},{1,5},{13,9},{2,6},{14,10},{3,7},{15,11},{16,20},{28,... | collective-permute-start | bytes 786440 | tf_op jit(solution)/shard_map/ppermute | solution.py:601
  346.2 17.3 %collective-permute-start.55 = (bf16[128,1024]{1,0:T(8,128)(2,1)S(1)}, bf16[128,1024]{1,0:T(8,128)(2,1)S(1)}, u32[]{:S(2)}, u32[]{:S(2)}) collective-permute-start(bf16[128,1024]{1,0:T(8,128)(2,1)S(1)} %get-tuple-element.118.refs_0_), channel_id=1, source_target_pairs={{4,0},{8,12},{5,1},{9,13},{6,2},{10,14},{7,3},{11,15},{20,16},{24,... | collective-permute-start | bytes 786440 | tf_op jit(solution)/shard_map/ppermute | solution.py:601
  363.5 9.0 %collective-permute-start.56 = (bf16[256,512]{1,0:T(8,128)(2,1)S(1)}, bf16[256,512]{1,0:T(8,128)(2,1)S(1)}, u32[]{:S(2)}, u32[]{:S(2)}) collective-permute-start(bf16[256,512]{1,0:T(8,128)(2,1)S(1)} %fusion.6), channel_id=1, source_target_pairs={{0,4},{12,8},{1,5},{13,9},{2,6},{14,10},{3,7},{15,11},{16,20},{28,... | collective-permute-start | bytes 786440 | tf_op jit(solution)/shard_map/ppermute | solution.py:601
  373.8 10.7 %collective-permute-start.75 = (f32[1,4096]{1,0:T(1,128)S(1)}, f32[1,4096]{1,0:T(1,128)S(1)}, u32[]{:S(2)}, u32[]{:S(2)}) collective-permute-start(f32[1,4096]{1,0:T(1,128)S(1)} %constant_dynamic-update-slice_fusion), channel_id=1, source_target_pairs={{0,4},{4,0},{8,12},{12,8},{1,5},{5,1},{9,13},{13,9},{2,6},{6,2},{1... | collective-permute-start | bytes 49160 | tf_op jit(solution)/shard_map/ppermute | solution.py:42
  382.6 9.8 %collective-permute-start.80 = (bf16[16,6656]{1,0:T(8,128)(2,1)S(1)}, bf16[16,6656]{1,0:T(8,128)(2,1)S(1)}, u32[]{:S(2)}, u32[]{:S(2)}) collective-permute-start(bf16[16,6656]{1,0:T(8,128)(2,1)S(1)} %convert_element_type.129), channel_id=1, source_target_pairs={{0,16},{16,0},{1,17},{17,1},{2,18},{18,2},{3,19},{19,3},{4,20},{20... | collective-permute-start | bytes 638984 | tf_op jit(solution)/shard_map/ppermute | solution.py:42
  384.5 9.3 %collective-permute-start.76 = (f32[1,4096]{1,0:T(1,128)S(1)}, f32[1,4096]{1,0:T(1,128)S(1)}, u32[]{:S(2)}, u32[]{:S(2)}) collective-permute-start(f32[1,4096]{1,0:T(1,128)S(1)} %add.221), channel_id=1, source_target_pairs={{0,8},{4,12},{8,0},{12,4},{1,9},{5,13},{9,1},{13,5},{2,10},{6,14},... | collective-permute-start | bytes 49160 | tf_op jit(solution)/shard_map/ppermute | solution.py:42
  389.2 8.3 %collective-permute-start.74 = (bf16[128,1024]{1,0:T(8,128)(2,1)S(1)}, bf16[128,1024]{1,0:T(8,128)(2,1)S(1)}, u32[]{:S(2)}, u32[]{:S(2)}) collective-permute-start(bf16[128,1024]{1,0:T(8,128)(2,1)S(1)} %collective-permute-done.50.refs_2_), channel_id=1, source_target_pairs={{4,0},{8,12},{5,1},{9,13},{6,2},{10,14},{7,3},{11,15},{20,16},{24,... | collective-permute-start | bytes 786440 | tf_op jit(solution)/shard_map/ppermute | solution.py:601
  390.4 9.8 %collective-permute-start.73 = (bf16[128,1024]{1,0:T(8,128)(2,1)S(1)}, bf16[128,1024]{1,0:T(8,128)(2,1)S(1)}, u32[]{:S(2)}, u32[]{:S(2)}) collective-permute-start(bf16[128,1024]{1,0:T(8,128)(2,1)S(1)} %collective-permute-done.65.refs_2_), channel_id=1, source_target_pairs={{4,0},{8,12},{5,1},{9,13},{6,2},{10,14},{7,3},{11,15},{20,16},{24,... | collective-permute-start | bytes 786440 | tf_op jit(solution)/shard_map/ppermute | solution.py:601
  392.4 10.6 %collective-permute-start.72 = (bf16[128,1024]{1,0:T(8,128)(2,1)S(1)}, bf16[128,1024]{1,0:T(8,128)(2,1)S(1)}, u32[]{:S(2)}, u32[]{:S(2)}) collective-permute-start(bf16[128,1024]{1,0:T(8,128)(2,1)S(1)} %collective-permute-done.54.refs_2_), channel_id=1, source_target_pairs={{4,0},{8,12},{5,1},{9,13},{6,2},{10,14},{7,3},{11,15},{20,16},{24,... | collective-permute-start | bytes 786440 | tf_op jit(solution)/shard_map/ppermute | solution.py:601
  393.7 10.4 %collective-permute-start.59 = (bf16[128,512]{1,0:T(8,128)(2,1)S(1)}, bf16[128,512]{1,0:T(8,128)(2,1)S(1)}, u32[]{:S(2)}, u32[]{:S(2)}) collective-permute-start(bf16[128,512]{1,0:T(8,128)(2,1)S(1)} %get-tuple-element.120.refs_0_), channel_id=1, source_target_pairs={{4,8},{8,4},{5,9},{9,5},{6,10},{10,6},{7,11},{11,7},{20,24},{24,20... | collective-permute-start | bytes 393224 | tf_op jit(solution)/shard_map/ppermute | solution.py:601
  397.4 13.2 %collective-permute-start.69 = (bf16[128,512]{1,0:T(8,128)(2,1)S(1)}, bf16[128,512]{1,0:T(8,128)(2,1)S(1)}, u32[]{:S(2)}, u32[]{:S(2)}) collective-permute-start(bf16[128,512]{1,0:T(8,128)(2,1)S(1)} %get-tuple-element.129.refs_0_), channel_id=1, source_target_pairs={{4,0},{8,12},{5,1},{9,13},{6,2},{10,14},{7,3},{11,15},{20,16},{24,... | collective-permute-start | bytes 393224 | tf_op jit(solution)/shard_map/ppermute | solution.py:601
  398.7 11.9 %collective-permute-start.71 = (bf16[128,512]{1,0:T(8,128)(2,1)S(1)}, bf16[128,512]{1,0:T(8,128)(2,1)S(1)}, u32[]{:S(2)}, u32[]{:S(2)}) collective-permute-start(bf16[128,512]{1,0:T(8,128)(2,1)S(1)} %collective-permute-done.70.refs_2_), channel_id=1, source_target_pairs={{4,0},{8,12},{5,1},{9,13},{6,2},{10,14},{7,3},{11,15},{20,16},{24,... | collective-permute-start | bytes 393224 | tf_op jit(solution)/shard_map/ppermute | solution.py:601
  400.2 12.3 %collective-permute-start.58 = (bf16[128,512]{1,0:T(8,128)(2,1)S(1)}, bf16[128,512]{1,0:T(8,128)(2,1)S(1)}, u32[]{:S(2)}, u32[]{:S(2)}) collective-permute-start(bf16[128,512]{1,0:T(8,128)(2,1)S(1)} %get-tuple-element.120.refs_0_), channel_id=1, source_target_pairs={{4,0},{8,12},{5,1},{9,13},{6,2},{10,14},{7,3},{11,15},{20,16},{24,... | collective-permute-start | bytes 393224 | tf_op jit(solution)/shard_map/ppermute | solution.py:601
  403.0 8.9 %collective-permute-start.77 = (f32[1,4096]{1,0:T(1,128)S(1)}, f32[1,4096]{1,0:T(1,128)S(1)}, u32[]{:S(2)}, u32[]{:S(2)}) collective-permute-start(f32[1,4096]{1,0:T(1,128)S(1)} %add.222), channel_id=1, source_target_pairs={{0,16},{16,0},{1,17},{17,1},{2,18},{18,2},{3,19},{19,3},{4,20},{20... | collective-permute-start | bytes 49160 | tf_op jit(solution)/shard_map/ppermute | solution.py:42
  404.2 8.3 %collective-permute-start.60 = (bf16[128,512]{1,0:T(8,128)(2,1)S(1)}, bf16[128,512]{1,0:T(8,128)(2,1)S(1)}, u32[]{:S(2)}, u32[]{:S(2)}) collective-permute-start(bf16[128,512]{1,0:T(8,128)(2,1)S(1)} %collective-permute-done.59.refs_2_), channel_id=1, source_target_pairs={{4,0},{8,12},{5,1},{9,13},{6,2},{10,14},{7,3},{11,15},{20,16},{24,... | collective-permute-start | bytes 393224 | tf_op jit(solution)/shard_map/ppermute | solution.py:601
  (114 other events, 1039.3 us)

commit v5 on v3

v5 whole, which is shorter than its diff:
```python
import jax
import jax.numpy as jnp
from jax import lax
from jax.experimental import pallas as pl
from jax.experimental.pallas import tpu as pltpu
from jax.sharding import PartitionSpec as P

MODEL_WIDTH = 16384
ADAPTER_SCALE = 0.5
VMEM_MIB = 12
MATMUL_VMEM_MIB = 18
COST_SHARE = 0.01

F32 = jnp.float32
BF16 = jnp.bfloat16
ANY = pl.BlockSpec(memory_space=pl.ANY)
RESIDENT = pl.BlockSpec(memory_space=pltpu.VMEM)


def bits_of(n):
    return n.bit_length() - 1


def reversed_bits(x, n):
    out = 0
    for i in range(n):
        out = out + (((x >> i) & 1) << (n - 1 - i))
    return out


def tile_of(n, cap):
    return max(t for t in range(128, cap + 1, 128) if n % t == 0)


def split_tiles(count, parts):
    edges = [count * i // parts for i in range(parts + 1)]
    return [(a, b - a) for a, b in zip(edges, edges[1:]) if b > a]


def swap(x, axis, n, mask):
    return lax.ppermute(x, axis, [(i, i ^ mask) for i in range(n)])


def double(x, axis, n, dim=0):
    for bit in reversed(range(bits_of(n))):
        x = jnp.concatenate([x, swap(x, axis, n, 1 << bit)], axis=dim)
    return x


def ordered(x, *first):
    return lax.optimization_barrier((x, *first))[0]


def total_of(parts, start, stop):
    out = parts[0][start:stop]
    for part in parts[1:]:
        out = out + part[start:stop].astype(F32)
    return out


def params(mib=VMEM_MIB):
    return pltpu.CompilerParams(vmem_limit_bytes=mib * 1024 * 1024)


def cost(flops, size):
    return pl.CostEstimate(
        flops=int(flops * COST_SHARE), bytes_accessed=int(size * COST_SHARE), transcendentals=0
    )


def normalize(stream, stats, steering, gain, down, h, hid, beside=None):
    tokens, width = stream.shape
    block = tokens // hid
    ranks = down.shape[0]
    n_beside = 0 if beside is None else 1

    def token_block(p, h_ref):
        return h_ref[0] ^ reversed_bits(p, bits_of(hid))

    def kernel(h_ref, x_ref, stat_ref, steer_ref, gain_ref, down_ref, *refs):
        steered = x_ref[...].astype(F32) + stat_ref[:, :1] * steer_ref[...]
        normed = (steered * stat_ref[:, 1:] * gain_ref[...]).astype(BF16)
        out_ref, low_ref = refs[n_beside : n_beside + 2]
        out_ref[...] = normed
        low_ref[...] = lax.dot_general(
            normed, down_ref[...], (((1,), (1,)), ((), ())), preferred_element_type=F32
        )
        if n_beside:
            refs[-1][:block, :] = refs[0][...]
            refs[-1][block:, :] = normed

    whole = lambda n: pl.BlockSpec((n, width), lambda p, h_ref: (0, 0))
    rows = lambda n, m: pl.BlockSpec((n, m), lambda p, h_ref: (p, 0))
    return pl.pallas_call(
        kernel,
        grid_spec=pltpu.PrefetchScalarGridSpec(
            num_scalar_prefetch=1,
            grid=(hid,),
            in_specs=[
                pl.BlockSpec((block, width), lambda p, h_ref: (token_block(p, h_ref), 0)),
                pl.BlockSpec((block, 2), lambda p, h_ref: (token_block(p, h_ref), 0)),
                whole(1),
                whole(1),
                whole(ranks),
            ]
            + [rows(block, width)] * n_beside,
            out_specs=[rows(block, width), rows(block, ranks)] + [rows(2 * block, width)] * n_beside,
        ),
        out_shape=[
            jax.ShapeDtypeStruct((tokens, width), BF16),
            jax.ShapeDtypeStruct((tokens, ranks), F32),
        ]
        + [jax.ShapeDtypeStruct((2 * tokens, width), BF16)] * n_beside,
        compiler_params=params(),
        cost_estimate=cost(2 * tokens * width * ranks, 4 * tokens * width),
        name="normalize",
    )(
        h.reshape(1),
        stream,
        stats,
        steering.reshape(1, width),
        gain.reshape(1, width),
        down,
        *((beside,) if n_beside else ()),
    )


def forward_matmul(x, weights, first, tiles, start, stop, tile, into=(), after=()):
    rows, depth = x.shape
    half = rows // 2

    def kernel(x_ref, w_ref, *refs):
        keep_ref, send_ref, token_ref = refs[-3:]
        token_ref[...] = jnp.zeros_like(token_ref)
        y = jnp.dot(x_ref[...], w_ref[0], preferred_element_type=F32)
        keep_ref[...] = y[:half]
        send_ref[...] = y[half:].astype(BF16)

    return pl.pallas_call(
        kernel,
        grid=(stop - start,),
        in_specs=[RESIDENT, pl.BlockSpec((1, depth, tile), lambda i: (0, 0, first + start + i))]
        + [ANY] * (len(into) + len(after)),
        out_specs=[pl.BlockSpec((half, tile), lambda i: (0, start + i))] * 2
        + [pl.BlockSpec((8, 128), lambda i: (0, 0))],
        out_shape=[
            jax.ShapeDtypeStruct((half, tiles * tile), F32),
            jax.ShapeDtypeStruct((half, tiles * tile), BF16),
            jax.ShapeDtypeStruct((8, 128), F32),
        ],
        input_output_aliases={2 + i: i for i in range(len(into))},
        compiler_params=params(MATMUL_VMEM_MIB),
        cost_estimate=cost(2 * rows * depth * (stop - start) * tile, 2 * depth * (rows + (stop - start) * tile) + 6 * half * (stop - start) * tile),
        name="forward_matmul",
    )(x, weights, *into, *after)


def share_sums(parts, rows, count, after=(), places=None):
    columns = parts[0].shape[1]
    tile = tile_of(columns, 1792)

    def kernel(*refs):
        total = refs[0][...].astype(F32)
        for ref in refs[1 : len(parts)]:
            total = total + ref[...].astype(F32)
        for i in range(count):
            refs[i - count][...] = total[i * rows : (i + 1) * rows].astype(BF16)

    return pl.pallas_call(
        kernel,
        grid=(columns // tile,),
        in_specs=[
            pl.BlockSpec((count * rows, tile), lambda i, at=at: (at, i)) for at in places or [1] * len(parts)
        ]
        + [ANY] * len(after),
        out_specs=[pl.BlockSpec((rows, tile), lambda i: (0, i))] * count,
        out_shape=[jax.ShapeDtypeStruct((rows, columns), BF16)] * count,
        compiler_params=params(),
        cost_estimate=cost(count * rows * columns, 8 * count * rows * columns),
        name="share_sums",
    )(*parts, *after)


def gated_gradients(d, mine, other, cotangent, first, low, up, own, after=()):
    columns = other.shape[1]
    rank = up.shape[1]
    tile = max(t for t in range(128, 2049, 128) if columns % t == 0 and first % t == 0)
    tiles = columns // tile
    base = first // tile

    def kernel(d_ref, *refs):
        mine_refs = refs[: len(mine)]
        other_ref, flow_ref, low_ref, up_ref = refs[len(mine) : len(mine) + 4]
        mine_out, other_out, back_ref = refs[-3:]
        own_is_gate = d_ref[0] == 0
        total = mine_refs[0][...].astype(F32)
        for ref in mine_refs[1:]:
            total = total + ref[...].astype(F32)
        passed = other_ref[...].astype(F32)
        low_terms = [
            ADAPTER_SCALE
            * jnp.dot(low_ref[:, k * rank : (k + 1) * rank], up_ref[k], preferred_element_type=F32)
            for k in range(2)
        ]
        gate = jnp.where(own_is_gate, total, passed) + low_terms[0]
        upper = jnp.where(own_is_gate, passed, total) + low_terms[1]
        sigma = 1.0 / (1.0 + jnp.exp(-gate))
        flow = flow_ref[...].astype(F32)
        gate_grad = (flow * upper * sigma * (1.0 + gate * (1.0 - sigma))).astype(BF16)
        upper_grad = (flow * gate * sigma).astype(BF16)
        mine_out[...] = jnp.where(own_is_gate, gate_grad, upper_grad)
        other_out[...] = jnp.where(own_is_gate, upper_grad, gate_grad)

        @pl.when(pl.program_id(0) == 0)
        def _():
            back_ref[...] = jnp.zeros_like(back_ref)

        contract = (((1,), (1,)), ((), ()))
        for k, grad in enumerate((gate_grad, upper_grad)):
            back_ref[:, k * rank : (k + 1) * rank] += lax.dot_general(
                grad, up_ref[k], contract, preferred_element_type=F32
            )
        back_ref[:, 2 * rank :] += jnp.sum(
            gate_grad.astype(F32) * gate + upper_grad.astype(F32) * upper, axis=1, keepdims=True
        )

    here = pl.BlockSpec((own, tile), lambda i, d_ref: (0, i))
    there = pl.BlockSpec((own, tile), lambda i, d_ref: (0, base + i))
    return pl.pallas_call(
        kernel,
        grid_spec=pltpu.PrefetchScalarGridSpec(
            num_scalar_prefetch=1,
            grid=(tiles,),
            in_specs=[here] * (len(mine) + 1)
            + [
                there,
                pl.BlockSpec((own, 2 * rank), lambda i, d_ref: (0, 0)),
                pl.BlockSpec((2, rank, tile), lambda i, d_ref: (0, 0, base + i)),
            ]
            + [ANY] * len(after),
            out_specs=[here, here, pl.BlockSpec((own, 2 * rank + 1), lambda i, d_ref: (0, 0))],
        ),
        out_shape=[
            jax.ShapeDtypeStruct((own, columns), BF16),
            jax.ShapeDtypeStruct((own, columns), BF16),
            jax.ShapeDtypeStruct((own, 2 * rank + 1), F32),
        ],
        compiler_params=params(),
        cost_estimate=cost(8 * own * columns * rank, 16 * own * columns),
        name="gated_gradients",
    )(d.reshape(1), *mine, other, cotangent, low, up, *after)


def backward_matmul(pieces, weights, hidden_start, first, tiles, tile, base=None, base_first=0, partial=False, after=()):
    rows = sum(g.shape[0] for g in pieces)
    half = rows // 2
    n_base = 0 if base is None else 1
    hidden = pieces[0].shape[1]

    def kernel(*refs):
        w_ref = refs[len(pieces)]
        g = jnp.concatenate([ref[...] for ref in refs[: len(pieces)]], axis=0)
        y = lax.dot_general(g, w_ref[0], (((1,), (1,)), ((), ())), preferred_element_type=F32)
        if n_base:
            y = y + refs[len(pieces) + 1][...]
        if partial:
            refs[-1][...] = y
        else:
            refs[-2][...] = y[:half]
            refs[-1][...] = y[half:].astype(BF16)

    if partial:
        out_specs = pl.BlockSpec((rows, tile), lambda i: (0, i))
        out_shape = jax.ShapeDtypeStruct((rows, tiles * tile), F32)
    else:
        out_specs = [pl.BlockSpec((half, tile), lambda i: (0, i))] * 2
        out_shape = [
            jax.ShapeDtypeStruct((half, tiles * tile), F32),
            jax.ShapeDtypeStruct((half, tiles * tile), BF16),
        ]
    return pl.pallas_call(
        kernel,
        grid=(tiles,),
        in_specs=[RESIDENT] * len(pieces)
        + [
            pl.BlockSpec(
                (pl.Element(1), pl.Element(tile), pl.Element(hidden)),
                lambda i: (0, (first + i) * tile, hidden_start),
            )
        ]
        + [pl.BlockSpec((rows, tile), lambda i: (0, first - base_first + i))] * n_base
        + [ANY] * len(after),
        out_specs=out_specs,
        out_shape=out_shape,
        compiler_params=params(MATMUL_VMEM_MIB),
        cost_estimate=cost(2 * rows * hidden * tiles * tile, 2 * hidden * (rows + tiles * tile) + (4 + 4 * n_base) * rows * tiles * tile),
        name="backward_matmul",
    )(*pieces, weights, *(() if base is None else (base,)), *after)


def adapter_products(low, groups):
    rank = low.shape[0]

    def kernel(*refs):
        at = 1
        for i, pieces in enumerate(groups):
            g = jnp.concatenate([ref[...] for ref in refs[at : at + len(pieces)]], axis=0)
            at += len(pieces)
            refs[i - len(groups)][...] = ADAPTER_SCALE * jnp.dot(
                refs[0][...], g, preferred_element_type=F32
            )

    operands = [g for pieces in groups for g in pieces]
    widths = [pieces[0].shape[1] for pieces in groups]
    return pl.pallas_call(
        kernel,
        grid=(1,),
        in_specs=[RESIDENT] * (1 + len(operands)),
        out_specs=[pl.BlockSpec((rank, w), lambda i: (0, 0)) for w in widths],
        out_shape=[jax.ShapeDtypeStruct((rank, w), F32) for w in widths],
        compiler_params=params(),
        cost_estimate=cost(2 * rank * low.shape[1] * sum(widths), 2 * low.shape[1] * sum(widths)),
        name="adapter_products",
    )(low, *operands)


def assemble(pieces, places, block, tokens, width, columns, into=None):
    chunk = pieces[0].shape[1]

    def kernel(place_ref, *refs):
        out_ref = refs[-1]
        i = 0
        for ref in refs[: len(pieces)]:
            for r in range(0, ref.shape[0], block):
                out_ref[pl.ds(pl.multiple_of(place_ref[i], block), block), :] = ref[r : r + block, :]
                i += 1

    n_into = 0 if into is None else 1
    return pl.pallas_call(
        kernel,
        grid_spec=pltpu.PrefetchScalarGridSpec(
            num_scalar_prefetch=1,
            grid=(1,),
            in_specs=[pl.BlockSpec(x.shape, lambda i, p: (0, 0)) for x in pieces] + [ANY] * n_into,
            out_specs=pl.BlockSpec((pl.Element(tokens), pl.Element(chunk)), lambda i, p: (0, columns)),
        ),
        out_shape=jax.ShapeDtypeStruct((tokens, width), BF16),
        input_output_aliases={len(pieces) + 1: 0} if n_into else {},
        compiler_params=params(),
        cost_estimate=cost(0, 4 * tokens * chunk),
        name="assemble",
    )(places, *pieces, *((into,) if n_into else ()))


def finish(parts, stream, stats, back, down, steering, gain, columns):
    rows = stream.shape[0]
    width = parts[0].shape[1]

    def kernel(*refs):
        part_refs = refs[: len(parts)]
        x_ref, s_ref, back_ref, down_ref, steer_ref, gain_ref, out_ref, sum_ref = refs[len(parts) :]
        total = part_refs[0][...].astype(F32)
        for ref in part_refs[1:]:
            total = total + ref[...].astype(F32)
        total = total + ADAPTER_SCALE * jnp.dot(back_ref[...], down_ref[...], preferred_element_type=F32)
        steered = x_ref[...].astype(F32) + s_ref[:, 0:1] * steer_ref[...]
        grad = s_ref[:, 1:2] * gain_ref[...] * total - s_ref[:, 2:3] * steered
        out_ref[...] = grad.astype(BF16)
        sum_ref[...] = jnp.sum(s_ref[:, 0:1] * grad, axis=0, keepdims=True)

    across = lambda n: pl.BlockSpec((pl.Element(n), pl.Element(width)), lambda i: (0, columns))
    return pl.pallas_call(
        kernel,
        grid=(1,),
        in_specs=[pl.BlockSpec((rows, width), lambda i: (0, 0))] * len(parts)
        + [
            across(rows),
            pl.BlockSpec(stats.shape, lambda i: (0, 0)),
            pl.BlockSpec(back.shape, lambda i: (0, 0)),
            across(down.shape[0]),
            across(1),
            across(1),
        ],
        out_specs=[pl.BlockSpec((rows, width), lambda i: (0, 0)), pl.BlockSpec((1, width), lambda i: (0, 0))],
        out_shape=[jax.ShapeDtypeStruct((rows, width), BF16), jax.ShapeDtypeStruct((1, width), F32)],
        compiler_params=params(),
        cost_estimate=cost(2 * rows * width * down.shape[0], 10 * rows * width),
        name="finish",
    )(*parts, stream, stats, back, down, steering.reshape(1, -1), gain.reshape(1, -1))


def make_local(dp, hid, ffn):
    def local(stream, steering, strength, gain, weights, down, up, cotangent):
        d, h, f = lax.axis_index("dp"), lax.axis_index("hid"), lax.axis_index("ffn")
        tokens, width = stream.shape
        hidden = weights.shape[2]
        own = tokens // hid
        rank = down.shape[2]
        first_pair = d == 0
        down_rows = jnp.transpose(down, (0, 2, 1)).reshape(2 * rank, width)

        peer_stream = swap(stream, "dp", dp, 1)
        rows = stream.astype(F32)
        total_rows, total_steer = lax.psum(
            (jnp.sum(rows * rows, axis=1), jnp.sum(steering * steering)), "hid"
        )
        stream_ms = total_rows / MODEL_WIDTH + 1e-06
        steer_ms = total_steer / MODEL_WIDTH + 1e-06
        scale = strength * jnp.sqrt(stream_ms / steer_ms)
        steered = rows + scale[:, None] * steering[None, :]
        steered_power = lax.psum(jnp.sum(steered * steered, axis=1), "hid")
        inv_rms = lax.rsqrt(steered_power / MODEL_WIDTH + 1e-05)
        stats = jnp.stack([scale, inv_rms], axis=1)
        peer_stats = swap(stats, "dp", dp, 1)

        tile = tile_of(hidden, 512)
        count = hidden // tile
        chunks = [(0, (count + 1) // 2), ((count + 1) // 2, count // 2)]
        last_bit = 1 << (bits_of(hid) - 1)
        own_normed, own_low = normalize(stream, stats, steering, gain, down_rows, h, hid)
        def forward(x, c, edges, afters):
            first, n = chunks[c]
            out, token = (), None
            for start, stop, after in zip(edges, edges[1:], afters):
                *out, token = forward_matmul(
                    x, weights, first, n, start, stop, tile, into=tuple(out), after=after(token)
                )
            keep, send = out
            parts = [keep, swap(send, "hid", hid, 1)]
            for bit in range(1, bits_of(hid) - 1):
                size = parts[-1].shape[0]
                send = total_of(parts, size // 2, size).astype(BF16)
                parts.append(swap(send, "hid", hid, 1 << bit))
            return parts

        own_parts = forward(own_normed, 0, (0, chunks[0][1]), (lambda t: (),))
        (own_send,) = share_sums(own_parts, own, 1)
        own_got = swap(own_send, "hid", hid, last_bit)
        peer_normed, peer_low, normed = normalize(
            peer_stream, ordered(peer_stats, own_send), steering, gain, down_rows, h, hid, own_normed
        )

        low, low_steps = jnp.stack([own_low, peer_low]), []
        for bit in range(bits_of(hid)):
            half = low.shape[1] // 2
            low = low[:, :half] + swap(low[:, half:], "hid", hid, 1 << bit)
            low_steps.append(low)
        low = low.astype(BF16)
        low_own = low[0]

        width_tile = tile_of(width, 512)
        tiles = width // width_tile
        steps = [(0, 3), (3, 3), (6, 2)] if tiles == 8 else split_tiles(tiles, 3)
        acts, others, grads = [], [], []

        n = chunks[0][1]
        peer_parts = forward(
            peer_normed, 0, (0, (n + 1) // 2, n), (lambda t: (own_send,), lambda t: (low_steps[0], own_got))
        )
        (peer_send,) = share_sums(peer_parts, own, 1, (low_own,))
        peer_got = swap(peer_send, "hid", hid, last_bit)
        acts.append(own_parts + [own_got])

        def pass_on(token):
            terms = peer_parts + [peer_got]
            (passed,) = share_sums(terms, own, 1, (token,), [0] * len(terms))
            others.append(swap(passed, "dp", dp, 1))
            return peer_got, passed

        n = chunks[1][1]
        first_send = peer_send
        parts = forward(
            normed, 1, (0, n // 3, n - 1, n), (lambda t: (first_send,), pass_on, lambda t: (others[0],))
        )
        own_send, peer_send = share_sums(parts, own, 2)
        peer_got = swap(peer_send, "hid", hid, last_bit)
        own_got = swap(own_send, "hid", hid, last_bit)
        (passed,) = share_sums(parts + [peer_got], own, 1, (), [1] * len(parts) + [0])
        acts.append(parts + [own_got])
        others.append(swap(passed, "dp", dp, 1))

        def gradients(c, after):
            mine_grad, other_grad, back_part = gated_gradients(
                d, acts[c], others[c], cotangent, chunks[c][0] * tile, low_own, up, own, after
            )
            return back_part, mine_grad, swap(other_grad, "dp", dp, 1)

        def spread(*gradients):
            pieces = []
            for g in gradients:
                blocks = [g]
                for bit in reversed(range(bits_of(hid))):
                    blocks += [swap(x, "hid", hid, 1 << bit) for x in blocks]
                pieces += blocks
            grads.append(pieces)

        back, mine_grad, peer_grad = gradients(0, ())
        (peer_grad,) = share_sums([peer_grad], own, 1, (peer_got,), [0])
        spread(mine_grad, peer_grad)
        bases = []

        def first_half(j, after):
            first, n = steps[j]
            bases.append(
                backward_matmul(
                    grads[0], weights, 0, first, n, width_tile, partial=True, after=after
                )
            )

        first_half(0, (passed,))
        more, mine_grad, peer_grad = gradients(1, (peer_grad, bases[0]))
        back = back + more
        for j in range(1, len(steps)):
            first_half(j, (mine_grad,) if j == 1 else (peer_grad,))
            if j == 1:
                peer_grad = ordered(peer_grad, bases[1])
        spread(mine_grad, peer_grad)

        for bit in range(bits_of(ffn)):
            back = back + swap(back, "ffn", ffn, 1 << bit)
        back = jnp.stack([back, swap(back, "dp", dp, 1)])
        shard = tokens // ffn
        place = reversed_bits(f, bits_of(ffn))
        products, received = [], []

        def halving_step(parts, bit):
            half = parts[-1].shape[0] // 2
            mine = (f >> bit) & 1
            sides = [
                [lax.dynamic_slice_in_dim(p, side * half, half, axis=0) for p in parts]
                for side in (mine, 1 - mine)
            ]
            return total_of(sides[0], 0, half), total_of(sides[1], 0, half).astype(BF16)

        first_steps = []
        for j, ((first, n), base) in enumerate(zip(steps, bases)):
            wait = (products[-1] if products else bases[-1],)
            if j == 2:
                first_steps.append(halving_step([products[0], received[0]], 0))
                wait += (first_steps[0][1],)
            keep, send = backward_matmul(
                grads[1], weights, chunks[1][0] * tile, first, n, width_tile, base=base, base_first=first,
                after=wait,
            )
            products.append(keep)
            received.append(swap(send, "dp", dp, 1))
        begun = first_steps[0][1] if first_steps else products[-1]
        back = double(ordered(back, begun), "hid", hid, dim=1)
        back_low = back[:, :, : 2 * rank].astype(BF16)
        acts_product = back[0, :, 2 * rank]

        block = min(own, shard)

        def natural(row):
            index = row // own
            return (h ^ reversed_bits(index, bits_of(hid))) * own + row % own

        def shard_rows(x):
            return jnp.concatenate(
                [
                    lax.dynamic_slice_in_dim(x, natural(place * shard + i * block), block, axis=0)
                    for i in range(shard // block)
                ],
                axis=0,
            )

        stats_shard = shard_rows(stats)
        dot_shard = lax.dynamic_slice_in_dim(acts_product, place * shard, shard, axis=0)
        dot_factor = stats_shard[:, 1] ** 2 * dot_shard / MODEL_WIDTH
        stats_shard = jnp.concatenate([stats_shard, dot_factor[:, None]], axis=1)
        stream_shard = shard_rows(stream)
        back_shard = lax.dynamic_slice_in_dim(back_low[0], place * shard, shard, axis=0)

        out, sums, gathered = None, [], []
        owners = [reversed_bits(f ^ reversed_bits(p, bits_of(ffn)), bits_of(ffn)) for p in range(ffn)]
        places = jnp.stack([natural(o * shard + i * block) for o in owners for i in range(shard // block)])
        for j, (first, n) in enumerate(steps):
            got = received[j]
            if j == 1:
                got = ordered(got, products[-1])
            elif j >= 2:
                got = ordered(got, gathered[j - 2][1])
            parts = [products[j], got]
            for bit in range(bits_of(ffn)):
                if bit == 0 and j < len(first_steps):
                    keep, send = first_steps[j]
                else:
                    keep, send = halving_step(parts, bit)
                if j == 2 and bit == 1:
                    send = ordered(send, gathered[0][-1])
                parts = [keep, swap(send, "ffn", ffn, 1 << bit)]
            result, sum_part = finish(
                parts, stream_shard, stats_shard, back_shard, down_rows, steering, gain, first * width_tile
            )
            sums.append(sum_part)
            blocks = [result]
            for bit in reversed(range(bits_of(ffn))):
                if j == len(steps) - 1 and bit == 0:
                    steering_gradient = lax.psum(jnp.concatenate(sums, axis=1), ("dp", "ffn"))
                    blocks = [ordered(x, steering_gradient) for x in blocks]
                blocks += [swap(x, "ffn", ffn, 1 << bit) for x in blocks]
            gathered.append(blocks)
            out = assemble(blocks, places, block, tokens, width, first * width_tile, into=out)

        low_mine = jnp.where(first_pair, low[:, :, :rank], low[:, :, rank:])
        low_mine = double(ordered(low_mine, begun), "hid", hid, dim=1).reshape(2 * tokens, rank)
        up_mine = jnp.concatenate(adapter_products(ordered(low_mine.T, products[-1]), grads), axis=1)
        up_other = swap(ordered(up_mine.astype(BF16), received[-1]), "dp", dp, 1).astype(F32)
        up_gradient = jnp.where(
            first_pair, jnp.stack([up_mine, up_other]), jnp.stack([up_other, up_mine])
        )
        back_rows = back_low.reshape(2, hid, own, 2 * rank).transpose(1, 0, 2, 3).reshape(2 * tokens, 2 * rank)
        (down_gradient,) = adapter_products(back_rows.T, [[normed]])
        down_gradient = jnp.transpose(
            down_gradient.reshape(2, rank, width), (0, 2, 1)
        )
        return out, steering_gradient.reshape(width), down_gradient, up_gradient

    return local


def solution(mesh):
    in_specs = (
        P("dp", "hid"),
        P("hid"),
        P("dp"),
        P("hid"),
        P("dp", "hid", "ffn"),
        P(None, "hid", None),
        P(None, None, "ffn"),
        P(("dp", "hid"), "ffn"),
    )
    out_specs = (P("dp", "hid"), P("hid"), P(None, "hid", None), P(None, None, "ffn"))
    local = make_local(mesh.shape["dp"], mesh.shape["hid"], mesh.shape["ffn"])
    return jax.shard_map(local, mesh=mesh, in_specs=in_specs, out_specs=out_specs, check_vma=False)
```

time: 356 us -> 390 us (1.096)
  blocking collectives: 13.3 us -> 49.6 us
  starting transfers between devices: 81.7 us -> 49.2 us
  waiting for transfers between devices: 82.1 us -> 104 us
  Pallas kernels: 124 us -> 131 us
  other arithmetic: 15.1 us -> 20.8 us
    psum x0 -> x1, blocking collectives: none -> 36.2 us  [local(): steering_gradient = lax.psum(jnp.concatenate(sums, axis=1), ('dp', 'ffn'))]
    ppermute x75 -> x53, starting transfers between devices: 81.7 us -> 49.2 us  [swap(): return lax.ppermute(x, axis, [(i, i ^ mask) for i in range(n)])]
    ppermute x75 -> x53, waiting for transfers between devices: 82.1 us -> 104 us  [swap(): return lax.ppermute(x, axis, [(i, i ^ mask) for i in range(n)])]
    pallas_call x6, Pallas kernels: 47.3 us -> 56.2 us  [forward_matmul(): pl.pallas_call(kernel, grid=(stop - start,), in_specs=[RESIDENT, pl.Block...]
    convert_element_type x11 -> x5, other arithmetic: 6.01 us -> 8.69 us  [halving_step(): total_of(sides[1], 0, half).astype(BF16)]
    unnamed x159 -> x145, local copies, waits for them, and re-layouts: 28.5 us -> 26.2 us
    pallas_call x8 -> x6, Pallas kernels: 51.7 us -> 49.5 us  [backward_matmul(): pl.pallas_call(kernel, grid=(tiles,), in_specs=[RESIDENT] * len(pieces) +...]
    pallas_call x3 -> x2, Pallas kernels: 8.19 us -> 7.08 us  [gated_gradients(): pl.pallas_call(kernel, grid_spec=pltpu.PrefetchScalarGridSpec(num_scalar_...]
  transfers between devices with their start and end apart: 75 -> 53, of which waited for: 30 -> 19; matrix products, arithmetic and copies ran while one was open for 6% -> 7% of each run, Pallas kernels for 26% -> 26%
where the time goes in v5:
time: 390 us; the launch traced here: 388 us
  Pallas kernels  131 us (34%)
  waiting for transfers between devices  104 us (27%)
  blocking collectives  49.6 us (13%)
  starting transfers between devices  49.2 us (13%)
  local copies, waits for them, and re-layouts  30.9 us (8%)
  other arithmetic  20.8 us (5%)
    ppermute x53, waiting for transfers between devices, swap(): return lax.ppermute(x, axis, [(i, i ^ mask) for i in range(n)])  104 us
    pallas_call x6, Pallas kernels, forward_matmul(): pl.pallas_call(kernel, grid=(stop - start,), in_specs=[RESIDENT, pl.Block...  56.2 us
    pallas_call x6, Pallas kernels, backward_matmul(): pl.pallas_call(kernel, grid=(tiles,), in_specs=[RESIDENT] * len(pieces) +...  49.5 us
    ppermute x53, starting transfers between devices, swap(): return lax.ppermute(x, axis, [(i, i ^ mask) for i in range(n)])  49.2 us
    psum x1, blocking collectives, local(): steering_gradient = lax.psum(jnp.concatenate(sums, axis=1), ('dp', 'ffn'))  36.2 us
    unnamed x145, local copies, waits for them, and re-layouts  26.2 us
    convert_element_type x5, other arithmetic, halving_step(): total_of(sides[1], 0, half).astype(BF16)  8.69 us
  transfers between devices with their start and end apart: 53, of which 19 were waited for; matrix products, arithmetic and copies ran while one was open for 7% of the time, Pallas kernels for 26%

profile of v5, /device:TPU:0, one launch (start us, length us, event | category | flops | bytes accessed | tf_op | source)
XLA Modules:
  0.0 387.7 jit_solution(3336618658181978088)
XLA Ops:
  0.7 3.0 collective-permute-start
  5.0 2.1 fusion
  7.1 7.4 %all-reduce = (f32[256]{0:T(256)S(1)}, f32[]{:T(128)}) all-reduce(f32[256]{0:T(256)S(1)} %fusion, f32[]{:T(128)} %multiply_reduce_fusion), channel_id=1, replica_groups=mesh['dp'=2,'ffn'=4,'hid'=4] {'hid'}, use_global_device_ids=true, to_apply=%region_1.0 | all-reduce | flops 257 | bytes 2056 | tf_op jit(solution)/shard_map/psum | solution.py:404
  16.0 6.1 %psum.30 = f32[256]{0:T(256)S(1)} all-reduce(f32[256]{0:T(256)S(1)} %fusion.2), channel_id=1, replica_groups=mesh['dp'=2,'ffn'=4,'hid'=4] {'hid'}, use_global_device_ids=true, to_apply=%region_5.0 | all-reduce | flops 256 | bytes 2048 | tf_op jit(solution)/shard_map/psum | solution.py:411
  22.9 1.7 normalize.2
  24.6 14.7 %forward_matmul.6 = (f32[128,3584]{1,0:T(8,128)S(1)}, bf16[128,3584]{1,0:T(8,128)(2,1)S(1)}, f32[8,128]{1,0:T(8,128)}) custom-call(bf16[256,4096]{1,0:T(8,128)(2,1)S(1)} %get-tuple-element.55.x_ref.refs_0_, bf16[1,4096,6656]{2,1,0:T(8,128)(2,1)} %refs_8_.11), custom_call_target="tpu_custom_call" | custom-call | flops 75161928 | bytes 342097 | tf_op jit(solution)/shard_map/forward_matmul/pallas_call | solution.py:139
  39.3 2.5 collective-permute-done.2.refs_1_
  43.5 8.8 %collective-permute-done.1.stat_ref = f32[256,2]{1,0:T(8,128)S(1)} collective-permute-done((f32[256,2]{1,0:T(8,128)S(1)}, f32[256,2]{1,0:T(8,128)S(1)}, u32[]{:S(2)}, u32[]{:S(2)}) %collective-permute-start.1) | collective-permute-done | bytes 2080 | tf_op jit(solution)/shard_map/ppermute | solution.py:41
  52.3 3.4 normalize.3
  55.9 10.5 %forward_matmul.7 = (f32[128,3584]{1,0:T(8,128)S(1)}, bf16[128,3584]{1,0:T(8,128)(2,1)S(1)}, f32[8,128]{1,0:T(8,128)}) custom-call(bf16[256,4096]{1,0:T(8,128)(2,1)S(1)} %get-tuple-element.60.x_ref, bf16[1,4096,6656]{2,1,0:T(8,128)(2,1)} %refs_8_.11, bf16[64,3584]{1,0:T(8,128)(2,1)S(1)} %share_sums.6.refs_0_), custom_call_target="tpu_custom_call" | custom-call | flops 42949672 | bytes 204472 | tf_op jit(solution)/shard_map/forward_matmul/pallas_call | solution.py:139
  66.4 7.8 %forward_matmul.8 = (f32[128,3584]{1,0:T(8,128)S(1)}, bf16[128,3584]{1,0:T(8,128)(2,1)S(1)}, f32[8,128]{1,0:T(8,128)}) custom-call(bf16[256,4096]{1,0:T(8,128)(2,1)S(1)} %get-tuple-element.60.x_ref, bf16[1,4096,6656]{2,1,0:T(8,128)(2,1)} %refs_8_.11, f32[128,3584]{1,0:T(8,128)S(1)} %get-tuple-element.61.refs_0_, ...), custom_call_target="tpu_custom_call", output_to_operand_aliasing={{0}: (2, {}), {1}: (3, {})} | custom-call | flops 32212254 | bytes 158597 | tf_op jit(solution)/shard_map/forward_matmul/pallas_call | solution.py:139
  74.3 1.8 collective-permute-start.6
  76.1 2.7 collective-permute-done.6
  79.1 1.8 collective-permute-start.7
  80.9 7.7 %forward_matmul.9 = (f32[256,3072]{1,0:T(8,128)S(1)}, bf16[256,3072]{1,0:T(8,128)(2,1)}, f32[8,128]{1,0:T(8,128)S(1)}) custom-call(bf16[512,4096]{1,0:T(8,128)(2,1)S(1)} %get-tuple-element.59.x_ref.refs_1_, bf16[1,4096,6656]{2,1,0:T(8,128)(2,1)} %refs_8_.11, bf16[64,3584]{1,0:T(8,128)(2,1)S(1)} %share_sums.7.refs_0_), custom_call_target="tpu_custom_call" | custom-call | flops 42949672 | bytes 141557 | tf_op jit(solution)/shard_map/forward_matmul/pallas_call | solution.py:139
  88.6 2.7 collective-permute-done.7.refs_2_
  91.6 1.8 collective-permute-start.8
  93.4 10.1 %forward_matmul.10 = (f32[256,3072]{1,0:T(8,128)S(1)}, bf16[256,3072]{1,0:T(8,128)(2,1)}, f32[8,128]{1,0:T(8,128)}) custom-call(bf16[512,4096]{1,0:T(8,128)(2,1)S(1)} %get-tuple-element.59.x_ref.refs_1_, bf16[1,4096,6656]{2,1,0:T(8,128)(2,1)} %refs_8_.11, f32[256,3072]{1,0:T(8,128)S(1)} %get-tuple-element.67.refs_0_, ...), custom_call_target="tpu_custom_call", output_to_operand_aliasing={{0}: (2, {}), {1}: (3, {})} | custom-call | flops 64424508 | bytes 191365 | tf_op jit(solution)/shard_map/forward_matmul/pallas_call | solution.py:139
  103.5 5.4 %forward_matmul.11 = (f32[256,3072]{1,0:T(8,128)S(1)}, bf16[256,3072]{1,0:T(8,128)(2,1)}, f32[8,128]{1,0:T(8,128)}) custom-call(bf16[512,4096]{1,0:T(8,128)(2,1)S(1)} %get-tuple-element.59.x_ref.refs_1_, bf16[1,4096,6656]{2,1,0:T(8,128)(2,1)} %refs_8_.11, f32[256,3072]{1,0:T(8,128)S(1)} %get-tuple-element.70.refs_0_, ...), custom_call_target="tpu_custom_call", output_to_operand_aliasing={{0}: (2, {}), {1}: (3, {})} | custom-call | flops 21474836 | bytes 91750 | tf_op jit(solution)/shard_map/forward_matmul/pallas_call | solution.py:139
  115.8 2.4 gated_gradients.2
  120.7 1.6 collective-permute-start.11
  122.8 8.4 %collective-permute-done.13.refs_0_ = bf16[64,3584]{1,0:T(8,128)(2,1)S(1)} collective-permute-done((bf16[64,3584]{1,0:T(8,128)(2,1)S(1)}, bf16[64,3584]{1,0:T(8,128)(2,1)S(1)}, u32[]{:S(2)}, u32[]{:S(2)}) %collective-permute-start.13) | collective-permute-done | bytes 458784 | tf_op jit(solution)/shard_map/ppermute | solution.py:41
  131.2 1.5 collective-permute-done.11.refs_2_.refs_1_
  132.9 1.6 collective-permute-start.17
  134.5 8.1 %collective-permute-done.14.refs_1_.refs_2_ = bf16[64,3584]{1,0:T(8,128)(2,1)S(1)} collective-permute-done((bf16[64,3584]{1,0:T(8,128)(2,1)S(1)}, bf16[64,3584]{1,0:T(8,128)(2,1)S(1)}, u32[]{:S(2)}, u32[]{:S(2)}) %collective-permute-start.14) | collective-permute-done | bytes 458784 | tf_op jit(solution)/shard_map/ppermute | solution.py:41
  143.0 8.6 %collective-permute-done.17.refs_5_.refs_6_ = bf16[64,3584]{1,0:T(8,128)(2,1)S(1)} collective-permute-done((bf16[64,3584]{1,0:T(8,128)(2,1)S(1)}, bf16[64,3584]{1,0:T(8,128)(2,1)S(1)}, u32[]{:S(2)}, u32[]{:S(2)}) %collective-permute-start.17) | collective-permute-done | bytes 458784 | tf_op jit(solution)/shard_map/ppermute | solution.py:41
  151.7 1.5 collective-permute-start.10
  155.4 9.0 %backward_matmul.6.refs_8_.refs_9_ = f32[512,1536]{1,0:T(8,128)S(1)} custom-call(bf16[64,3584]{1,0:T(8,128)(2,1)S(1)} %get-tuple-element.77.refs_0_.refs_1_, bf16[64,3584]{1,0:T(8,128)(2,1)S(1)} %collective-permute-done.14.refs_1_.refs_2_, bf16[64,3584]{1,0:T(8,128)(2,1)S(1)} %collective-permute-done.15.refs_2_.refs_3_, ...), custom_call_target="tpu_custom_call" | custom-call | flops 56371444 | bytes 178257 | tf_op jit(solution)/shard_map/backward_matmul/pallas_call | solution.py:281
  165.7 4.7 %gated_gradients.3 = (bf16[64,3072]{1,0:T(8,128)(2,1)S(1)}, bf16[64,3072]{1,0:T(8,128)(2,1)S(1)}, f32[64,33]{1,0:T(8,128)S(1)}) custom-call(s32[1]{0:T(128)} %bitcast.4.d_ref, f32[256,3072]{1,0:T(8,128)S(1)} %get-tuple-element.72.refs_0_, bf16[256,3072]{1,0:T(8,128)(2,1)} %collective-permute-done.9.refs_1_, ...), custom_call_target="tpu_custom_call" | custom-call | flops 251658 | bytes 31457 | tf_op jit(solution)/shard_map/gated_gradients/pallas_call | solution.py:229
  172.5 8.7 %backward_matmul.7.refs_9_ = f32[512,1536]{1,0:T(8,128)S(1)} custom-call(bf16[64,3584]{1,0:T(8,128)(2,1)S(1)} %get-tuple-element.77.refs_0_.refs_1_, bf16[64,3584]{1,0:T(8,128)(2,1)S(1)} %collective-permute-done.14.refs_1_.refs_2_, bf16[64,3584]{1,0:T(8,128)(2,1)S(1)} %collective-permute-done.15.refs_2_.refs_3_, ...), custom_call_target="tpu_custom_call" | custom-call | flops 56371444 | bytes 178257 | tf_op jit(solution)/shard_map/backward_matmul/pallas_call | solution.py:281
  181.3 1.6 copy-done.8
  182.9 1.5 collective-permute-start.24
  184.9 8.0 %collective-permute-done.24.refs_5_.refs_14_ = bf16[64,3072]{1,0:T(8,128)(2,1)} collective-permute-done((bf16[64,3072]{1,0:T(8,128)(2,1)S(1)}, bf16[64,3072]{1,0:T(8,128)(2,1)}, u32[]{:S(2)}, u32[]{:S(2)}) %collective-permute-start.24) | collective-permute-done | bytes 393248 | tf_op jit(solution)/shard_map/ppermute | solution.py:41
  201.1 6.5 %backward_matmul.8.refs_10_.refs_9_ = f32[512,1024]{1,0:T(8,128)S(1)} custom-call(bf16[64,3584]{1,0:T(8,128)(2,1)S(1)} %copy-done.13, bf16[64,3584]{1,0:T(8,128)(2,1)S(1)} %copy-done.16, bf16[64,3584]{1,0:T(8,128)(2,1)S(1)} %copy-done.22, bf16[64,3584]{1,0:T(8,128)(2,1)S(1)} %copy-done.25, bf16[64,3584]{1,0:T(8,128)(2,1)S(1)} %copy-done.6, ...), custom_call_target="tpu_custom_call" | custom-call | flops 37580964 | bytes 131072 | tf_op jit(solution)/shard_map/backward_matmul/pallas_call | solution.py:281
  207.7 9.1 %backward_matmul.9 = (f32[256,1536]{1,0:T(8,128)S(1)}, bf16[256,1536]{1,0:T(8,128)(2,1)}) custom-call(bf16[64,3072]{1,0:T(8,128)(2,1)S(1)} %get-tuple-element.78.refs_9_.refs_0_, bf16[64,3072]{1,0:T(8,128)(2,1)} %collective-permute-done.20.refs_1_.refs_10_, bf16[64,3072]{1,0:T(8,128)(2,1)} %collective-permute-done.21.refs_2_.refs_11_, ...), custom_call_target="tpu_custom_call" | custom-call | flops 48318384 | bytes 188743 | tf_op jit(solution)/shard_map/backward_matmul/pallas_call | solution.py:281
  218.0 9.1 %backward_matmul.10 = (f32[256,1536]{1,0:T(8,128)S(1)}, bf16[256,1536]{1,0:T(8,128)(2,1)}) custom-call(bf16[64,3072]{1,0:T(8,128)(2,1)S(1)} %get-tuple-element.78.refs_9_.refs_0_, bf16[64,3072]{1,0:T(8,128)(2,1)} %collective-permute-done.20.refs_1_.refs_10_, bf16[64,3072]{1,0:T(8,128)(2,1)} %collective-permute-done.21.refs_2_.refs_11_, ...), custom_call_target="tpu_custom_call" | custom-call | flops 48318384 | bytes 188743 | tf_op jit(solution)/shard_map/backward_matmul/pallas_call | solution.py:281
  230.3 1.6 collective-permute-start.31
  232.1 2.2 collective-permute-done.31
  234.3 2.6 collective-permute-start.32
  237.6 1.5 collective-permute-done.32
  240.3 2.8 convert_add_fusion.2
  243.0 1.5 collective-permute-start.50
  244.6 10.0 %collective-permute-done.33 = f32[64,33]{1,0:T(8,128)S(1)} collective-permute-done((f32[64,33]{1,0:T(8,128)S(1)}, f32[64,33]{1,0:T(8,128)S(1)}, u32[]{:S(2)}, u32[]{:S(2)}) %collective-permute-start.33) | collective-permute-done | bytes 8480 | tf_op jit(solution)/shard_map/ppermute | solution.py:41
  255.4 1.5 collective-permute-start.34
  257.0 1.6 collective-permute-start.29
  261.1 7.0 %backward_matmul.11 = (f32[256,1024]{1,0:T(8,128)S(1)}, bf16[256,1024]{1,0:T(8,128)(2,1)}) custom-call(bf16[64,3072]{1,0:T(8,128)(2,1)S(1)} %get-tuple-element.78.refs_9_.refs_0_, bf16[64,3072]{1,0:T(8,128)(2,1)} %collective-permute-done.20.refs_1_.refs_10_, bf16[64,3072]{1,0:T(8,128)(2,1)} %collective-permute-done.21.refs_2_.refs_11_, ...), custom_call_target="tpu_custom_call" | custom-call | flops 32212254 | bytes 136314 | tf_op jit(solution)/shard_map/backward_matmul/pallas_call | solution.py:281
  271.2 2.9 add_convert_fusion
  274.8 2.6 adapter_products.3
  282.0 2.6 collective-permute-start.30
  285.0 9.2 %collective-permute-done.30.refs_1_ = bf16[64,1536]{1,0:T(8,128)(2,1)S(1)} collective-permute-done((bf16[64,1536]{1,0:T(8,128)(2,1)S(1)}, bf16[64,1536]{1,0:T(8,128)(2,1)S(1)}, u32[]{:S(2)}, u32[]{:S(2)}) %collective-permute-start.30) | collective-permute-done | bytes 196640 | tf_op jit(solution)/shard_map/ppermute | solution.py:41
  296.0 2.9 collective-permute-start.42
  298.9 12.9 %collective-permute-done.36.refs_1_ = bf16[64,1536]{1,0:T(8,128)(2,1)S(1)} collective-permute-done((bf16[64,1536]{1,0:T(8,128)(2,1)S(1)}, bf16[64,1536]{1,0:T(8,128)(2,1)S(1)}, u32[]{:S(2)}, u32[]{:S(2)}) %collective-permute-start.36) | collective-permute-done | bytes 196640 | tf_op jit(solution)/shard_map/ppermute | solution.py:41
  311.7 2.0 add_convert_fusion.2
  315.5 2.0 collective-permute-start.38
  317.9 2.2 copy-done.1
  320.1 1.6 adapter_products.2
  322.2 3.2 collective-permute-done.37
  326.5 6.6 %collective-permute-done.38.refs_3_ = bf16[64,1536]{1,0:T(8,128)(2,1)S(1)} collective-permute-done((bf16[64,1536]{1,0:T(8,128)(2,1)S(1)}, bf16[64,1536]{1,0:T(8,128)(2,1)S(1)}, u32[]{:S(2)}, u32[]{:S(2)}) %collective-permute-start.38) | collective-permute-done | bytes 196640 | tf_op jit(solution)/shard_map/ppermute | solution.py:41
  333.9 1.6 collective-permute-start.48
  335.4 5.7 %collective-permute-done.39.refs_1_ = bf16[64,1024]{1,0:T(8,128)(2,1)S(1)} collective-permute-done((bf16[64,1024]{1,0:T(8,128)(2,1)S(1)}, bf16[64,1024]{1,0:T(8,128)(2,1)S(1)}, u32[]{:S(2)}, u32[]{:S(2)}) %collective-permute-start.39) | collective-permute-done | bytes 131104 | tf_op jit(solution)/shard_map/ppermute | solution.py:41
  341.3 1.7 collective-permute-start.43
  343.0 36.2 %psum.31 = f32[1,4096]{1,0:T(1,128)} all-reduce(f32[1,4096]{1,0:T(1,128)S(1)} %pad_maximum_fusion.4), channel_id=1, replica_groups=mesh['dp'=2,'ffn'=4,'hid'=4] {'dp','ffn'}, use_global_device_ids=true, to_apply=%region_6.7 | all-reduce | flops 4096 | bytes 32768 | tf_op jit(solution)/shard_map/psum | solution.py:599
  379.2 2.0 collective-permute-start.45
  381.2 2.1 maximum_select_fusion
  (271 shorter events, 59.0 us)
Async XLA Ops:
  0.7 51.7 %collective-permute-start = (bf16[256,4096]{1,0:T(8,128)(2,1)}, bf16[256,4096]{1,0:T(8,128)(2,1)}, u32[]{:S(2)}, u32[]{:S(2)}) collective-permute-start(bf16[256,4096]{1,0:T(8,128)(2,1)} %x_ref.1), channel_id=1, source_target_pairs={{0,16},{16,0},{1,17},{17,1},{2,18},{18,2},{3,19},{19,3},{4,20},{20... | collective-permute-start | bytes 6291464 | tf_op jit(solution)/shard_map/ppermute | solution.py:41
  39.3 2.5 collective-permute-start.2
  42.0 24.4 %collective-permute-start.4 = (bf16[64,3584]{1,0:T(8,128)(2,1)S(1)}, bf16[64,3584]{1,0:T(8,128)(2,1)S(1)}, u32[]{:S(2)}, u32[]{:S(2)}) collective-permute-start(bf16[64,3584]{1,0:T(8,128)(2,1)S(1)} %share_sums.6.refs_0_), channel_id=1, source_target_pairs={{0,2},{1,3},{2,0},{3,1},{4,6},{5,7},{6,4},{7,5},{8,10},{9,11},{10,... | collective-permute-start | bytes 1376264 | tf_op jit(solution)/shard_map/ppermute | solution.py:41
  42.9 9.4 %collective-permute-start.1 = (f32[256,2]{1,0:T(8,128)S(1)}, f32[256,2]{1,0:T(8,128)S(1)}, u32[]{:S(2)}, u32[]{:S(2)}) collective-permute-start(f32[256,2]{1,0:T(8,128)S(1)} %copy.48.stat_ref), channel_id=1, source_target_pairs={{0,16},{16,0},{1,17},{17,1},{2,18},{18,2},{3,19},{19,3},{4,20},{20... | collective-permute-start | bytes 6152 | tf_op jit(solution)/shard_map/ppermute | solution.py:41
  55.8 47.7 %copy-start = (bf16[512,4096]{1,0:T(8,128)(2,1)}, bf16[512,4096]{1,0:T(8,128)(2,1)S(1)}, u32[]{:S(2)}) copy-start(bf16[512,4096]{1,0:T(8,128)(2,1)S(1)} %get-tuple-element.59.x_ref.refs_1_) | copy-start | bytes 12582916
  55.8 10.6 %collective-permute-start.3 = (f32[2,128,32]{2,1,0:T(8,128)S(1)}, f32[2,128,32]{2,1,0:T(8,128)S(1)}, u32[]{:S(2)}, u32[]{:S(2)}) collective-permute-start(f32[2,128,32]{2,1,0:T(8,128)S(1)} %pad_maximum_fusion), channel_id=1, source_target_pairs={{0,1},{1,0},{2,3},{3,2},{4,5},{5,4},{6,7},{7,6},{8,9},{9,8},{10,11... | collective-permute-start | bytes 98312 | tf_op jit(solution)/shard_map/ppermute | solution.py:41
  74.3 4.6 %collective-permute-start.5 = (bf16[128,3584]{1,0:T(8,128)(2,1)S(1)}, bf16[128,3584]{1,0:T(8,128)(2,1)S(1)}, u32[]{:S(2)}, u32[]{:S(2)}) collective-permute-start(bf16[128,3584]{1,0:T(8,128)(2,1)S(1)} %get-tuple-element.66), channel_id=1, source_target_pairs={{0,1},{1,0},{2,3},{3,2},{4,5},{5,4},{6,7},{7,6},{8,9},{9,8},{10,11... | collective-permute-start | bytes 2752520 | tf_op jit(solution)/shard_map/ppermute | solution.py:41
  74.3 4.5 %collective-permute-start.6 = (f32[2,64,32]{2,1,0:T(8,128)S(1)}, f32[2,64,32]{2,1,0:T(8,128)S(1)}, u32[]{:S(2)}, u32[]{:S(2)}) collective-permute-start(f32[2,64,32]{2,1,0:T(8,128)S(1)} %slice.49), channel_id=1, source_target_pairs={{0,2},{1,3},{2,0},{3,1},{4,6},{5,7},{6,4},{7,5},{8,10},{9,11},{10,... | collective-permute-start | bytes 49160 | tf_op jit(solution)/shard_map/ppermute | solution.py:41
  79.1 12.1 %collective-permute-start.7 = (bf16[64,3584]{1,0:T(8,128)(2,1)S(1)}, bf16[64,3584]{1,0:T(8,128)(2,1)S(1)}, u32[]{:S(2)}, u32[]{:S(2)}) collective-permute-start(bf16[64,3584]{1,0:T(8,128)(2,1)S(1)} %share_sums.7.refs_0_), channel_id=1, source_target_pairs={{0,2},{1,3},{2,0},{3,1},{4,6},{5,7},{6,4},{7,5},{8,10},{9,11},{10,... | collective-permute-start | bytes 1376264 | tf_op jit(solution)/shard_map/ppermute | solution.py:41
  91.6 11.8 %collective-permute-start.8 = (bf16[64,3584]{1,0:T(8,128)(2,1)S(1)}, bf16[64,3584]{1,0:T(8,128)(2,1)S(1)}, u32[]{:S(2)}, u32[]{:S(2)}) collective-permute-start(bf16[64,3584]{1,0:T(8,128)(2,1)S(1)} %share_sums.8.refs_3_), channel_id=1, source_target_pairs={{0,16},{16,0},{1,17},{17,1},{2,18},{18,2},{3,19},{19,3},{4,20},{20... | collective-permute-start | bytes 1376264 | tf_op jit(solution)/shard_map/ppermute | solution.py:41
  108.9 10.5 %collective-permute-start.9 = (bf16[256,3072]{1,0:T(8,128)(2,1)}, bf16[256,3072]{1,0:T(8,128)(2,1)}, u32[]{:S(2)}, u32[]{:S(2)}) collective-permute-start(bf16[256,3072]{1,0:T(8,128)(2,1)} %get-tuple-element.73), channel_id=1, source_target_pairs={{0,1},{1,0},{2,3},{3,2},{4,5},{5,4},{6,7},{7,6},{8,9},{9,8},{10,11... | collective-permute-start | bytes 4718600 | tf_op jit(solution)/shard_map/ppermute | solution.py:41
  118.2 54.3 %copy-start.12 = (bf16[64,3584]{1,0:T(8,128)(2,1)}, bf16[64,3584]{1,0:T(8,128)(2,1)S(1)}, u32[]{:S(2)}) copy-start(bf16[64,3584]{1,0:T(8,128)(2,1)S(1)} %get-tuple-element.77.refs_0_.refs_1_) | copy-start | bytes 1376260
  118.2 13.0 %collective-permute-start.13 = (bf16[64,3584]{1,0:T(8,128)(2,1)S(1)}, bf16[64,3584]{1,0:T(8,128)(2,1)S(1)}, u32[]{:S(2)}, u32[]{:S(2)}) collective-permute-start(bf16[64,3584]{1,0:T(8,128)(2,1)S(1)} %get-tuple-element.76), channel_id=1, source_target_pairs={{0,16},{16,0},{1,17},{17,1},{2,18},{18,2},{3,19},{19,3},{4,20},{20... | collective-permute-start | bytes 1376264 | tf_op jit(solution)/shard_map/ppermute | solution.py:41
  120.7 12.0 %collective-permute-start.11 = (bf16[64,3072]{1,0:T(8,128)(2,1)S(1)}, bf16[64,3072]{1,0:T(8,128)(2,1)S(1)}, u32[]{:S(2)}, u32[]{:S(2)}) collective-permute-start(bf16[64,3072]{1,0:T(8,128)(2,1)S(1)} %get-tuple-element.75), channel_id=1, source_target_pairs={{0,2},{1,3},{2,0},{3,1},{4,6},{5,7},{6,4},{7,5},{8,10},{9,11},{10,... | collective-permute-start | bytes 1179656 | tf_op jit(solution)/shard_map/ppermute | solution.py:41
  122.3 20.3 %collective-permute-start.14 = (bf16[64,3584]{1,0:T(8,128)(2,1)S(1)}, bf16[64,3584]{1,0:T(8,128)(2,1)S(1)}, u32[]{:S(2)}, u32[]{:S(2)}) collective-permute-start(bf16[64,3584]{1,0:T(8,128)(2,1)S(1)} %get-tuple-element.77.refs_0_.refs_1_), channel_id=1, source_target_pairs={{0,2},{1,3},{2,0},{3,1},{4,6},{5,7},{6,4},{7,5},{8,10},{9,11},{10,... | collective-permute-start | bytes 1376264 | tf_op jit(solution)/shard_map/ppermute | solution.py:41
  132.9 39.6 %copy-start.5 = (bf16[64,3584]{1,0:T(8,128)(2,1)}, bf16[64,3584]{1,0:T(8,128)(2,1)S(1)}, u32[]{:S(2)}) copy-start(bf16[64,3584]{1,0:T(8,128)(2,1)S(1)} %share_sums.11.refs_4_.refs_7_.refs_5_) | copy-start | bytes 1376260
  132.9 18.8 %collective-permute-start.17 = (bf16[64,3584]{1,0:T(8,128)(2,1)S(1)}, bf16[64,3584]{1,0:T(8,128)(2,1)S(1)}, u32[]{:S(2)}, u32[]{:S(2)}) collective-permute-start(bf16[64,3584]{1,0:T(8,128)(2,1)S(1)} %share_sums.11.refs_4_.refs_7_.refs_5_), channel_id=1, source_target_pairs={{0,2},{1,3},{2,0},{3,1},{4,6},{5,7},{6,4},{7,5},{8,10},{9,11},{10,... | collective-permute-start | bytes 1376264 | tf_op jit(solution)/shard_map/ppermute | solution.py:41
  134.5 19.9 %collective-permute-start.15 = (bf16[64,3584]{1,0:T(8,128)(2,1)S(1)}, bf16[64,3584]{1,0:T(8,128)(2,1)S(1)}, u32[]{:S(2)}, u32[]{:S(2)}) collective-permute-start(bf16[64,3584]{1,0:T(8,128)(2,1)S(1)} %get-tuple-element.77.refs_0_.refs_1_), channel_id=1, source_target_pairs={{0,1},{1,0},{2,3},{3,2},{4,5},{5,4},{6,7},{7,6},{8,9},{9,8},{10,11... | collective-permute-start | bytes 1376264 | tf_op jit(solution)/shard_map/ppermute | solution.py:41
  142.5 29.9 %copy-start.15 = (bf16[64,3584]{1,0:T(8,128)(2,1)}, bf16[64,3584]{1,0:T(8,128)(2,1)S(1)}, u32[]{:S(2)}) copy-start(bf16[64,3584]{1,0:T(8,128)(2,1)S(1)} %collective-permute-done.14.refs_1_.refs_2_) | copy-start | bytes 1376260
  142.5 12.8 %collective-permute-start.16 = (bf16[64,3584]{1,0:T(8,128)(2,1)S(1)}, bf16[64,3584]{1,0:T(8,128)(2,1)S(1)}, u32[]{:S(2)}, u32[]{:S(2)}) collective-permute-start(bf16[64,3584]{1,0:T(8,128)(2,1)S(1)} %collective-permute-done.14.refs_1_.refs_2_), channel_id=1, source_target_pairs={{0,1},{1,0},{2,3},{3,2},{4,5},{5,4},{6,7},{7,6},{8,9},{9,8},{10,11... | collective-permute-start | bytes 1376264 | tf_op jit(solution)/shard_map/ppermute | solution.py:41
  142.5 12.9 %collective-permute-start.18 = (bf16[64,3584]{1,0:T(8,128)(2,1)S(1)}, bf16[64,3584]{1,0:T(8,128)(2,1)S(1)}, u32[]{:S(2)}, u32[]{:S(2)}) collective-permute-start(bf16[64,3584]{1,0:T(8,128)(2,1)S(1)} %share_sums.11.refs_4_.refs_7_.refs_5_), channel_id=1, source_target_pairs={{0,1},{1,0},{2,3},{3,2},{4,5},{5,4},{6,7},{7,6},{8,9},{9,8},{10,11... | collective-permute-start | bytes 1376264 | tf_op jit(solution)/shard_map/ppermute | solution.py:41
  151.7 20.8 %copy-start.18 = (bf16[64,3584]{1,0:T(8,128)(2,1)}, bf16[64,3584]{1,0:T(8,128)(2,1)S(1)}, u32[]{:S(2)}) copy-start(bf16[64,3584]{1,0:T(8,128)(2,1)S(1)} %collective-permute-done.17.refs_5_.refs_6_) | copy-start | bytes 1376260
  151.7 3.7 collective-permute-start.19
  151.7 12.8 %collective-permute-start.10 = (bf16[64,3072]{1,0:T(8,128)(2,1)S(1)}, bf16[64,3072]{1,0:T(8,128)(2,1)S(1)}, u32[]{:S(2)}, u32[]{:S(2)}) collective-permute-start(bf16[64,3072]{1,0:T(8,128)(2,1)S(1)} %get-tuple-element.74), channel_id=1, source_target_pairs={{0,2},{1,3},{2,0},{3,1},{4,6},{5,7},{6,4},{7,5},{8,10},{9,11},{10,... | collective-permute-start | bytes 1179656 | tf_op jit(solution)/shard_map/ppermute | solution.py:41
  154.4 18.1 %copy-start.21 = (bf16[64,3584]{1,0:T(8,128)(2,1)}, bf16[64,3584]{1,0:T(8,128)(2,1)S(1)}, u32[]{:S(2)}) copy-start(bf16[64,3584]{1,0:T(8,128)(2,1)S(1)} %collective-permute-done.15.refs_2_.refs_3_) | copy-start | bytes 1376260
  154.4 11.3 %collective-permute-start.12 = (bf16[64,3072]{1,0:T(8,128)(2,1)S(1)}, bf16[64,3072]{1,0:T(8,128)(2,1)S(1)}, u32[]{:S(2)}, u32[]{:S(2)}) collective-permute-start(bf16[64,3072]{1,0:T(8,128)(2,1)S(1)} %share_sums.10.refs_9_), channel_id=1, source_target_pairs={{0,16},{16,0},{1,17},{17,1},{2,18},{18,2},{3,19},{19,3},{4,20},{20... | collective-permute-start | bytes 1179656 | tf_op jit(solution)/shard_map/ppermute | solution.py:41
  171.0 11.9 %collective-permute-start.23 = (bf16[64,3072]{1,0:T(8,128)(2,1)S(1)}, bf16[64,3072]{1,0:T(8,128)(2,1)S(1)}, u32[]{:S(2)}, u32[]{:S(2)}) collective-permute-start(bf16[64,3072]{1,0:T(8,128)(2,1)S(1)} %get-tuple-element.79), channel_id=1, source_target_pairs={{0,16},{16,0},{1,17},{17,1},{2,18},{18,2},{3,19},{19,3},{4,20},{20... | collective-permute-start | bytes 1179656 | tf_op jit(solution)/shard_map/ppermute | solution.py:41
  172.0 13.0 %collective-permute-start.20 = (bf16[64,3072]{1,0:T(8,128)(2,1)S(1)}, bf16[64,3072]{1,0:T(8,128)(2,1)}, u32[]{:S(2)}, u32[]{:S(2)}) collective-permute-start(bf16[64,3072]{1,0:T(8,128)(2,1)S(1)} %get-tuple-element.78.refs_9_.refs_0_), channel_id=1, source_target_pairs={{0,2},{1,3},{2,0},{3,1},{4,6},{5,7},{6,4},{7,5},{8,10},{9,11},{10,... | collective-permute-start | bytes 1179656 | tf_op jit(solution)/shard_map/ppermute | solution.py:41
  182.9 10.1 %collective-permute-start.24 = (bf16[64,3072]{1,0:T(8,128)(2,1)S(1)}, bf16[64,3072]{1,0:T(8,128)(2,1)}, u32[]{:S(2)}, u32[]{:S(2)}) collective-permute-start(bf16[64,3072]{1,0:T(8,128)(2,1)S(1)} %collective-permute-done.23.refs_9_.refs_4_.refs_13_), channel_id=1, source_target_pairs={{0,2},{1,3},{2,0},{3,1},{4,6},{5,7},{6,4},{7,5},{8,10},{9,11},{10,... | collective-permute-start | bytes 1179656 | tf_op jit(solution)/shard_map/ppermute | solution.py:41
  184.4 23.2 %collective-permute-start.21 = (bf16[64,3072]{1,0:T(8,128)(2,1)S(1)}, bf16[64,3072]{1,0:T(8,128)(2,1)}, u32[]{:S(2)}, u32[]{:S(2)}) collective-permute-start(bf16[64,3072]{1,0:T(8,128)(2,1)S(1)} %get-tuple-element.78.refs_9_.refs_0_), channel_id=1, source_target_pairs={{0,1},{1,0},{2,3},{3,2},{4,5},{5,4},{6,7},{7,6},{8,9},{9,8},{10,11... | collective-permute-start | bytes 1179656 | tf_op jit(solution)/shard_map/ppermute | solution.py:41
  184.4 23.2 %collective-permute-start.25 = (bf16[64,3072]{1,0:T(8,128)(2,1)S(1)}, bf16[64,3072]{1,0:T(8,128)(2,1)}, u32[]{:S(2)}, u32[]{:S(2)}) collective-permute-start(bf16[64,3072]{1,0:T(8,128)(2,1)S(1)} %collective-permute-done.23.refs_9_.refs_4_.refs_13_), channel_id=1, source_target_pairs={{0,1},{1,0},{2,3},{3,2},{4,5},{5,4},{6,7},{7,6},{8,9},{9,8},{10,11... | collective-permute-start | bytes 1179656 | tf_op jit(solution)/shard_map/ppermute | solution.py:41
  184.9 22.7 %collective-permute-start.22 = (bf16[64,3072]{1,0:T(8,128)(2,1)}, bf16[64,3072]{1,0:T(8,128)(2,1)}, u32[]{:S(2)}, u32[]{:S(2)}) collective-permute-start(bf16[64,3072]{1,0:T(8,128)(2,1)} %collective-permute-done.20.refs_1_.refs_10_), channel_id=1, source_target_pairs={{0,1},{1,0},{2,3},{3,2},{4,5},{5,4},{6,7},{7,6},{8,9},{9,8},{10,11... | collective-permute-start | bytes 1179656 | tf_op jit(solution)/shard_map/ppermute | solution.py:41
  192.9 14.7 %collective-permute-start.26 = (bf16[64,3072]{1,0:T(8,128)(2,1)}, bf16[64,3072]{1,0:T(8,128)(2,1)}, u32[]{:S(2)}, u32[]{:S(2)}) collective-permute-start(bf16[64,3072]{1,0:T(8,128)(2,1)} %collective-permute-done.24.refs_5_.refs_14_), channel_id=1, source_target_pairs={{0,1},{1,0},{2,3},{3,2},{4,5},{5,4},{6,7},{7,6},{8,9},{9,8},{10,11... | collective-permute-start | bytes 1179656 | tf_op jit(solution)/shard_map/ppermute | solution.py:41
  216.8 23.4 %collective-permute-start.27 = (bf16[256,1536]{1,0:T(8,128)(2,1)}, bf16[256,1536]{1,0:T(8,128)(2,1)}, u32[]{:S(2)}, u32[]{:S(2)}) collective-permute-start(bf16[256,1536]{1,0:T(8,128)(2,1)} %get-tuple-element.83), channel_id=1, source_target_pairs={{0,16},{16,0},{1,17},{17,1},{2,18},{18,2},{3,19},{19,3},{4,20},{20... | collective-permute-start | bytes 2359304 | tf_op jit(solution)/shard_map/ppermute | solution.py:41
  218.0 19.0 %copy-start.66 = (bf16[2,64,32]{2,1,0:T(8,128)(2,1)S(1)}, bf16[2,64,32]{2,1,0:T(8,128)(2,1)}, u32[]{:S(2)}) copy-start(bf16[2,64,32]{2,1,0:T(8,128)(2,1)} %copy-done.65) | copy-start | bytes 24580
  228.2 42.1 %collective-permute-start.40 = (bf16[256,1536]{1,0:T(8,128)(2,1)}, bf16[256,1536]{1,0:T(8,128)(2,1)}, u32[]{:S(2)}, u32[]{:S(2)}) collective-permute-start(bf16[256,1536]{1,0:T(8,128)(2,1)} %get-tuple-element.94), channel_id=1, source_target_pairs={{0,16},{16,0},{1,17},{17,1},{2,18},{18,2},{3,19},{19,3},{4,20},{20... | collective-permute-start | bytes 2359304 | tf_op jit(solution)/shard_map/ppermute | solution.py:41
  230.3 4.0 %collective-permute-start.31 = (f32[64,33]{1,0:T(8,128)S(1)}, f32[64,33]{1,0:T(8,128)S(1)}, u32[]{:S(2)}, u32[]{:S(2)}) collective-permute-start(f32[64,33]{1,0:T(8,128)S(1)} %add.210), channel_id=1, source_target_pairs={{0,4},{4,0},{8,12},{12,8},{1,5},{5,1},{9,13},{13,9},{2,6},{6,2},{1... | collective-permute-start | bytes 25352 | tf_op jit(solution)/shard_map/ppermute | solution.py:41
  234.3 4.8 %collective-permute-start.32 = (f32[64,33]{1,0:T(8,128)S(1)}, f32[64,33]{1,0:T(8,128)S(1)}, u32[]{:S(2)}, u32[]{:S(2)}) collective-permute-start(f32[64,33]{1,0:T(8,128)S(1)} %add.211), channel_id=1, source_target_pairs={{0,8},{4,12},{8,0},{12,4},{1,9},{5,13},{9,1},{13,5},{2,10},{6,14},... | collective-permute-start | bytes 25352 | tf_op jit(solution)/shard_map/ppermute | solution.py:41
  239.1 15.4 %collective-permute-start.33 = (f32[64,33]{1,0:T(8,128)S(1)}, f32[64,33]{1,0:T(8,128)S(1)}, u32[]{:S(2)}, u32[]{:S(2)}) collective-permute-start(f32[64,33]{1,0:T(8,128)S(1)} %add.212), channel_id=1, source_target_pairs={{0,16},{16,0},{1,17},{17,1},{2,18},{18,2},{3,19},{19,3},{4,20},{20... | collective-permute-start | bytes 25352 | tf_op jit(solution)/shard_map/ppermute | solution.py:41
  243.0 27.2 %collective-permute-start.50 = (bf16[2,64,16]{2,1,0:T(8,128)(2,1)}, bf16[2,64,16]{2,1,0:T(8,128)(2,1)}, u32[]{:S(2)}, u32[]{:S(2)}) collective-permute-start(bf16[2,64,16]{2,1,0:T(8,128)(2,1)} %slice_select_fusion), channel_id=1, source_target_pairs={{0,2},{1,3},{2,0},{3,1},{4,6},{5,7},{6,4},{7,5},{8,10},{9,11},{10,... | collective-permute-start | bytes 12296 | tf_op jit(solution)/shard_map/ppermute | solution.py:41
  255.4 22.7 %collective-permute-start.34 = (f32[2,64,33]{2,1,0:T(8,128)S(1)}, f32[2,64,33]{2,1,0:T(8,128)}, u32[]{:S(2)}, u32[]{:S(2)}) collective-permute-start(f32[2,64,33]{2,1,0:T(8,128)S(1)} %pad_maximum_fusion.2), channel_id=1, source_target_pairs={{0,2},{1,3},{2,0},{3,1},{4,6},{5,7},{6,4},{7,5},{8,10},{9,11},{10,... | collective-permute-start | bytes 50696 | tf_op jit(solution)/shard_map/ppermute | solution.py:41
  257.0 23.7 %collective-permute-start.29 = (bf16[128,1536]{1,0:T(8,128)(2,1)}, bf16[128,1536]{1,0:T(8,128)(2,1)}, u32[]{:S(2)}, u32[]{:S(2)}) collective-permute-start(bf16[128,1536]{1,0:T(8,128)(2,1)} %get-tuple-element.113.refs_11_), channel_id=1, source_target_pairs={{0,4},{4,0},{8,12},{12,8},{1,5},{5,1},{9,13},{13,9},{2,6},{6,2},{1... | collective-permute-start | bytes 1179656 | tf_op jit(solution)/shard_map/ppermute | solution.py:41
  269.1 29.8 %collective-permute-start.28 = (bf16[256,1024]{1,0:T(8,128)(2,1)}, bf16[256,1024]{1,0:T(8,128)(2,1)}, u32[]{:S(2)}, u32[]{:S(2)}) collective-permute-start(bf16[256,1024]{1,0:T(8,128)(2,1)} %get-tuple-element.85), channel_id=1, source_target_pairs={{0,16},{16,0},{1,17},{17,1},{2,18},{18,2},{3,19},{19,3},{4,20},{20... | collective-permute-start | bytes 1572872 | tf_op jit(solution)/shard_map/ppermute | solution.py:41
  271.2 3.4 collective-permute-start.51
  274.2 20.4 %collective-permute-start.41 = (bf16[128,1536]{1,0:T(8,128)(2,1)}, bf16[128,1536]{1,0:T(8,128)(2,1)}, u32[]{:S(2)}, u32[]{:S(2)}) collective-permute-start(bf16[128,1536]{1,0:T(8,128)(2,1)} %get-tuple-element.110), channel_id=1, source_target_pairs={{0,4},{4,0},{8,12},{12,8},{1,5},{5,1},{9,13},{13,9},{2,6},{6,2},{1... | collective-permute-start | bytes 1179656 | tf_op jit(solution)/shard_map/ppermute | solution.py:41
  279.2 1.3 collective-permute-start.35
  282.0 29.7 %copy-start.50 = (f32[256,1024]{1,0:T(8,128)S(1)}, f32[256,1024]{1,0:T(8,128)}, u32[]{:S(2)}) copy-start(f32[256,1024]{1,0:T(8,128)} %copy-done.49) | copy-start | bytes 3145732
  282.0 12.1 %collective-permute-start.30 = (bf16[64,1536]{1,0:T(8,128)(2,1)S(1)}, bf16[64,1536]{1,0:T(8,128)(2,1)S(1)}, u32[]{:S(2)}, u32[]{:S(2)}) collective-permute-start(bf16[64,1536]{1,0:T(8,128)(2,1)S(1)} %get-tuple-element.118), channel_id=1, source_target_pairs={{0,8},{4,12},{8,0},{12,4},{1,9},{5,13},{9,1},{13,5},{2,10},{6,14},... | collective-permute-start | bytes 589832 | tf_op jit(solution)/shard_map/ppermute | solution.py:41
  294.5 19.3 %copy-start.56 = (f32[16,3072]{1,0:T(8,128)S(1)}, f32[16,3072]{1,0:T(8,128)}, u32[]{:S(2)}) copy-start(f32[16,3072]{1,0:T(8,128)} %copy-done.55) | copy-start | bytes 589828
  294.5 19.3 %copy-start.61 = (f32[16,6656]{1,0:T(8,128)S(1)}, f32[16,6656]{1,0:T(8,128)}, u32[]{:S(2)}) copy-start(f32[16,6656]{1,0:T(8,128)} %constant_dynamic-update-slice_fusion.1) | copy-start | bytes 1277956
  294.5 17.2 %collective-permute-start.36 = (bf16[64,1536]{1,0:T(8,128)(2,1)S(1)}, bf16[64,1536]{1,0:T(8,128)(2,1)S(1)}, u32[]{:S(2)}, u32[]{:S(2)}) collective-permute-start(bf16[64,1536]{1,0:T(8,128)(2,1)S(1)} %get-tuple-element.89.refs_0_), channel_id=1, source_target_pairs={{0,8},{4,12},{8,0},{12,4},{1,9},{5,13},{9,1},{13,5},{2,10},{6,14},... | collective-permute-start | bytes 589832 | tf_op jit(solution)/shard_map/ppermute | solution.py:41
  296.0 25.8 %collective-permute-start.42 = (bf16[64,1536]{1,0:T(8,128)(2,1)S(1)}, bf16[64,1536]{1,0:T(8,128)(2,1)S(1)}, u32[]{:S(2)}, u32[]{:S(2)}) collective-permute-start(bf16[64,1536]{1,0:T(8,128)(2,1)S(1)} %get-tuple-element.116), channel_id=1, source_target_pairs={{0,8},{4,12},{8,0},{12,4},{1,9},{5,13},{9,1},{13,5},{2,10},{6,14},... | collective-permute-start | bytes 589832 | tf_op jit(solution)/shard_map/ppermute | solution.py:41
  313.8 11.7 %collective-permute-start.37 = (bf16[128,1024]{1,0:T(8,128)(2,1)}, bf16[128,1024]{1,0:T(8,128)(2,1)}, u32[]{:S(2)}, u32[]{:S(2)}) collective-permute-start(bf16[128,1024]{1,0:T(8,128)(2,1)} %get-tuple-element.114), channel_id=1, source_target_pairs={{0,4},{4,0},{8,12},{12,8},{1,5},{5,1},{9,13},{13,9},{2,6},{6,2},{1... | collective-permute-start | bytes 786440 | tf_op jit(solution)/shard_map/ppermute | solution.py:41
  314.6 18.5 %collective-permute-start.52 = (bf16[16,6656]{1,0:T(8,128)(2,1)}, bf16[16,6656]{1,0:T(8,128)(2,1)S(1)}, u32[]{:S(2)}, u32[]{:S(2)}) collective-permute-start(bf16[16,6656]{1,0:T(8,128)(2,1)} %convert_element_type.85), channel_id=1, source_target_pairs={{0,16},{16,0},{1,17},{17,1},{2,18},{18,2},{3,19},{19,3},{4,20},{20... | collective-permute-start | bytes 638984 | tf_op jit(solution)/shard_map/ppermute | solution.py:41
  315.5 17.5 %collective-permute-start.38 = (bf16[64,1536]{1,0:T(8,128)(2,1)S(1)}, bf16[64,1536]{1,0:T(8,128)(2,1)S(1)}, u32[]{:S(2)}, u32[]{:S(2)}) collective-permute-start(bf16[64,1536]{1,0:T(8,128)(2,1)S(1)} %collective-permute-done.36.refs_1_), channel_id=1, source_target_pairs={{0,4},{4,0},{8,12},{12,8},{1,5},{5,1},{9,13},{13,9},{2,6},{6,2},{1... | collective-permute-start | bytes 589832 | tf_op jit(solution)/shard_map/ppermute | solution.py:41
  321.7 61.6 %collective-permute-start.49 = (bf16[64,1536]{1,0:T(8,128)(2,1)S(1)}, bf16[64,1536]{1,0:T(8,128)(2,1)S(1)}, u32[]{:S(2)}, u32[]{:S(2)}) collective-permute-start(bf16[64,1536]{1,0:T(8,128)(2,1)S(1)} %get-tuple-element.89.refs_0_), channel_id=1, source_target_pairs={{0,4},{4,0},{8,12},{12,8},{1,5},{5,1},{9,13},{13,9},{2,6},{6,2},{1... | collective-permute-start | bytes 589832 | tf_op jit(solution)/shard_map/ppermute | solution.py:41
  321.8 59.5 %copy-start.63 = (f32[16,6656]{1,0:T(8,128)S(1)}, f32[16,6656]{1,0:T(8,128)}, u32[]{:S(2)}) copy-start(f32[16,6656]{1,0:T(8,128)} %copy-done.62) | copy-start | bytes 1277956
  322.0 11.8 %collective-permute-start.46 = (bf16[64,1536]{1,0:T(8,128)(2,1)S(1)}, bf16[64,1536]{1,0:T(8,128)(2,1)S(1)}, u32[]{:S(2)}, u32[]{:S(2)}) collective-permute-start(bf16[64,1536]{1,0:T(8,128)(2,1)S(1)} %get-tuple-element.100.refs_0_), channel_id=1, source_target_pairs={{0,8},{4,12},{8,0},{12,4},{1,9},{5,13},{9,1},{13,5},{2,10},{6,14},... | collective-permute-start | bytes 589832 | tf_op jit(solution)/shard_map/ppermute | solution.py:41
  325.4 59.4 %collective-permute-start.47 = (bf16[64,1536]{1,0:T(8,128)(2,1)S(1)}, bf16[64,1536]{1,0:T(8,128)(2,1)S(1)}, u32[]{:S(2)}, u32[]{:S(2)}) collective-permute-start(bf16[64,1536]{1,0:T(8,128)(2,1)S(1)} %get-tuple-element.100.refs_0_), channel_id=1, source_target_pairs={{0,4},{4,0},{8,12},{12,8},{1,5},{5,1},{9,13},{13,9},{2,6},{6,2},{1... | collective-permute-start | bytes 589832 | tf_op jit(solution)/shard_map/ppermute | solution.py:41
  333.1 8.0 %collective-permute-start.39 = (bf16[64,1024]{1,0:T(8,128)(2,1)S(1)}, bf16[64,1024]{1,0:T(8,128)(2,1)S(1)}, u32[]{:S(2)}, u32[]{:S(2)}) collective-permute-start(bf16[64,1024]{1,0:T(8,128)(2,1)S(1)} %get-tuple-element.91), channel_id=1, source_target_pairs={{0,8},{4,12},{8,0},{12,4},{1,9},{5,13},{9,1},{13,5},{2,10},{6,14},... | collective-permute-start | bytes 393224 | tf_op jit(solution)/shard_map/ppermute | solution.py:41
  333.9 51.0 %collective-permute-start.48 = (bf16[64,1536]{1,0:T(8,128)(2,1)S(1)}, bf16[64,1536]{1,0:T(8,128)(2,1)S(1)}, u32[]{:S(2)}, u32[]{:S(2)}) collective-permute-start(bf16[64,1536]{1,0:T(8,128)(2,1)S(1)} %collective-permute-done.46.refs_1_), channel_id=1, source_target_pairs={{0,4},{4,0},{8,12},{12,8},{1,5},{5,1},{9,13},{13,9},{2,6},{6,2},{1... | collective-permute-start | bytes 589832 | tf_op jit(solution)/shard_map/ppermute | solution.py:41
  341.3 37.9 %collective-permute-start.43 = (bf16[64,1024]{1,0:T(8,128)(2,1)S(1)}, bf16[64,1024]{1,0:T(8,128)(2,1)S(1)}, u32[]{:S(2)}, u32[]{:S(2)}) collective-permute-start(bf16[64,1024]{1,0:T(8,128)(2,1)S(1)} %get-tuple-element.98.refs_0_), channel_id=1, source_target_pairs={{0,8},{4,12},{8,0},{12,4},{1,9},{5,13},{9,1},{13,5},{2,10},{6,14},... | collective-permute-start | bytes 393224 | tf_op jit(solution)/shard_map/ppermute | solution.py:41
  379.2 7.1 %collective-permute-start.44 = (bf16[64,1024]{1,0:T(8,128)(2,1)S(1)}, bf16[64,1024]{1,0:T(8,128)(2,1)S(1)}, u32[]{:S(2)}, u32[]{:S(2)}) collective-permute-start(bf16[64,1024]{1,0:T(8,128)(2,1)S(1)} %get-tuple-element.98.refs_0_), channel_id=1, source_target_pairs={{0,4},{4,0},{8,12},{12,8},{1,5},{5,1},{9,13},{13,9},{2,6},{6,2},{1... | collective-permute-start | bytes 393224 | tf_op jit(solution)/shard_map/ppermute | solution.py:41
  379.2 7.1 %collective-permute-start.45 = (bf16[64,1024]{1,0:T(8,128)(2,1)S(1)}, bf16[64,1024]{1,0:T(8,128)(2,1)S(1)}, u32[]{:S(2)}, u32[]{:S(2)}) collective-permute-start(bf16[64,1024]{1,0:T(8,128)(2,1)S(1)} %collective-permute-done.43.refs_1_), channel_id=1, source_target_pairs={{0,4},{4,0},{8,12},{12,8},{1,5},{5,1},{9,13},{13,9},{2,6},{6,2},{1... | collective-permute-start | bytes 393224 | tf_op jit(solution)/shard_map/ppermute | solution.py:41
  (61 other events, 415.2 us)

commit v6 on v5

--- a/solution.py
+++ b/solution.py
@@ -8,7 +8,7 @@
 MODEL_WIDTH = 16384
 ADAPTER_SCALE = 0.5
 VMEM_MIB = 12
-MATMUL_VMEM_MIB = 18
+MATMUL_VMEM_MIB = 24
 COST_SHARE = 0.01
 
 F32 = jnp.float32
@@ -281,7 +281,9 @@
     return pl.pallas_call(
         kernel,
         grid=(tiles,),
-        in_specs=[RESIDENT] * len(pieces)
+        in_specs=[
+            pl.BlockSpec(g.shape, lambda i: (0, 0), pipeline_mode=pl.Buffered(1)) for g in pieces
+        ]
         + [
             pl.BlockSpec(
                 (pl.Element(1), pl.Element(tile), pl.Element(hidden)),
@@ -298,7 +300,7 @@
     )(*pieces, weights, *(() if base is None else (base,)), *after)
 
 
-def adapter_products(low, groups):
+def adapter_products(low, groups, after=()):
     rank = low.shape[0]
 
     def kernel(*refs):
@@ -315,23 +317,23 @@
     return pl.pallas_call(
         kernel,
         grid=(1,),
-        in_specs=[RESIDENT] * (1 + len(operands)),
+        in_specs=[pl.BlockSpec(x.shape, lambda i: (0, 0)) for x in [low] + operands] + [ANY] * len(after),
         out_specs=[pl.BlockSpec((rank, w), lambda i: (0, 0)) for w in widths],
         out_shape=[jax.ShapeDtypeStruct((rank, w), F32) for w in widths],
         compiler_params=params(),
         cost_estimate=cost(2 * rank * low.shape[1] * sum(widths), 2 * low.shape[1] * sum(widths)),
         name="adapter_products",
-    )(low, *operands)
-
-
-def assemble(pieces, places, block, tokens, width, columns, into=None):
+    )(low, *operands, *after)
+
+
+def assemble(pieces, places, block, rows, tokens, width, columns, into=None):
     chunk = pieces[0].shape[1]
 
     def kernel(place_ref, *refs):
         out_ref = refs[-1]
         i = 0
         for ref in refs[: len(pieces)]:
-            for r in range(0, ref.shape[0], block):
+            for r in range(0, rows, block):
                 out_ref[pl.ds(pl.multiple_of(place_ref[i], block), block), :] = ref[r : r + block, :]
                 i += 1
 
@@ -352,13 +354,14 @@
     )(places, *pieces, *((into,) if n_into else ()))
 
 
-def finish(parts, stream, stats, back, down, steering, gain, columns):
+def finish(parts, stream, stats, back, down, steering, gain, columns, after=()):
     rows = stream.shape[0]
     width = parts[0].shape[1]
 
     def kernel(*refs):
         part_refs = refs[: len(parts)]
-        x_ref, s_ref, back_ref, down_ref, steer_ref, gain_ref, out_ref, sum_ref = refs[len(parts) :]
+        x_ref, s_ref, back_ref, down_ref, steer_ref, gain_ref = refs[len(parts) : len(parts) + 6]
+        out_ref, sum_ref = refs[-2:]
         total = part_refs[0][...].astype(F32)
         for ref in part_refs[1:]:
             total = total + ref[...].astype(F32)
@@ -380,13 +383,14 @@
             across(down.shape[0]),
             across(1),
             across(1),
-        ],
+        ]
+        + [ANY] * len(after),
         out_specs=[pl.BlockSpec((rows, width), lambda i: (0, 0)), pl.BlockSpec((1, width), lambda i: (0, 0))],
         out_shape=[jax.ShapeDtypeStruct((rows, width), BF16), jax.ShapeDtypeStruct((1, width), F32)],
         compiler_params=params(),
         cost_estimate=cost(2 * rows * width * down.shape[0], 10 * rows * width),
         name="finish",
-    )(*parts, stream, stats, back, down, steering.reshape(1, -1), gain.reshape(1, -1))
+    )(*parts, stream, stats, back, down, steering.reshape(1, -1), gain.reshape(1, -1), *after)
 
 
 def make_local(dp, hid, ffn):
@@ -453,6 +457,18 @@
         steps = [(0, 3), (3, 3), (6, 2)] if tiles == 8 else split_tiles(tiles, 3)
         acts, others, grads = [], [], []
 
+        def gradients(c, after):
+            mine_grad, other_grad, back_part = gated_gradients(
+                d, acts[c], others[c], cotangent, chunks[c][0] * tile, low_own, up, own, after
+            )
+            return back_part, mine_grad, swap(other_grad, "dp", dp, 1)
+
+        def spread(g):
+            blocks = [g]
+            for bit in reversed(range(bits_of(hid))):
+                blocks += [swap(x, "hid", hid, 1 << bit) for x in blocks]
+            return blocks
+
         n = chunks[0][1]
         peer_parts = forward(
             peer_normed, 0, (0, (n + 1) // 2, n), (lambda t: (own_send,), lambda t: (low_steps[0], own_got))
@@ -469,34 +485,21 @@
 
         n = chunks[1][1]
         first_send = peer_send
+        first_half_done = []
+
+        def first_gradients(token):
+            more, mine_grad, peer_grad = gradients(0, (token,))
+            own_pieces, peer_pieces = spread(mine_grad), spread(peer_grad)
+            grads.append(own_pieces + peer_pieces)
+            first_half_done.append(more)
+            return peer_grad, own_pieces[1]
+
         parts = forward(
-            normed, 1, (0, n // 3, n - 1, n), (lambda t: (first_send,), pass_on, lambda t: (others[0],))
+            normed, 1, (0, n // 3, n - 1, n), (lambda t: (first_send,), pass_on, first_gradients)
         )
         own_send, peer_send = share_sums(parts, own, 2)
         peer_got = swap(peer_send, "hid", hid, last_bit)
         own_got = swap(own_send, "hid", hid, last_bit)
-        (passed,) = share_sums(parts + [peer_got], own, 1, (), [1] * len(parts) + [0])
-        acts.append(parts + [own_got])
-        others.append(swap(passed, "dp", dp, 1))
-
-        def gradients(c, after):
-            mine_grad, other_grad, back_part = gated_gradients(
-                d, acts[c], others[c], cotangent, chunks[c][0] * tile, low_own, up, own, after
-            )
-            return back_part, mine_grad, swap(other_grad, "dp", dp, 1)
-
-        def spread(*gradients):
-            pieces = []
-            for g in gradients:
-                blocks = [g]
-                for bit in reversed(range(bits_of(hid))):
-                    blocks += [swap(x, "hid", hid, 1 << bit) for x in blocks]
-                pieces += blocks
-            grads.append(pieces)
-
-        back, mine_grad, peer_grad = gradients(0, ())
-        (peer_grad,) = share_sums([peer_grad], own, 1, (peer_got,), [0])
-        spread(mine_grad, peer_grad)
         bases = []
 
         def first_half(j, after):
@@ -507,18 +510,25 @@
                 )
             )
 
-        first_half(0, (passed,))
-        more, mine_grad, peer_grad = gradients(1, (peer_grad, bases[0]))
-        back = back + more
-        for j in range(1, len(steps)):
-            first_half(j, (mine_grad,) if j == 1 else (peer_grad,))
-            if j == 1:
-                peer_grad = ordered(peer_grad, bases[1])
-        spread(mine_grad, peer_grad)
-
+        first_half(0, (own_send,))
+        (passed,) = share_sums(parts + [peer_got], own, 1, (bases[0],), [1] * len(parts) + [0])
+        acts.append(parts + [own_got])
+        others.append(swap(passed, "dp", dp, 1))
+        more, mine_grad, peer_grad = gradients(1, ())
+        back = first_half_done[0] + more
         for bit in range(bits_of(ffn)):
             back = back + swap(back, "ffn", ffn, 1 << bit)
         back = jnp.stack([back, swap(back, "dp", dp, 1)])
+        for j in range(1, len(steps)):
+            first_half(j, (mine_grad,) if j == 1 else (peer_grad, back))
+            if j == 1:
+                (peer_grad,) = share_sums([peer_grad], own, 1, (bases[1],), [0])
+        own_pieces = spread(mine_grad)
+        grads.append(own_pieces + spread(peer_grad))
+
+        back = double(back, "hid", hid, dim=1)
+        low_mine = jnp.where(first_pair, low[:, :, :rank], low[:, :, rank:])
+        low_mine = double(low_mine, "hid", hid, dim=1).reshape(2 * tokens, rank).T
         shard = tokens // ffn
         place = reversed_bits(f, bits_of(ffn))
         products, received = [], []
@@ -534,18 +544,16 @@
 
         first_steps = []
         for j, ((first, n), base) in enumerate(zip(steps, bases)):
-            wait = (products[-1] if products else bases[-1],)
+            wait = (products[-1],) if products else tuple(bases)
             if j == 2:
                 first_steps.append(halving_step([products[0], received[0]], 0))
-                wait += (first_steps[0][1],)
+                wait += (first_steps[0][1], back, low_mine)
             keep, send = backward_matmul(
                 grads[1], weights, chunks[1][0] * tile, first, n, width_tile, base=base, base_first=first,
                 after=wait,
             )
             products.append(keep)
             received.append(swap(send, "dp", dp, 1))
-        begun = first_steps[0][1] if first_steps else products[-1]
-        back = double(ordered(back, begun), "hid", hid, dim=1)
         back_low = back[:, :, : 2 * rank].astype(BF16)
         acts_product = back[0, :, 2 * rank]
 
@@ -590,21 +598,32 @@
                     send = ordered(send, gathered[0][-1])
                 parts = [keep, swap(send, "ffn", ffn, 1 << bit)]
             result, sum_part = finish(
-                parts, stream_shard, stats_shard, back_shard, down_rows, steering, gain, first * width_tile
+                parts, stream_shard, stats_shard, back_shard, down_rows, steering, gain, first * width_tile,
+                after=tuple(gathered[j - 1][1:2] if j else ()) + tuple(gathered[j - 2][2:] if j >= 2 else ()),
             )
             sums.append(sum_part)
+            if j == len(steps) - 1:
+                sums = jnp.concatenate(sums, axis=1).reshape(-1, result.shape[1])
+                high = sums.astype(BF16)
+                low_term = (sums - high.astype(F32)).astype(BF16)
+                rows = 2 * sums.shape[0]
+                empty = jnp.zeros((-rows % 16, result.shape[1]), BF16)
+                result = jnp.concatenate([result, high, low_term, empty], axis=0)
             blocks = [result]
             for bit in reversed(range(bits_of(ffn))):
-                if j == len(steps) - 1 and bit == 0:
-                    steering_gradient = lax.psum(jnp.concatenate(sums, axis=1), ("dp", "ffn"))
-                    blocks = [ordered(x, steering_gradient) for x in blocks]
                 blocks += [swap(x, "ffn", ffn, 1 << bit) for x in blocks]
             gathered.append(blocks)
-            out = assemble(blocks, places, block, tokens, width, first * width_tile, into=out)
-
-        low_mine = jnp.where(first_pair, low[:, :, :rank], low[:, :, rank:])
-        low_mine = double(ordered(low_mine, begun), "hid", hid, dim=1).reshape(2 * tokens, rank)
-        up_mine = jnp.concatenate(adapter_products(ordered(low_mine.T, products[-1]), grads), axis=1)
+            out = assemble(blocks, places, block, shard, tokens, width, first * width_tile, into=out)
+
+        half = rows // 2
+        terms = [
+            x[shard : shard + half].astype(F32) + x[shard + half : shard + rows].astype(F32) for x in blocks
+        ]
+        while len(terms) > 1:
+            terms = [a + b for a, b in zip(terms[: len(terms) // 2], terms[len(terms) // 2 :])]
+        steering_gradient = terms[0] + swap(terms[0], "dp", dp, 1)
+
+        up_mine = jnp.concatenate(adapter_products(low_mine, grads, products[-1:]), axis=1)
         up_other = swap(ordered(up_mine.astype(BF16), received[-1]), "dp", dp, 1).astype(F32)
         up_gradient = jnp.where(
             first_pair, jnp.stack([up_mine, up_other]), jnp.stack([up_other, up_mine])

time: 390 us -> 352 us (0.903)
  blocking collectives: 49.6 us -> 13.4 us
    psum x1 -> x0, blocking collectives: 36.2 us -> none  [local(): steering_gradient = lax.psum(jnp.concatenate(sums, axis=1), ('dp', 'ffn'))]
    convert_element_type x5, other arithmetic: 8.69 us -> 4.38 us  [halving_step(): total_of(sides[1], 0, half).astype(BF16)]
    ppermute x53 -> x54, starting transfers between devices: 49.2 us -> 52.6 us  [swap(): return lax.ppermute(x, axis, [(i, i ^ mask) for i in range(n)])]
    unnamed x145 -> x136, local copies, waits for them, and re-layouts: 26.2 us -> 22.9 us
    ppermute x53 -> x54, waiting for transfers between devices: 104 us -> 106 us  [swap(): return lax.ppermute(x, axis, [(i, i ^ mask) for i in range(n)])]
  transfers between devices with their start and end apart: 53 -> 54, of which waited for: 19 -> 27; matrix products, arithmetic and copies ran while one was open for 7% -> 7% of each run, Pallas kernels for 26% -> 28%
where the time goes in v6:
time: 352 us; the launch traced here: 350 us
  Pallas kernels  130 us (37%)
  waiting for transfers between devices  106 us (30%)
  starting transfers between devices  52.6 us (15%)
  local copies, waits for them, and re-layouts  27.8 us (8%)
  other arithmetic  18.1 us (5%)
  blocking collectives  13.4 us (4%)
    ppermute x54, waiting for transfers between devices, swap(): return lax.ppermute(x, axis, [(i, i ^ mask) for i in range(n)])  106 us
    pallas_call x6, Pallas kernels, forward_matmul(): pl.pallas_call(kernel, grid=(stop - start,), in_specs=[RESIDENT, pl.Block...  56.1 us
    ppermute x54, starting transfers between devices, swap(): return lax.ppermute(x, axis, [(i, i ^ mask) for i in range(n)])  52.6 us
    pallas_call x6, Pallas kernels, backward_matmul(): pl.pallas_call(kernel, grid=(tiles,), in_specs=[pl.BlockSpec(g.shape, lam...  49.8 us
    unnamed x136, local copies, waits for them, and re-layouts  22.9 us
    psum x1, blocking collectives, local(): lax.psum((jnp.sum(rows * rows, axis=1), jnp.sum(steering * steering)), 'h...  7.37 us
  transfers between devices with their start and end apart: 54, of which 27 were waited for; matrix products, arithmetic and copies ran while one was open for 7% of the time, Pallas kernels for 28%

profile of v6, /device:TPU:0, one launch (start us, length us, event | category | flops | bytes accessed | tf_op | source)
XLA Modules:
  0.0 350.3 jit_solution(7483607266957551873)
XLA Ops:
  0.7 3.0 collective-permute-start
  5.0 2.1 fusion
  7.1 7.4 %all-reduce = (f32[256]{0:T(256)S(1)}, f32[]{:T(128)}) all-reduce(f32[256]{0:T(256)S(1)} %fusion, f32[]{:T(128)} %multiply_reduce_fusion), channel_id=1, replica_groups=mesh['dp'=2,'ffn'=4,'hid'=4] {'hid'}, use_global_device_ids=true, to_apply=%region_1.0 | all-reduce | flops 257 | bytes 2056 | tf_op jit(solution)/shard_map/psum | solution.py:408
  16.0 6.1 %psum.23 = f32[256]{0:T(256)S(1)} all-reduce(f32[256]{0:T(256)S(1)} %fusion.2), channel_id=1, replica_groups=mesh['dp'=2,'ffn'=4,'hid'=4] {'hid'}, use_global_device_ids=true, to_apply=%region_5.0 | all-reduce | flops 256 | bytes 2048 | tf_op jit(solution)/shard_map/psum | solution.py:415
  22.9 1.7 normalize.2
  24.6 14.6 %forward_matmul.6 = (f32[128,3584]{1,0:T(8,128)S(1)}, bf16[128,3584]{1,0:T(8,128)(2,1)S(1)}, f32[8,128]{1,0:T(8,128)}) custom-call(bf16[256,4096]{1,0:T(8,128)(2,1)S(1)} %get-tuple-element.50.x_ref.refs_0_, bf16[1,4096,6656]{2,1,0:T(8,128)(2,1)} %refs_8_.11), custom_call_target="tpu_custom_call" | custom-call | flops 75161928 | bytes 342097 | tf_op jit(solution)/shard_map/forward_matmul/pallas_call | solution.py:139
  39.1 2.5 collective-permute-done.2.refs_1_
  43.4 9.0 %collective-permute-done.1.stat_ref = f32[256,2]{1,0:T(8,128)S(1)} collective-permute-done((f32[256,2]{1,0:T(8,128)S(1)}, f32[256,2]{1,0:T(8,128)S(1)}, u32[]{:S(2)}, u32[]{:S(2)}) %collective-permute-start.1) | collective-permute-done | bytes 2080 | tf_op jit(solution)/shard_map/ppermute | solution.py:41
  52.3 3.4 normalize.3
  55.9 10.4 %forward_matmul.7 = (f32[128,3584]{1,0:T(8,128)S(1)}, bf16[128,3584]{1,0:T(8,128)(2,1)S(1)}, f32[8,128]{1,0:T(8,128)}) custom-call(bf16[256,4096]{1,0:T(8,128)(2,1)S(1)} %get-tuple-element.55.x_ref, bf16[1,4096,6656]{2,1,0:T(8,128)(2,1)} %refs_8_.11, bf16[64,3584]{1,0:T(8,128)(2,1)S(1)} %share_sums.6.refs_0_), custom_call_target="tpu_custom_call" | custom-call | flops 42949672 | bytes 204472 | tf_op jit(solution)/shard_map/forward_matmul/pallas_call | solution.py:139
  66.3 7.8 %forward_matmul.8 = (f32[128,3584]{1,0:T(8,128)S(1)}, bf16[128,3584]{1,0:T(8,128)(2,1)S(1)}, f32[8,128]{1,0:T(8,128)}) custom-call(bf16[256,4096]{1,0:T(8,128)(2,1)S(1)} %get-tuple-element.55.x_ref, bf16[1,4096,6656]{2,1,0:T(8,128)(2,1)} %refs_8_.11, f32[128,3584]{1,0:T(8,128)S(1)} %get-tuple-element.56.refs_0_, ...), custom_call_target="tpu_custom_call", output_to_operand_aliasing={{0}: (2, {}), {1}: (3, {})} | custom-call | flops 32212254 | bytes 158597 | tf_op jit(solution)/shard_map/forward_matmul/pallas_call | solution.py:139
  74.1 1.8 collective-permute-start.6
  75.9 2.7 collective-permute-done.6
  79.5 1.8 collective-permute-start.7
  81.3 7.7 %forward_matmul.9 = (f32[256,3072]{1,0:T(8,128)S(1)}, bf16[256,3072]{1,0:T(8,128)(2,1)}, f32[8,128]{1,0:T(8,128)S(1)}) custom-call(bf16[512,4096]{1,0:T(8,128)(2,1)S(1)} %get-tuple-element.54.x_ref.refs_1_, bf16[1,4096,6656]{2,1,0:T(8,128)(2,1)} %refs_8_.11, bf16[64,3584]{1,0:T(8,128)(2,1)S(1)} %share_sums.7.refs_0_), custom_call_target="tpu_custom_call" | custom-call | flops 42949672 | bytes 141557 | tf_op jit(solution)/shard_map/forward_matmul/pallas_call | solution.py:139
  89.0 2.7 collective-permute-done.7.refs_2_
  92.7 1.7 collective-permute-start.8
  94.4 2.2 copy-done.1
  97.6 10.1 %forward_matmul.10 = (f32[256,3072]{1,0:T(8,128)S(1)}, bf16[256,3072]{1,0:T(8,128)(2,1)}, f32[8,128]{1,0:T(8,128)S(1)}) custom-call(bf16[512,4096]{1,0:T(8,128)(2,1)S(1)} %copy-done.1, bf16[1,4096,6656]{2,1,0:T(8,128)(2,1)} %refs_8_.11, f32[256,3072]{1,0:T(8,128)S(1)} %get-tuple-element.62.refs_0_, ...), custom_call_target="tpu_custom_call", output_to_operand_aliasing={{0}: (2, {}), {1}: (3, {})} | custom-call | flops 64424508 | bytes 191365 | tf_op jit(solution)/shard_map/forward_matmul/pallas_call | solution.py:139
  107.8 3.0 gated_gradients.2
  111.2 1.7 collective-permute-start.10
  112.9 8.8 %collective-permute-done.9.refs_2_.refs_4_.refs_5_ = bf16[64,3584]{1,0:T(8,128)(2,1)S(1)} collective-permute-done((bf16[64,3584]{1,0:T(8,128)(2,1)S(1)}, bf16[64,3584]{1,0:T(8,128)(2,1)S(1)}, u32[]{:S(2)}, u32[]{:S(2)}) %collective-permute-start.9) | collective-permute-done | bytes 458784 | tf_op jit(solution)/shard_map/ppermute | solution.py:41
  121.8 5.5 %forward_matmul.11 = (f32[256,3072]{1,0:T(8,128)S(1)}, bf16[256,3072]{1,0:T(8,128)(2,1)}, f32[8,128]{1,0:T(8,128)}) custom-call(bf16[512,4096]{1,0:T(8,128)(2,1)S(1)} %copy-done.1, bf16[1,4096,6656]{2,1,0:T(8,128)(2,1)} %refs_8_.11, f32[256,3072]{1,0:T(8,128)S(1)} %get-tuple-element.65.refs_0_, ...), custom_call_target="tpu_custom_call", output_to_operand_aliasing={{0}: (2, {}), {1}: (3, {})} | custom-call | flops 21474836 | bytes 91750 | tf_op jit(solution)/shard_map/forward_matmul/pallas_call | solution.py:139
  127.3 1.6 collective-permute-start.16
  129.7 10.6 %collective-permute-done.16.refs_5_.refs_6_ = bf16[64,3584]{1,0:T(8,128)(2,1)S(1)} collective-permute-done((bf16[64,3584]{1,0:T(8,128)(2,1)S(1)}, bf16[64,3584]{1,0:T(8,128)(2,1)S(1)}, u32[]{:S(2)}, u32[]{:S(2)}) %collective-permute-start.16) | collective-permute-done | bytes 458784 | tf_op jit(solution)/shard_map/ppermute | solution.py:41
  140.7 1.7 collective-permute-start.13
  142.8 9.0 %backward_matmul.6.refs_3_.refs_9_.refs_10_ = f32[512,1536]{1,0:T(8,128)S(1)} custom-call(bf16[64,3584]{1,0:T(8,128)(2,1)S(1)} %get-tuple-element.69.refs_0_.refs_1_, bf16[64,3584]{1,0:T(8,128)(2,1)S(1)} %collective-permute-done.10.refs_3_.refs_1_.refs_2_, bf16[64,3584]{1,0:T(8,128)(2,1)S(1)} %collective-permute-done.14.refs_2_.refs_3_, ...), custom_call_target="tpu_custom_call" | custom-call | flops 56371444 | bytes 178257 | tf_op jit(solution)/shard_map/backward_matmul/pallas_call | solution.py:281
  153.6 1.6 collective-permute-start.19
  155.1 5.6 %collective-permute-done.12.refs_2_ = bf16[64,3072]{1,0:T(8,128)(2,1)S(1)} collective-permute-done((bf16[64,3072]{1,0:T(8,128)(2,1)S(1)}, bf16[64,3072]{1,0:T(8,128)(2,1)S(1)}, u32[]{:S(2)}, u32[]{:S(2)}) %collective-permute-start.12) | collective-permute-done | bytes 393248 | tf_op jit(solution)/shard_map/ppermute | solution.py:41
  160.7 3.8 %collective-permute-done.19.refs_3_ = bf16[64,3072]{1,0:T(8,128)(2,1)S(1)} collective-permute-done((bf16[64,3072]{1,0:T(8,128)(2,1)S(1)}, bf16[64,3072]{1,0:T(8,128)(2,1)S(1)}, u32[]{:S(2)}, u32[]{:S(2)}) %collective-permute-start.19) | collective-permute-done | bytes 393248 | tf_op jit(solution)/shard_map/ppermute | solution.py:41
  164.5 3.7 %gated_gradients.3 = (bf16[64,3072]{1,0:T(8,128)(2,1)}, bf16[64,3072]{1,0:T(8,128)(2,1)S(1)}, f32[64,33]{1,0:T(8,128)S(1)}) custom-call(s32[1]{0:T(128)} %bitcast.4.d_ref, f32[256,3072]{1,0:T(8,128)S(1)} %get-tuple-element.70.refs_0_, bf16[256,3072]{1,0:T(8,128)(2,1)S(1)} %collective-permute-done.11.refs_1_, ...), custom_call_target="tpu_custom_call" | custom-call | flops 251658 | bytes 31457 | tf_op jit(solution)/shard_map/gated_gradients/pallas_call | solution.py:229
  168.3 1.6 collective-permute-start.23
  169.8 1.5 collective-permute-start.20
  171.4 8.7 %backward_matmul.7.refs_1_.refs_11_.refs_9_ = f32[512,1536]{1,0:T(8,128)S(1)} custom-call(bf16[64,3584]{1,0:T(8,128)(2,1)S(1)} %get-tuple-element.69.refs_0_.refs_1_, bf16[64,3584]{1,0:T(8,128)(2,1)S(1)} %collective-permute-done.10.refs_3_.refs_1_.refs_2_, bf16[64,3584]{1,0:T(8,128)(2,1)S(1)} %collective-permute-done.14.refs_2_.refs_3_, ...), custom_call_target="tpu_custom_call" | custom-call | flops 56371444 | bytes 178257 | tf_op jit(solution)/shard_map/backward_matmul/pallas_call | solution.py:281
  180.9 1.6 collective-permute-start.27
  182.5 2.3 collective-permute-done.27
  185.4 2.6 collective-permute-start.28
  188.0 2.5 collective-permute-done.28
  193.3 2.0 constant_dynamic-slice_fusion.1.refs_2_
  205.1 6.5 %backward_matmul.8.refs_12_.refs_9_ = f32[512,1024]{1,0:T(8,128)S(1)} custom-call(bf16[64,3584]{1,0:T(8,128)(2,1)S(1)} %copy-done.18, bf16[64,3584]{1,0:T(8,128)(2,1)S(1)} %copy-done.12, bf16[64,3584]{1,0:T(8,128)(2,1)S(1)} %copy-done.24, bf16[64,3584]{1,0:T(8,128)(2,1)S(1)} %copy-done.30, bf16[64,3584]{1,0:T(8,128)(2,1)S(1)} %copy-done.9, ...), custom_call_target="tpu_custom_call" | custom-call | flops 37580964 | bytes 131072 | tf_op jit(solution)/shard_map/backward_matmul/pallas_call | solution.py:281
  211.7 9.8 %backward_matmul.9 = (f32[256,1536]{1,0:T(8,128)S(1)}, bf16[256,1536]{1,0:T(8,128)(2,1)}) custom-call(bf16[64,3072]{1,0:T(8,128)(2,1)} %get-tuple-element.74.refs_9_.refs_0_, bf16[64,3072]{1,0:T(8,128)(2,1)} %collective-permute-done.20.refs_1_.refs_10_, bf16[64,3072]{1,0:T(8,128)(2,1)} %collective-permute-done.21.refs_2_.refs_11_, ...), custom_call_target="tpu_custom_call" | custom-call | flops 48318384 | bytes 188743 | tf_op jit(solution)/shard_map/backward_matmul/pallas_call | solution.py:281
  230.6 3.1 collective-permute-done.31
  236.0 8.6 %backward_matmul.10 = (f32[256,1536]{1,0:T(8,128)S(1)}, bf16[256,1536]{1,0:T(8,128)(2,1)S(1)}) custom-call(bf16[64,3072]{1,0:T(8,128)(2,1)} %get-tuple-element.74.refs_9_.refs_0_, bf16[64,3072]{1,0:T(8,128)(2,1)} %collective-permute-done.20.refs_1_.refs_10_, bf16[64,3072]{1,0:T(8,128)(2,1)} %collective-permute-done.21.refs_2_.refs_11_, ...), custom_call_target="tpu_custom_call" | custom-call | flops 48318384 | bytes 188743 | tf_op jit(solution)/shard_map/backward_matmul/pallas_call | solution.py:281
  249.3 1.6 collective-permute-start.36
  250.9 7.2 %backward_matmul.11 = (f32[256,1024]{1,0:T(8,128)S(1)}, bf16[256,1024]{1,0:T(8,128)(2,1)}) custom-call(bf16[64,3072]{1,0:T(8,128)(2,1)} %get-tuple-element.74.refs_9_.refs_0_, bf16[64,3072]{1,0:T(8,128)(2,1)} %collective-permute-done.20.refs_1_.refs_10_, bf16[64,3072]{1,0:T(8,128)(2,1)} %collective-permute-done.21.refs_2_.refs_11_, ...), custom_call_target="tpu_custom_call" | custom-call | flops 32212254 | bytes 136314 | tf_op jit(solution)/shard_map/backward_matmul/pallas_call | solution.py:281
  258.1 6.5 %collective-permute-done.42 = bf16[256,1536]{1,0:T(8,128)(2,1)S(1)} collective-permute-done((bf16[256,1536]{1,0:T(8,128)(2,1)S(1)}, bf16[256,1536]{1,0:T(8,128)(2,1)S(1)}, u32[]{:S(2)}, u32[]{:S(2)}) %collective-permute-start.42) | collective-permute-done | bytes 786464 | tf_op jit(solution)/shard_map/ppermute | solution.py:41
  265.8 1.6 collective-permute-start.43
  269.5 2.8 collective-permute-start.37
  276.8 2.8 adapter_products.3
  280.4 3.3 collective-permute-start.38
  285.0 13.0 %collective-permute-done.38.refs_8_.refs_1_ = bf16[64,1536]{1,0:T(8,128)(2,1)S(1)} collective-permute-done((bf16[64,1536]{1,0:T(8,128)(2,1)S(1)}, bf16[64,1536]{1,0:T(8,128)(2,1)S(1)}, u32[]{:S(2)}, u32[]{:S(2)}) %collective-permute-start.38) | collective-permute-done | bytes 196640 | tf_op jit(solution)/shard_map/ppermute | solution.py:41
  299.2 2.0 collective-permute-start.40
  301.7 2.4 collective-permute-start.45
  304.1 8.4 %collective-permute-done.39 = bf16[128,1024]{1,0:T(8,128)(2,1)S(1)} collective-permute-done((bf16[128,1024]{1,0:T(8,128)(2,1)S(1)}, bf16[128,1024]{1,0:T(8,128)(2,1)S(1)}, u32[]{:S(2)}, u32[]{:S(2)}) %collective-permute-start.39) | collective-permute-done | bytes 262176 | tf_op jit(solution)/shard_map/ppermute | solution.py:41
  312.5 4.4 %collective-permute-done.40.refs_10_.refs_3_ = bf16[64,1536]{1,0:T(8,128)(2,1)S(1)} collective-permute-done((bf16[64,1536]{1,0:T(8,128)(2,1)S(1)}, bf16[64,1536]{1,0:T(8,128)(2,1)S(1)}, u32[]{:S(2)}, u32[]{:S(2)}) %collective-permute-start.40) | collective-permute-done | bytes 196640 | tf_op jit(solution)/shard_map/ppermute | solution.py:41
  319.0 6.1 %collective-permute-done.41.refs_1_ = bf16[64,1024]{1,0:T(8,128)(2,1)S(1)} collective-permute-done((bf16[64,1024]{1,0:T(8,128)(2,1)S(1)}, bf16[64,1024]{1,0:T(8,128)(2,1)S(1)}, u32[]{:S(2)}, u32[]{:S(2)}) %collective-permute-start.41) | collective-permute-done | bytes 131104 | tf_op jit(solution)/shard_map/ppermute | solution.py:41
  326.0 2.2 copy-done.2
  328.2 1.6 adapter_products.2
  330.2 1.6 collective-permute-done.47.refs_1_
  331.9 2.1 collective-permute-start.50
  334.1 2.9 collective-permute-done.48.refs_2_
  336.9 3.5 %collective-permute-done.49.refs_3_ = bf16[80,1024]{1,0:T(8,128)(2,1)S(1)} collective-permute-done((bf16[80,1024]{1,0:T(8,128)(2,1)S(1)}, bf16[80,1024]{1,0:T(8,128)(2,1)S(1)}, u32[]{:S(2)}, u32[]{:S(2)}) %collective-permute-start.49) | collective-permute-done | bytes 163872 | tf_op jit(solution)/shard_map/ppermute | solution.py:41
  344.7 2.1 collective-permute-done.51.refs_3_
  346.8 1.5 assemble.4.refs_4_
  (267 shorter events, 62.5 us)
Async XLA Ops:
  0.7 51.7 %collective-permute-start = (bf16[256,4096]{1,0:T(8,128)(2,1)}, bf16[256,4096]{1,0:T(8,128)(2,1)}, u32[]{:S(2)}, u32[]{:S(2)}) collective-permute-start(bf16[256,4096]{1,0:T(8,128)(2,1)} %x_ref.1), channel_id=1, source_target_pairs={{0,16},{16,0},{1,17},{17,1},{2,18},{18,2},{3,19},{19,3},{4,20},{20... | collective-permute-start | bytes 6291464 | tf_op jit(solution)/shard_map/ppermute | solution.py:41
  39.1 2.5 collective-permute-start.2
  41.9 24.4 %collective-permute-start.4 = (bf16[64,3584]{1,0:T(8,128)(2,1)S(1)}, bf16[64,3584]{1,0:T(8,128)(2,1)S(1)}, u32[]{:S(2)}, u32[]{:S(2)}) collective-permute-start(bf16[64,3584]{1,0:T(8,128)(2,1)S(1)} %share_sums.6.refs_0_), channel_id=1, source_target_pairs={{0,2},{1,3},{2,0},{3,1},{4,6},{5,7},{6,4},{7,5},{8,10},{9,11},{10,... | collective-permute-start | bytes 1376264 | tf_op jit(solution)/shard_map/ppermute | solution.py:41
  42.8 9.5 %collective-permute-start.1 = (f32[256,2]{1,0:T(8,128)S(1)}, f32[256,2]{1,0:T(8,128)S(1)}, u32[]{:S(2)}, u32[]{:S(2)}) collective-permute-start(f32[256,2]{1,0:T(8,128)S(1)} %copy.63.stat_ref), channel_id=1, source_target_pairs={{0,16},{16,0},{1,17},{17,1},{2,18},{18,2},{3,19},{19,3},{4,20},{20... | collective-permute-start | bytes 6152 | tf_op jit(solution)/shard_map/ppermute | solution.py:41
  55.8 25.6 %copy-start = (bf16[512,4096]{1,0:T(8,128)(2,1)}, bf16[512,4096]{1,0:T(8,128)(2,1)S(1)}, u32[]{:S(2)}) copy-start(bf16[512,4096]{1,0:T(8,128)(2,1)S(1)} %get-tuple-element.54.x_ref.refs_1_) | copy-start | bytes 12582916
  55.8 10.5 %collective-permute-start.3 = (f32[2,128,32]{2,1,0:T(8,128)S(1)}, f32[2,128,32]{2,1,0:T(8,128)S(1)}, u32[]{:S(2)}, u32[]{:S(2)}) collective-permute-start(f32[2,128,32]{2,1,0:T(8,128)S(1)} %pad_maximum_fusion.1), channel_id=1, source_target_pairs={{0,1},{1,0},{2,3},{3,2},{4,5},{5,4},{6,7},{7,6},{8,9},{9,8},{10,11... | collective-permute-start | bytes 98312 | tf_op jit(solution)/shard_map/ppermute | solution.py:41
  74.1 4.6 %collective-permute-start.5 = (bf16[128,3584]{1,0:T(8,128)(2,1)S(1)}, bf16[128,3584]{1,0:T(8,128)(2,1)S(1)}, u32[]{:S(2)}, u32[]{:S(2)}) collective-permute-start(bf16[128,3584]{1,0:T(8,128)(2,1)S(1)} %get-tuple-element.61), channel_id=1, source_target_pairs={{0,1},{1,0},{2,3},{3,2},{4,5},{5,4},{6,7},{7,6},{8,9},{9,8},{10,11... | collective-permute-start | bytes 2752520 | tf_op jit(solution)/shard_map/ppermute | solution.py:41
  74.1 4.5 %collective-permute-start.6 = (f32[2,64,32]{2,1,0:T(8,128)S(1)}, f32[2,64,32]{2,1,0:T(8,128)S(1)}, u32[]{:S(2)}, u32[]{:S(2)}) collective-permute-start(f32[2,64,32]{2,1,0:T(8,128)S(1)} %slice.73), channel_id=1, source_target_pairs={{0,2},{1,3},{2,0},{3,1},{4,6},{5,7},{6,4},{7,5},{8,10},{9,11},{10,... | collective-permute-start | bytes 49160 | tf_op jit(solution)/shard_map/ppermute | solution.py:41
  79.5 12.2 %collective-permute-start.7 = (bf16[64,3584]{1,0:T(8,128)(2,1)S(1)}, bf16[64,3584]{1,0:T(8,128)(2,1)S(1)}, u32[]{:S(2)}, u32[]{:S(2)}) collective-permute-start(bf16[64,3584]{1,0:T(8,128)(2,1)S(1)} %share_sums.7.refs_0_), channel_id=1, source_target_pairs={{0,2},{1,3},{2,0},{3,1},{4,6},{5,7},{6,4},{7,5},{8,10},{9,11},{10,... | collective-permute-start | bytes 1376264 | tf_op jit(solution)/shard_map/ppermute | solution.py:41
  92.7 15.1 %collective-permute-start.8 = (bf16[64,3584]{1,0:T(8,128)(2,1)}, bf16[64,3584]{1,0:T(8,128)(2,1)}, u32[]{:S(2)}, u32[]{:S(2)}) collective-permute-start(bf16[64,3584]{1,0:T(8,128)(2,1)} %share_sums.8.refs_3_), channel_id=1, source_target_pairs={{0,16},{16,0},{1,17},{17,1},{2,18},{18,2},{3,19},{19,3},{4,20},{20... | collective-permute-start | bytes 1376264 | tf_op jit(solution)/shard_map/ppermute | solution.py:41
  110.8 60.6 %copy-start.17 = (bf16[64,3584]{1,0:T(8,128)(2,1)}, bf16[64,3584]{1,0:T(8,128)(2,1)S(1)}, u32[]{:S(2)}) copy-start(bf16[64,3584]{1,0:T(8,128)(2,1)S(1)} %get-tuple-element.69.refs_0_.refs_1_) | copy-start | bytes 1376260
  110.8 11.0 %collective-permute-start.9 = (bf16[64,3584]{1,0:T(8,128)(2,1)S(1)}, bf16[64,3584]{1,0:T(8,128)(2,1)S(1)}, u32[]{:S(2)}, u32[]{:S(2)}) collective-permute-start(bf16[64,3584]{1,0:T(8,128)(2,1)S(1)} %get-tuple-element.68), channel_id=1, source_target_pairs={{0,16},{16,0},{1,17},{17,1},{2,18},{18,2},{3,19},{19,3},{4,20},{20... | collective-permute-start | bytes 1376264 | tf_op jit(solution)/shard_map/ppermute | solution.py:41
  111.2 10.6 %collective-permute-start.10 = (bf16[64,3584]{1,0:T(8,128)(2,1)S(1)}, bf16[64,3584]{1,0:T(8,128)(2,1)S(1)}, u32[]{:S(2)}, u32[]{:S(2)}) collective-permute-start(bf16[64,3584]{1,0:T(8,128)(2,1)S(1)} %get-tuple-element.69.refs_0_.refs_1_), channel_id=1, source_target_pairs={{0,2},{1,3},{2,0},{3,1},{4,6},{5,7},{6,4},{7,5},{8,10},{9,11},{10,... | collective-permute-start | bytes 1376264 | tf_op jit(solution)/shard_map/ppermute | solution.py:41
  121.7 49.6 %copy-start.8 = (bf16[64,3584]{1,0:T(8,128)(2,1)}, bf16[64,3584]{1,0:T(8,128)(2,1)S(1)}, u32[]{:S(2)}) copy-start(bf16[64,3584]{1,0:T(8,128)(2,1)S(1)} %collective-permute-done.9.refs_2_.refs_4_.refs_5_) | copy-start | bytes 1376260
  121.8 49.5 %copy-start.11 = (bf16[64,3584]{1,0:T(8,128)(2,1)}, bf16[64,3584]{1,0:T(8,128)(2,1)S(1)}, u32[]{:S(2)}) copy-start(bf16[64,3584]{1,0:T(8,128)(2,1)S(1)} %collective-permute-done.10.refs_3_.refs_1_.refs_2_) | copy-start | bytes 1376260
  127.3 12.9 %collective-permute-start.11 = (bf16[256,3072]{1,0:T(8,128)(2,1)}, bf16[256,3072]{1,0:T(8,128)(2,1)S(1)}, u32[]{:S(2)}, u32[]{:S(2)}) collective-permute-start(bf16[256,3072]{1,0:T(8,128)(2,1)} %get-tuple-element.71), channel_id=1, source_target_pairs={{0,1},{1,0},{2,3},{3,2},{4,5},{5,4},{6,7},{7,6},{8,9},{9,8},{10,11... | collective-permute-start | bytes 4718600 | tf_op jit(solution)/shard_map/ppermute | solution.py:41
  127.3 12.9 %collective-permute-start.16 = (bf16[64,3584]{1,0:T(8,128)(2,1)S(1)}, bf16[64,3584]{1,0:T(8,128)(2,1)S(1)}, u32[]{:S(2)}, u32[]{:S(2)}) collective-permute-start(bf16[64,3584]{1,0:T(8,128)(2,1)S(1)} %collective-permute-done.9.refs_2_.refs_4_.refs_5_), channel_id=1, source_target_pairs={{0,2},{1,3},{2,0},{3,1},{4,6},{5,7},{6,4},{7,5},{8,10},{9,11},{10,... | collective-permute-start | bytes 1376264 | tf_op jit(solution)/shard_map/ppermute | solution.py:41
  128.9 13.4 %collective-permute-start.14 = (bf16[64,3584]{1,0:T(8,128)(2,1)S(1)}, bf16[64,3584]{1,0:T(8,128)(2,1)S(1)}, u32[]{:S(2)}, u32[]{:S(2)}) collective-permute-start(bf16[64,3584]{1,0:T(8,128)(2,1)S(1)} %get-tuple-element.69.refs_0_.refs_1_), channel_id=1, source_target_pairs={{0,1},{1,0},{2,3},{3,2},{4,5},{5,4},{6,7},{7,6},{8,9},{9,8},{10,11... | collective-permute-start | bytes 1376264 | tf_op jit(solution)/shard_map/ppermute | solution.py:41
  129.2 13.6 %collective-permute-start.17 = (bf16[64,3584]{1,0:T(8,128)(2,1)S(1)}, bf16[64,3584]{1,0:T(8,128)(2,1)S(1)}, u32[]{:S(2)}, u32[]{:S(2)}) collective-permute-start(bf16[64,3584]{1,0:T(8,128)(2,1)S(1)} %collective-permute-done.9.refs_2_.refs_4_.refs_5_), channel_id=1, source_target_pairs={{0,1},{1,0},{2,3},{3,2},{4,5},{5,4},{6,7},{7,6},{8,9},{9,8},{10,11... | collective-permute-start | bytes 1376264 | tf_op jit(solution)/shard_map/ppermute | solution.py:41
  129.4 13.4 %collective-permute-start.15 = (bf16[64,3584]{1,0:T(8,128)(2,1)S(1)}, bf16[64,3584]{1,0:T(8,128)(2,1)S(1)}, u32[]{:S(2)}, u32[]{:S(2)}) collective-permute-start(bf16[64,3584]{1,0:T(8,128)(2,1)S(1)} %collective-permute-done.10.refs_3_.refs_1_.refs_2_), channel_id=1, source_target_pairs={{0,1},{1,0},{2,3},{3,2},{4,5},{5,4},{6,7},{7,6},{8,9},{9,8},{10,11... | collective-permute-start | bytes 1376264 | tf_op jit(solution)/shard_map/ppermute | solution.py:41
  140.3 31.1 %copy-start.20 = (bf16[64,3584]{1,0:T(8,128)(2,1)}, bf16[64,3584]{1,0:T(8,128)(2,1)S(1)}, u32[]{:S(2)}) copy-start(bf16[64,3584]{1,0:T(8,128)(2,1)S(1)} %collective-permute-done.16.refs_5_.refs_6_) | copy-start | bytes 1376260
  140.3 2.5 collective-permute-start.18
  140.7 12.0 %collective-permute-start.13 = (bf16[64,3072]{1,0:T(8,128)(2,1)S(1)}, bf16[64,3072]{1,0:T(8,128)(2,1)S(1)}, u32[]{:S(2)}, u32[]{:S(2)}) collective-permute-start(bf16[64,3072]{1,0:T(8,128)(2,1)S(1)} %get-tuple-element.73), channel_id=1, source_target_pairs={{0,2},{1,3},{2,0},{3,1},{4,6},{5,7},{6,4},{7,5},{8,10},{9,11},{10,... | collective-permute-start | bytes 1179656 | tf_op jit(solution)/shard_map/ppermute | solution.py:41
  142.4 29.0 %copy-start.23 = (bf16[64,3584]{1,0:T(8,128)(2,1)}, bf16[64,3584]{1,0:T(8,128)(2,1)S(1)}, u32[]{:S(2)}) copy-start(bf16[64,3584]{1,0:T(8,128)(2,1)S(1)} %collective-permute-done.14.refs_2_.refs_3_) | copy-start | bytes 1376260
  142.4 18.3 %collective-permute-start.12 = (bf16[64,3072]{1,0:T(8,128)(2,1)S(1)}, bf16[64,3072]{1,0:T(8,128)(2,1)S(1)}, u32[]{:S(2)}, u32[]{:S(2)}) collective-permute-start(bf16[64,3072]{1,0:T(8,128)(2,1)S(1)} %get-tuple-element.72.refs_9_), channel_id=1, source_target_pairs={{0,2},{1,3},{2,0},{3,1},{4,6},{5,7},{6,4},{7,5},{8,10},{9,11},{10,... | collective-permute-start | bytes 1179656 | tf_op jit(solution)/shard_map/ppermute | solution.py:41
  142.8 28.6 %copy-start.26 = (bf16[64,3584]{1,0:T(8,128)(2,1)}, bf16[64,3584]{1,0:T(8,128)(2,1)S(1)}, u32[]{:S(2)}) copy-start(bf16[64,3584]{1,0:T(8,128)(2,1)S(1)} %collective-permute-done.17.refs_6_.refs_7_) | copy-start | bytes 1376260
  142.8 28.6 %copy-start.29 = (bf16[64,3584]{1,0:T(8,128)(2,1)}, bf16[64,3584]{1,0:T(8,128)(2,1)S(1)}, u32[]{:S(2)}) copy-start(bf16[64,3584]{1,0:T(8,128)(2,1)S(1)} %collective-permute-done.15.refs_3_.refs_4_) | copy-start | bytes 1376260
  142.8 28.6 %copy-start.32 = (bf16[64,3584]{1,0:T(8,128)(2,1)}, bf16[64,3584]{1,0:T(8,128)(2,1)S(1)}, u32[]{:S(2)}) copy-start(bf16[64,3584]{1,0:T(8,128)(2,1)S(1)} %collective-permute-done.18.refs_7_.refs_8_) | copy-start | bytes 1376260
  153.6 10.9 %collective-permute-start.19 = (bf16[64,3072]{1,0:T(8,128)(2,1)S(1)}, bf16[64,3072]{1,0:T(8,128)(2,1)S(1)}, u32[]{:S(2)}, u32[]{:S(2)}) collective-permute-start(bf16[64,3072]{1,0:T(8,128)(2,1)S(1)} %share_sums.10), channel_id=1, source_target_pairs={{0,16},{16,0},{1,17},{17,1},{2,18},{18,2},{3,19},{19,3},{4,20},{20... | collective-permute-start | bytes 1179656 | tf_op jit(solution)/shard_map/ppermute | solution.py:41
  168.3 11.9 %collective-permute-start.23 = (bf16[64,3072]{1,0:T(8,128)(2,1)S(1)}, bf16[64,3072]{1,0:T(8,128)(2,1)S(1)}, u32[]{:S(2)}, u32[]{:S(2)}) collective-permute-start(bf16[64,3072]{1,0:T(8,128)(2,1)S(1)} %get-tuple-element.75), channel_id=1, source_target_pairs={{0,16},{16,0},{1,17},{17,1},{2,18},{18,2},{3,19},{19,3},{4,20},{20... | collective-permute-start | bytes 1179656 | tf_op jit(solution)/shard_map/ppermute | solution.py:41
  169.8 22.9 %collective-permute-start.20 = (bf16[64,3072]{1,0:T(8,128)(2,1)}, bf16[64,3072]{1,0:T(8,128)(2,1)}, u32[]{:S(2)}, u32[]{:S(2)}) collective-permute-start(bf16[64,3072]{1,0:T(8,128)(2,1)} %get-tuple-element.74.refs_9_.refs_0_), channel_id=1, source_target_pairs={{0,2},{1,3},{2,0},{3,1},{4,6},{5,7},{6,4},{7,5},{8,10},{9,11},{10,... | collective-permute-start | bytes 1179656 | tf_op jit(solution)/shard_map/ppermute | solution.py:41
  180.3 12.9 %collective-permute-start.24 = (bf16[64,3072]{1,0:T(8,128)(2,1)S(1)}, bf16[64,3072]{1,0:T(8,128)(2,1)}, u32[]{:S(2)}, u32[]{:S(2)}) collective-permute-start(bf16[64,3072]{1,0:T(8,128)(2,1)S(1)} %share_sums.11.refs_9_.refs_4_.refs_13_), channel_id=1, source_target_pairs={{0,2},{1,3},{2,0},{3,1},{4,6},{5,7},{6,4},{7,5},{8,10},{9,11},{10,... | collective-permute-start | bytes 1179656 | tf_op jit(solution)/shard_map/ppermute | solution.py:41
  180.9 3.9 %collective-permute-start.27 = (f32[64,33]{1,0:T(8,128)S(1)}, f32[64,33]{1,0:T(8,128)S(1)}, u32[]{:S(2)}, u32[]{:S(2)}) collective-permute-start(f32[64,33]{1,0:T(8,128)S(1)} %add.223), channel_id=1, source_target_pairs={{0,4},{4,0},{8,12},{12,8},{1,5},{5,1},{9,13},{13,9},{2,6},{6,2},{1... | collective-permute-start | bytes 25352 | tf_op jit(solution)/shard_map/ppermute | solution.py:41
  185.4 5.1 %collective-permute-start.28 = (f32[64,33]{1,0:T(8,128)}, f32[64,33]{1,0:T(8,128)}, u32[]{:S(2)}, u32[]{:S(2)}) collective-permute-start(f32[64,33]{1,0:T(8,128)} %add.224), channel_id=1, source_target_pairs={{0,8},{4,12},{8,0},{12,4},{1,9},{5,13},{9,1},{13,5},{2,10},{6,14},... | collective-permute-start | bytes 25352 | tf_op jit(solution)/shard_map/ppermute | solution.py:41
  188.0 23.7 %collective-permute-start.21 = (bf16[64,3072]{1,0:T(8,128)(2,1)}, bf16[64,3072]{1,0:T(8,128)(2,1)}, u32[]{:S(2)}, u32[]{:S(2)}) collective-permute-start(bf16[64,3072]{1,0:T(8,128)(2,1)} %get-tuple-element.74.refs_9_.refs_0_), channel_id=1, source_target_pairs={{0,1},{1,0},{2,3},{3,2},{4,5},{5,4},{6,7},{7,6},{8,9},{9,8},{10,11... | collective-permute-start | bytes 1179656 | tf_op jit(solution)/shard_map/ppermute | solution.py:41
  191.9 4.2 %collective-permute-start.29 = (f32[64,33]{1,0:T(8,128)}, f32[64,33]{1,0:T(8,128)}, u32[]{:S(2)}, u32[]{:S(2)}) collective-permute-start(f32[64,33]{1,0:T(8,128)} %add.225), channel_id=1, source_target_pairs={{0,16},{16,0},{1,17},{17,1},{2,18},{18,2},{3,19},{19,3},{4,20},{20... | collective-permute-start | bytes 25352 | tf_op jit(solution)/shard_map/ppermute | solution.py:41
  192.7 19.0 %collective-permute-start.25 = (bf16[64,3072]{1,0:T(8,128)(2,1)S(1)}, bf16[64,3072]{1,0:T(8,128)(2,1)}, u32[]{:S(2)}, u32[]{:S(2)}) collective-permute-start(bf16[64,3072]{1,0:T(8,128)(2,1)S(1)} %share_sums.11.refs_9_.refs_4_.refs_13_), channel_id=1, source_target_pairs={{0,1},{1,0},{2,3},{3,2},{4,5},{5,4},{6,7},{7,6},{8,9},{9,8},{10,11... | collective-permute-start | bytes 1179656 | tf_op jit(solution)/shard_map/ppermute | solution.py:41
  192.7 19.0 %collective-permute-start.22 = (bf16[64,3072]{1,0:T(8,128)(2,1)}, bf16[64,3072]{1,0:T(8,128)(2,1)}, u32[]{:S(2)}, u32[]{:S(2)}) collective-permute-start(bf16[64,3072]{1,0:T(8,128)(2,1)} %collective-permute-done.20.refs_1_.refs_10_), channel_id=1, source_target_pairs={{0,1},{1,0},{2,3},{3,2},{4,5},{5,4},{6,7},{7,6},{8,9},{9,8},{10,11... | collective-permute-start | bytes 1179656 | tf_op jit(solution)/shard_map/ppermute | solution.py:41
  193.2 18.5 %collective-permute-start.26 = (bf16[64,3072]{1,0:T(8,128)(2,1)}, bf16[64,3072]{1,0:T(8,128)(2,1)}, u32[]{:S(2)}, u32[]{:S(2)}) collective-permute-start(bf16[64,3072]{1,0:T(8,128)(2,1)} %collective-permute-done.24.refs_5_.refs_14_), channel_id=1, source_target_pairs={{0,1},{1,0},{2,3},{3,2},{4,5},{5,4},{6,7},{7,6},{8,9},{9,8},{10,11... | collective-permute-start | bytes 1179656 | tf_op jit(solution)/shard_map/ppermute | solution.py:41
  222.7 25.3 %collective-permute-start.30 = (bf16[256,1536]{1,0:T(8,128)(2,1)}, bf16[256,1536]{1,0:T(8,128)(2,1)}, u32[]{:S(2)}, u32[]{:S(2)}) collective-permute-start(bf16[256,1536]{1,0:T(8,128)(2,1)} %get-tuple-element.80), channel_id=1, source_target_pairs={{0,16},{16,0},{1,17},{17,1},{2,18},{18,2},{3,19},{19,3},{4,20},{20... | collective-permute-start | bytes 2359304 | tf_op jit(solution)/shard_map/ppermute | solution.py:41
  224.1 4.2 %collective-permute-start.33 = (bf16[2,64,16]{2,1,0:T(8,128)(2,1)}, bf16[2,64,16]{2,1,0:T(8,128)(2,1)}, u32[]{:S(2)}, u32[]{:S(2)}) collective-permute-start(bf16[2,64,16]{2,1,0:T(8,128)(2,1)} %slice_select_fusion), channel_id=1, source_target_pairs={{0,2},{1,3},{2,0},{3,1},{4,6},{5,7},{6,4},{7,5},{8,10},{9,11},{10,... | collective-permute-start | bytes 12296 | tf_op jit(solution)/shard_map/ppermute | solution.py:41
  229.2 4.5 %collective-permute-start.31 = (f32[2,64,33]{2,1,0:T(8,128)}, f32[2,64,33]{2,1,0:T(8,128)S(1)}, u32[]{:S(2)}, u32[]{:S(2)}) collective-permute-start(f32[2,64,33]{2,1,0:T(8,128)} %copy-done.56), channel_id=1, source_target_pairs={{0,2},{1,3},{2,0},{3,1},{4,6},{5,7},{6,4},{7,5},{8,10},{9,11},{10,... | collective-permute-start | bytes 50696 | tf_op jit(solution)/shard_map/ppermute | solution.py:41
  230.6 15.3 %collective-permute-start.34 = (bf16[2,128,16]{1,2,0:T(8,128)(2,1)S(1)}, bf16[2,128,16]{1,2,0:T(8,128)(2,1)S(1)}, u32[]{:S(2)}, u32[]{:S(2)}) collective-permute-start(bf16[2,128,16]{1,2,0:T(8,128)(2,1)S(1)} %pad_maximum_fusion.4), channel_id=1, source_target_pairs={{0,1},{1,0},{2,3},{3,2},{4,5},{5,4},{6,7},{7,6},{8,9},{9,8},{10,11... | collective-permute-start | bytes 24584 | tf_op jit(solution)/shard_map/ppermute | solution.py:41
  234.5 11.5 %collective-permute-start.32 = (f32[2,128,33]{2,1,0:T(8,128)S(1)}, f32[2,128,33]{2,1,0:T(8,128)S(1)}, u32[]{:S(2)}, u32[]{:S(2)}) collective-permute-start(f32[2,128,33]{2,1,0:T(8,128)S(1)} %pad_maximum_fusion.2), channel_id=1, source_target_pairs={{0,1},{1,0},{2,3},{3,2},{4,5},{5,4},{6,7},{7,6},{8,9},{9,8},{10,11... | collective-permute-start | bytes 101384 | tf_op jit(solution)/shard_map/ppermute | solution.py:41
  244.5 20.0 %collective-permute-start.42 = (bf16[256,1536]{1,0:T(8,128)(2,1)S(1)}, bf16[256,1536]{1,0:T(8,128)(2,1)S(1)}, u32[]{:S(2)}, u32[]{:S(2)}) collective-permute-start(bf16[256,1536]{1,0:T(8,128)(2,1)S(1)} %get-tuple-element.86), channel_id=1, source_target_pairs={{0,16},{16,0},{1,17},{17,1},{2,18},{18,2},{3,19},{19,3},{4,20},{20... | collective-permute-start | bytes 2359304 | tf_op jit(solution)/shard_map/ppermute | solution.py:41
  249.3 19.3 %collective-permute-start.36 = (bf16[128,1536]{1,0:T(8,128)(2,1)S(1)}, bf16[128,1536]{1,0:T(8,128)(2,1)S(1)}, u32[]{:S(2)}, u32[]{:S(2)}) collective-permute-start(bf16[128,1536]{1,0:T(8,128)(2,1)S(1)} %get-tuple-element.101.refs_11_), channel_id=1, source_target_pairs={{0,4},{4,0},{8,12},{12,8},{1,5},{5,1},{9,13},{13,9},{2,6},{6,2},{1... | collective-permute-start | bytes 1179656 | tf_op jit(solution)/shard_map/ppermute | solution.py:41
  265.8 18.0 %collective-permute-start.43 = (bf16[128,1536]{1,0:T(8,128)(2,1)}, bf16[128,1536]{1,0:T(8,128)(2,1)}, u32[]{:S(2)}, u32[]{:S(2)}) collective-permute-start(bf16[128,1536]{1,0:T(8,128)(2,1)} %get-tuple-element.98), channel_id=1, source_target_pairs={{0,4},{4,0},{8,12},{12,8},{1,5},{5,1},{9,13},{13,9},{2,6},{6,2},{1... | collective-permute-start | bytes 1179656 | tf_op jit(solution)/shard_map/ppermute | solution.py:41
  267.3 17.6 %collective-permute-start.35 = (bf16[256,1024]{1,0:T(8,128)(2,1)}, bf16[256,1024]{1,0:T(8,128)(2,1)}, u32[]{:S(2)}, u32[]{:S(2)}) collective-permute-start(bf16[256,1024]{1,0:T(8,128)(2,1)} %get-tuple-element.82), channel_id=1, source_target_pairs={{0,16},{16,0},{1,17},{17,1},{2,18},{18,2},{3,19},{19,3},{4,20},{20... | collective-permute-start | bytes 1572872 | tf_op jit(solution)/shard_map/ppermute | solution.py:41
  269.5 10.6 %collective-permute-start.37 = (bf16[64,1536]{1,0:T(8,128)(2,1)}, bf16[64,1536]{1,0:T(8,128)(2,1)S(1)}, u32[]{:S(2)}, u32[]{:S(2)}) collective-permute-start(bf16[64,1536]{1,0:T(8,128)(2,1)} %get-tuple-element.106), channel_id=1, source_target_pairs={{0,8},{4,12},{8,0},{12,4},{1,9},{5,13},{9,1},{13,5},{2,10},{6,14},... | collective-permute-start | bytes 589832 | tf_op jit(solution)/shard_map/ppermute | solution.py:41
  280.4 17.6 %collective-permute-start.38 = (bf16[64,1536]{1,0:T(8,128)(2,1)S(1)}, bf16[64,1536]{1,0:T(8,128)(2,1)S(1)}, u32[]{:S(2)}, u32[]{:S(2)}) collective-permute-start(bf16[64,1536]{1,0:T(8,128)(2,1)S(1)} %get-tuple-element.83.refs_0_), channel_id=1, source_target_pairs={{0,8},{4,12},{8,0},{12,4},{1,9},{5,13},{9,1},{13,5},{2,10},{6,14},... | collective-permute-start | bytes 589832 | tf_op jit(solution)/shard_map/ppermute | solution.py:41
  284.9 16.5 %collective-permute-start.44 = (bf16[64,1536]{1,0:T(8,128)(2,1)S(1)}, bf16[64,1536]{1,0:T(8,128)(2,1)S(1)}, u32[]{:S(2)}, u32[]{:S(2)}) collective-permute-start(bf16[64,1536]{1,0:T(8,128)(2,1)S(1)} %get-tuple-element.104), channel_id=1, source_target_pairs={{0,8},{4,12},{8,0},{12,4},{1,9},{5,13},{9,1},{13,5},{2,10},{6,14},... | collective-permute-start | bytes 589832 | tf_op jit(solution)/shard_map/ppermute | solution.py:41
  299.2 13.3 %collective-permute-start.39 = (bf16[128,1024]{1,0:T(8,128)(2,1)S(1)}, bf16[128,1024]{1,0:T(8,128)(2,1)S(1)}, u32[]{:S(2)}, u32[]{:S(2)}) collective-permute-start(bf16[128,1024]{1,0:T(8,128)(2,1)S(1)} %get-tuple-element.102), channel_id=1, source_target_pairs={{0,4},{4,0},{8,12},{12,8},{1,5},{5,1},{9,13},{13,9},{2,6},{6,2},{1... | collective-permute-start | bytes 786440 | tf_op jit(solution)/shard_map/ppermute | solution.py:41
  299.2 17.6 %collective-permute-start.40 = (bf16[64,1536]{1,0:T(8,128)(2,1)S(1)}, bf16[64,1536]{1,0:T(8,128)(2,1)S(1)}, u32[]{:S(2)}, u32[]{:S(2)}) collective-permute-start(bf16[64,1536]{1,0:T(8,128)(2,1)S(1)} %collective-permute-done.38.refs_8_.refs_1_), channel_id=1, source_target_pairs={{0,4},{4,0},{8,12},{12,8},{1,5},{5,1},{9,13},{13,9},{2,6},{6,2},{1... | collective-permute-start | bytes 589832 | tf_op jit(solution)/shard_map/ppermute | solution.py:41
  301.3 17.7 %collective-permute-start.46 = (bf16[64,1536]{1,0:T(8,128)(2,1)S(1)}, bf16[64,1536]{1,0:T(8,128)(2,1)S(1)}, u32[]{:S(2)}, u32[]{:S(2)}) collective-permute-start(bf16[64,1536]{1,0:T(8,128)(2,1)S(1)} %get-tuple-element.83.refs_0_), channel_id=1, source_target_pairs={{0,4},{4,0},{8,12},{12,8},{1,5},{5,1},{9,13},{13,9},{2,6},{6,2},{1... | collective-permute-start | bytes 589832 | tf_op jit(solution)/shard_map/ppermute | solution.py:41
  301.7 23.7 %copy-start.66 = (bf16[80]{0:T(256)(128)(2,1)S(1)}, bf16[80]{0:T(256)(128)(2,1)}, u32[]{:S(2)}) copy-start(bf16[80]{0:T(256)(128)(2,1)} %pad.7.clone) | copy-start | bytes 484
  301.7 17.3 %collective-permute-start.45 = (bf16[64,1536]{1,0:T(8,128)(2,1)S(1)}, bf16[64,1536]{1,0:T(8,128)(2,1)S(1)}, u32[]{:S(2)}, u32[]{:S(2)}) collective-permute-start(bf16[64,1536]{1,0:T(8,128)(2,1)S(1)} %get-tuple-element.88.refs_0_), channel_id=1, source_target_pairs={{0,8},{4,12},{8,0},{12,4},{1,9},{5,13},{9,1},{13,5},{2,10},{6,14},... | collective-permute-start | bytes 589832 | tf_op jit(solution)/shard_map/ppermute | solution.py:41
  316.9 8.2 %collective-permute-start.41 = (bf16[64,1024]{1,0:T(8,128)(2,1)S(1)}, bf16[64,1024]{1,0:T(8,128)(2,1)S(1)}, u32[]{:S(2)}, u32[]{:S(2)}) collective-permute-start(bf16[64,1024]{1,0:T(8,128)(2,1)S(1)} %get-tuple-element.85), channel_id=1, source_target_pairs={{0,8},{4,12},{8,0},{12,4},{1,9},{5,13},{9,1},{13,5},{2,10},{6,14},... | collective-permute-start | bytes 393224 | tf_op jit(solution)/shard_map/ppermute | solution.py:41
  316.9 14.9 %collective-permute-start.53 = (bf16[16,6656]{1,0:T(8,128)(2,1)S(1)}, bf16[16,6656]{1,0:T(8,128)(2,1)S(1)}, u32[]{:S(2)}, u32[]{:S(2)}) collective-permute-start(bf16[16,6656]{1,0:T(8,128)(2,1)S(1)} %convert_element_type.126), channel_id=1, source_target_pairs={{0,16},{16,0},{1,17},{17,1},{2,18},{18,2},{3,19},{19,3},{4,20},{20... | collective-permute-start | bytes 638984 | tf_op jit(solution)/shard_map/ppermute | solution.py:41
  325.5 6.3 %collective-permute-start.47 = (bf16[80,1024]{1,0:T(8,128)(2,1)S(1)}, bf16[80,1024]{1,0:T(8,128)(2,1)S(1)}, u32[]{:S(2)}, u32[]{:S(2)}) collective-permute-start(bf16[80,1024]{1,0:T(8,128)(2,1)S(1)} %maximum_maximum_fusion.refs_0_), channel_id=1, source_target_pairs={{0,8},{4,12},{8,0},{12,4},{1,9},{5,13},{9,1},{13,5},{2,10},{6,14},... | collective-permute-start | bytes 491528 | tf_op jit(solution)/shard_map/ppermute | solution.py:41
  329.8 7.1 %collective-permute-start.48 = (bf16[80,1024]{1,0:T(8,128)(2,1)S(1)}, bf16[80,1024]{1,0:T(8,128)(2,1)S(1)}, u32[]{:S(2)}, u32[]{:S(2)}) collective-permute-start(bf16[80,1024]{1,0:T(8,128)(2,1)S(1)} %maximum_maximum_fusion.refs_0_), channel_id=1, source_target_pairs={{0,4},{4,0},{8,12},{12,8},{1,5},{5,1},{9,13},{13,9},{2,6},{6,2},{1... | collective-permute-start | bytes 491528 | tf_op jit(solution)/shard_map/ppermute | solution.py:41
  331.9 8.6 %collective-permute-start.49 = (bf16[80,1024]{1,0:T(8,128)(2,1)S(1)}, bf16[80,1024]{1,0:T(8,128)(2,1)S(1)}, u32[]{:S(2)}, u32[]{:S(2)}) collective-permute-start(bf16[80,1024]{1,0:T(8,128)(2,1)S(1)} %collective-permute-done.47.refs_1_), channel_id=1, source_target_pairs={{0,4},{4,0},{8,12},{12,8},{1,5},{5,1},{9,13},{13,9},{2,6},{6,2},{1... | collective-permute-start | bytes 491528 | tf_op jit(solution)/shard_map/ppermute | solution.py:41
  331.9 12.8 %collective-permute-start.50 = (bf16[64,1536]{1,0:T(8,128)(2,1)S(1)}, bf16[64,1536]{1,0:T(8,128)(2,1)S(1)}, u32[]{:S(2)}, u32[]{:S(2)}) collective-permute-start(bf16[64,1536]{1,0:T(8,128)(2,1)S(1)} %get-tuple-element.88.refs_0_), channel_id=1, source_target_pairs={{0,4},{4,0},{8,12},{12,8},{1,5},{5,1},{9,13},{13,9},{2,6},{6,2},{1... | collective-permute-start | bytes 589832 | tf_op jit(solution)/shard_map/ppermute | solution.py:41
  334.0 12.8 %collective-permute-start.51 = (bf16[64,1536]{1,0:T(8,128)(2,1)S(1)}, bf16[64,1536]{1,0:T(8,128)(2,1)S(1)}, u32[]{:S(2)}, u32[]{:S(2)}) collective-permute-start(bf16[64,1536]{1,0:T(8,128)(2,1)S(1)} %collective-permute-done.45.refs_8_.refs_1_), channel_id=1, source_target_pairs={{0,4},{4,0},{8,12},{12,8},{1,5},{5,1},{9,13},{13,9},{2,6},{6,2},{1... | collective-permute-start | bytes 589832 | tf_op jit(solution)/shard_map/ppermute | solution.py:41
  340.5 9.2 %collective-permute-start.52 = (f32[4,1024]{1,0:T(4,128)S(1)}, f32[4,1024]{1,0:T(4,128)S(1)}, u32[]{:S(2)}, u32[]{:S(2)}) collective-permute-start(f32[4,1024]{1,0:T(4,128)S(1)} %fusion.8), channel_id=1, source_target_pairs={{0,16},{16,0},{1,17},{17,1},{2,18},{18,2},{3,19},{19,3},{4,20},{20... | collective-permute-start | bytes 49160 | tf_op jit(solution)/shard_map/ppermute | solution.py:41
  (57 other events, 372.1 us)

commit v7 on v6

--- a/solution.py
+++ b/solution.py
@@ -7,8 +7,7 @@
 
 MODEL_WIDTH = 16384
 ADAPTER_SCALE = 0.5
-VMEM_MIB = 12
-MATMUL_VMEM_MIB = 24
+VMEM_MIB = 40
 COST_SHARE = 0.01
 
 F32 = jnp.float32
@@ -47,10 +46,6 @@
     return x
 
 
-def ordered(x, *first):
-    return lax.optimization_barrier((x, *first))[0]
-
-
 def total_of(parts, start, stop):
     out = parts[0][start:stop]
     for part in parts[1:]:
@@ -58,8 +53,8 @@
     return out
 
 
-def params(mib=VMEM_MIB):
-    return pltpu.CompilerParams(vmem_limit_bytes=mib * 1024 * 1024)
+def params():
+    return pltpu.CompilerParams(vmem_limit_bytes=VMEM_MIB * 1024 * 1024)
 
 
 def cost(flops, size):
@@ -68,11 +63,10 @@
     )
 
 
-def normalize(stream, stats, steering, gain, down, h, hid, beside=None):
+def normalize(stream, stats, steering, gain, down, h, hid, after=()):
     tokens, width = stream.shape
     block = tokens // hid
     ranks = down.shape[0]
-    n_beside = 0 if beside is None else 1
 
     def token_block(p, h_ref):
         return h_ref[0] ^ reversed_bits(p, bits_of(hid))
@@ -80,14 +74,10 @@
     def kernel(h_ref, x_ref, stat_ref, steer_ref, gain_ref, down_ref, *refs):
         steered = x_ref[...].astype(F32) + stat_ref[:, :1] * steer_ref[...]
         normed = (steered * stat_ref[:, 1:] * gain_ref[...]).astype(BF16)
-        out_ref, low_ref = refs[n_beside : n_beside + 2]
-        out_ref[...] = normed
-        low_ref[...] = lax.dot_general(
+        refs[-2][...] = normed
+        refs[-1][...] = lax.dot_general(
             normed, down_ref[...], (((1,), (1,)), ((), ())), preferred_element_type=F32
         )
-        if n_beside:
-            refs[-1][:block, :] = refs[0][...]
-            refs[-1][block:, :] = normed
 
     whole = lambda n: pl.BlockSpec((n, width), lambda p, h_ref: (0, 0))
     rows = lambda n, m: pl.BlockSpec((n, m), lambda p, h_ref: (p, 0))
@@ -103,14 +93,13 @@
                 whole(1),
                 whole(ranks),
             ]
-            + [rows(block, width)] * n_beside,
-            out_specs=[rows(block, width), rows(block, ranks)] + [rows(2 * block, width)] * n_beside,
+            + [ANY] * len(after),
+            out_specs=[rows(block, width), rows(block, ranks)],
         ),
         out_shape=[
             jax.ShapeDtypeStruct((tokens, width), BF16),
             jax.ShapeDtypeStruct((tokens, ranks), F32),
-        ]
-        + [jax.ShapeDtypeStruct((2 * tokens, width), BF16)] * n_beside,
+        ],
         compiler_params=params(),
         cost_estimate=cost(2 * tokens * width * ranks, 4 * tokens * width),
         name="normalize",
@@ -121,8 +110,25 @@
         steering.reshape(1, width),
         gain.reshape(1, width),
         down,
-        *((beside,) if n_beside else ()),
+        *after,
     )
+
+
+def relay(x, after):
+    def kernel(x_ref, *refs):
+        refs[-1][...] = x_ref[...]
+
+    whole = pl.BlockSpec(x.shape, lambda i: (0,) * x.ndim)
+    return pl.pallas_call(
+        kernel,
+        grid=(1,),
+        in_specs=[whole] + [ANY] * len(after),
+        out_specs=whole,
+        out_shape=jax.ShapeDtypeStruct(x.shape, x.dtype),
+        compiler_params=params(),
+        cost_estimate=cost(0, 4 * x.size),
+        name="relay",
+    )(x, *after)
 
 
 def forward_matmul(x, weights, first, tiles, start, stop, tile, into=(), after=()):
@@ -149,7 +155,7 @@
             jax.ShapeDtypeStruct((8, 128), F32),
         ],
         input_output_aliases={2 + i: i for i in range(len(into))},
-        compiler_params=params(MATMUL_VMEM_MIB),
+        compiler_params=params(),
         cost_estimate=cost(2 * rows * depth * (stop - start) * tile, 2 * depth * (rows + (stop - start) * tile) + 6 * half * (stop - start) * tile),
         name="forward_matmul",
     )(x, weights, *into, *after)
@@ -294,7 +300,7 @@
         + [ANY] * len(after),
         out_specs=out_specs,
         out_shape=out_shape,
-        compiler_params=params(MATMUL_VMEM_MIB),
+        compiler_params=params(),
         cost_estimate=cost(2 * rows * hidden * tiles * tile, 2 * hidden * (rows + tiles * tile) + (4 + 4 * n_base) * rows * tiles * tile),
         name="backward_matmul",
     )(*pieces, weights, *(() if base is None else (base,)), *after)
@@ -422,6 +428,7 @@
         chunks = [(0, (count + 1) // 2), ((count + 1) // 2, count // 2)]
         last_bit = 1 << (bits_of(hid) - 1)
         own_normed, own_low = normalize(stream, stats, steering, gain, down_rows, h, hid)
+
         def forward(x, c, edges, afters):
             first, n = chunks[c]
             out, token = (), None
@@ -435,31 +442,64 @@
                 size = parts[-1].shape[0]
                 send = total_of(parts, size // 2, size).astype(BF16)
                 parts.append(swap(send, "hid", hid, 1 << bit))
-            return parts
-
-        own_parts = forward(own_normed, 0, (0, chunks[0][1]), (lambda t: (),))
-        (own_send,) = share_sums(own_parts, own, 1)
-        own_got = swap(own_send, "hid", hid, last_bit)
-        peer_normed, peer_low, normed = normalize(
-            peer_stream, ordered(peer_stats, own_send), steering, gain, down_rows, h, hid, own_normed
-        )
-
-        low, low_steps = jnp.stack([own_low, peer_low]), []
-        for bit in range(bits_of(hid)):
-            half = low.shape[1] // 2
-            low = low[:, :half] + swap(low[:, half:], "hid", hid, 1 << bit)
-            low_steps.append(low)
-        low = low.astype(BF16)
-        low_own = low[0]
+            return parts, token
 
         width_tile = tile_of(width, 512)
         tiles = width // width_tile
-        steps = [(0, 3), (3, 3), (6, 2)] if tiles == 8 else split_tiles(tiles, 3)
-        acts, others, grads = [], [], []
+        steps = [(0, 2), (2, 3), (5, 3)] if tiles == 8 else split_tiles(tiles, 3)
+
+        own_parts, own_sends, own_gots = [], [], []
+        for c in range(2):
+            wait = tuple(own_sends)
+            parts, token = forward(own_normed, c, (0, chunks[c][1]), (lambda t: wait,))
+            own_parts.append(parts)
+            (send,) = share_sums(own_parts[c], own, 1)
+            own_sends.append(send)
+            own_gots.append(swap(send, "hid", hid, last_bit))
+
+        peer_normed, _ = normalize(
+            peer_stream, peer_stats, steering, gain, down_rows, h, hid, (own_sends[0], token)
+        )
+
+        low, low_steps = relay(own_low, (peer_normed,)), []
+        for bit in range(bits_of(hid)):
+            half = low.shape[0] // 2
+            low = low[:half] + swap(low[half:], "hid", hid, 1 << bit)
+            low_steps.append(low)
+        low_own = low.astype(BF16)
+
+        passed, others = [], []
+
+        def pass_on(c, after):
+            terms = peer_parts[c] + [peer_gots[c]]
+            (sums,) = share_sums(terms, own, 1, after, [0] * len(terms))
+            passed.append(sums)
+            others.append(swap(sums, "dp", dp, 1))
+
+        def after_first_part(token):
+            pass_on(0, (token,))
+            return (passed[0],)
+
+        peer_parts, peer_sends, peer_gots = [], [], []
+        waits = [
+            (
+                lambda t: (own_sends[1],),
+                lambda t: (own_gots[0], low_steps[0]),
+                lambda t: (own_gots[1],),
+            ),
+            (lambda t: (peer_sends[0],), after_first_part),
+        ]
+        for c in range(2):
+            n = chunks[c][1]
+            edges = (0, 2 * n // 3, n) if c else (0, 3 * n // 7, 5 * n // 7, n)
+            peer_parts.append(forward(peer_normed, c, edges, waits[c])[0])
+            (send,) = share_sums(peer_parts[c], own, 1, () if c else (low_own,))
+            peer_sends.append(send)
+            peer_gots.append(swap(send, "hid", hid, last_bit))
 
         def gradients(c, after):
             mine_grad, other_grad, back_part = gated_gradients(
-                d, acts[c], others[c], cotangent, chunks[c][0] * tile, low_own, up, own, after
+                d, own_parts[c] + [own_gots[c]], others[c], cotangent, chunks[c][0] * tile, low_own, up, own, after
             )
             return back_part, mine_grad, swap(other_grad, "dp", dp, 1)
 
@@ -469,66 +509,29 @@
                 blocks += [swap(x, "hid", hid, 1 << bit) for x in blocks]
             return blocks
 
-        n = chunks[0][1]
-        peer_parts = forward(
-            peer_normed, 0, (0, (n + 1) // 2, n), (lambda t: (own_send,), lambda t: (low_steps[0], own_got))
-        )
-        (peer_send,) = share_sums(peer_parts, own, 1, (low_own,))
-        peer_got = swap(peer_send, "hid", hid, last_bit)
-        acts.append(own_parts + [own_got])
-
-        def pass_on(token):
-            terms = peer_parts + [peer_got]
-            (passed,) = share_sums(terms, own, 1, (token,), [0] * len(terms))
-            others.append(swap(passed, "dp", dp, 1))
-            return peer_got, passed
-
-        n = chunks[1][1]
-        first_send = peer_send
-        first_half_done = []
-
-        def first_gradients(token):
-            more, mine_grad, peer_grad = gradients(0, (token,))
-            own_pieces, peer_pieces = spread(mine_grad), spread(peer_grad)
-            grads.append(own_pieces + peer_pieces)
-            first_half_done.append(more)
-            return peer_grad, own_pieces[1]
-
-        parts = forward(
-            normed, 1, (0, n // 3, n - 1, n), (lambda t: (first_send,), pass_on, first_gradients)
-        )
-        own_send, peer_send = share_sums(parts, own, 2)
-        peer_got = swap(peer_send, "hid", hid, last_bit)
-        own_got = swap(own_send, "hid", hid, last_bit)
-        bases = []
+        back, mine_grad, peer_grad = gradients(0, (peer_sends[1],))
+        own_pieces = spread(mine_grad)
+        pass_on(1, (own_pieces[1],))
+        peer_pieces = spread(relay(peer_grad, (passed[1],)))
+        grads = [own_pieces + peer_pieces]
+        more, mine_grad, peer_grad = gradients(1, (peer_pieces[1],))
+        back = back + more
 
         def first_half(j, after):
             first, n = steps[j]
-            bases.append(
-                backward_matmul(
-                    grads[0], weights, 0, first, n, width_tile, partial=True, after=after
-                )
-            )
-
-        first_half(0, (own_send,))
-        (passed,) = share_sums(parts + [peer_got], own, 1, (bases[0],), [1] * len(parts) + [0])
-        acts.append(parts + [own_got])
-        others.append(swap(passed, "dp", dp, 1))
-        more, mine_grad, peer_grad = gradients(1, ())
-        back = first_half_done[0] + more
+            return backward_matmul(grads[0], weights, 0, first, n, width_tile, partial=True, after=after)
+
+        bases = [first_half(0, (mine_grad,))]
+        own_pieces = spread(mine_grad)
+        peer_pieces = spread(relay(peer_grad, (bases[0],)))
+        grads.append(own_pieces + peer_pieces)
+        back_steps = []
         for bit in range(bits_of(ffn)):
             back = back + swap(back, "ffn", ffn, 1 << bit)
-        back = jnp.stack([back, swap(back, "dp", dp, 1)])
+            back_steps.append(back)
         for j in range(1, len(steps)):
-            first_half(j, (mine_grad,) if j == 1 else (peer_grad, back))
-            if j == 1:
-                (peer_grad,) = share_sums([peer_grad], own, 1, (bases[1],), [0])
-        own_pieces = spread(mine_grad)
-        grads.append(own_pieces + spread(peer_grad))
-
-        back = double(back, "hid", hid, dim=1)
-        low_mine = jnp.where(first_pair, low[:, :, :rank], low[:, :, rank:])
-        low_mine = double(low_mine, "hid", hid, dim=1).reshape(2 * tokens, rank).T
+            bases.append(first_half(j, (own_pieces[1], back_steps[0], bases[-1])))
+
         shard = tokens // ffn
         place = reversed_bits(f, bits_of(ffn))
         products, received = [], []
@@ -542,20 +545,27 @@
             ]
             return total_of(sides[0], 0, half), total_of(sides[1], 0, half).astype(BF16)
 
-        first_steps = []
-        for j, ((first, n), base) in enumerate(zip(steps, bases)):
-            wait = (products[-1],) if products else tuple(bases)
+        begun = []
+        for j, (first, n) in enumerate(steps):
+            wait = (products[-1],) if products else (bases[-1], back_steps[-1])
             if j == 2:
-                first_steps.append(halving_step([products[0], received[0]], 0))
-                wait += (first_steps[0][1], back, low_mine)
+                back = double(relay(back, (products[0],)), "hid", hid)
+                keep, send = halving_step([products[0], received[0]], 0)
+                begun = [keep, swap(send, "ffn", ffn, 1)]
+                wait += (back, begun[1])
             keep, send = backward_matmul(
-                grads[1], weights, chunks[1][0] * tile, first, n, width_tile, base=base, base_first=first,
+                grads[1], weights, chunks[1][0] * tile, first, n, width_tile, base=bases[j], base_first=first,
                 after=wait,
             )
             products.append(keep)
             received.append(swap(send, "dp", dp, 1))
-        back_low = back[:, :, : 2 * rank].astype(BF16)
-        acts_product = back[0, :, 2 * rank]
+        low_all = double(relay(low_own, (products[-1],)), "hid", hid)
+        low_mine = jnp.where(first_pair, low_all[:, :rank], low_all[:, rank:])
+        low_other = swap(jnp.where(first_pair, low_all[:, rank:], low_all[:, :rank]), "dp", dp, 1)
+        if len(steps) < 3:
+            back = double(back, "hid", hid)
+        back_low = back[:, : 2 * rank].astype(BF16)
+        acts_product = back[:, 2 * rank]
 
         block = min(own, shard)
 
@@ -577,25 +587,18 @@
         dot_factor = stats_shard[:, 1] ** 2 * dot_shard / MODEL_WIDTH
         stats_shard = jnp.concatenate([stats_shard, dot_factor[:, None]], axis=1)
         stream_shard = shard_rows(stream)
-        back_shard = lax.dynamic_slice_in_dim(back_low[0], place * shard, shard, axis=0)
+        back_shard = lax.dynamic_slice_in_dim(back_low, place * shard, shard, axis=0)
 
         out, sums, gathered = None, [], []
         owners = [reversed_bits(f ^ reversed_bits(p, bits_of(ffn)), bits_of(ffn)) for p in range(ffn)]
         places = jnp.stack([natural(o * shard + i * block) for o in owners for i in range(shard // block)])
         for j, (first, n) in enumerate(steps):
-            got = received[j]
-            if j == 1:
-                got = ordered(got, products[-1])
-            elif j >= 2:
-                got = ordered(got, gathered[j - 2][1])
-            parts = [products[j], got]
+            parts = [products[j], received[j]]
             for bit in range(bits_of(ffn)):
-                if bit == 0 and j < len(first_steps):
-                    keep, send = first_steps[j]
-                else:
-                    keep, send = halving_step(parts, bit)
-                if j == 2 and bit == 1:
-                    send = ordered(send, gathered[0][-1])
+                if j == 0 and bit == 0 and begun:
+                    parts = begun
+                    continue
+                keep, send = halving_step(parts, bit)
                 parts = [keep, swap(send, "ffn", ffn, 1 << bit)]
             result, sum_part = finish(
                 parts, stream_shard, stats_shard, back_shard, down_rows, steering, gain, first * width_tile,
@@ -603,7 +606,8 @@
             )
             sums.append(sum_part)
             if j == len(steps) - 1:
-                sums = jnp.concatenate(sums, axis=1).reshape(-1, result.shape[1])
+                sums = jnp.concatenate(sums, axis=1)
+                sums = jnp.pad(sums, ((0, 0), (0, -width % result.shape[1]))).reshape(-1, result.shape[1])
                 high = sums.astype(BF16)
                 low_term = (sums - high.astype(F32)).astype(BF16)
                 rows = 2 * sums.shape[0]
@@ -623,17 +627,19 @@
             terms = [a + b for a, b in zip(terms[: len(terms) // 2], terms[len(terms) // 2 :])]
         steering_gradient = terms[0] + swap(terms[0], "dp", dp, 1)
 
-        up_mine = jnp.concatenate(adapter_products(low_mine, grads, products[-1:]), axis=1)
-        up_other = swap(ordered(up_mine.astype(BF16), received[-1]), "dp", dp, 1).astype(F32)
+        low_rows = jnp.concatenate([low_mine, low_other], axis=0).T
+        up_mine = jnp.concatenate(adapter_products(low_rows, grads, (received[-1],)), axis=1)
+        up_other = swap(up_mine.astype(BF16), "dp", dp, 1).astype(F32)
         up_gradient = jnp.where(
             first_pair, jnp.stack([up_mine, up_other]), jnp.stack([up_other, up_mine])
         )
-        back_rows = back_low.reshape(2, hid, own, 2 * rank).transpose(1, 0, 2, 3).reshape(2 * tokens, 2 * rank)
-        (down_gradient,) = adapter_products(back_rows.T, [[normed]])
+        peer_back = swap(relay(back_low, (received[-1],)), "dp", dp, 1)
+        back_rows = jnp.concatenate([back_low, peer_back], axis=0).T
+        (down_gradient,) = adapter_products(back_rows, [[own_normed, peer_normed]])
         down_gradient = jnp.transpose(
             down_gradient.reshape(2, rank, width), (0, 2, 1)
         )
-        return out, steering_gradient.reshape(width), down_gradient, up_gradient
+        return out, steering_gradient.reshape(-1)[:width], down_gradient, up_gradient
 
     return local
 

time: 352 us -> 393 us (1.12)
  local copies, waits for them, and re-layouts: 27.8 us -> 56.6 us
  waiting for transfers between devices: 106 us -> 86 us
  Pallas kernels: 130 us -> 147 us
  other arithmetic: 18.1 us -> 26.5 us
  starting transfers between devices: 52.6 us -> 58.1 us
    unnamed x136 -> x191, local copies, waits for them, and re-layouts: 22.9 us -> 46.5 us
    ppermute x54 -> x56, waiting for transfers between devices: 106 us -> 86 us  [swap(): return lax.ppermute(x, axis, [(i, i ^ mask) for i in range(n)])]
    convert_element_type x5, other arithmetic: 4.38 us -> 10.8 us  [halving_step(): total_of(sides[1], 0, half).astype(BF16)]
    ppermute x54 -> x56, starting transfers between devices: 52.6 us -> 58.1 us  [swap(): return lax.ppermute(x, axis, [(i, i ^ mask) for i in range(n)])]
    pallas_call x3, Pallas kernels: 0.75 us -> 4.93 us  [finish(): pl.pallas_call(kernel, grid=(1,), in_specs=[pl.BlockSpec((rows, width), l...]
    pallas_call x6 -> x7, Pallas kernels: 56.1 us -> 60.2 us  [forward_matmul(): pl.pallas_call(kernel, grid=(stop - start,), in_specs=[RESIDENT, pl.Block...]
  transfers between devices with their start and end apart: 54 -> 56, of which waited for: 27 -> 22; matrix products, arithmetic and copies ran while one was open for 7% -> 9% of each run, Pallas kernels for 28% -> 32%
where the time goes in v7:
time: 393 us; the launch traced here: 389 us
  Pallas kernels  147 us (37%)
  waiting for transfers between devices  86 us (22%)
  starting transfers between devices  58.1 us (15%)
  local copies, waits for them, and re-layouts  56.6 us (14%)
  other arithmetic  26.5 us (7%)
  blocking collectives  13.4 us (3%)
    ppermute x56, waiting for transfers between devices, swap(): return lax.ppermute(x, axis, [(i, i ^ mask) for i in range(n)])  86 us
    pallas_call x7, Pallas kernels, forward_matmul(): pl.pallas_call(kernel, grid=(stop - start,), in_specs=[RESIDENT, pl.Block...  60.2 us
    ppermute x56, starting transfers between devices, swap(): return lax.ppermute(x, axis, [(i, i ^ mask) for i in range(n)])  58.1 us
    pallas_call x6, Pallas kernels, backward_matmul(): pl.pallas_call(kernel, grid=(tiles,), in_specs=[pl.BlockSpec(g.shape, lam...  51.9 us
    unnamed x191, local copies, waits for them, and re-layouts  46.5 us
    convert_element_type x5, other arithmetic, halving_step(): total_of(sides[1], 0, half).astype(BF16)  10.8 us
    pallas_call x2, Pallas kernels, gated_gradients(): pl.pallas_call(kernel, grid_spec=pltpu.PrefetchScalarGridSpec(num_scalar_...  8.25 us
  transfers between devices with their start and end apart: 56, of which 22 were waited for; matrix products, arithmetic and copies ran while one was open for 9% of the time, Pallas kernels for 32%

profile of v7, /device:TPU:0, one launch (start us, length us, event | category | flops | bytes accessed | tf_op | source)
XLA Modules:
  0.0 389.5 jit_solution(2575735899960527754)
XLA Ops:
  0.7 3.0 collective-permute-start.3
  3.7 2.1 fusion
  7.2 7.3 %all-reduce.1 = (f32[256]{0:T(256)S(1)}, f32[]{:T(128)}) all-reduce(f32[256]{0:T(256)S(1)} %fusion, f32[]{:T(128)} %multiply_reduce_fusion), channel_id=1, replica_groups=mesh['dp'=2,'ffn'=4,'hid'=4] {'hid'}, use_global_device_ids=true, to_apply=%region_1.0 | all-reduce | flops 257 | bytes 2056 | tf_op jit(solution)/shard_map/psum | solution.py:414
  16.0 6.1 %psum.23 = f32[256]{0:T(256)S(1)} all-reduce(f32[256]{0:T(256)S(1)} %fusion.2), channel_id=1, replica_groups=mesh['dp'=2,'ffn'=4,'hid'=4] {'hid'}, use_global_device_ids=true, to_apply=%region_5.0 | all-reduce | flops 256 | bytes 2048 | tf_op jit(solution)/shard_map/psum | solution.py:421
  22.7 1.7 normalize.2
  24.4 15.3 %forward_matmul.7 = (f32[128,3584]{1,0:T(8,128)S(1)}, bf16[128,3584]{1,0:T(8,128)(2,1)S(1)}, f32[8,128]{1,0:T(8,128)}) custom-call(bf16[256,4096]{1,0:T(8,128)(2,1)S(1)} %get-tuple-element.43.x_ref.refs_1_, bf16[1,4096,6656]{2,1,0:T(8,128)(2,1)} %refs_8_.11), custom_call_target="tpu_custom_call" | custom-call | flops 75161928 | bytes 342097 | tf_op jit(solution)/shard_map/forward_matmul/pallas_call | solution.py:145
  39.7 2.5 collective-permute-done.refs_1_
  44.5 12.1 %forward_matmul.8 = (f32[128,3072]{1,0:T(8,128)S(1)}, bf16[128,3072]{1,0:T(8,128)(2,1)S(1)}, f32[8,128]{1,0:T(8,128)S(1)}) custom-call(bf16[256,4096]{1,0:T(8,128)(2,1)S(1)} %get-tuple-element.43.x_ref.refs_1_, bf16[1,4096,6656]{2,1,0:T(8,128)(2,1)} %refs_8_.11, bf16[64,3584]{1,0:T(8,128)(2,1)} %share_sums.6.refs_0_), custom_call_target="tpu_custom_call" | custom-call | flops 64424508 | bytes 296222 | tf_op jit(solution)/shard_map/forward_matmul/pallas_call | solution.py:145
  62.2 3.1 collective-permute-done.4
  65.4 4.2 %normalize.3 = (bf16[256,4096]{1,0:T(8,128)(2,1)S(1)}, f32[256,32]{1,0:T(8,128)}) custom-call(s32[1]{0:T(128)} %bitcast.5.h_ref, bf16[256,4096]{1,0:T(8,128)(2,1)} %collective-permute-done.3.x_ref, f32[256,2]{1,0:T(8,128)S(1)} %copy.21.stat_ref, f32[1,4096]{1,0:T(1,128)S(1)} %bitcast.30, f32[1,4096]{1,0:T(1,128)S(1)} %bitcast.35, ...), custom_call_target="tpu_custom_call" | custom-call | flops 671088 | bytes 41943 | tf_op jit(solution)/shard_map/normalize/pallas_call | solution.py:84
  69.7 7.5 %forward_matmul.9 = (f32[128,3584]{1,0:T(8,128)S(1)}, bf16[128,3584]{1,0:T(8,128)(2,1)S(1)}, f32[8,128]{1,0:T(8,128)}) custom-call(bf16[256,4096]{1,0:T(8,128)(2,1)S(1)} %get-tuple-element.49.x_ref.refs_0_.refs_2_, bf16[1,4096,6656]{2,1,0:T(8,128)(2,1)} %refs_8_.11, bf16[64,3072]{1,0:T(8,128)(2,1)} %share_sums.7.refs_0_), custom_call_target="tpu_custom_call" | custom-call | flops 32212254 | bytes 158597 | tf_op jit(solution)/shard_map/forward_matmul/pallas_call | solution.py:145
  77.3 5.3 %forward_matmul.10 = (f32[128,3584]{1,0:T(8,128)S(1)}, bf16[128,3584]{1,0:T(8,128)(2,1)S(1)}, f32[8,128]{1,0:T(8,128)}) custom-call(bf16[256,4096]{1,0:T(8,128)(2,1)S(1)} %get-tuple-element.49.x_ref.refs_0_.refs_2_, bf16[1,4096,6656]{2,1,0:T(8,128)(2,1)} %refs_8_.11, ...), custom_call_target="tpu_custom_call", output_to_operand_aliasing={{0}: (2, {}), {1}: (3, {})} | custom-call | flops 21474836 | bytes 112721 | tf_op jit(solution)/shard_map/forward_matmul/pallas_call | solution.py:145
  82.6 5.3 %forward_matmul.11 = (f32[128,3584]{1,0:T(8,128)S(1)}, bf16[128,3584]{1,0:T(8,128)(2,1)S(1)}, f32[8,128]{1,0:T(8,128)}) custom-call(bf16[256,4096]{1,0:T(8,128)(2,1)S(1)} %get-tuple-element.49.x_ref.refs_0_.refs_2_, bf16[1,4096,6656]{2,1,0:T(8,128)(2,1)} %refs_8_.11, ...), custom_call_target="tpu_custom_call", output_to_operand_aliasing={{0}: (2, {}), {1}: (3, {})} | custom-call | flops 21474836 | bytes 112721 | tf_op jit(solution)/shard_map/forward_matmul/pallas_call | solution.py:145
  89.6 2.8 collective-permute-done.8
  93.9 9.2 %forward_matmul.12 = (f32[128,3072]{1,0:T(8,128)S(1)}, bf16[128,3072]{1,0:T(8,128)(2,1)}, f32[8,128]{1,0:T(8,128)S(1)}) custom-call(bf16[256,4096]{1,0:T(8,128)(2,1)S(1)} %get-tuple-element.49.x_ref.refs_0_.refs_2_, bf16[1,4096,6656]{2,1,0:T(8,128)(2,1)} %refs_8_.11, bf16[64,3584]{1,0:T(8,128)(2,1)S(1)} %share_sums.8.refs_0_), custom_call_target="tpu_custom_call" | custom-call | flops 42949672 | bytes 204472 | tf_op jit(solution)/shard_map/forward_matmul/pallas_call | solution.py:145
  105.0 5.4 %forward_matmul.13 = (f32[128,3072]{1,0:T(8,128)S(1)}, bf16[128,3072]{1,0:T(8,128)(2,1)}, f32[8,128]{1,0:T(8,128)}) custom-call(bf16[256,4096]{1,0:T(8,128)(2,1)S(1)} %get-tuple-element.49.x_ref.refs_0_.refs_2_, bf16[1,4096,6656]{2,1,0:T(8,128)(2,1)} %refs_8_.11, ...), custom_call_target="tpu_custom_call", output_to_operand_aliasing={{0}: (2, {}), {1}: (3, {})} | custom-call | flops 21474836 | bytes 112721 | tf_op jit(solution)/shard_map/forward_matmul/pallas_call | solution.py:145
  112.1 2.0 collective-permute-done.10.refs_1_
  114.1 1.7 copy-done.11
  116.0 8.8 %collective-permute-done.12.refs_3_ = bf16[64,3584]{1,0:T(8,128)(2,1)} collective-permute-done((bf16[64,3584]{1,0:T(8,128)(2,1)}, bf16[64,3584]{1,0:T(8,128)(2,1)}, u32[]{:S(2)}, u32[]{:S(2)}) %collective-permute-start.12) | collective-permute-done | bytes 458784 | tf_op jit(solution)/shard_map/ppermute | solution.py:40
  128.2 3.2 gated_gradients.2
  134.1 17.9 %collective-permute-done.11.refs_2_ = bf16[64,3072]{1,0:T(8,128)(2,1)S(1)} collective-permute-done((bf16[64,3072]{1,0:T(8,128)(2,1)S(1)}, bf16[64,3072]{1,0:T(8,128)(2,1)S(1)}, u32[]{:S(2)}, u32[]{:S(2)}) %collective-permute-start.11) | collective-permute-done | bytes 393248 | tf_op jit(solution)/shard_map/ppermute | solution.py:40
  154.8 8.9 %collective-permute-done.16.refs_7_.refs_5_.refs_6_ = bf16[64,3584]{1,0:T(8,128)(2,1)S(1)} collective-permute-done((bf16[64,3584]{1,0:T(8,128)(2,1)S(1)}, bf16[64,3584]{1,0:T(8,128)(2,1)S(1)}, u32[]{:S(2)}, u32[]{:S(2)}) %collective-permute-start.16) | collective-permute-done | bytes 458784 | tf_op jit(solution)/shard_map/ppermute | solution.py:40
  163.8 5.1 %gated_gradients.3 = (bf16[64,3072]{1,0:T(8,128)(2,1)}, bf16[64,3072]{1,0:T(8,128)(2,1)S(1)}, f32[64,33]{1,0:T(8,128)S(1)}) custom-call(s32[1]{0:T(128)} %bitcast.4.d_ref, f32[128,3072]{1,0:T(8,128)S(1)} %copy-done.49, bf16[128,3072]{1,0:T(8,128)(2,1)S(1)} %copy-done.58, bf16[64,3072]{1,0:T(8,128)(2,1)} %collective-permute-done.2.refs_2_, ...), custom_call_target="tpu_custom_call" | custom-call | flops 251658 | bytes 31457 | tf_op jit(solution)/shard_map/gated_gradients/pallas_call | solution.py:235
  170.8 7.0 %backward_matmul.6.refs_0_.refs_11_.refs_9_ = f32[512,1024]{1,0:T(8,128)S(1)} custom-call(bf16[64,3584]{1,0:T(8,128)(2,1)S(1)} %get-tuple-element.62.refs_0_.refs_1_, bf16[64,3584]{1,0:T(8,128)(2,1)S(1)} %collective-permute-done.13.refs_3_.refs_1_.refs_2_, bf16[64,3584]{1,0:T(8,128)(2,1)S(1)} %collective-permute-done.21.refs_2_.refs_3_, ...), custom_call_target="tpu_custom_call" | custom-call | flops 37580964 | bytes 131072 | tf_op jit(solution)/shard_map/backward_matmul/pallas_call | solution.py:287
  177.8 2.6 collective-permute-done.20.x_ref
  184.2 9.4 %collective-permute-done.25.refs_5_.refs_14_ = bf16[64,3072]{1,0:T(8,128)(2,1)} collective-permute-done((bf16[64,3072]{1,0:T(8,128)(2,1)}, bf16[64,3072]{1,0:T(8,128)(2,1)}, u32[]{:S(2)}, u32[]{:S(2)}) %collective-permute-start.25) | collective-permute-done | bytes 393248 | tf_op jit(solution)/shard_map/ppermute | solution.py:40
  193.6 1.6 collective-permute-start.28
  195.2 2.3 collective-permute-done.28
  197.5 2.6 collective-permute-start.29
  200.2 2.2 collective-permute-done.29
  210.1 8.7 %backward_matmul.7.refs_11_.refs_9_ = f32[512,1536]{1,0:T(8,128)S(1)} custom-call(bf16[64,3584]{1,0:T(8,128)(2,1)S(1)} %copy-done.24, bf16[64,3584]{1,0:T(8,128)(2,1)S(1)} %collective-permute-done.13.refs_3_.refs_1_.refs_2_, bf16[64,3584]{1,0:T(8,128)(2,1)S(1)} %copy-done.28, bf16[64,3584]{1,0:T(8,128)(2,1)S(1)} %copy-done.36, ...), custom_call_target="tpu_custom_call" | custom-call | flops 56371444 | bytes 178257 | tf_op jit(solution)/shard_map/backward_matmul/pallas_call | solution.py:287
  218.9 9.7 %backward_matmul.8.refs_10_.refs_9_ = f32[512,1536]{1,0:T(8,128)S(1)} custom-call(bf16[64,3584]{1,0:T(8,128)(2,1)S(1)} %copy-done.25, bf16[64,3584]{1,0:T(8,128)(2,1)S(1)} %collective-permute-done.13.refs_3_.refs_1_.refs_2_, bf16[64,3584]{1,0:T(8,128)(2,1)S(1)} %copy-done.29, bf16[64,3584]{1,0:T(8,128)(2,1)S(1)} %copy-done.37, ...), custom_call_target="tpu_custom_call" | custom-call | flops 56371444 | bytes 178257 | tf_op jit(solution)/shard_map/backward_matmul/pallas_call | solution.py:287
  228.7 8.2 %backward_matmul.9 = (f32[256,1024]{1,0:T(8,128)S(1)}, bf16[256,1024]{1,0:T(8,128)(2,1)}) custom-call(bf16[64,3072]{1,0:T(8,128)(2,1)} %get-tuple-element.64.refs_9_.refs_0_, bf16[64,3072]{1,0:T(8,128)(2,1)S(1)} %collective-permute-done.17.refs_9_.refs_1_.refs_10_, bf16[64,3072]{1,0:T(8,128)(2,1)} %collective-permute-done.18.refs_2_.refs_11_, ...), custom_call_target="tpu_custom_call" | custom-call | flops 32212254 | bytes 136314 | tf_op jit(solution)/shard_map/backward_matmul/pallas_call | solution.py:287
  237.5 2.0 constant_dynamic-slice_fusion.4.refs_2_
  240.9 1.9 copy-done.6
  244.0 9.1 %backward_matmul.10 = (f32[256,1536]{1,0:T(8,128)S(1)}, bf16[256,1536]{1,0:T(8,128)(2,1)}) custom-call(bf16[64,3072]{1,0:T(8,128)(2,1)} %get-tuple-element.64.refs_9_.refs_0_, bf16[64,3072]{1,0:T(8,128)(2,1)S(1)} %collective-permute-done.17.refs_9_.refs_1_.refs_10_, bf16[64,3072]{1,0:T(8,128)(2,1)} %collective-permute-done.18.refs_2_.refs_11_, ...), custom_call_target="tpu_custom_call" | custom-call | flops 48318384 | bytes 188743 | tf_op jit(solution)/shard_map/backward_matmul/pallas_call | solution.py:287
  256.4 2.4 convert_add_fusion.3
  264.6 3.1 collective-permute-done.33.refs_12_
  267.7 1.9 copy-done.4
  271.0 9.1 %backward_matmul.11 = (f32[256,1536]{1,0:T(8,128)S(1)}, bf16[256,1536]{1,0:T(8,128)(2,1)}) custom-call(bf16[64,3072]{1,0:T(8,128)(2,1)} %get-tuple-element.64.refs_9_.refs_0_, bf16[64,3072]{1,0:T(8,128)(2,1)S(1)} %collective-permute-done.17.refs_9_.refs_1_.refs_10_, bf16[64,3072]{1,0:T(8,128)(2,1)} %collective-permute-done.18.refs_2_.refs_11_, ...), custom_call_target="tpu_custom_call" | custom-call | flops 48318384 | bytes 188743 | tf_op jit(solution)/shard_map/backward_matmul/pallas_call | solution.py:287
  280.9 2.3 add_convert_fusion
  285.7 1.9 add_convert_fusion.5
  287.6 2.8 collective-permute-start.40
  291.7 4.2 %collective-permute-done.40.refs_1_ = bf16[64,1024]{1,0:T(8,128)(2,1)} collective-permute-done((bf16[64,1024]{1,0:T(8,128)(2,1)}, bf16[64,1024]{1,0:T(8,128)(2,1)}, u32[]{:S(2)}, u32[]{:S(2)}) %collective-permute-start.40) | collective-permute-done | bytes 131104 | tf_op jit(solution)/shard_map/ppermute | solution.py:40
  298.9 1.8 finish.3
  301.4 3.4 collective-permute-start.41
  304.7 2.8 add_convert_fusion.1
  307.8 1.9 add_convert_fusion.3
  309.7 2.9 collective-permute-start.39
  317.9 2.0 collective-permute-start.44
  319.9 2.0 collective-permute-done.39.refs_1_
  327.1 1.9 finish.4
  329.5 3.4 collective-permute-start.42
  339.0 2.8 adapter_products.3
  341.9 2.0 add_convert_fusion.4
  343.9 2.9 collective-permute-start.36
  349.5 3.6 collective-permute-done.36.refs_1_
  366.0 2.2 collective-permute-start.49
  368.3 2.4 assemble.3.refs_4_
  371.4 1.6 adapter_products.2
  373.2 2.6 assemble.4.refs_4_
  377.8 4.1 %collective-permute-done.46.refs_2_ = bf16[80,1536]{1,0:T(8,128)(2,1)S(1)} collective-permute-done((bf16[80,1536]{1,0:T(8,128)(2,1)S(1)}, bf16[80,1536]{1,0:T(8,128)(2,1)S(1)}, u32[]{:S(2)}, u32[]{:S(2)}) %collective-permute-start.46) | collective-permute-done | bytes 245792 | tf_op jit(solution)/shard_map/ppermute | solution.py:40
  381.9 2.6 collective-permute-done.47.refs_3_
  384.6 1.8 collective-permute-start.50
  (335 shorter events, 101.1 us)
Async XLA Ops:
  0.7 64.7 %collective-permute-start.3 = (bf16[256,4096]{1,0:T(8,128)(2,1)}, bf16[256,4096]{1,0:T(8,128)(2,1)}, u32[]{:S(2)}, u32[]{:S(2)}) collective-permute-start(bf16[256,4096]{1,0:T(8,128)(2,1)} %x_ref.1), channel_id=1, source_target_pairs={{0,16},{16,0},{1,17},{17,1},{2,18},{18,2},{3,19},{19,3},{4,20},{20... | collective-permute-start | bytes 6291464 | tf_op jit(solution)/shard_map/ppermute | solution.py:40
  3.7 19.0 %copy-start.71 = (f32[4096]{0:T(1024)S(1)}, f32[4096]{0:T(1024)}, u32[]{:S(2)}) copy-start(f32[4096]{0:T(1024)} %param.11) | copy-start | bytes 49156
  39.7 2.5 collective-permute-start
  56.6 2.4 collective-permute-start.1
  56.8 20.4 %collective-permute-start.5 = (bf16[64,3584]{1,0:T(8,128)(2,1)}, bf16[64,3584]{1,0:T(8,128)(2,1)}, u32[]{:S(2)}, u32[]{:S(2)}) collective-permute-start(bf16[64,3584]{1,0:T(8,128)(2,1)} %share_sums.6.refs_0_), channel_id=1, source_target_pairs={{0,2},{1,3},{2,0},{3,1},{4,6},{5,7},{6,4},{7,5},{8,10},{9,11},{10,... | collective-permute-start | bytes 1376264 | tf_op jit(solution)/shard_map/ppermute | solution.py:40
  60.8 21.8 %collective-permute-start.2 = (bf16[64,3072]{1,0:T(8,128)(2,1)}, bf16[64,3072]{1,0:T(8,128)(2,1)}, u32[]{:S(2)}, u32[]{:S(2)}) collective-permute-start(bf16[64,3072]{1,0:T(8,128)(2,1)} %share_sums.7.refs_0_), channel_id=1, source_target_pairs={{0,2},{1,3},{2,0},{3,1},{4,6},{5,7},{6,4},{7,5},{8,10},{9,11},{10,... | collective-permute-start | bytes 1179656 | tf_op jit(solution)/shard_map/ppermute | solution.py:40
  61.7 3.6 collective-permute-start.4
  69.6 7.6 %collective-permute-start.6 = (f32[128,32]{1,0:T(8,128)S(1)}, f32[128,32]{1,0:T(8,128)S(1)}, u32[]{:S(2)}, u32[]{:S(2)}) collective-permute-start(f32[128,32]{1,0:T(8,128)S(1)} %slice.68), channel_id=1, source_target_pairs={{0,1},{1,0},{2,3},{3,2},{4,5},{5,4},{6,7},{7,6},{8,9},{9,8},{10,11... | collective-permute-start | bytes 49160 | tf_op jit(solution)/shard_map/ppermute | solution.py:40
  87.9 4.4 %collective-permute-start.7 = (bf16[128,3584]{1,0:T(8,128)(2,1)S(1)}, bf16[128,3584]{1,0:T(8,128)(2,1)S(1)}, u32[]{:S(2)}, u32[]{:S(2)}) collective-permute-start(bf16[128,3584]{1,0:T(8,128)(2,1)S(1)} %get-tuple-element.56), channel_id=1, source_target_pairs={{0,1},{1,0},{2,3},{3,2},{4,5},{5,4},{6,7},{7,6},{8,9},{9,8},{10,11... | collective-permute-start | bytes 2752520 | tf_op jit(solution)/shard_map/ppermute | solution.py:40
  88.4 3.9 %collective-permute-start.8 = (f32[64,32]{1,0:T(8,128)S(1)}, f32[64,32]{1,0:T(8,128)S(1)}, u32[]{:S(2)}, u32[]{:S(2)}) collective-permute-start(f32[64,32]{1,0:T(8,128)S(1)} %slice.70), channel_id=1, source_target_pairs={{0,2},{1,3},{2,0},{3,1},{4,6},{5,7},{6,4},{7,5},{8,10},{9,11},{10,... | collective-permute-start | bytes 24584 | tf_op jit(solution)/shard_map/ppermute | solution.py:40
  92.6 11.4 %collective-permute-start.9 = (bf16[64,3584]{1,0:T(8,128)(2,1)S(1)}, bf16[64,3584]{1,0:T(8,128)(2,1)S(1)}, u32[]{:S(2)}, u32[]{:S(2)}) collective-permute-start(bf16[64,3584]{1,0:T(8,128)(2,1)S(1)} %share_sums.8.refs_0_), channel_id=1, source_target_pairs={{0,2},{1,3},{2,0},{3,1},{4,6},{5,7},{6,4},{7,5},{8,10},{9,11},{10,... | collective-permute-start | bytes 1376264 | tf_op jit(solution)/shard_map/ppermute | solution.py:40
  111.6 2.5 collective-permute-start.10
  111.6 13.2 %collective-permute-start.12 = (bf16[64,3584]{1,0:T(8,128)(2,1)}, bf16[64,3584]{1,0:T(8,128)(2,1)}, u32[]{:S(2)}, u32[]{:S(2)}) collective-permute-start(bf16[64,3584]{1,0:T(8,128)(2,1)} %share_sums.9.refs_2_), channel_id=1, source_target_pairs={{0,16},{16,0},{1,17},{17,1},{2,18},{18,2},{3,19},{19,3},{4,20},{20... | collective-permute-start | bytes 1376264 | tf_op jit(solution)/shard_map/ppermute | solution.py:40
  128.2 23.9 %copy-start.12 = (f32[128,3072]{1,0:T(8,128)S(1)}, f32[128,3072]{1,0:T(8,128)}, u32[]{:S(2)}) copy-start(f32[128,3072]{1,0:T(8,128)} %copy-done.10) | copy-start | bytes 4718596
  128.2 23.9 %copy-start.60 = (bf16[128,3072]{1,0:T(8,128)(2,1)S(1)}, bf16[128,3072]{1,0:T(8,128)(2,1)}, u32[]{:S(2)}) copy-start(bf16[128,3072]{1,0:T(8,128)(2,1)} %copy-done.59) | copy-start | bytes 2359300
  131.4 39.3 %copy-start.23 = (bf16[64,3584]{1,0:T(8,128)(2,1)}, bf16[64,3584]{1,0:T(8,128)(2,1)S(1)}, u32[]{:S(2)}) copy-start(bf16[64,3584]{1,0:T(8,128)(2,1)S(1)} %get-tuple-element.62.refs_0_.refs_1_) | copy-start | bytes 1376260
  131.4 20.6 %collective-permute-start.13 = (bf16[64,3584]{1,0:T(8,128)(2,1)S(1)}, bf16[64,3584]{1,0:T(8,128)(2,1)S(1)}, u32[]{:S(2)}, u32[]{:S(2)}) collective-permute-start(bf16[64,3584]{1,0:T(8,128)(2,1)S(1)} %get-tuple-element.62.refs_0_.refs_1_), channel_id=1, source_target_pairs={{0,2},{1,3},{2,0},{3,1},{4,6},{5,7},{6,4},{7,5},{8,10},{9,11},{10,... | collective-permute-start | bytes 1376264 | tf_op jit(solution)/shard_map/ppermute | solution.py:40
  132.6 31.1 %copy-start.49 = (f32[128,3072]{1,0:T(8,128)S(1)}, f32[128,3072]{1,0:T(8,128)}, u32[]{:S(2)}) copy-start(f32[128,3072]{1,0:T(8,128)} %copy-done.48) | copy-start | bytes 4718596
  132.6 31.2 %copy-start.56 = (bf16[64,6656]{1,0:T(8,128)(2,1)S(1)}, bf16[64,6656]{1,0:T(8,128)(2,1)}, u32[]{:S(2)}) copy-start(bf16[64,6656]{1,0:T(8,128)(2,1)} %refs_4_.3) | copy-start | bytes 2555908
  132.6 31.2 %copy-start.58 = (bf16[128,3072]{1,0:T(8,128)(2,1)S(1)}, bf16[128,3072]{1,0:T(8,128)(2,1)}, u32[]{:S(2)}) copy-start(bf16[128,3072]{1,0:T(8,128)(2,1)} %copy-done.57) | copy-start | bytes 2359300
  132.6 31.2 %copy-start.62 = (bf16[2,16,6656]{2,1,0:T(8,128)(2,1)S(1)}, bf16[2,16,6656]{2,1,0:T(8,128)(2,1)}, u32[]{:S(2)}) copy-start(bf16[2,16,6656]{2,1,0:T(8,128)(2,1)} %refs_6_.3) | copy-start | bytes 1277956
  132.6 19.7 %collective-permute-start.15 = (bf16[64,3584]{1,0:T(8,128)(2,1)S(1)}, bf16[64,3584]{1,0:T(8,128)(2,1)S(1)}, u32[]{:S(2)}, u32[]{:S(2)}) collective-permute-start(bf16[64,3584]{1,0:T(8,128)(2,1)S(1)} %get-tuple-element.63), channel_id=1, source_target_pairs={{0,16},{16,0},{1,17},{17,1},{2,18},{18,2},{3,19},{19,3},{4,20},{20... | collective-permute-start | bytes 1376264 | tf_op jit(solution)/shard_map/ppermute | solution.py:40
  133.4 18.7 %collective-permute-start.11 = (bf16[64,3072]{1,0:T(8,128)(2,1)S(1)}, bf16[64,3072]{1,0:T(8,128)(2,1)S(1)}, u32[]{:S(2)}, u32[]{:S(2)}) collective-permute-start(bf16[64,3072]{1,0:T(8,128)(2,1)S(1)} %share_sums.10.refs_7_), channel_id=1, source_target_pairs={{0,2},{1,3},{2,0},{3,1},{4,6},{5,7},{6,4},{7,5},{8,10},{9,11},{10,... | collective-permute-start | bytes 1179656 | tf_op jit(solution)/shard_map/ppermute | solution.py:40
  152.4 11.3 %collective-permute-start.16 = (bf16[64,3584]{1,0:T(8,128)(2,1)S(1)}, bf16[64,3584]{1,0:T(8,128)(2,1)S(1)}, u32[]{:S(2)}, u32[]{:S(2)}) collective-permute-start(bf16[64,3584]{1,0:T(8,128)(2,1)S(1)} %relay.7.refs_4_.refs_5_), channel_id=1, source_target_pairs={{0,2},{1,3},{2,0},{3,1},{4,6},{5,7},{6,4},{7,5},{8,10},{9,11},{10,... | collective-permute-start | bytes 1376264 | tf_op jit(solution)/shard_map/ppermute | solution.py:40
  153.7 10.1 %collective-permute-start.14 = (bf16[64,3072]{1,0:T(8,128)(2,1)S(1)}, bf16[64,3072]{1,0:T(8,128)(2,1)S(1)}, u32[]{:S(2)}, u32[]{:S(2)}) collective-permute-start(bf16[64,3072]{1,0:T(8,128)(2,1)S(1)} %share_sums.11.refs_0_), channel_id=1, source_target_pairs={{0,16},{16,0},{1,17},{17,1},{2,18},{18,2},{3,19},{19,3},{4,20},{20... | collective-permute-start | bytes 1179656 | tf_op jit(solution)/shard_map/ppermute | solution.py:40
  154.3 15.1 %collective-permute-start.21 = (bf16[64,3584]{1,0:T(8,128)(2,1)S(1)}, bf16[64,3584]{1,0:T(8,128)(2,1)S(1)}, u32[]{:S(2)}, u32[]{:S(2)}) collective-permute-start(bf16[64,3584]{1,0:T(8,128)(2,1)S(1)} %get-tuple-element.62.refs_0_.refs_1_), channel_id=1, source_target_pairs={{0,1},{1,0},{2,3},{3,2},{4,5},{5,4},{6,7},{7,6},{8,9},{9,8},{10,11... | collective-permute-start | bytes 1376264 | tf_op jit(solution)/shard_map/ppermute | solution.py:40
  154.3 16.4 %collective-permute-start.23 = (bf16[64,3584]{1,0:T(8,128)(2,1)S(1)}, bf16[64,3584]{1,0:T(8,128)(2,1)S(1)}, u32[]{:S(2)}, u32[]{:S(2)}) collective-permute-start(bf16[64,3584]{1,0:T(8,128)(2,1)S(1)} %relay.7.refs_4_.refs_5_), channel_id=1, source_target_pairs={{0,1},{1,0},{2,3},{3,2},{4,5},{5,4},{6,7},{7,6},{8,9},{9,8},{10,11... | collective-permute-start | bytes 1376264 | tf_op jit(solution)/shard_map/ppermute | solution.py:40
  154.8 15.9 %collective-permute-start.22 = (bf16[64,3584]{1,0:T(8,128)(2,1)S(1)}, bf16[64,3584]{1,0:T(8,128)(2,1)S(1)}, u32[]{:S(2)}, u32[]{:S(2)}) collective-permute-start(bf16[64,3584]{1,0:T(8,128)(2,1)S(1)} %collective-permute-done.13.refs_3_.refs_1_.refs_2_), channel_id=1, source_target_pairs={{0,1},{1,0},{2,3},{3,2},{4,5},{5,4},{6,7},{7,6},{8,9},{9,8},{10,11... | collective-permute-start | bytes 1376264 | tf_op jit(solution)/shard_map/ppermute | solution.py:40
  163.8 7.0 %collective-permute-start.24 = (bf16[64,3584]{1,0:T(8,128)(2,1)S(1)}, bf16[64,3584]{1,0:T(8,128)(2,1)S(1)}, u32[]{:S(2)}, u32[]{:S(2)}) collective-permute-start(bf16[64,3584]{1,0:T(8,128)(2,1)S(1)} %collective-permute-done.16.refs_7_.refs_5_.refs_6_), channel_id=1, source_target_pairs={{0,1},{1,0},{2,3},{3,2},{4,5},{5,4},{6,7},{7,6},{8,9},{9,8},{10,11... | collective-permute-start | bytes 1376264 | tf_op jit(solution)/shard_map/ppermute | solution.py:40
  168.9 11.5 %collective-permute-start.20 = (bf16[64,3072]{1,0:T(8,128)(2,1)S(1)}, bf16[64,3072]{1,0:T(8,128)(2,1)S(1)}, u32[]{:S(2)}, u32[]{:S(2)}) collective-permute-start(bf16[64,3072]{1,0:T(8,128)(2,1)S(1)} %get-tuple-element.65), channel_id=1, source_target_pairs={{0,16},{16,0},{1,17},{17,1},{2,18},{18,2},{3,19},{19,3},{4,20},{20... | collective-permute-start | bytes 1179656 | tf_op jit(solution)/shard_map/ppermute | solution.py:40
  169.4 14.2 %collective-permute-start.17 = (bf16[64,3072]{1,0:T(8,128)(2,1)}, bf16[64,3072]{1,0:T(8,128)(2,1)S(1)}, u32[]{:S(2)}, u32[]{:S(2)}) collective-permute-start(bf16[64,3072]{1,0:T(8,128)(2,1)} %get-tuple-element.64.refs_9_.refs_0_), channel_id=1, source_target_pairs={{0,2},{1,3},{2,0},{3,1},{4,6},{5,7},{6,4},{7,5},{8,10},{9,11},{10,... | collective-permute-start | bytes 1179656 | tf_op jit(solution)/shard_map/ppermute | solution.py:40
  182.5 11.1 %collective-permute-start.25 = (bf16[64,3072]{1,0:T(8,128)(2,1)}, bf16[64,3072]{1,0:T(8,128)(2,1)}, u32[]{:S(2)}, u32[]{:S(2)}) collective-permute-start(bf16[64,3072]{1,0:T(8,128)(2,1)} %relay.8.refs_4_.refs_13_), channel_id=1, source_target_pairs={{0,2},{1,3},{2,0},{3,1},{4,6},{5,7},{6,4},{7,5},{8,10},{9,11},{10,... | collective-permute-start | bytes 1179656 | tf_op jit(solution)/shard_map/ppermute | solution.py:40
  183.7 45.0 %collective-permute-start.18 = (bf16[64,3072]{1,0:T(8,128)(2,1)}, bf16[64,3072]{1,0:T(8,128)(2,1)}, u32[]{:S(2)}, u32[]{:S(2)}) collective-permute-start(bf16[64,3072]{1,0:T(8,128)(2,1)} %get-tuple-element.64.refs_9_.refs_0_), channel_id=1, source_target_pairs={{0,1},{1,0},{2,3},{3,2},{4,5},{5,4},{6,7},{7,6},{8,9},{9,8},{10,11... | collective-permute-start | bytes 1179656 | tf_op jit(solution)/shard_map/ppermute | solution.py:40
  183.7 45.0 %collective-permute-start.19 = (bf16[64,3072]{1,0:T(8,128)(2,1)S(1)}, bf16[64,3072]{1,0:T(8,128)(2,1)}, u32[]{:S(2)}, u32[]{:S(2)}) collective-permute-start(bf16[64,3072]{1,0:T(8,128)(2,1)S(1)} %collective-permute-done.17.refs_9_.refs_1_.refs_10_), channel_id=1, source_target_pairs={{0,1},{1,0},{2,3},{3,2},{4,5},{5,4},{6,7},{7,6},{8,9},{9,8},{10,11... | collective-permute-start | bytes 1179656 | tf_op jit(solution)/shard_map/ppermute | solution.py:40
  184.2 44.5 %collective-permute-start.26 = (bf16[64,3072]{1,0:T(8,128)(2,1)}, bf16[64,3072]{1,0:T(8,128)(2,1)}, u32[]{:S(2)}, u32[]{:S(2)}) collective-permute-start(bf16[64,3072]{1,0:T(8,128)(2,1)} %relay.8.refs_4_.refs_13_), channel_id=1, source_target_pairs={{0,1},{1,0},{2,3},{3,2},{4,5},{5,4},{6,7},{7,6},{8,9},{9,8},{10,11... | collective-permute-start | bytes 1179656 | tf_op jit(solution)/shard_map/ppermute | solution.py:40
  193.5 35.1 %collective-permute-start.27 = (bf16[64,3072]{1,0:T(8,128)(2,1)}, bf16[64,3072]{1,0:T(8,128)(2,1)}, u32[]{:S(2)}, u32[]{:S(2)}) collective-permute-start(bf16[64,3072]{1,0:T(8,128)(2,1)} %collective-permute-done.25.refs_5_.refs_14_), channel_id=1, source_target_pairs={{0,1},{1,0},{2,3},{3,2},{4,5},{5,4},{6,7},{7,6},{8,9},{9,8},{10,11... | collective-permute-start | bytes 1179656 | tf_op jit(solution)/shard_map/ppermute | solution.py:40
  193.6 4.0 %collective-permute-start.28 = (f32[64,33]{1,0:T(8,128)S(1)}, f32[64,33]{1,0:T(8,128)S(1)}, u32[]{:S(2)}, u32[]{:S(2)}) collective-permute-start(f32[64,33]{1,0:T(8,128)S(1)} %add.225), channel_id=1, source_target_pairs={{0,4},{4,0},{8,12},{12,8},{1,5},{5,1},{9,13},{13,9},{2,6},{6,2},{1... | collective-permute-start | bytes 25352 | tf_op jit(solution)/shard_map/ppermute | solution.py:40
  197.5 4.8 %collective-permute-start.29 = (f32[64,33]{1,0:T(8,128)S(1)}, f32[64,33]{1,0:T(8,128)S(1)}, u32[]{:S(2)}, u32[]{:S(2)}) collective-permute-start(f32[64,33]{1,0:T(8,128)S(1)} %add.226.refs_10_), channel_id=1, source_target_pairs={{0,8},{4,12},{8,0},{12,4},{1,9},{5,13},{9,1},{13,5},{2,10},{6,14},... | collective-permute-start | bytes 25352 | tf_op jit(solution)/shard_map/ppermute | solution.py:40
  236.9 19.5 %collective-permute-start.32 = (bf16[256,1024]{1,0:T(8,128)(2,1)}, bf16[256,1024]{1,0:T(8,128)(2,1)}, u32[]{:S(2)}, u32[]{:S(2)}) collective-permute-start(bf16[256,1024]{1,0:T(8,128)(2,1)} %get-tuple-element.70), channel_id=1, source_target_pairs={{0,16},{16,0},{1,17},{17,1},{2,18},{18,2},{3,19},{19,3},{4,20},{20... | collective-permute-start | bytes 1572872 | tf_op jit(solution)/shard_map/ppermute | solution.py:40
  239.6 16.7 %collective-permute-start.30 = (f32[64,33]{0,1:T(8,128)S(1)}, f32[64,33]{0,1:T(8,128)S(1)}, u32[]{:S(2)}, u32[]{:S(2)}) collective-permute-start(f32[64,33]{0,1:T(8,128)S(1)} %copy.24), channel_id=1, source_target_pairs={{0,2},{1,3},{2,0},{3,1},{4,6},{5,7},{6,4},{7,5},{8,10},{9,11},{10,... | collective-permute-start | bytes 25352 | tf_op jit(solution)/shard_map/ppermute | solution.py:40
  254.3 26.7 %collective-permute-start.37 = (bf16[256,1536]{1,0:T(8,128)(2,1)}, bf16[256,1536]{1,0:T(8,128)(2,1)}, u32[]{:S(2)}, u32[]{:S(2)}) collective-permute-start(bf16[256,1536]{1,0:T(8,128)(2,1)} %get-tuple-element.73), channel_id=1, source_target_pairs={{0,16},{16,0},{1,17},{17,1},{2,18},{18,2},{3,19},{19,3},{4,20},{20... | collective-permute-start | bytes 2359304 | tf_op jit(solution)/shard_map/ppermute | solution.py:40
  256.3 3.9 %collective-permute-start.31 = (f32[128,33]{0,1:T(8,128)S(1)}, f32[128,33]{0,1:T(8,128)S(1)}, u32[]{:S(2)}, u32[]{:S(2)}) collective-permute-start(f32[128,33]{0,1:T(8,128)S(1)} %pad_maximum_fusion.1), channel_id=1, source_target_pairs={{0,1},{1,0},{2,3},{3,2},{4,5},{5,4},{6,7},{7,6},{8,9},{9,8},{10,11... | collective-permute-start | bytes 50696 | tf_op jit(solution)/shard_map/ppermute | solution.py:40
  258.7 9.0 %collective-permute-start.33 = (bf16[128,1024]{1,0:T(8,128)(2,1)}, bf16[128,1024]{1,0:T(8,128)(2,1)}, u32[]{:S(2)}, u32[]{:S(2)}) collective-permute-start(bf16[128,1024]{1,0:T(8,128)(2,1)} %get-tuple-element.89), channel_id=1, source_target_pairs={{0,4},{4,0},{8,12},{12,8},{1,5},{5,1},{9,13},{13,9},{2,6},{6,2},{1... | collective-permute-start | bytes 786440 | tf_op jit(solution)/shard_map/ppermute | solution.py:40
  280.2 24.6 %collective-permute-start.34 = (bf16[256,1536]{1,0:T(8,128)(2,1)}, bf16[256,1536]{1,0:T(8,128)(2,1)}, u32[]{:S(2)}, u32[]{:S(2)}) collective-permute-start(bf16[256,1536]{1,0:T(8,128)(2,1)} %get-tuple-element.72), channel_id=1, source_target_pairs={{0,16},{16,0},{1,17},{17,1},{2,18},{18,2},{3,19},{19,3},{4,20},{20... | collective-permute-start | bytes 2359304 | tf_op jit(solution)/shard_map/ppermute | solution.py:40
  283.2 24.6 %collective-permute-start.38 = (bf16[128,1536]{1,0:T(8,128)(2,1)}, bf16[128,1536]{1,0:T(8,128)(2,1)}, u32[]{:S(2)}, u32[]{:S(2)}) collective-permute-start(bf16[128,1536]{1,0:T(8,128)(2,1)} %get-tuple-element.84), channel_id=1, source_target_pairs={{0,4},{4,0},{8,12},{12,8},{1,5},{5,1},{9,13},{13,9},{2,6},{6,2},{1... | collective-permute-start | bytes 1179656 | tf_op jit(solution)/shard_map/ppermute | solution.py:40
  284.9 5.5 %collective-permute-start.52 = (bf16[64,32]{0,1:T(8,128)(2,1)S(1)}, bf16[64,32]{0,1:T(8,128)(2,1)S(1)}, u32[]{:S(2)}, u32[]{:S(2)}) collective-permute-start(bf16[64,32]{0,1:T(8,128)(2,1)S(1)} %copy.36), channel_id=1, source_target_pairs={{0,2},{1,3},{2,0},{3,1},{4,6},{5,7},{6,4},{7,5},{8,10},{9,11},{10,... | collective-permute-start | bytes 12296 | tf_op jit(solution)/shard_map/ppermute | solution.py:40
  287.6 8.4 %collective-permute-start.40 = (bf16[64,1024]{1,0:T(8,128)(2,1)}, bf16[64,1024]{1,0:T(8,128)(2,1)}, u32[]{:S(2)}, u32[]{:S(2)}) collective-permute-start(bf16[64,1024]{1,0:T(8,128)(2,1)} %get-tuple-element.94), channel_id=1, source_target_pairs={{0,8},{4,12},{8,0},{12,4},{1,9},{5,13},{9,1},{13,5},{2,10},{6,14},... | collective-permute-start | bytes 393224 | tf_op jit(solution)/shard_map/ppermute | solution.py:40
  290.5 1.2 collective-permute-start.53
  301.4 16.6 %collective-permute-start.41 = (bf16[64,1024]{1,0:T(8,128)(2,1)}, bf16[64,1024]{1,0:T(8,128)(2,1)S(1)}, u32[]{:S(2)}, u32[]{:S(2)}) collective-permute-start(bf16[64,1024]{1,0:T(8,128)(2,1)} %get-tuple-element.74.refs_0_), channel_id=1, source_target_pairs={{0,8},{4,12},{8,0},{12,4},{1,9},{5,13},{9,1},{13,5},{2,10},{6,14},... | collective-permute-start | bytes 393224 | tf_op jit(solution)/shard_map/ppermute | solution.py:40
  307.5 34.3 %collective-permute-start.35 = (bf16[128,1536]{1,0:T(8,128)(2,1)}, bf16[128,1536]{1,0:T(8,128)(2,1)}, u32[]{:S(2)}, u32[]{:S(2)}) collective-permute-start(bf16[128,1536]{1,0:T(8,128)(2,1)} %get-tuple-element.86), channel_id=1, source_target_pairs={{0,4},{4,0},{8,12},{12,8},{1,5},{5,1},{9,13},{13,9},{2,6},{6,2},{1... | collective-permute-start | bytes 1179656 | tf_op jit(solution)/shard_map/ppermute | solution.py:40
  309.7 12.2 %collective-permute-start.39 = (bf16[64,1536]{1,0:T(8,128)(2,1)}, bf16[64,1536]{1,0:T(8,128)(2,1)}, u32[]{:S(2)}, u32[]{:S(2)}) collective-permute-start(bf16[64,1536]{1,0:T(8,128)(2,1)} %get-tuple-element.90), channel_id=1, source_target_pairs={{0,8},{4,12},{8,0},{12,4},{1,9},{5,13},{9,1},{13,5},{2,10},{6,14},... | collective-permute-start | bytes 589832 | tf_op jit(solution)/shard_map/ppermute | solution.py:40
  313.2 4.0 %collective-permute-start.54 = (bf16[256,16]{0,1:T(8,128)(2,1)}, bf16[256,16]{0,1:T(8,128)(2,1)}, u32[]{:S(2)}, u32[]{:S(2)}) collective-permute-start(bf16[256,16]{0,1:T(8,128)(2,1)} %get-tuple-element.99), channel_id=1, source_target_pairs={{0,16},{16,0},{1,17},{17,1},{2,18},{18,2},{3,19},{19,3},{4,20},{20... | collective-permute-start | bytes 24584 | tf_op jit(solution)/shard_map/ppermute | solution.py:40
  317.9 30.3 %collective-permute-start.43 = (bf16[64,1024]{1,0:T(8,128)(2,1)}, bf16[64,1024]{1,0:T(8,128)(2,1)}, u32[]{:S(2)}, u32[]{:S(2)}) collective-permute-start(bf16[64,1024]{1,0:T(8,128)(2,1)} %get-tuple-element.74.refs_0_), channel_id=1, source_target_pairs={{0,4},{4,0},{8,12},{12,8},{1,5},{5,1},{9,13},{13,9},{2,6},{6,2},{1... | collective-permute-start | bytes 393224 | tf_op jit(solution)/shard_map/ppermute | solution.py:40
  317.9 31.6 %collective-permute-start.44 = (bf16[64,1024]{1,0:T(8,128)(2,1)S(1)}, bf16[64,1024]{1,0:T(8,128)(2,1)}, u32[]{:S(2)}, u32[]{:S(2)}) collective-permute-start(bf16[64,1024]{1,0:T(8,128)(2,1)S(1)} %collective-permute-done.41.refs_8_.refs_1_), channel_id=1, source_target_pairs={{0,4},{4,0},{8,12},{12,8},{1,5},{5,1},{9,13},{13,9},{2,6},{6,2},{1... | collective-permute-start | bytes 393224 | tf_op jit(solution)/shard_map/ppermute | solution.py:40
  329.5 20.0 %collective-permute-start.42 = (bf16[64,1536]{1,0:T(8,128)(2,1)}, bf16[64,1536]{1,0:T(8,128)(2,1)}, u32[]{:S(2)}, u32[]{:S(2)}) collective-permute-start(bf16[64,1536]{1,0:T(8,128)(2,1)} %get-tuple-element.75.refs_0_), channel_id=1, source_target_pairs={{0,8},{4,12},{8,0},{12,4},{1,9},{5,13},{9,1},{13,5},{2,10},{6,14},... | collective-permute-start | bytes 589832 | tf_op jit(solution)/shard_map/ppermute | solution.py:40
  332.9 40.1 %collective-permute-start.48 = (bf16[64,1536]{1,0:T(8,128)(2,1)}, bf16[64,1536]{1,0:T(8,128)(2,1)}, u32[]{:S(2)}, u32[]{:S(2)}) collective-permute-start(bf16[64,1536]{1,0:T(8,128)(2,1)} %get-tuple-element.75.refs_0_), channel_id=1, source_target_pairs={{0,4},{4,0},{8,12},{12,8},{1,5},{5,1},{9,13},{13,9},{2,6},{6,2},{1... | collective-permute-start | bytes 589832 | tf_op jit(solution)/shard_map/ppermute | solution.py:40
  343.9 9.2 %collective-permute-start.36 = (bf16[64,1536]{1,0:T(8,128)(2,1)}, bf16[64,1536]{1,0:T(8,128)(2,1)}, u32[]{:S(2)}, u32[]{:S(2)}) collective-permute-start(bf16[64,1536]{1,0:T(8,128)(2,1)} %get-tuple-element.92), channel_id=1, source_target_pairs={{0,8},{4,12},{8,0},{12,4},{1,9},{5,13},{9,1},{13,5},{2,10},{6,14},... | collective-permute-start | bytes 589832 | tf_op jit(solution)/shard_map/ppermute | solution.py:40
  348.2 22.5 %collective-permute-start.51 = (bf16[256,32]{0,1:T(8,128)(2,1)}, bf16[256,32]{0,1:T(8,128)(2,1)}, u32[]{:S(2)}, u32[]{:S(2)}) collective-permute-start(bf16[256,32]{0,1:T(8,128)(2,1)} %copy.33), channel_id=1, source_target_pairs={{0,16},{16,0},{1,17},{17,1},{2,18},{18,2},{3,19},{19,3},{4,20},{20... | collective-permute-start | bytes 49160 | tf_op jit(solution)/shard_map/ppermute | solution.py:40
  361.2 15.5 %collective-permute-start.45 = (bf16[80,1536]{1,0:T(8,128)(2,1)S(1)}, bf16[80,1536]{1,0:T(8,128)(2,1)S(1)}, u32[]{:S(2)}, u32[]{:S(2)}) collective-permute-start(bf16[80,1536]{1,0:T(8,128)(2,1)S(1)} %maximum_maximum_fusion.refs_0_), channel_id=1, source_target_pairs={{0,8},{4,12},{8,0},{12,4},{1,9},{5,13},{9,1},{13,5},{2,10},{6,14},... | collective-permute-start | bytes 737288 | tf_op jit(solution)/shard_map/ppermute | solution.py:40
  364.6 13.2 %collective-permute-start.55 = (bf16[16,6656]{1,0:T(8,128)(2,1)S(1)}, bf16[16,6656]{1,0:T(8,128)(2,1)S(1)}, u32[]{:S(2)}, u32[]{:S(2)}) collective-permute-start(bf16[16,6656]{1,0:T(8,128)(2,1)S(1)} %convert_element_type.128), channel_id=1, source_target_pairs={{0,16},{16,0},{1,17},{17,1},{2,18},{18,2},{3,19},{19,3},{4,20},{20... | collective-permute-start | bytes 638984 | tf_op jit(solution)/shard_map/ppermute | solution.py:40
  366.0 7.2 %collective-permute-start.49 = (bf16[64,1536]{1,0:T(8,128)(2,1)}, bf16[64,1536]{1,0:T(8,128)(2,1)S(1)}, u32[]{:S(2)}, u32[]{:S(2)}) collective-permute-start(bf16[64,1536]{1,0:T(8,128)(2,1)} %collective-permute-done.42.refs_8_.refs_1_), channel_id=1, source_target_pairs={{0,4},{4,0},{8,12},{12,8},{1,5},{5,1},{9,13},{13,9},{2,6},{6,2},{1... | collective-permute-start | bytes 589832 | tf_op jit(solution)/shard_map/ppermute | solution.py:40
  375.8 6.2 %collective-permute-start.46 = (bf16[80,1536]{1,0:T(8,128)(2,1)S(1)}, bf16[80,1536]{1,0:T(8,128)(2,1)S(1)}, u32[]{:S(2)}, u32[]{:S(2)}) collective-permute-start(bf16[80,1536]{1,0:T(8,128)(2,1)S(1)} %maximum_maximum_fusion.refs_0_), channel_id=1, source_target_pairs={{0,4},{4,0},{8,12},{12,8},{1,5},{5,1},{9,13},{13,9},{2,6},{6,2},{1... | collective-permute-start | bytes 737288 | tf_op jit(solution)/shard_map/ppermute | solution.py:40
  376.7 7.9 %collective-permute-start.47 = (bf16[80,1536]{1,0:T(8,128)(2,1)S(1)}, bf16[80,1536]{1,0:T(8,128)(2,1)S(1)}, u32[]{:S(2)}, u32[]{:S(2)}) collective-permute-start(bf16[80,1536]{1,0:T(8,128)(2,1)S(1)} %collective-permute-done.45.refs_1_), channel_id=1, source_target_pairs={{0,4},{4,0},{8,12},{12,8},{1,5},{5,1},{9,13},{13,9},{2,6},{6,2},{1... | collective-permute-start | bytes 737288 | tf_op jit(solution)/shard_map/ppermute | solution.py:40
  384.6 4.2 %collective-permute-start.50 = (f32[3,1536]{1,0:T(4,128)S(1)}, f32[3,1536]{1,0:T(4,128)S(1)}, u32[]{:S(2)}, u32[]{:S(2)}) collective-permute-start(f32[3,1536]{1,0:T(4,128)S(1)} %fusion.6), channel_id=1, source_target_pairs={{0,16},{16,0},{1,17},{17,1},{2,18},{18,2},{3,19},{19,3},{4,20},{20... | collective-permute-start | bytes 55304 | tf_op jit(solution)/shard_map/ppermute | solution.py:40
  (87 other events, 483.8 us)

commit v8 on v7

--- a/solution.py
+++ b/solution.py
@@ -7,7 +7,8 @@
 
 MODEL_WIDTH = 16384
 ADAPTER_SCALE = 0.5
-VMEM_MIB = 40
+VMEM_MIB = 12
+MATMUL_VMEM_MIB = 24
 COST_SHARE = 0.01
 
 F32 = jnp.float32
@@ -53,8 +54,8 @@
     return out
 
 
-def params():
-    return pltpu.CompilerParams(vmem_limit_bytes=VMEM_MIB * 1024 * 1024)
+def params(mib=VMEM_MIB):
+    return pltpu.CompilerParams(vmem_limit_bytes=mib * 1024 * 1024)
 
 
 def cost(flops, size):
@@ -155,7 +156,7 @@
             jax.ShapeDtypeStruct((8, 128), F32),
         ],
         input_output_aliases={2 + i: i for i in range(len(into))},
-        compiler_params=params(),
+        compiler_params=params(MATMUL_VMEM_MIB),
         cost_estimate=cost(2 * rows * depth * (stop - start) * tile, 2 * depth * (rows + (stop - start) * tile) + 6 * half * (stop - start) * tile),
         name="forward_matmul",
     )(x, weights, *into, *after)
@@ -300,7 +301,7 @@
         + [ANY] * len(after),
         out_specs=out_specs,
         out_shape=out_shape,
-        compiler_params=params(),
+        compiler_params=params(MATMUL_VMEM_MIB),
         cost_estimate=cost(2 * rows * hidden * tiles * tile, 2 * hidden * (rows + tiles * tile) + (4 + 4 * n_base) * rows * tiles * tile),
         name="backward_matmul",
     )(*pieces, weights, *(() if base is None else (base,)), *after)
@@ -509,28 +510,25 @@
                 blocks += [swap(x, "hid", hid, 1 << bit) for x in blocks]
             return blocks
 
-        back, mine_grad, peer_grad = gradients(0, (peer_sends[1],))
+        pass_on(1, (others[0],))
+        back, mine_grad, peer_grad = gradients(0, (passed[1],))
         own_pieces = spread(mine_grad)
-        pass_on(1, (own_pieces[1],))
-        peer_pieces = spread(relay(peer_grad, (passed[1],)))
-        grads = [own_pieces + peer_pieces]
-        more, mine_grad, peer_grad = gradients(1, (peer_pieces[1],))
+        more, mine_grad, second_peer_grad = gradients(1, (own_pieces[1],))
         back = back + more
+        grads = [own_pieces + spread(relay(peer_grad, (mine_grad,)))]
 
         def first_half(j, after):
             first, n = steps[j]
             return backward_matmul(grads[0], weights, 0, first, n, width_tile, partial=True, after=after)
 
-        bases = [first_half(0, (mine_grad,))]
         own_pieces = spread(mine_grad)
-        peer_pieces = spread(relay(peer_grad, (bases[0],)))
-        grads.append(own_pieces + peer_pieces)
+        peer_grad = relay(second_peer_grad, (own_pieces[1],))
+        grads.append(own_pieces + spread(peer_grad))
         back_steps = []
         for bit in range(bits_of(ffn)):
             back = back + swap(back, "ffn", ffn, 1 << bit)
             back_steps.append(back)
-        for j in range(1, len(steps)):
-            bases.append(first_half(j, (own_pieces[1], back_steps[0], bases[-1])))
+        bases = [first_half(0, (peer_grad, back_steps[0]))]
 
         shard = tokens // ffn
         place = reversed_bits(f, bits_of(ffn))
@@ -547,7 +545,9 @@
 
         begun = []
         for j, (first, n) in enumerate(steps):
-            wait = (products[-1],) if products else (bases[-1], back_steps[-1])
+            wait = (products[-1],) if products else (back_steps[-1],)
+            if j:
+                bases.append(first_half(j, wait))
             if j == 2:
                 back = double(relay(back, (products[0],)), "hid", hid)
                 keep, send = halving_step([products[0], received[0]], 0)

time: 393 us -> 379 us (0.964)
  waiting for transfers between devices: 86 us -> 78.7 us
  Pallas kernels: 147 us -> 142 us
    ppermute x56, waiting for transfers between devices: 86 us -> 78.7 us  [swap(): return lax.ppermute(x, axis, [(i, i ^ mask) for i in range(n)])]
    unnamed x191 -> x193, local copies, waits for them, and re-layouts: 46.5 us -> 44.6 us
  transfers between devices with their start and end apart: 56 -> 56, of which waited for: 22 -> 23; matrix products, arithmetic and copies ran while one was open for 9% -> 11% of each run, Pallas kernels for 32% -> 32%
where the time goes in v8:
time: 379 us; the launch traced here: 376 us
  Pallas kernels  142 us (37%)
  waiting for transfers between devices  78.7 us (21%)
  local copies, waits for them, and re-layouts  57.6 us (15%)
  starting transfers between devices  55.2 us (15%)
  other arithmetic  27 us (7%)
  blocking collectives  13.4 us (4%)
    ppermute x56, waiting for transfers between devices, swap(): return lax.ppermute(x, axis, [(i, i ^ mask) for i in range(n)])  78.7 us
    pallas_call x7, Pallas kernels, forward_matmul(): pl.pallas_call(kernel, grid=(stop - start,), in_specs=[RESIDENT, pl.Block...  59.5 us
    ppermute x56, starting transfers between devices, swap(): return lax.ppermute(x, axis, [(i, i ^ mask) for i in range(n)])  55.2 us
    pallas_call x6, Pallas kernels, backward_matmul(): pl.pallas_call(kernel, grid=(tiles,), in_specs=[pl.BlockSpec(g.shape, lam...  49.8 us
    unnamed x193, local copies, waits for them, and re-layouts  44.6 us
    convert_element_type x5, other arithmetic, halving_step(): total_of(sides[1], 0, half).astype(BF16)  10.5 us
    pallas_call x2, Pallas kernels, gated_gradients(): pl.pallas_call(kernel, grid_spec=pltpu.PrefetchScalarGridSpec(num_scalar_...  8.24 us
  transfers between devices with their start and end apart: 56, of which 23 were waited for; matrix products, arithmetic and copies ran while one was open for 11% of the time, Pallas kernels for 32%

profile of v8, /device:TPU:0, one launch (start us, length us, event | category | flops | bytes accessed | tf_op | source)
XLA Modules:
  0.0 376.1 jit_solution(1003807733266715919)
XLA Ops:
  0.7 3.0 collective-permute-start.3
  3.7 2.1 fusion
  7.1 7.3 %all-reduce.1 = (f32[256]{0:T(256)S(1)}, f32[]{:T(128)}) all-reduce(f32[256]{0:T(256)S(1)} %fusion, f32[]{:T(128)} %multiply_reduce_fusion), channel_id=1, replica_groups=mesh['dp'=2,'ffn'=4,'hid'=4] {'hid'}, use_global_device_ids=true, to_apply=%region_1.0 | all-reduce | flops 257 | bytes 2056 | tf_op jit(solution)/shard_map/psum | solution.py:415
  16.0 6.1 %psum.23 = f32[256]{0:T(256)S(1)} all-reduce(f32[256]{0:T(256)S(1)} %fusion.2), channel_id=1, replica_groups=mesh['dp'=2,'ffn'=4,'hid'=4] {'hid'}, use_global_device_ids=true, to_apply=%region_5.0 | all-reduce | flops 256 | bytes 2048 | tf_op jit(solution)/shard_map/psum | solution.py:422
  22.3 1.7 normalize.2
  24.6 15.3 %forward_matmul.7 = (f32[128,3584]{1,0:T(8,128)S(1)}, bf16[128,3584]{1,0:T(8,128)(2,1)S(1)}, f32[8,128]{1,0:T(8,128)}) custom-call(bf16[256,4096]{1,0:T(8,128)(2,1)S(1)} %get-tuple-element.43.x_ref.refs_1_, bf16[1,4096,6656]{2,1,0:T(8,128)(2,1)} %refs_8_.11), custom_call_target="tpu_custom_call" | custom-call | flops 75161928 | bytes 342097 | tf_op jit(solution)/shard_map/forward_matmul/pallas_call | solution.py:146
  39.9 2.5 collective-permute-done.refs_1_
  44.9 12.1 %forward_matmul.8 = (f32[128,3072]{1,0:T(8,128)S(1)}, bf16[128,3072]{1,0:T(8,128)(2,1)S(1)}, f32[8,128]{1,0:T(8,128)S(1)}) custom-call(bf16[256,4096]{1,0:T(8,128)(2,1)S(1)} %get-tuple-element.43.x_ref.refs_1_, bf16[1,4096,6656]{2,1,0:T(8,128)(2,1)} %refs_8_.11, bf16[64,3584]{1,0:T(8,128)(2,1)S(1)} %share_sums.6.refs_0_), custom_call_target="tpu_custom_call" | custom-call | flops 64424508 | bytes 296222 | tf_op jit(solution)/shard_map/forward_matmul/pallas_call | solution.py:146
  62.6 3.0 collective-permute-done.4
  65.7 4.2 %normalize.3 = (bf16[256,4096]{1,0:T(8,128)(2,1)S(1)}, f32[256,32]{1,0:T(8,128)}) custom-call(s32[1]{0:T(128)} %bitcast.5.h_ref, bf16[256,4096]{1,0:T(8,128)(2,1)} %collective-permute-done.3.x_ref, f32[256,2]{1,0:T(8,128)S(1)} %copy.21.stat_ref, f32[1,4096]{1,0:T(1,128)S(1)} %bitcast.30, f32[1,4096]{1,0:T(1,128)S(1)} %bitcast.35, ...), custom_call_target="tpu_custom_call" | custom-call | flops 671088 | bytes 41943 | tf_op jit(solution)/shard_map/normalize/pallas_call | solution.py:85
  70.9 7.5 %forward_matmul.9 = (f32[128,3584]{1,0:T(8,128)S(1)}, bf16[128,3584]{1,0:T(8,128)(2,1)S(1)}, f32[8,128]{1,0:T(8,128)}) custom-call(bf16[256,4096]{1,0:T(8,128)(2,1)S(1)} %get-tuple-element.49.x_ref.refs_0_.refs_2_, bf16[1,4096,6656]{2,1,0:T(8,128)(2,1)} %refs_8_.11, bf16[64,3072]{1,0:T(8,128)(2,1)} %share_sums.7.refs_0_), custom_call_target="tpu_custom_call" | custom-call | flops 32212254 | bytes 158597 | tf_op jit(solution)/shard_map/forward_matmul/pallas_call | solution.py:146
  78.4 5.5 %forward_matmul.10 = (f32[128,3584]{1,0:T(8,128)S(1)}, bf16[128,3584]{1,0:T(8,128)(2,1)S(1)}, f32[8,128]{1,0:T(8,128)}) custom-call(bf16[256,4096]{1,0:T(8,128)(2,1)S(1)} %get-tuple-element.49.x_ref.refs_0_.refs_2_, bf16[1,4096,6656]{2,1,0:T(8,128)(2,1)} %refs_8_.11, ...), custom_call_target="tpu_custom_call", output_to_operand_aliasing={{0}: (2, {}), {1}: (3, {})} | custom-call | flops 21474836 | bytes 112721 | tf_op jit(solution)/shard_map/forward_matmul/pallas_call | solution.py:146
  83.9 5.3 %forward_matmul.11 = (f32[128,3584]{1,0:T(8,128)S(1)}, bf16[128,3584]{1,0:T(8,128)(2,1)S(1)}, f32[8,128]{1,0:T(8,128)}) custom-call(bf16[256,4096]{1,0:T(8,128)(2,1)S(1)} %get-tuple-element.49.x_ref.refs_0_.refs_2_, bf16[1,4096,6656]{2,1,0:T(8,128)(2,1)} %refs_8_.11, ...), custom_call_target="tpu_custom_call", output_to_operand_aliasing={{0}: (2, {}), {1}: (3, {})} | custom-call | flops 21474836 | bytes 112721 | tf_op jit(solution)/shard_map/forward_matmul/pallas_call | solution.py:146
  90.9 2.8 collective-permute-done.8
  95.2 8.5 %forward_matmul.12 = (f32[128,3072]{1,0:T(8,128)S(1)}, bf16[128,3072]{1,0:T(8,128)(2,1)S(1)}, f32[8,128]{1,0:T(8,128)S(1)}) custom-call(bf16[256,4096]{1,0:T(8,128)(2,1)S(1)} %get-tuple-element.49.x_ref.refs_0_.refs_2_, bf16[1,4096,6656]{2,1,0:T(8,128)(2,1)} %refs_8_.11, bf16[64,3584]{1,0:T(8,128)(2,1)S(1)} %share_sums.8.refs_0_), custom_call_target="tpu_custom_call" | custom-call | flops 42949672 | bytes 204472 | tf_op jit(solution)/shard_map/forward_matmul/pallas_call | solution.py:146
  103.7 1.7 collective-permute-done.9.refs_2_
  106.4 5.3 %forward_matmul.13 = (f32[128,3072]{1,0:T(8,128)S(1)}, bf16[128,3072]{1,0:T(8,128)(2,1)S(1)}, f32[8,128]{1,0:T(8,128)}) custom-call(bf16[256,4096]{1,0:T(8,128)(2,1)S(1)} %get-tuple-element.49.x_ref.refs_0_.refs_2_, bf16[1,4096,6656]{2,1,0:T(8,128)(2,1)} %refs_8_.11, ...), custom_call_target="tpu_custom_call", output_to_operand_aliasing={{0}: (2, {}), {1}: (3, {})} | custom-call | flops 21474836 | bytes 112721 | tf_op jit(solution)/shard_map/forward_matmul/pallas_call | solution.py:146
  112.3 1.7 collective-permute-done.10.refs_1_
  117.3 7.7 %collective-permute-done.12.refs_3_ = bf16[64,3584]{1,0:T(8,128)(2,1)} collective-permute-done((bf16[64,3584]{1,0:T(8,128)(2,1)}, bf16[64,3584]{1,0:T(8,128)(2,1)}, u32[]{:S(2)}, u32[]{:S(2)}) %collective-permute-start.12) | collective-permute-done | bytes 458784 | tf_op jit(solution)/shard_map/ppermute | solution.py:41
  125.0 2.6 collective-permute-done.11.refs_2_
  133.8 3.1 gated_gradients.2
  140.1 10.0 %collective-permute-done.13.refs_3_ = bf16[64,3072]{1,0:T(8,128)(2,1)S(1)} collective-permute-done((bf16[64,3072]{1,0:T(8,128)(2,1)S(1)}, bf16[64,3072]{1,0:T(8,128)(2,1)S(1)}, u32[]{:S(2)}, u32[]{:S(2)}) %collective-permute-start.13) | collective-permute-done | bytes 393248 | tf_op jit(solution)/shard_map/ppermute | solution.py:41
  150.2 5.2 %gated_gradients.3 = (bf16[64,3072]{1,0:T(8,128)(2,1)}, bf16[64,3072]{1,0:T(8,128)(2,1)S(1)}, f32[64,33]{1,0:T(8,128)S(1)}) custom-call(s32[1]{0:T(128)} %bitcast.4.d_ref, f32[128,3072]{1,0:T(8,128)S(1)} %copy-done.47, bf16[128,3072]{1,0:T(8,128)(2,1)S(1)} %copy-done.53, bf16[64,3072]{1,0:T(8,128)(2,1)} %collective-permute-done.2.refs_2_, ...), custom_call_target="tpu_custom_call" | custom-call | flops 251658 | bytes 31457 | tf_op jit(solution)/shard_map/gated_gradients/pallas_call | solution.py:236
  156.8 3.2 collective-permute-done.24.x_ref
  161.5 6.2 %collective-permute-done.15.refs_0_.refs_1_.refs_10_ = bf16[64,3072]{1,0:T(8,128)(2,1)} collective-permute-done((bf16[64,3072]{1,0:T(8,128)(2,1)}, bf16[64,3072]{1,0:T(8,128)(2,1)}, u32[]{:S(2)}, u32[]{:S(2)}) %collective-permute-start.15) | collective-permute-done | bytes 393248 | tf_op jit(solution)/shard_map/ppermute | solution.py:41
  167.7 1.6 collective-permute-start.28
  169.4 2.3 collective-permute-done.28
  174.2 2.6 collective-permute-start.29
  176.8 2.2 collective-permute-done.29
  187.3 6.6 %backward_matmul.6.refs_9_ = f32[512,1024]{1,0:T(8,128)S(1)} custom-call(bf16[64,3584]{1,0:T(8,128)(2,1)S(1)} %copy-done.23, bf16[64,3584]{1,0:T(8,128)(2,1)S(1)} %collective-permute-done.14.refs_7_.refs_1_.refs_2_, bf16[64,3584]{1,0:T(8,128)(2,1)S(1)} %copy-done.28, bf16[64,3584]{1,0:T(8,128)(2,1)S(1)} %copy-done.38, ...), custom_call_target="tpu_custom_call" | custom-call | flops 37580964 | bytes 131072 | tf_op jit(solution)/shard_map/backward_matmul/pallas_call | solution.py:288
  194.0 7.2 %backward_matmul.7 = (f32[256,1024]{1,0:T(8,128)S(1)}, bf16[256,1024]{1,0:T(8,128)(2,1)}) custom-call(bf16[64,3072]{1,0:T(8,128)(2,1)} %get-tuple-element.63.refs_0_.refs_9_, bf16[64,3072]{1,0:T(8,128)(2,1)} %collective-permute-done.15.refs_0_.refs_1_.refs_10_, bf16[64,3072]{1,0:T(8,128)(2,1)} %collective-permute-done.16.refs_2_.refs_11_, ...), custom_call_target="tpu_custom_call" | custom-call | flops 32212254 | bytes 136314 | tf_op jit(solution)/shard_map/backward_matmul/pallas_call | solution.py:288
  201.9 2.0 constant_dynamic-slice_fusion.4.refs_2_
  212.8 8.8 %backward_matmul.8.refs_9_ = f32[512,1536]{1,0:T(8,128)S(1)} custom-call(bf16[64,3584]{1,0:T(8,128)(2,1)S(1)} %copy-done.24, bf16[64,3584]{1,0:T(8,128)(2,1)S(1)} %copy-done.10, bf16[64,3584]{1,0:T(8,128)(2,1)S(1)} %copy-done.29, bf16[64,3584]{1,0:T(8,128)(2,1)S(1)} %copy-done.39, bf16[64,3584]{1,0:T(8,128)(2,1)S(1)} %copy-done.14, ...), custom_call_target="tpu_custom_call" | custom-call | flops 56371444 | bytes 178257 | tf_op jit(solution)/shard_map/backward_matmul/pallas_call | solution.py:288
  221.7 9.3 %backward_matmul.9 = (f32[256,1536]{1,0:T(8,128)S(1)}, bf16[256,1536]{1,0:T(8,128)(2,1)}) custom-call(bf16[64,3072]{1,0:T(8,128)(2,1)} %get-tuple-element.63.refs_0_.refs_9_, bf16[64,3072]{1,0:T(8,128)(2,1)} %collective-permute-done.15.refs_0_.refs_1_.refs_10_, bf16[64,3072]{1,0:T(8,128)(2,1)} %collective-permute-done.16.refs_2_.refs_11_, ...), custom_call_target="tpu_custom_call" | custom-call | flops 48318384 | bytes 188743 | tf_op jit(solution)/shard_map/backward_matmul/pallas_call | solution.py:288
  232.4 8.8 %backward_matmul.10.refs_9_ = f32[512,1536]{1,0:T(8,128)S(1)} custom-call(bf16[64,3584]{1,0:T(8,128)(2,1)S(1)} %copy-done.25, bf16[64,3584]{1,0:T(8,128)(2,1)S(1)} %copy-done.11, bf16[64,3584]{1,0:T(8,128)(2,1)S(1)} %copy-done.30, bf16[64,3584]{1,0:T(8,128)(2,1)S(1)} %copy-done.40, bf16[64,3584]{1,0:T(8,128)(2,1)S(1)} %copy-done.15, ...), custom_call_target="tpu_custom_call" | custom-call | flops 56371444 | bytes 178257 | tf_op jit(solution)/shard_map/backward_matmul/pallas_call | solution.py:288
  241.2 1.7 copy-done.7
  243.0 2.0 convert_add_fusion.3
  248.1 5.8 %collective-permute-done.33.refs_12_ = bf16[128,1024]{1,0:T(8,128)(2,1)S(1)} collective-permute-done((bf16[128,1024]{1,0:T(8,128)(2,1)}, bf16[128,1024]{1,0:T(8,128)(2,1)S(1)}, u32[]{:S(2)}, u32[]{:S(2)}) %collective-permute-start.33) | collective-permute-done | bytes 262176 | tf_op jit(solution)/shard_map/ppermute | solution.py:41
  255.4 1.9 copy-done.8
  257.3 9.1 %backward_matmul.11 = (f32[256,1536]{1,0:T(8,128)S(1)}, bf16[256,1536]{1,0:T(8,128)(2,1)}) custom-call(bf16[64,3072]{1,0:T(8,128)(2,1)} %get-tuple-element.63.refs_0_.refs_9_, bf16[64,3072]{1,0:T(8,128)(2,1)} %collective-permute-done.15.refs_0_.refs_1_.refs_10_, bf16[64,3072]{1,0:T(8,128)(2,1)} %collective-permute-done.16.refs_2_.refs_11_, ...), custom_call_target="tpu_custom_call" | custom-call | flops 48318384 | bytes 188743 | tf_op jit(solution)/shard_map/backward_matmul/pallas_call | solution.py:288
  270.8 1.7 add_convert_fusion.5
  272.5 2.6 collective-permute-start.40
  275.1 2.9 add_convert_fusion
  278.0 1.6 collective-permute-start.38
  287.9 1.8 finish.3
  290.7 2.8 add_convert_fusion.1
  293.9 1.9 add_convert_fusion.3
  295.9 2.6 collective-permute-start.39
  305.8 2.2 collective-permute-done.39.refs_1_
  313.2 1.9 finish.4
  315.0 3.4 collective-permute-start.42
  323.7 3.0 adapter_products.3
  328.1 3.0 collective-permute-start.36
  331.8 6.7 %collective-permute-done.36.refs_1_ = bf16[64,1536]{1,0:T(8,128)(2,1)S(1)} collective-permute-done((bf16[64,1536]{1,0:T(8,128)(2,1)S(1)}, bf16[64,1536]{1,0:T(8,128)(2,1)S(1)}, u32[]{:S(2)}, u32[]{:S(2)}) %collective-permute-start.36) | collective-permute-done | bytes 196640 | tf_op jit(solution)/shard_map/ppermute | solution.py:41
  339.2 1.6 constant_dynamic-update-slice_fusion
  340.8 1.7 convert_element_type.128
  345.3 2.9 collective-permute-start.49
  348.2 2.3 assemble.3.refs_4_
  350.5 1.6 adapter_products.2
  352.2 3.7 collective-permute-done.49.refs_3_
  355.9 2.5 assemble.4.refs_4_
  358.4 2.0 collective-permute-start.47
  361.4 5.8 %collective-permute-done.46.refs_2_ = bf16[80,1536]{1,0:T(8,128)(2,1)S(1)} collective-permute-done((bf16[80,1536]{1,0:T(8,128)(2,1)S(1)}, bf16[80,1536]{1,0:T(8,128)(2,1)S(1)}, u32[]{:S(2)}, u32[]{:S(2)}) %collective-permute-start.46) | collective-permute-done | bytes 245792 | tf_op jit(solution)/shard_map/ppermute | solution.py:41
  367.2 4.3 %collective-permute-done.47.refs_3_ = bf16[80,1536]{1,0:T(8,128)(2,1)S(1)} collective-permute-done((bf16[80,1536]{1,0:T(8,128)(2,1)S(1)}, bf16[80,1536]{1,0:T(8,128)(2,1)S(1)}, u32[]{:S(2)}, u32[]{:S(2)}) %collective-permute-start.47) | collective-permute-done | bytes 245792 | tf_op jit(solution)/shard_map/ppermute | solution.py:41
  (337 shorter events, 101.9 us)
Async XLA Ops:
  0.7 21.6 %copy-start.42 = (bf16[2,4096,16]{1,2,0:T(8,128)(2,1)S(1)}, bf16[2,4096,16]{1,2,0:T(8,128)(2,1)}, u32[]{:S(2)}) copy-start(bf16[2,4096,16]{1,2,0:T(8,128)(2,1)} %param.13) | copy-start | bytes 786436
  0.7 21.6 %copy-start.71 = (f32[4096]{0:T(1024)S(1)}, f32[4096]{0:T(1024)}, u32[]{:S(2)}) copy-start(f32[4096]{0:T(1024)} %param.11) | copy-start | bytes 49156
  0.7 65.0 %collective-permute-start.3 = (bf16[256,4096]{1,0:T(8,128)(2,1)}, bf16[256,4096]{1,0:T(8,128)(2,1)}, u32[]{:S(2)}, u32[]{:S(2)}) collective-permute-start(bf16[256,4096]{1,0:T(8,128)(2,1)} %x_ref.1), channel_id=1, source_target_pairs={{0,16},{16,0},{1,17},{17,1},{2,18},{18,2},{3,19},{19,3},{4,20},{20... | collective-permute-start | bytes 6291464 | tf_op jit(solution)/shard_map/ppermute | solution.py:41
  39.9 2.5 collective-permute-start
  57.0 2.4 collective-permute-start.1
  57.2 21.2 %collective-permute-start.5 = (bf16[64,3584]{1,0:T(8,128)(2,1)S(1)}, bf16[64,3584]{1,0:T(8,128)(2,1)S(1)}, u32[]{:S(2)}, u32[]{:S(2)}) collective-permute-start(bf16[64,3584]{1,0:T(8,128)(2,1)S(1)} %share_sums.6.refs_0_), channel_id=1, source_target_pairs={{0,2},{1,3},{2,0},{3,1},{4,6},{5,7},{6,4},{7,5},{8,10},{9,11},{10,... | collective-permute-start | bytes 1376264 | tf_op jit(solution)/shard_map/ppermute | solution.py:41
  61.1 22.8 %collective-permute-start.2 = (bf16[64,3072]{1,0:T(8,128)(2,1)}, bf16[64,3072]{1,0:T(8,128)(2,1)}, u32[]{:S(2)}, u32[]{:S(2)}) collective-permute-start(bf16[64,3072]{1,0:T(8,128)(2,1)} %share_sums.7.refs_0_), channel_id=1, source_target_pairs={{0,2},{1,3},{2,0},{3,1},{4,6},{5,7},{6,4},{7,5},{8,10},{9,11},{10,... | collective-permute-start | bytes 1179656 | tf_op jit(solution)/shard_map/ppermute | solution.py:41
  62.0 3.6 collective-permute-start.4
  70.8 7.6 %collective-permute-start.6 = (f32[128,32]{1,0:T(8,128)S(1)}, f32[128,32]{1,0:T(8,128)S(1)}, u32[]{:S(2)}, u32[]{:S(2)}) collective-permute-start(f32[128,32]{1,0:T(8,128)S(1)} %slice.68), channel_id=1, source_target_pairs={{0,1},{1,0},{2,3},{3,2},{4,5},{5,4},{6,7},{7,6},{8,9},{9,8},{10,11... | collective-permute-start | bytes 49160 | tf_op jit(solution)/shard_map/ppermute | solution.py:41
  89.3 4.4 %collective-permute-start.7 = (bf16[128,3584]{1,0:T(8,128)(2,1)S(1)}, bf16[128,3584]{1,0:T(8,128)(2,1)S(1)}, u32[]{:S(2)}, u32[]{:S(2)}) collective-permute-start(bf16[128,3584]{1,0:T(8,128)(2,1)S(1)} %get-tuple-element.56), channel_id=1, source_target_pairs={{0,1},{1,0},{2,3},{3,2},{4,5},{5,4},{6,7},{7,6},{8,9},{9,8},{10,11... | collective-permute-start | bytes 2752520 | tf_op jit(solution)/shard_map/ppermute | solution.py:41
  89.8 3.9 %collective-permute-start.8 = (f32[64,32]{1,0:T(8,128)S(1)}, f32[64,32]{1,0:T(8,128)S(1)}, u32[]{:S(2)}, u32[]{:S(2)}) collective-permute-start(f32[64,32]{1,0:T(8,128)S(1)} %slice.70), channel_id=1, source_target_pairs={{0,2},{1,3},{2,0},{3,1},{4,6},{5,7},{6,4},{7,5},{8,10},{9,11},{10,... | collective-permute-start | bytes 24584 | tf_op jit(solution)/shard_map/ppermute | solution.py:41
  94.0 11.4 %collective-permute-start.9 = (bf16[64,3584]{1,0:T(8,128)(2,1)S(1)}, bf16[64,3584]{1,0:T(8,128)(2,1)S(1)}, u32[]{:S(2)}, u32[]{:S(2)}) collective-permute-start(bf16[64,3584]{1,0:T(8,128)(2,1)S(1)} %share_sums.8.refs_0_), channel_id=1, source_target_pairs={{0,2},{1,3},{2,0},{3,1},{4,6},{5,7},{6,4},{7,5},{8,10},{9,11},{10,... | collective-permute-start | bytes 1376264 | tf_op jit(solution)/shard_map/ppermute | solution.py:41
  111.7 2.3 collective-permute-start.10
  111.7 13.2 %collective-permute-start.12 = (bf16[64,3584]{1,0:T(8,128)(2,1)}, bf16[64,3584]{1,0:T(8,128)(2,1)}, u32[]{:S(2)}, u32[]{:S(2)}) collective-permute-start(bf16[64,3584]{1,0:T(8,128)(2,1)} %share_sums.9.refs_2_), channel_id=1, source_target_pairs={{0,16},{16,0},{1,17},{17,1},{2,18},{18,2},{3,19},{19,3},{4,20},{20... | collective-permute-start | bytes 1376264 | tf_op jit(solution)/shard_map/ppermute | solution.py:41
  116.1 11.4 %collective-permute-start.11 = (bf16[64,3072]{1,0:T(8,128)(2,1)}, bf16[64,3072]{1,0:T(8,128)(2,1)S(1)}, u32[]{:S(2)}, u32[]{:S(2)}) collective-permute-start(bf16[64,3072]{1,0:T(8,128)(2,1)} %share_sums.10), channel_id=1, source_target_pairs={{0,2},{1,3},{2,0},{3,1},{4,6},{5,7},{6,4},{7,5},{8,10},{9,11},{10,... | collective-permute-start | bytes 1179656 | tf_op jit(solution)/shard_map/ppermute | solution.py:41
  136.9 24.1 %copy-start.22 = (bf16[64,3584]{1,0:T(8,128)(2,1)}, bf16[64,3584]{1,0:T(8,128)(2,1)S(1)}, u32[]{:S(2)}) copy-start(bf16[64,3584]{1,0:T(8,128)(2,1)S(1)} %get-tuple-element.62.refs_0_.refs_1_) | copy-start | bytes 1376260
  136.9 13.3 %collective-permute-start.14 = (bf16[64,3584]{1,0:T(8,128)(2,1)S(1)}, bf16[64,3584]{1,0:T(8,128)(2,1)S(1)}, u32[]{:S(2)}, u32[]{:S(2)}) collective-permute-start(bf16[64,3584]{1,0:T(8,128)(2,1)S(1)} %get-tuple-element.62.refs_0_.refs_1_), channel_id=1, source_target_pairs={{0,2},{1,3},{2,0},{3,1},{4,6},{5,7},{6,4},{7,5},{8,10},{9,11},{10,... | collective-permute-start | bytes 1376264 | tf_op jit(solution)/shard_map/ppermute | solution.py:41
  138.1 12.1 %collective-permute-start.13 = (bf16[64,3072]{1,0:T(8,128)(2,1)S(1)}, bf16[64,3072]{1,0:T(8,128)(2,1)S(1)}, u32[]{:S(2)}, u32[]{:S(2)}) collective-permute-start(bf16[64,3072]{1,0:T(8,128)(2,1)S(1)} %share_sums.11.refs_7_), channel_id=1, source_target_pairs={{0,16},{16,0},{1,17},{17,1},{2,18},{18,2},{3,19},{19,3},{4,20},{20... | collective-permute-start | bytes 1179656 | tf_op jit(solution)/shard_map/ppermute | solution.py:41
  138.8 21.2 %collective-permute-start.24 = (bf16[64,3584]{1,0:T(8,128)(2,1)S(1)}, bf16[64,3584]{1,0:T(8,128)(2,1)S(1)}, u32[]{:S(2)}, u32[]{:S(2)}) collective-permute-start(bf16[64,3584]{1,0:T(8,128)(2,1)S(1)} %get-tuple-element.65), channel_id=1, source_target_pairs={{0,16},{16,0},{1,17},{17,1},{2,18},{18,2},{3,19},{19,3},{4,20},{20... | collective-permute-start | bytes 1376264 | tf_op jit(solution)/shard_map/ppermute | solution.py:41
  150.2 33.1 %copy-start.9 = (bf16[64,3584]{1,0:T(8,128)(2,1)}, bf16[64,3584]{1,0:T(8,128)(2,1)S(1)}, u32[]{:S(2)}) copy-start(bf16[64,3584]{1,0:T(8,128)(2,1)S(1)} %collective-permute-done.14.refs_7_.refs_1_.refs_2_) | copy-start | bytes 1376260
  155.3 12.4 %collective-permute-start.15 = (bf16[64,3072]{1,0:T(8,128)(2,1)}, bf16[64,3072]{1,0:T(8,128)(2,1)}, u32[]{:S(2)}, u32[]{:S(2)}) collective-permute-start(bf16[64,3072]{1,0:T(8,128)(2,1)} %get-tuple-element.63.refs_0_.refs_9_), channel_id=1, source_target_pairs={{0,2},{1,3},{2,0},{3,1},{4,6},{5,7},{6,4},{7,5},{8,10},{9,11},{10,... | collective-permute-start | bytes 1179656 | tf_op jit(solution)/shard_map/ppermute | solution.py:41
  156.2 11.5 %collective-permute-start.18 = (bf16[64,3072]{1,0:T(8,128)(2,1)S(1)}, bf16[64,3072]{1,0:T(8,128)(2,1)S(1)}, u32[]{:S(2)}, u32[]{:S(2)}) collective-permute-start(bf16[64,3072]{1,0:T(8,128)(2,1)S(1)} %get-tuple-element.64), channel_id=1, source_target_pairs={{0,16},{16,0},{1,17},{17,1},{2,18},{18,2},{3,19},{19,3},{4,20},{20... | collective-permute-start | bytes 1179656 | tf_op jit(solution)/shard_map/ppermute | solution.py:41
  160.0 34.0 %copy-start.13 = (bf16[64,3584]{1,0:T(8,128)(2,1)}, bf16[64,3584]{1,0:T(8,128)(2,1)S(1)}, u32[]{:S(2)}) copy-start(bf16[64,3584]{1,0:T(8,128)(2,1)S(1)} %relay.8.refs_4_.refs_5_) | copy-start | bytes 1376260
  160.1 13.3 %collective-permute-start.25 = (bf16[64,3584]{1,0:T(8,128)(2,1)S(1)}, bf16[64,3584]{1,0:T(8,128)(2,1)}, u32[]{:S(2)}, u32[]{:S(2)}) collective-permute-start(bf16[64,3584]{1,0:T(8,128)(2,1)S(1)} %relay.8.refs_4_.refs_5_), channel_id=1, source_target_pairs={{0,2},{1,3},{2,0},{3,1},{4,6},{5,7},{6,4},{7,5},{8,10},{9,11},{10,... | collective-permute-start | bytes 1376264 | tf_op jit(solution)/shard_map/ppermute | solution.py:41
  161.0 12.4 %collective-permute-start.22 = (bf16[64,3584]{1,0:T(8,128)(2,1)S(1)}, bf16[64,3584]{1,0:T(8,128)(2,1)S(1)}, u32[]{:S(2)}, u32[]{:S(2)}) collective-permute-start(bf16[64,3584]{1,0:T(8,128)(2,1)S(1)} %get-tuple-element.62.refs_0_.refs_1_), channel_id=1, source_target_pairs={{0,1},{1,0},{2,3},{3,2},{4,5},{5,4},{6,7},{7,6},{8,9},{9,8},{10,11... | collective-permute-start | bytes 1376264 | tf_op jit(solution)/shard_map/ppermute | solution.py:41
  161.0 18.0 %collective-permute-start.26 = (bf16[64,3584]{1,0:T(8,128)(2,1)S(1)}, bf16[64,3584]{1,0:T(8,128)(2,1)S(1)}, u32[]{:S(2)}, u32[]{:S(2)}) collective-permute-start(bf16[64,3584]{1,0:T(8,128)(2,1)S(1)} %relay.8.refs_4_.refs_5_), channel_id=1, source_target_pairs={{0,1},{1,0},{2,3},{3,2},{4,5},{5,4},{6,7},{7,6},{8,9},{9,8},{10,11... | collective-permute-start | bytes 1376264 | tf_op jit(solution)/shard_map/ppermute | solution.py:41
  167.7 12.6 %collective-permute-start.23 = (bf16[64,3584]{1,0:T(8,128)(2,1)S(1)}, bf16[64,3584]{1,0:T(8,128)(2,1)S(1)}, u32[]{:S(2)}, u32[]{:S(2)}) collective-permute-start(bf16[64,3584]{1,0:T(8,128)(2,1)S(1)} %collective-permute-done.14.refs_7_.refs_1_.refs_2_), channel_id=1, source_target_pairs={{0,1},{1,0},{2,3},{3,2},{4,5},{5,4},{6,7},{7,6},{8,9},{9,8},{10,11... | collective-permute-start | bytes 1376264 | tf_op jit(solution)/shard_map/ppermute | solution.py:41
  167.7 4.0 %collective-permute-start.28 = (f32[64,33]{1,0:T(8,128)S(1)}, f32[64,33]{1,0:T(8,128)S(1)}, u32[]{:S(2)}, u32[]{:S(2)}) collective-permute-start(f32[64,33]{1,0:T(8,128)S(1)} %add.225), channel_id=1, source_target_pairs={{0,4},{4,0},{8,12},{12,8},{1,5},{5,1},{9,13},{13,9},{2,6},{6,2},{1... | collective-permute-start | bytes 25352 | tf_op jit(solution)/shard_map/ppermute | solution.py:41
  171.7 10.9 %collective-permute-start.19 = (bf16[64,3072]{1,0:T(8,128)(2,1)S(1)}, bf16[64,3072]{1,0:T(8,128)(2,1)}, u32[]{:S(2)}, u32[]{:S(2)}) collective-permute-start(bf16[64,3072]{1,0:T(8,128)(2,1)S(1)} %relay.7.refs_9_.refs_4_.refs_13_), channel_id=1, source_target_pairs={{0,2},{1,3},{2,0},{3,1},{4,6},{5,7},{6,4},{7,5},{8,10},{9,11},{10,... | collective-permute-start | bytes 1179656 | tf_op jit(solution)/shard_map/ppermute | solution.py:41
  173.4 9.9 %collective-permute-start.27 = (bf16[64,3584]{1,0:T(8,128)(2,1)}, bf16[64,3584]{1,0:T(8,128)(2,1)}, u32[]{:S(2)}, u32[]{:S(2)}) collective-permute-start(bf16[64,3584]{1,0:T(8,128)(2,1)} %collective-permute-done.25.refs_5_.refs_6_), channel_id=1, source_target_pairs={{0,1},{1,0},{2,3},{3,2},{4,5},{5,4},{6,7},{7,6},{8,9},{9,8},{10,11... | collective-permute-start | bytes 1376264 | tf_op jit(solution)/shard_map/ppermute | solution.py:41
  174.2 4.8 %collective-permute-start.29 = (f32[64,33]{1,0:T(8,128)S(1)}, f32[64,33]{1,0:T(8,128)S(1)}, u32[]{:S(2)}, u32[]{:S(2)}) collective-permute-start(f32[64,33]{1,0:T(8,128)S(1)} %add.226.refs_10_), channel_id=1, source_target_pairs={{0,8},{4,12},{8,0},{12,4},{1,9},{5,13},{9,1},{13,5},{2,10},{6,14},... | collective-permute-start | bytes 25352 | tf_op jit(solution)/shard_map/ppermute | solution.py:41
  179.0 15.0 %collective-permute-start.16 = (bf16[64,3072]{1,0:T(8,128)(2,1)}, bf16[64,3072]{1,0:T(8,128)(2,1)}, u32[]{:S(2)}, u32[]{:S(2)}) collective-permute-start(bf16[64,3072]{1,0:T(8,128)(2,1)} %get-tuple-element.63.refs_0_.refs_9_), channel_id=1, source_target_pairs={{0,1},{1,0},{2,3},{3,2},{4,5},{5,4},{6,7},{7,6},{8,9},{9,8},{10,11... | collective-permute-start | bytes 1179656 | tf_op jit(solution)/shard_map/ppermute | solution.py:41
  179.8 14.2 %collective-permute-start.20 = (bf16[64,3072]{1,0:T(8,128)(2,1)S(1)}, bf16[64,3072]{1,0:T(8,128)(2,1)}, u32[]{:S(2)}, u32[]{:S(2)}) collective-permute-start(bf16[64,3072]{1,0:T(8,128)(2,1)S(1)} %relay.7.refs_9_.refs_4_.refs_13_), channel_id=1, source_target_pairs={{0,1},{1,0},{2,3},{3,2},{4,5},{5,4},{6,7},{7,6},{8,9},{9,8},{10,11... | collective-permute-start | bytes 1179656 | tf_op jit(solution)/shard_map/ppermute | solution.py:41
  181.1 12.9 %collective-permute-start.17 = (bf16[64,3072]{1,0:T(8,128)(2,1)}, bf16[64,3072]{1,0:T(8,128)(2,1)}, u32[]{:S(2)}, u32[]{:S(2)}) collective-permute-start(bf16[64,3072]{1,0:T(8,128)(2,1)} %collective-permute-done.15.refs_0_.refs_1_.refs_10_), channel_id=1, source_target_pairs={{0,1},{1,0},{2,3},{3,2},{4,5},{5,4},{6,7},{7,6},{8,9},{9,8},{10,11... | collective-permute-start | bytes 1179656 | tf_op jit(solution)/shard_map/ppermute | solution.py:41
  182.6 11.4 %collective-permute-start.21 = (bf16[64,3072]{1,0:T(8,128)(2,1)}, bf16[64,3072]{1,0:T(8,128)(2,1)}, u32[]{:S(2)}, u32[]{:S(2)}) collective-permute-start(bf16[64,3072]{1,0:T(8,128)(2,1)} %collective-permute-done.19.refs_5_.refs_14_), channel_id=1, source_target_pairs={{0,1},{1,0},{2,3},{3,2},{4,5},{5,4},{6,7},{7,6},{8,9},{9,8},{10,11... | collective-permute-start | bytes 1179656 | tf_op jit(solution)/shard_map/ppermute | solution.py:41
  201.2 41.8 %collective-permute-start.32 = (bf16[256,1024]{1,0:T(8,128)(2,1)}, bf16[256,1024]{1,0:T(8,128)(2,1)}, u32[]{:S(2)}, u32[]{:S(2)}) collective-permute-start(bf16[256,1024]{1,0:T(8,128)(2,1)} %get-tuple-element.70), channel_id=1, source_target_pairs={{0,16},{16,0},{1,17},{17,1},{2,18},{18,2},{3,19},{19,3},{4,20},{20... | collective-permute-start | bytes 1572872 | tf_op jit(solution)/shard_map/ppermute | solution.py:41
  205.9 37.0 %collective-permute-start.30 = (f32[64,33]{0,1:T(8,128)}, f32[64,33]{0,1:T(8,128)S(1)}, u32[]{:S(2)}, u32[]{:S(2)}) collective-permute-start(f32[64,33]{0,1:T(8,128)} %copy.24), channel_id=1, source_target_pairs={{0,2},{1,3},{2,0},{3,1},{4,6},{5,7},{6,4},{7,5},{8,10},{9,11},{10,... | collective-permute-start | bytes 25352 | tf_op jit(solution)/shard_map/ppermute | solution.py:41
  230.9 44.2 %collective-permute-start.37 = (bf16[256,1536]{1,0:T(8,128)(2,1)}, bf16[256,1536]{1,0:T(8,128)(2,1)}, u32[]{:S(2)}, u32[]{:S(2)}) collective-permute-start(bf16[256,1536]{1,0:T(8,128)(2,1)} %get-tuple-element.73), channel_id=1, source_target_pairs={{0,16},{16,0},{1,17},{17,1},{2,18},{18,2},{3,19},{19,3},{4,20},{20... | collective-permute-start | bytes 2359304 | tf_op jit(solution)/shard_map/ppermute | solution.py:41
  243.0 3.6 collective-permute-start.31
  245.1 8.9 %collective-permute-start.33 = (bf16[128,1024]{1,0:T(8,128)(2,1)}, bf16[128,1024]{1,0:T(8,128)(2,1)S(1)}, u32[]{:S(2)}, u32[]{:S(2)}) collective-permute-start(bf16[128,1024]{1,0:T(8,128)(2,1)} %get-tuple-element.89), channel_id=1, source_target_pairs={{0,4},{4,0},{8,12},{12,8},{1,5},{5,1},{9,13},{13,9},{2,6},{6,2},{1... | collective-permute-start | bytes 786440 | tf_op jit(solution)/shard_map/ppermute | solution.py:41
  266.4 24.3 %collective-permute-start.34 = (bf16[256,1536]{1,0:T(8,128)(2,1)}, bf16[256,1536]{1,0:T(8,128)(2,1)}, u32[]{:S(2)}, u32[]{:S(2)}) collective-permute-start(bf16[256,1536]{1,0:T(8,128)(2,1)} %get-tuple-element.72), channel_id=1, source_target_pairs={{0,16},{16,0},{1,17},{17,1},{2,18},{18,2},{3,19},{19,3},{4,20},{20... | collective-permute-start | bytes 2359304 | tf_op jit(solution)/shard_map/ppermute | solution.py:41
  269.5 10.0 %collective-permute-start.52 = (bf16[64,32]{0,1:T(8,128)(2,1)}, bf16[64,32]{0,1:T(8,128)(2,1)S(1)}, u32[]{:S(2)}, u32[]{:S(2)}) collective-permute-start(bf16[64,32]{0,1:T(8,128)(2,1)} %copy.36), channel_id=1, source_target_pairs={{0,2},{1,3},{2,0},{3,1},{4,6},{5,7},{6,4},{7,5},{8,10},{9,11},{10,... | collective-permute-start | bytes 12296 | tf_op jit(solution)/shard_map/ppermute | solution.py:41
  272.5 13.2 %collective-permute-start.40 = (bf16[64,1024]{1,0:T(8,128)(2,1)}, bf16[64,1024]{1,0:T(8,128)(2,1)}, u32[]{:S(2)}, u32[]{:S(2)}) collective-permute-start(bf16[64,1024]{1,0:T(8,128)(2,1)} %get-tuple-element.94), channel_id=1, source_target_pairs={{0,8},{4,12},{8,0},{12,4},{1,9},{5,13},{9,1},{13,5},{2,10},{6,14},... | collective-permute-start | bytes 393224 | tf_op jit(solution)/shard_map/ppermute | solution.py:41
  278.0 16.0 %collective-permute-start.38 = (bf16[128,1536]{1,0:T(8,128)(2,1)}, bf16[128,1536]{1,0:T(8,128)(2,1)}, u32[]{:S(2)}, u32[]{:S(2)}) collective-permute-start(bf16[128,1536]{1,0:T(8,128)(2,1)} %get-tuple-element.84), channel_id=1, source_target_pairs={{0,4},{4,0},{8,12},{12,8},{1,5},{5,1},{9,13},{13,9},{2,6},{6,2},{1... | collective-permute-start | bytes 1179656 | tf_op jit(solution)/shard_map/ppermute | solution.py:41
  281.5 3.4 collective-permute-start.53
  290.3 14.9 %collective-permute-start.41 = (bf16[64,1024]{1,0:T(8,128)(2,1)}, bf16[64,1024]{1,0:T(8,128)(2,1)S(1)}, u32[]{:S(2)}, u32[]{:S(2)}) collective-permute-start(bf16[64,1024]{1,0:T(8,128)(2,1)} %get-tuple-element.74.refs_0_), channel_id=1, source_target_pairs={{0,8},{4,12},{8,0},{12,4},{1,9},{5,13},{9,1},{13,5},{2,10},{6,14},... | collective-permute-start | bytes 393224 | tf_op jit(solution)/shard_map/ppermute | solution.py:41
  293.5 26.1 %copy-start.12 = (bf16[64,3584]{1,0:T(8,128)(2,1)S(1)}, bf16[64,3584]{1,0:T(8,128)(2,1)}, u32[]{:S(2)}) copy-start(bf16[64,3584]{1,0:T(8,128)(2,1)} %copy-done.9) | copy-start | bytes 1376260
  293.5 26.1 %copy-start.16 = (bf16[64,3584]{1,0:T(8,128)(2,1)S(1)}, bf16[64,3584]{1,0:T(8,128)(2,1)}, u32[]{:S(2)}) copy-start(bf16[64,3584]{1,0:T(8,128)(2,1)} %copy-done.13) | copy-start | bytes 1376260
  293.5 33.3 %collective-permute-start.35 = (bf16[128,1536]{1,0:T(8,128)(2,1)}, bf16[128,1536]{1,0:T(8,128)(2,1)}, u32[]{:S(2)}, u32[]{:S(2)}) collective-permute-start(bf16[128,1536]{1,0:T(8,128)(2,1)} %get-tuple-element.86), channel_id=1, source_target_pairs={{0,4},{4,0},{8,12},{12,8},{1,5},{5,1},{9,13},{13,9},{2,6},{6,2},{1... | collective-permute-start | bytes 1179656 | tf_op jit(solution)/shard_map/ppermute | solution.py:41
  295.9 12.1 %collective-permute-start.39 = (bf16[64,1536]{1,0:T(8,128)(2,1)}, bf16[64,1536]{1,0:T(8,128)(2,1)}, u32[]{:S(2)}, u32[]{:S(2)}) collective-permute-start(bf16[64,1536]{1,0:T(8,128)(2,1)} %get-tuple-element.90), channel_id=1, source_target_pairs={{0,8},{4,12},{8,0},{12,4},{1,9},{5,13},{9,1},{13,5},{2,10},{6,14},... | collective-permute-start | bytes 589832 | tf_op jit(solution)/shard_map/ppermute | solution.py:41
  299.0 4.0 %collective-permute-start.54 = (bf16[256,16]{0,1:T(8,128)(2,1)}, bf16[256,16]{0,1:T(8,128)(2,1)}, u32[]{:S(2)}, u32[]{:S(2)}) collective-permute-start(bf16[256,16]{0,1:T(8,128)(2,1)} %get-tuple-element.99), channel_id=1, source_target_pairs={{0,16},{16,0},{1,17},{17,1},{2,18},{18,2},{3,19},{19,3},{4,20},{20... | collective-permute-start | bytes 24584 | tf_op jit(solution)/shard_map/ppermute | solution.py:41
  303.7 28.0 %collective-permute-start.43 = (bf16[64,1024]{1,0:T(8,128)(2,1)}, bf16[64,1024]{1,0:T(8,128)(2,1)S(1)}, u32[]{:S(2)}, u32[]{:S(2)}) collective-permute-start(bf16[64,1024]{1,0:T(8,128)(2,1)} %get-tuple-element.74.refs_0_), channel_id=1, source_target_pairs={{0,4},{4,0},{8,12},{12,8},{1,5},{5,1},{9,13},{13,9},{2,6},{6,2},{1... | collective-permute-start | bytes 393224 | tf_op jit(solution)/shard_map/ppermute | solution.py:41
  305.3 26.5 %collective-permute-start.44 = (bf16[64,1024]{1,0:T(8,128)(2,1)S(1)}, bf16[64,1024]{1,0:T(8,128)(2,1)S(1)}, u32[]{:S(2)}, u32[]{:S(2)}) collective-permute-start(bf16[64,1024]{1,0:T(8,128)(2,1)S(1)} %collective-permute-done.41.refs_8_.refs_1_), channel_id=1, source_target_pairs={{0,4},{4,0},{8,12},{12,8},{1,5},{5,1},{9,13},{13,9},{2,6},{6,2},{1... | collective-permute-start | bytes 393224 | tf_op jit(solution)/shard_map/ppermute | solution.py:41
  315.0 16.7 %collective-permute-start.42 = (bf16[64,1536]{1,0:T(8,128)(2,1)}, bf16[64,1536]{1,0:T(8,128)(2,1)S(1)}, u32[]{:S(2)}, u32[]{:S(2)}) collective-permute-start(bf16[64,1536]{1,0:T(8,128)(2,1)} %get-tuple-element.75.refs_0_), channel_id=1, source_target_pairs={{0,8},{4,12},{8,0},{12,4},{1,9},{5,13},{9,1},{13,5},{2,10},{6,14},... | collective-permute-start | bytes 589832 | tf_op jit(solution)/shard_map/ppermute | solution.py:41
  318.4 33.8 %collective-permute-start.48 = (bf16[64,1536]{1,0:T(8,128)(2,1)}, bf16[64,1536]{1,0:T(8,128)(2,1)}, u32[]{:S(2)}, u32[]{:S(2)}) collective-permute-start(bf16[64,1536]{1,0:T(8,128)(2,1)} %get-tuple-element.75.refs_0_), channel_id=1, source_target_pairs={{0,4},{4,0},{8,12},{12,8},{1,5},{5,1},{9,13},{13,9},{2,6},{6,2},{1... | collective-permute-start | bytes 589832 | tf_op jit(solution)/shard_map/ppermute | solution.py:41
  328.1 10.4 %collective-permute-start.36 = (bf16[64,1536]{1,0:T(8,128)(2,1)S(1)}, bf16[64,1536]{1,0:T(8,128)(2,1)S(1)}, u32[]{:S(2)}, u32[]{:S(2)}) collective-permute-start(bf16[64,1536]{1,0:T(8,128)(2,1)S(1)} %get-tuple-element.92), channel_id=1, source_target_pairs={{0,8},{4,12},{8,0},{12,4},{1,9},{5,13},{9,1},{13,5},{2,10},{6,14},... | collective-permute-start | bytes 589832 | tf_op jit(solution)/shard_map/ppermute | solution.py:41
  339.1 19.3 %collective-permute-start.45 = (bf16[80,1536]{1,0:T(8,128)(2,1)S(1)}, bf16[80,1536]{1,0:T(8,128)(2,1)S(1)}, u32[]{:S(2)}, u32[]{:S(2)}) collective-permute-start(bf16[80,1536]{1,0:T(8,128)(2,1)S(1)} %maximum_maximum_fusion.refs_0_), channel_id=1, source_target_pairs={{0,8},{4,12},{8,0},{12,4},{1,9},{5,13},{9,1},{13,5},{2,10},{6,14},... | collective-permute-start | bytes 737288 | tf_op jit(solution)/shard_map/ppermute | solution.py:41
  342.5 17.9 %collective-permute-start.55 = (bf16[16,6656]{1,0:T(8,128)(2,1)}, bf16[16,6656]{1,0:T(8,128)(2,1)}, u32[]{:S(2)}, u32[]{:S(2)}) collective-permute-start(bf16[16,6656]{1,0:T(8,128)(2,1)} %convert_element_type.128), channel_id=1, source_target_pairs={{0,16},{16,0},{1,17},{17,1},{2,18},{18,2},{3,19},{19,3},{4,20},{20... | collective-permute-start | bytes 638984 | tf_op jit(solution)/shard_map/ppermute | solution.py:41
  344.6 6.0 %collective-permute-start.51 = (bf16[256,32]{0,1:T(8,128)(2,1)}, bf16[256,32]{0,1:T(8,128)(2,1)S(1)}, u32[]{:S(2)}, u32[]{:S(2)}) collective-permute-start(bf16[256,32]{0,1:T(8,128)(2,1)} %copy.33), channel_id=1, source_target_pairs={{0,16},{16,0},{1,17},{17,1},{2,18},{18,2},{3,19},{19,3},{4,20},{20... | collective-permute-start | bytes 49160 | tf_op jit(solution)/shard_map/ppermute | solution.py:41
  345.3 10.6 %collective-permute-start.49 = (bf16[64,1536]{1,0:T(8,128)(2,1)S(1)}, bf16[64,1536]{1,0:T(8,128)(2,1)S(1)}, u32[]{:S(2)}, u32[]{:S(2)}) collective-permute-start(bf16[64,1536]{1,0:T(8,128)(2,1)S(1)} %copy-done.63), channel_id=1, source_target_pairs={{0,4},{4,0},{8,12},{12,8},{1,5},{5,1},{9,13},{13,9},{2,6},{6,2},{1... | collective-permute-start | bytes 589832 | tf_op jit(solution)/shard_map/ppermute | solution.py:41
  352.2 20.8 %copy-start.87 = (f32[16,6656]{1,0:T(8,128)S(1)}, f32[16,6656]{1,0:T(8,128)}, u32[]{:S(2)}) copy-start(f32[16,6656]{1,0:T(8,128)} %constant_dynamic-update-slice_fusion) | copy-start | bytes 1277956
  358.4 8.8 %collective-permute-start.46 = (bf16[80,1536]{1,0:T(8,128)(2,1)S(1)}, bf16[80,1536]{1,0:T(8,128)(2,1)S(1)}, u32[]{:S(2)}, u32[]{:S(2)}) collective-permute-start(bf16[80,1536]{1,0:T(8,128)(2,1)S(1)} %maximum_maximum_fusion.refs_0_), channel_id=1, source_target_pairs={{0,4},{4,0},{8,12},{12,8},{1,5},{5,1},{9,13},{13,9},{2,6},{6,2},{1... | collective-permute-start | bytes 737288 | tf_op jit(solution)/shard_map/ppermute | solution.py:41
  358.4 13.1 %collective-permute-start.47 = (bf16[80,1536]{1,0:T(8,128)(2,1)S(1)}, bf16[80,1536]{1,0:T(8,128)(2,1)S(1)}, u32[]{:S(2)}, u32[]{:S(2)}) collective-permute-start(bf16[80,1536]{1,0:T(8,128)(2,1)S(1)} %collective-permute-done.45.refs_1_), channel_id=1, source_target_pairs={{0,4},{4,0},{8,12},{12,8},{1,5},{5,1},{9,13},{13,9},{2,6},{6,2},{1... | collective-permute-start | bytes 737288 | tf_op jit(solution)/shard_map/ppermute | solution.py:41
  371.6 3.9 %collective-permute-start.50 = (f32[3,1536]{1,0:T(4,128)S(1)}, f32[3,1536]{1,0:T(4,128)S(1)}, u32[]{:S(2)}, u32[]{:S(2)}) collective-permute-start(f32[3,1536]{1,0:T(4,128)S(1)} %fusion.6), channel_id=1, source_target_pairs={{0,16},{16,0},{1,17},{17,1},{2,18},{18,2},{3,19},{19,3},{4,20},{20... | collective-permute-start | bytes 55304 | tf_op jit(solution)/shard_map/ppermute | solution.py:41
  (88 other events, 519.9 us)

commit v9 on v6

--- a/solution.py
+++ b/solution.py
@@ -153,6 +153,23 @@
         cost_estimate=cost(2 * rows * depth * (stop - start) * tile, 2 * depth * (rows + (stop - start) * tile) + 6 * half * (stop - start) * tile),
         name="forward_matmul",
     )(x, weights, *into, *after)
+
+
+def relay(x, after):
+    def kernel(x_ref, *refs):
+        refs[-1][...] = x_ref[...]
+
+    whole = pl.BlockSpec(x.shape, lambda i: (0,) * x.ndim)
+    return pl.pallas_call(
+        kernel,
+        grid=(1,),
+        in_specs=[whole] + [ANY] * len(after),
+        out_specs=whole,
+        out_shape=jax.ShapeDtypeStruct(x.shape, x.dtype),
+        compiler_params=params(),
+        cost_estimate=cost(0, 4 * x.size),
+        name="relay",
+    )(x, *after)
 
 
 def share_sums(parts, rows, count, after=(), places=None):
@@ -516,19 +533,13 @@
         others.append(swap(passed, "dp", dp, 1))
         more, mine_grad, peer_grad = gradients(1, ())
         back = first_half_done[0] + more
-        for bit in range(bits_of(ffn)):
-            back = back + swap(back, "ffn", ffn, 1 << bit)
-        back = jnp.stack([back, swap(back, "dp", dp, 1)])
         for j in range(1, len(steps)):
-            first_half(j, (mine_grad,) if j == 1 else (peer_grad, back))
+            first_half(j, (mine_grad,) if j == 1 else (peer_grad,))
             if j == 1:
                 (peer_grad,) = share_sums([peer_grad], own, 1, (bases[1],), [0])
         own_pieces = spread(mine_grad)
         grads.append(own_pieces + spread(peer_grad))
 
-        back = double(back, "hid", hid, dim=1)
-        low_mine = jnp.where(first_pair, low[:, :, :rank], low[:, :, rank:])
-        low_mine = double(low_mine, "hid", hid, dim=1).reshape(2 * tokens, rank).T
         shard = tokens // ffn
         place = reversed_bits(f, bits_of(ffn))
         products, received = [], []
@@ -546,16 +557,27 @@
         for j, ((first, n), base) in enumerate(zip(steps, bases)):
             wait = (products[-1],) if products else tuple(bases)
             if j == 2:
+                back = relay(back, (products[1],))
+                for bit in range(bits_of(ffn)):
+                    back = back + swap(back, "ffn", ffn, 1 << bit)
+                back = double(back, "hid", hid)
                 first_steps.append(halving_step([products[0], received[0]], 0))
-                wait += (first_steps[0][1], back, low_mine)
+                wait += (first_steps[0][1], back)
             keep, send = backward_matmul(
                 grads[1], weights, chunks[1][0] * tile, first, n, width_tile, base=base, base_first=first,
                 after=wait,
             )
             products.append(keep)
             received.append(swap(send, "dp", dp, 1))
-        back_low = back[:, :, : 2 * rank].astype(BF16)
-        acts_product = back[0, :, 2 * rank]
+        if len(steps) < 3:
+            for bit in range(bits_of(ffn)):
+                back = back + swap(back, "ffn", ffn, 1 << bit)
+            back = double(back, "hid", hid)
+        low = relay(low, (products[-1],))
+        low_mine = jnp.where(first_pair, low[:, :, :rank], low[:, :, rank:])
+        low_mine = double(low_mine, "hid", hid, dim=1).reshape(2 * tokens, rank).T
+        back_low = back[:, : 2 * rank].astype(BF16)
+        acts_product = back[:, 2 * rank]
 
         block = min(own, shard)
 
@@ -577,7 +599,7 @@
         dot_factor = stats_shard[:, 1] ** 2 * dot_shard / MODEL_WIDTH
         stats_shard = jnp.concatenate([stats_shard, dot_factor[:, None]], axis=1)
         stream_shard = shard_rows(stream)
-        back_shard = lax.dynamic_slice_in_dim(back_low[0], place * shard, shard, axis=0)
+        back_shard = lax.dynamic_slice_in_dim(back_low, place * shard, shard, axis=0)
 
         out, sums, gathered = None, [], []
         owners = [reversed_bits(f ^ reversed_bits(p, bits_of(ffn)), bits_of(ffn)) for p in range(ffn)]
@@ -628,7 +650,8 @@
         up_gradient = jnp.where(
             first_pair, jnp.stack([up_mine, up_other]), jnp.stack([up_other, up_mine])
         )
-        back_rows = back_low.reshape(2, hid, own, 2 * rank).transpose(1, 0, 2, 3).reshape(2 * tokens, 2 * rank)
+        peer_back = swap(relay(back_low, (received[-1],)), "dp", dp, 1)
+        back_rows = jnp.stack([back_low, peer_back]).reshape(2, hid, own, 2 * rank).transpose(1, 0, 2, 3).reshape(2 * tokens, 2 * rank)
         (down_gradient,) = adapter_products(back_rows.T, [[normed]])
         down_gradient = jnp.transpose(
             down_gradient.reshape(2, rank, width), (0, 2, 1)

time: 352 us -> 347 us (0.986)
  Pallas kernels: 130 us -> 122 us
  waiting for transfers between devices: 106 us -> 112 us
  local copies, waits for them, and re-layouts: 27.8 us -> 23.2 us
    ppermute x54, waiting for transfers between devices: 106 us -> 112 us  [swap(): return lax.ppermute(x, axis, [(i, i ^ mask) for i in range(n)])]
    unnamed x136 -> x154, local copies, waits for them, and re-layouts: 22.9 us -> 19.9 us
  transfers between devices with their start and end apart: 54 -> 54, of which waited for: 27 -> 26; matrix products, arithmetic and copies ran while one was open for 7% -> 6% of each run, Pallas kernels for 28% -> 25%
where the time goes in v9:
time: 347 us; the launch traced here: 345 us
  Pallas kernels  122 us (35%)
  waiting for transfers between devices  112 us (32%)
  starting transfers between devices  55.5 us (16%)
  local copies, waits for them, and re-layouts  23.2 us (7%)
  other arithmetic  16.7 us (5%)
  blocking collectives  13.4 us (4%)
    ppermute x54, waiting for transfers between devices, swap(): return lax.ppermute(x, axis, [(i, i ^ mask) for i in range(n)])  112 us
    ppermute x54, starting transfers between devices, swap(): return lax.ppermute(x, axis, [(i, i ^ mask) for i in range(n)])  55.5 us
    pallas_call x6, Pallas kernels, forward_matmul(): pl.pallas_call(kernel, grid=(stop - start,), in_specs=[RESIDENT, pl.Block...  54.4 us
    pallas_call x6, Pallas kernels, backward_matmul(): pl.pallas_call(kernel, grid=(tiles,), in_specs=[pl.BlockSpec(g.shape, lam...  46.3 us
    unnamed x154, local copies, waits for them, and re-layouts  19.9 us
    psum x1, blocking collectives, local(): lax.psum((jnp.sum(rows * rows, axis=1), jnp.sum(steering * steering)), 'h...  7.37 us
  transfers between devices with their start and end apart: 54, of which 26 were waited for; matrix products, arithmetic and copies ran while one was open for 6% of the time, Pallas kernels for 25%

profile of v9, /device:TPU:0, one launch (start us, length us, event | category | flops | bytes accessed | tf_op | source)
XLA Modules:
  0.0 345.4 jit_solution(15150618975847269302)
XLA Ops:
  0.7 3.0 collective-permute-start
  5.0 2.1 fusion
  7.1 7.4 %all-reduce = (f32[256]{0:T(256)S(1)}, f32[]{:T(128)}) all-reduce(f32[256]{0:T(256)S(1)} %fusion, f32[]{:T(128)} %multiply_reduce_fusion), channel_id=1, replica_groups=mesh['dp'=2,'ffn'=4,'hid'=4] {'hid'}, use_global_device_ids=true, to_apply=%region_1.0 | all-reduce | flops 257 | bytes 2056 | tf_op jit(solution)/shard_map/psum | solution.py:425
  16.0 6.1 %psum.23 = f32[256]{0:T(256)S(1)} all-reduce(f32[256]{0:T(256)S(1)} %fusion.2), channel_id=1, replica_groups=mesh['dp'=2,'ffn'=4,'hid'=4] {'hid'}, use_global_device_ids=true, to_apply=%region_5.0 | all-reduce | flops 256 | bytes 2048 | tf_op jit(solution)/shard_map/psum | solution.py:432
  22.3 1.7 normalize.2
  24.0 14.6 %forward_matmul.6 = (f32[128,3584]{1,0:T(8,128)S(1)}, bf16[128,3584]{1,0:T(8,128)(2,1)S(1)}, f32[8,128]{1,0:T(8,128)}) custom-call(bf16[256,4096]{1,0:T(8,128)(2,1)S(1)} %get-tuple-element.50.x_ref.refs_0_, bf16[1,4096,6656]{2,1,0:T(8,128)(2,1)} %refs_8_.11), custom_call_target="tpu_custom_call" | custom-call | flops 75161928 | bytes 342097 | tf_op jit(solution)/shard_map/forward_matmul/pallas_call | solution.py:139
  38.6 2.5 collective-permute-done.2.refs_1_
  42.8 9.5 %collective-permute-done.1.stat_ref = f32[256,2]{1,0:T(8,128)S(1)} collective-permute-done((f32[256,2]{1,0:T(8,128)S(1)}, f32[256,2]{1,0:T(8,128)S(1)}, u32[]{:S(2)}, u32[]{:S(2)}) %collective-permute-start.1) | collective-permute-done | bytes 2080 | tf_op jit(solution)/shard_map/ppermute | solution.py:41
  52.3 3.4 normalize.3
  55.9 10.4 %forward_matmul.7 = (f32[128,3584]{1,0:T(8,128)S(1)}, bf16[128,3584]{1,0:T(8,128)(2,1)S(1)}, f32[8,128]{1,0:T(8,128)}) custom-call(bf16[256,4096]{1,0:T(8,128)(2,1)S(1)} %get-tuple-element.55.x_ref, bf16[1,4096,6656]{2,1,0:T(8,128)(2,1)} %refs_8_.11, bf16[64,3584]{1,0:T(8,128)(2,1)S(1)} %share_sums.6.refs_0_), custom_call_target="tpu_custom_call" | custom-call | flops 42949672 | bytes 204472 | tf_op jit(solution)/shard_map/forward_matmul/pallas_call | solution.py:139
  66.3 7.8 %forward_matmul.8 = (f32[128,3584]{1,0:T(8,128)S(1)}, bf16[128,3584]{1,0:T(8,128)(2,1)S(1)}, f32[8,128]{1,0:T(8,128)}) custom-call(bf16[256,4096]{1,0:T(8,128)(2,1)S(1)} %get-tuple-element.55.x_ref, bf16[1,4096,6656]{2,1,0:T(8,128)(2,1)} %refs_8_.11, f32[128,3584]{1,0:T(8,128)S(1)} %get-tuple-element.56.refs_0_, ...), custom_call_target="tpu_custom_call", output_to_operand_aliasing={{0}: (2, {}), {1}: (3, {})} | custom-call | flops 32212254 | bytes 158597 | tf_op jit(solution)/shard_map/forward_matmul/pallas_call | solution.py:139
  74.1 1.8 collective-permute-start.6
  75.9 2.7 collective-permute-done.6
  79.0 1.8 collective-permute-start.7
  80.8 7.0 %forward_matmul.9 = (f32[256,3072]{1,0:T(8,128)S(1)}, bf16[256,3072]{1,0:T(8,128)(2,1)S(1)}, f32[8,128]{1,0:T(8,128)S(1)}) custom-call(bf16[512,4096]{1,0:T(8,128)(2,1)S(1)} %get-tuple-element.54.x_ref.refs_1_, bf16[1,4096,6656]{2,1,0:T(8,128)(2,1)} %refs_8_.11, bf16[64,3584]{1,0:T(8,128)(2,1)S(1)} %share_sums.7.refs_0_), custom_call_target="tpu_custom_call" | custom-call | flops 42949672 | bytes 141557 | tf_op jit(solution)/shard_map/forward_matmul/pallas_call | solution.py:139
  87.8 3.3 collective-permute-done.7.refs_2_
  92.2 1.7 collective-permute-start.8
  93.8 2.2 copy-done.1
  98.5 9.5 %forward_matmul.10 = (f32[256,3072]{1,0:T(8,128)S(1)}, bf16[256,3072]{1,0:T(8,128)(2,1)S(1)}, f32[8,128]{1,0:T(8,128)S(1)}) custom-call(bf16[512,4096]{1,0:T(8,128)(2,1)S(1)} %copy-done.1, bf16[1,4096,6656]{2,1,0:T(8,128)(2,1)} %refs_8_.11, f32[256,3072]{1,0:T(8,128)S(1)} %get-tuple-element.62.refs_0_, ...), custom_call_target="tpu_custom_call", output_to_operand_aliasing={{0}: (2, {}), {1}: (3, {})} | custom-call | flops 64424508 | bytes 191365 | tf_op jit(solution)/shard_map/forward_matmul/pallas_call | solution.py:139
  108.0 3.0 gated_gradients.2
  111.0 1.6 collective-permute-start.10
  113.1 8.8 %collective-permute-done.10.refs_3_.refs_1_.refs_2_ = bf16[64,3584]{1,0:T(8,128)(2,1)S(1)} collective-permute-done((bf16[64,3584]{1,0:T(8,128)(2,1)S(1)}, bf16[64,3584]{1,0:T(8,128)(2,1)S(1)}, u32[]{:S(2)}, u32[]{:S(2)}) %collective-permute-start.10) | collective-permute-done | bytes 458784 | tf_op jit(solution)/shard_map/ppermute | solution.py:41
  123.2 5.2 %forward_matmul.11 = (f32[256,3072]{1,0:T(8,128)S(1)}, bf16[256,3072]{1,0:T(8,128)(2,1)S(1)}, f32[8,128]{1,0:T(8,128)}) custom-call(bf16[512,4096]{1,0:T(8,128)(2,1)S(1)} %copy-done.1, bf16[1,4096,6656]{2,1,0:T(8,128)(2,1)} %refs_8_.11, f32[256,3072]{1,0:T(8,128)S(1)} %get-tuple-element.65.refs_0_, ...), custom_call_target="tpu_custom_call", output_to_operand_aliasing={{0}: (2, {}), {1}: (3, {})} | custom-call | flops 21474836 | bytes 91750 | tf_op jit(solution)/shard_map/forward_matmul/pallas_call | solution.py:139
  130.8 11.7 %collective-permute-done.16.refs_5_.refs_6_ = bf16[64,3584]{1,0:T(8,128)(2,1)S(1)} collective-permute-done((bf16[64,3584]{1,0:T(8,128)(2,1)S(1)}, bf16[64,3584]{1,0:T(8,128)(2,1)S(1)}, u32[]{:S(2)}, u32[]{:S(2)}) %collective-permute-start.16) | collective-permute-done | bytes 458784 | tf_op jit(solution)/shard_map/ppermute | solution.py:41
  145.0 9.0 %backward_matmul.6.refs_3_.refs_9_.refs_10_ = f32[512,1536]{1,0:T(8,128)S(1)} custom-call(bf16[64,3584]{1,0:T(8,128)(2,1)S(1)} %get-tuple-element.69.refs_0_.refs_1_, bf16[64,3584]{1,0:T(8,128)(2,1)S(1)} %collective-permute-done.10.refs_3_.refs_1_.refs_2_, bf16[64,3584]{1,0:T(8,128)(2,1)S(1)} %collective-permute-done.14.refs_2_.refs_3_, ...), custom_call_target="tpu_custom_call" | custom-call | flops 56371444 | bytes 178257 | tf_op jit(solution)/shard_map/backward_matmul/pallas_call | solution.py:298
  155.8 7.1 %collective-permute-done.12.refs_2_ = bf16[64,3072]{1,0:T(8,128)(2,1)S(1)} collective-permute-done((bf16[64,3072]{1,0:T(8,128)(2,1)S(1)}, bf16[64,3072]{1,0:T(8,128)(2,1)S(1)}, u32[]{:S(2)}, u32[]{:S(2)}) %collective-permute-start.12) | collective-permute-done | bytes 393248 | tf_op jit(solution)/shard_map/ppermute | solution.py:41
  162.9 2.7 collective-permute-done.19.refs_3_
  165.6 3.3 gated_gradients.3
  170.0 8.5 %backward_matmul.7.refs_1_.refs_11_.refs_9_ = f32[512,1536]{1,0:T(8,128)S(1)} custom-call(bf16[64,3584]{1,0:T(8,128)(2,1)S(1)} %get-tuple-element.69.refs_0_.refs_1_, bf16[64,3584]{1,0:T(8,128)(2,1)S(1)} %collective-permute-done.10.refs_3_.refs_1_.refs_2_, bf16[64,3584]{1,0:T(8,128)(2,1)S(1)} %collective-permute-done.14.refs_2_.refs_3_, ...), custom_call_target="tpu_custom_call" | custom-call | flops 56371444 | bytes 178257 | tf_op jit(solution)/shard_map/backward_matmul/pallas_call | solution.py:298
  178.7 1.6 collective-permute-start.24
  180.9 6.7 %collective-permute-done.24.refs_5_.refs_14_ = bf16[64,3072]{1,0:T(8,128)(2,1)S(1)} collective-permute-done((bf16[64,3072]{1,0:T(8,128)(2,1)S(1)}, bf16[64,3072]{1,0:T(8,128)(2,1)S(1)}, u32[]{:S(2)}, u32[]{:S(2)}) %collective-permute-start.24) | collective-permute-done | bytes 393248 | tf_op jit(solution)/shard_map/ppermute | solution.py:41
  187.7 6.4 %backward_matmul.8.refs_12_.refs_9_ = f32[512,1024]{1,0:T(8,128)S(1)} custom-call(bf16[64,3584]{1,0:T(8,128)(2,1)S(1)} %get-tuple-element.69.refs_0_.refs_1_, bf16[64,3584]{1,0:T(8,128)(2,1)S(1)} %collective-permute-done.10.refs_3_.refs_1_.refs_2_, bf16[64,3584]{1,0:T(8,128)(2,1)S(1)} %collective-permute-done.14.refs_2_.refs_3_, ...), custom_call_target="tpu_custom_call" | custom-call | flops 37580964 | bytes 131072 | tf_op jit(solution)/shard_map/backward_matmul/pallas_call | solution.py:298
  194.2 8.2 %backward_matmul.9 = (f32[256,1536]{1,0:T(8,128)S(1)}, bf16[256,1536]{1,0:T(8,128)(2,1)S(1)}) custom-call(bf16[64,3072]{1,0:T(8,128)(2,1)S(1)} %get-tuple-element.74.refs_9_.refs_0_, bf16[64,3072]{1,0:T(8,128)(2,1)S(1)} %collective-permute-done.20.refs_1_.refs_10_, bf16[64,3072]{1,0:T(8,128)(2,1)S(1)} %collective-permute-done.21.refs_2_.refs_11_, ...), custom_call_target="tpu_custom_call" | custom-call | flops 48318384 | bytes 188743 | tf_op jit(solution)/shard_map/backward_matmul/pallas_call | solution.py:298
  203.3 8.2 %backward_matmul.10 = (f32[256,1536]{1,0:T(8,128)S(1)}, bf16[256,1536]{1,0:T(8,128)(2,1)S(1)}) custom-call(bf16[64,3072]{1,0:T(8,128)(2,1)S(1)} %get-tuple-element.74.refs_9_.refs_0_, bf16[64,3072]{1,0:T(8,128)(2,1)S(1)} %collective-permute-done.20.refs_1_.refs_10_, bf16[64,3072]{1,0:T(8,128)(2,1)S(1)} %collective-permute-done.21.refs_2_.refs_11_, ...), custom_call_target="tpu_custom_call" | custom-call | flops 48318384 | bytes 188743 | tf_op jit(solution)/shard_map/backward_matmul/pallas_call | solution.py:298
  212.7 1.6 collective-permute-start.28
  214.4 2.3 collective-permute-done.28
  216.7 2.7 collective-permute-start.29
  221.5 1.6 collective-permute-start.30
  226.3 1.6 collective-permute-start.39
  230.0 10.2 %collective-permute-done.27 = bf16[256,1536]{1,0:T(8,128)(2,1)} collective-permute-done((bf16[256,1536]{1,0:T(8,128)(2,1)}, bf16[256,1536]{1,0:T(8,128)(2,1)}, u32[]{:S(2)}, u32[]{:S(2)}) %collective-permute-start.27) | collective-permute-done | bytes 786464 | tf_op jit(solution)/shard_map/ppermute | solution.py:41
  240.2 2.8 convert_add_fusion.2
  242.9 1.6 collective-permute-start.33
  244.6 5.9 %backward_matmul.11 = (f32[256,1024]{1,0:T(8,128)S(1)}, bf16[256,1024]{1,0:T(8,128)(2,1)S(1)}) custom-call(bf16[64,3072]{1,0:T(8,128)(2,1)S(1)} %copy-done.11, bf16[64,3072]{1,0:T(8,128)(2,1)S(1)} %copy-done.31, bf16[64,3072]{1,0:T(8,128)(2,1)S(1)} %copy-done.37, bf16[64,3072]{1,0:T(8,128)(2,1)S(1)} %copy-done.43, ...), custom_call_target="tpu_custom_call" | custom-call | flops 32212254 | bytes 136314 | tf_op jit(solution)/shard_map/backward_matmul/pallas_call | solution.py:298
  251.7 1.6 collective-permute-start.51
  253.4 1.6 collective-permute-start.32
  255.0 2.0 collective-permute-done.39
  257.0 2.8 add_convert_fusion
  259.8 1.6 collective-permute-start.40
  272.7 2.7 collective-permute-done.34.refs_1_
  276.9 3.0 collective-permute-start.41
  279.8 9.4 %collective-permute-done.35.refs_8_.refs_1_ = bf16[64,1536]{1,0:T(8,128)(2,1)S(1)} collective-permute-done((bf16[64,1536]{1,0:T(8,128)(2,1)S(1)}, bf16[64,1536]{1,0:T(8,128)(2,1)S(1)}, u32[]{:S(2)}, u32[]{:S(2)}) %collective-permute-start.35) | collective-permute-done | bytes 196640 | tf_op jit(solution)/shard_map/ppermute | solution.py:41
  293.8 3.4 collective-permute-start.42
  297.2 6.6 %collective-permute-done.36 = bf16[128,1024]{1,0:T(8,128)(2,1)S(1)} collective-permute-done((bf16[128,1024]{1,0:T(8,128)(2,1)S(1)}, bf16[128,1024]{1,0:T(8,128)(2,1)S(1)}, u32[]{:S(2)}, u32[]{:S(2)}) %collective-permute-start.36) | collective-permute-done | bytes 262176 | tf_op jit(solution)/shard_map/ppermute | solution.py:41
  303.9 4.1 %collective-permute-done.37.refs_10_.refs_3_ = bf16[64,1536]{1,0:T(8,128)(2,1)S(1)} collective-permute-done((bf16[64,1536]{1,0:T(8,128)(2,1)S(1)}, bf16[64,1536]{1,0:T(8,128)(2,1)S(1)}, u32[]{:S(2)}, u32[]{:S(2)}) %collective-permute-start.37) | collective-permute-done | bytes 196640 | tf_op jit(solution)/shard_map/ppermute | solution.py:41
  308.0 2.0 collective-permute-start.38
  312.3 4.2 %collective-permute-done.38.refs_1_ = bf16[64,1024]{1,0:T(8,128)(2,1)S(1)} collective-permute-done((bf16[64,1024]{1,0:T(8,128)(2,1)S(1)}, bf16[64,1024]{1,0:T(8,128)(2,1)S(1)}, u32[]{:S(2)}, u32[]{:S(2)}) %collective-permute-start.38) | collective-permute-done | bytes 131104 | tf_op jit(solution)/shard_map/ppermute | solution.py:41
  317.6 2.2 copy-done.2
  319.8 1.6 adapter_products.2
  321.5 2.9 collective-permute-start.45
  324.4 2.2 collective-permute-done.44.refs_1_
  326.6 2.1 collective-permute-start.47
  330.1 3.6 %collective-permute-done.46.refs_3_ = bf16[80,1024]{1,0:T(8,128)(2,1)S(1)} collective-permute-done((bf16[80,1024]{1,0:T(8,128)(2,1)S(1)}, bf16[80,1024]{1,0:T(8,128)(2,1)S(1)}, u32[]{:S(2)}, u32[]{:S(2)}) %collective-permute-start.46) | collective-permute-done | bytes 163872 | tf_op jit(solution)/shard_map/ppermute | solution.py:41
  333.8 1.6 collective-permute-start.49
  337.9 4.0 %collective-permute-done.48.refs_3_ = bf16[64,1536]{1,0:T(8,128)(2,1)S(1)} collective-permute-done((bf16[64,1536]{1,0:T(8,128)(2,1)S(1)}, bf16[64,1536]{1,0:T(8,128)(2,1)S(1)}, u32[]{:S(2)}, u32[]{:S(2)}) %collective-permute-start.48) | collective-permute-done | bytes 196640 | tf_op jit(solution)/shard_map/ppermute | solution.py:41
  (286 shorter events, 56.9 us)
Async XLA Ops:
  0.7 51.7 %collective-permute-start = (bf16[256,4096]{1,0:T(8,128)(2,1)}, bf16[256,4096]{1,0:T(8,128)(2,1)}, u32[]{:S(2)}, u32[]{:S(2)}) collective-permute-start(bf16[256,4096]{1,0:T(8,128)(2,1)} %x_ref.1), channel_id=1, source_target_pairs={{0,16},{16,0},{1,17},{17,1},{2,18},{18,2},{3,19},{19,3},{4,20},{20... | collective-permute-start | bytes 6291464 | tf_op jit(solution)/shard_map/ppermute | solution.py:41
  38.6 2.5 collective-permute-start.2
  41.3 25.0 %collective-permute-start.4 = (bf16[64,3584]{1,0:T(8,128)(2,1)S(1)}, bf16[64,3584]{1,0:T(8,128)(2,1)S(1)}, u32[]{:S(2)}, u32[]{:S(2)}) collective-permute-start(bf16[64,3584]{1,0:T(8,128)(2,1)S(1)} %share_sums.6.refs_0_), channel_id=1, source_target_pairs={{0,2},{1,3},{2,0},{3,1},{4,6},{5,7},{6,4},{7,5},{8,10},{9,11},{10,... | collective-permute-start | bytes 1376264 | tf_op jit(solution)/shard_map/ppermute | solution.py:41
  42.2 10.1 %collective-permute-start.1 = (f32[256,2]{1,0:T(8,128)S(1)}, f32[256,2]{1,0:T(8,128)S(1)}, u32[]{:S(2)}, u32[]{:S(2)}) collective-permute-start(f32[256,2]{1,0:T(8,128)S(1)} %copy.69.stat_ref), channel_id=1, source_target_pairs={{0,16},{16,0},{1,17},{17,1},{2,18},{18,2},{3,19},{19,3},{4,20},{20... | collective-permute-start | bytes 6152 | tf_op jit(solution)/shard_map/ppermute | solution.py:41
  55.8 25.0 %copy-start = (bf16[512,4096]{1,0:T(8,128)(2,1)}, bf16[512,4096]{1,0:T(8,128)(2,1)S(1)}, u32[]{:S(2)}) copy-start(bf16[512,4096]{1,0:T(8,128)(2,1)S(1)} %get-tuple-element.54.x_ref.refs_1_) | copy-start | bytes 12582916
  55.8 10.5 %collective-permute-start.3 = (f32[2,128,32]{2,1,0:T(8,128)S(1)}, f32[2,128,32]{2,1,0:T(8,128)S(1)}, u32[]{:S(2)}, u32[]{:S(2)}) collective-permute-start(f32[2,128,32]{2,1,0:T(8,128)S(1)} %pad_maximum_fusion), channel_id=1, source_target_pairs={{0,1},{1,0},{2,3},{3,2},{4,5},{5,4},{6,7},{7,6},{8,9},{9,8},{10,11... | collective-permute-start | bytes 98312 | tf_op jit(solution)/shard_map/ppermute | solution.py:41
  74.1 4.6 %collective-permute-start.5 = (bf16[128,3584]{1,0:T(8,128)(2,1)S(1)}, bf16[128,3584]{1,0:T(8,128)(2,1)S(1)}, u32[]{:S(2)}, u32[]{:S(2)}) collective-permute-start(bf16[128,3584]{1,0:T(8,128)(2,1)S(1)} %get-tuple-element.61), channel_id=1, source_target_pairs={{0,1},{1,0},{2,3},{3,2},{4,5},{5,4},{6,7},{7,6},{8,9},{9,8},{10,11... | collective-permute-start | bytes 2752520 | tf_op jit(solution)/shard_map/ppermute | solution.py:41
  74.1 4.5 %collective-permute-start.6 = (f32[2,64,32]{2,1,0:T(8,128)S(1)}, f32[2,64,32]{2,1,0:T(8,128)S(1)}, u32[]{:S(2)}, u32[]{:S(2)}) collective-permute-start(f32[2,64,32]{2,1,0:T(8,128)S(1)} %slice.68), channel_id=1, source_target_pairs={{0,2},{1,3},{2,0},{3,1},{4,6},{5,7},{6,4},{7,5},{8,10},{9,11},{10,... | collective-permute-start | bytes 49160 | tf_op jit(solution)/shard_map/ppermute | solution.py:41
  79.0 12.2 %collective-permute-start.7 = (bf16[64,3584]{1,0:T(8,128)(2,1)S(1)}, bf16[64,3584]{1,0:T(8,128)(2,1)S(1)}, u32[]{:S(2)}, u32[]{:S(2)}) collective-permute-start(bf16[64,3584]{1,0:T(8,128)(2,1)S(1)} %share_sums.7.refs_0_), channel_id=1, source_target_pairs={{0,2},{1,3},{2,0},{3,1},{4,6},{5,7},{6,4},{7,5},{8,10},{9,11},{10,... | collective-permute-start | bytes 1376264 | tf_op jit(solution)/shard_map/ppermute | solution.py:41
  92.2 15.8 %collective-permute-start.8 = (bf16[64,3584]{1,0:T(8,128)(2,1)}, bf16[64,3584]{1,0:T(8,128)(2,1)}, u32[]{:S(2)}, u32[]{:S(2)}) collective-permute-start(bf16[64,3584]{1,0:T(8,128)(2,1)} %share_sums.8.refs_3_), channel_id=1, source_target_pairs={{0,16},{16,0},{1,17},{17,1},{2,18},{18,2},{3,19},{19,3},{4,20},{20... | collective-permute-start | bytes 1376264 | tf_op jit(solution)/shard_map/ppermute | solution.py:41
  111.0 76.6 %copy-start.16 = (bf16[64,3584]{1,0:T(8,128)(2,1)}, bf16[64,3584]{1,0:T(8,128)(2,1)S(1)}, u32[]{:S(2)}) copy-start(bf16[64,3584]{1,0:T(8,128)(2,1)S(1)} %get-tuple-element.69.refs_0_.refs_1_) | copy-start | bytes 1376260
  111.0 11.0 %collective-permute-start.10 = (bf16[64,3584]{1,0:T(8,128)(2,1)S(1)}, bf16[64,3584]{1,0:T(8,128)(2,1)S(1)}, u32[]{:S(2)}, u32[]{:S(2)}) collective-permute-start(bf16[64,3584]{1,0:T(8,128)(2,1)S(1)} %get-tuple-element.69.refs_0_.refs_1_), channel_id=1, source_target_pairs={{0,2},{1,3},{2,0},{3,1},{4,6},{5,7},{6,4},{7,5},{8,10},{9,11},{10,... | collective-permute-start | bytes 1376264 | tf_op jit(solution)/shard_map/ppermute | solution.py:41
  112.6 10.6 %collective-permute-start.9 = (bf16[64,3584]{1,0:T(8,128)(2,1)S(1)}, bf16[64,3584]{1,0:T(8,128)(2,1)S(1)}, u32[]{:S(2)}, u32[]{:S(2)}) collective-permute-start(bf16[64,3584]{1,0:T(8,128)(2,1)S(1)} %get-tuple-element.68), channel_id=1, source_target_pairs={{0,16},{16,0},{1,17},{17,1},{2,18},{18,2},{3,19},{19,3},{4,20},{20... | collective-permute-start | bytes 1376264 | tf_op jit(solution)/shard_map/ppermute | solution.py:41
  122.0 65.7 %copy-start.6 = (bf16[64,3584]{1,0:T(8,128)(2,1)}, bf16[64,3584]{1,0:T(8,128)(2,1)S(1)}, u32[]{:S(2)}) copy-start(bf16[64,3584]{1,0:T(8,128)(2,1)S(1)} %collective-permute-done.10.refs_3_.refs_1_.refs_2_) | copy-start | bytes 1376260
  123.2 64.4 %copy-start.8 = (bf16[64,3584]{1,0:T(8,128)(2,1)}, bf16[64,3584]{1,0:T(8,128)(2,1)S(1)}, u32[]{:S(2)}) copy-start(bf16[64,3584]{1,0:T(8,128)(2,1)S(1)} %collective-permute-done.9.refs_2_.refs_4_.refs_5_) | copy-start | bytes 1376260
  129.5 12.9 %collective-permute-start.11 = (bf16[256,3072]{1,0:T(8,128)(2,1)}, bf16[256,3072]{1,0:T(8,128)(2,1)S(1)}, u32[]{:S(2)}, u32[]{:S(2)}) collective-permute-start(bf16[256,3072]{1,0:T(8,128)(2,1)} %copy-done.51), channel_id=1, source_target_pairs={{0,1},{1,0},{2,3},{3,2},{4,5},{5,4},{6,7},{7,6},{8,9},{9,8},{10,11... | collective-permute-start | bytes 4718600 | tf_op jit(solution)/shard_map/ppermute | solution.py:41
  129.5 12.9 %collective-permute-start.16 = (bf16[64,3584]{1,0:T(8,128)(2,1)S(1)}, bf16[64,3584]{1,0:T(8,128)(2,1)S(1)}, u32[]{:S(2)}, u32[]{:S(2)}) collective-permute-start(bf16[64,3584]{1,0:T(8,128)(2,1)S(1)} %collective-permute-done.9.refs_2_.refs_4_.refs_5_), channel_id=1, source_target_pairs={{0,2},{1,3},{2,0},{3,1},{4,6},{5,7},{6,4},{7,5},{8,10},{9,11},{10,... | collective-permute-start | bytes 1376264 | tf_op jit(solution)/shard_map/ppermute | solution.py:41
  130.0 13.4 %collective-permute-start.14 = (bf16[64,3584]{1,0:T(8,128)(2,1)S(1)}, bf16[64,3584]{1,0:T(8,128)(2,1)S(1)}, u32[]{:S(2)}, u32[]{:S(2)}) collective-permute-start(bf16[64,3584]{1,0:T(8,128)(2,1)S(1)} %get-tuple-element.69.refs_0_.refs_1_), channel_id=1, source_target_pairs={{0,1},{1,0},{2,3},{3,2},{4,5},{5,4},{6,7},{7,6},{8,9},{9,8},{10,11... | collective-permute-start | bytes 1376264 | tf_op jit(solution)/shard_map/ppermute | solution.py:41
  130.3 14.7 %collective-permute-start.15 = (bf16[64,3584]{1,0:T(8,128)(2,1)S(1)}, bf16[64,3584]{1,0:T(8,128)(2,1)S(1)}, u32[]{:S(2)}, u32[]{:S(2)}) collective-permute-start(bf16[64,3584]{1,0:T(8,128)(2,1)S(1)} %collective-permute-done.10.refs_3_.refs_1_.refs_2_), channel_id=1, source_target_pairs={{0,1},{1,0},{2,3},{3,2},{4,5},{5,4},{6,7},{7,6},{8,9},{9,8},{10,11... | collective-permute-start | bytes 1376264 | tf_op jit(solution)/shard_map/ppermute | solution.py:41
  130.6 14.5 %collective-permute-start.17 = (bf16[64,3584]{1,0:T(8,128)(2,1)S(1)}, bf16[64,3584]{1,0:T(8,128)(2,1)S(1)}, u32[]{:S(2)}, u32[]{:S(2)}) collective-permute-start(bf16[64,3584]{1,0:T(8,128)(2,1)S(1)} %collective-permute-done.9.refs_2_.refs_4_.refs_5_), channel_id=1, source_target_pairs={{0,1},{1,0},{2,3},{3,2},{4,5},{5,4},{6,7},{7,6},{8,9},{9,8},{10,11... | collective-permute-start | bytes 1376264 | tf_op jit(solution)/shard_map/ppermute | solution.py:41
  142.5 45.2 %copy-start.18 = (bf16[64,3584]{1,0:T(8,128)(2,1)}, bf16[64,3584]{1,0:T(8,128)(2,1)S(1)}, u32[]{:S(2)}) copy-start(bf16[64,3584]{1,0:T(8,128)(2,1)S(1)} %collective-permute-done.16.refs_5_.refs_6_) | copy-start | bytes 1376260
  142.5 2.5 collective-permute-start.18
  142.9 12.0 %collective-permute-start.13 = (bf16[64,3072]{1,0:T(8,128)(2,1)S(1)}, bf16[64,3072]{1,0:T(8,128)(2,1)S(1)}, u32[]{:S(2)}, u32[]{:S(2)}) collective-permute-start(bf16[64,3072]{1,0:T(8,128)(2,1)S(1)} %get-tuple-element.73), channel_id=1, source_target_pairs={{0,2},{1,3},{2,0},{3,1},{4,6},{5,7},{6,4},{7,5},{8,10},{9,11},{10,... | collective-permute-start | bytes 1179656 | tf_op jit(solution)/shard_map/ppermute | solution.py:41
  143.5 44.2 %copy-start.20 = (bf16[64,3584]{1,0:T(8,128)(2,1)}, bf16[64,3584]{1,0:T(8,128)(2,1)S(1)}, u32[]{:S(2)}) copy-start(bf16[64,3584]{1,0:T(8,128)(2,1)S(1)} %collective-permute-done.14.refs_2_.refs_3_) | copy-start | bytes 1376260
  143.5 19.4 %collective-permute-start.12 = (bf16[64,3072]{1,0:T(8,128)(2,1)S(1)}, bf16[64,3072]{1,0:T(8,128)(2,1)S(1)}, u32[]{:S(2)}, u32[]{:S(2)}) collective-permute-start(bf16[64,3072]{1,0:T(8,128)(2,1)S(1)} %get-tuple-element.72.refs_9_), channel_id=1, source_target_pairs={{0,2},{1,3},{2,0},{3,1},{4,6},{5,7},{6,4},{7,5},{8,10},{9,11},{10,... | collective-permute-start | bytes 1179656 | tf_op jit(solution)/shard_map/ppermute | solution.py:41
  145.0 42.7 %copy-start.22 = (bf16[64,3584]{1,0:T(8,128)(2,1)}, bf16[64,3584]{1,0:T(8,128)(2,1)S(1)}, u32[]{:S(2)}) copy-start(bf16[64,3584]{1,0:T(8,128)(2,1)S(1)} %collective-permute-done.15.refs_3_.refs_4_) | copy-start | bytes 1376260
  145.0 42.7 %copy-start.24 = (bf16[64,3584]{1,0:T(8,128)(2,1)}, bf16[64,3584]{1,0:T(8,128)(2,1)S(1)}, u32[]{:S(2)}) copy-start(bf16[64,3584]{1,0:T(8,128)(2,1)S(1)} %collective-permute-done.17.refs_6_.refs_7_) | copy-start | bytes 1376260
  145.0 42.7 %copy-start.26 = (bf16[64,3584]{1,0:T(8,128)(2,1)}, bf16[64,3584]{1,0:T(8,128)(2,1)S(1)}, u32[]{:S(2)}) copy-start(bf16[64,3584]{1,0:T(8,128)(2,1)S(1)} %collective-permute-done.18.refs_7_.refs_8_) | copy-start | bytes 1376260
  155.2 10.4 %collective-permute-start.19 = (bf16[64,3072]{1,0:T(8,128)(2,1)S(1)}, bf16[64,3072]{1,0:T(8,128)(2,1)S(1)}, u32[]{:S(2)}, u32[]{:S(2)}) collective-permute-start(bf16[64,3072]{1,0:T(8,128)(2,1)S(1)} %share_sums.10), channel_id=1, source_target_pairs={{0,16},{16,0},{1,17},{17,1},{2,18},{18,2},{3,19},{19,3},{4,20},{20... | collective-permute-start | bytes 1179656 | tf_op jit(solution)/shard_map/ppermute | solution.py:41
  168.9 34.4 %copy-start.10 = (bf16[64,3072]{1,0:T(8,128)(2,1)}, bf16[64,3072]{1,0:T(8,128)(2,1)S(1)}, u32[]{:S(2)}) copy-start(bf16[64,3072]{1,0:T(8,128)(2,1)S(1)} %get-tuple-element.74.refs_9_.refs_0_) | copy-start | bytes 1179652
  168.9 9.6 %collective-permute-start.23 = (bf16[64,3072]{1,0:T(8,128)(2,1)S(1)}, bf16[64,3072]{1,0:T(8,128)(2,1)S(1)}, u32[]{:S(2)}, u32[]{:S(2)}) collective-permute-start(bf16[64,3072]{1,0:T(8,128)(2,1)S(1)} %get-tuple-element.75), channel_id=1, source_target_pairs={{0,16},{16,0},{1,17},{17,1},{2,18},{18,2},{3,19},{19,3},{4,20},{20... | collective-permute-start | bytes 1179656 | tf_op jit(solution)/shard_map/ppermute | solution.py:41
  169.5 11.3 %collective-permute-start.20 = (bf16[64,3072]{1,0:T(8,128)(2,1)S(1)}, bf16[64,3072]{1,0:T(8,128)(2,1)S(1)}, u32[]{:S(2)}, u32[]{:S(2)}) collective-permute-start(bf16[64,3072]{1,0:T(8,128)(2,1)S(1)} %get-tuple-element.74.refs_9_.refs_0_), channel_id=1, source_target_pairs={{0,2},{1,3},{2,0},{3,1},{4,6},{5,7},{6,4},{7,5},{8,10},{9,11},{10,... | collective-permute-start | bytes 1179656 | tf_op jit(solution)/shard_map/ppermute | solution.py:41
  178.7 8.9 %collective-permute-start.24 = (bf16[64,3072]{1,0:T(8,128)(2,1)S(1)}, bf16[64,3072]{1,0:T(8,128)(2,1)S(1)}, u32[]{:S(2)}, u32[]{:S(2)}) collective-permute-start(bf16[64,3072]{1,0:T(8,128)(2,1)S(1)} %share_sums.11.refs_9_.refs_4_.refs_13_), channel_id=1, source_target_pairs={{0,2},{1,3},{2,0},{3,1},{4,6},{5,7},{6,4},{7,5},{8,10},{9,11},{10,... | collective-permute-start | bytes 1179656 | tf_op jit(solution)/shard_map/ppermute | solution.py:41
  180.3 13.8 %collective-permute-start.21 = (bf16[64,3072]{1,0:T(8,128)(2,1)S(1)}, bf16[64,3072]{1,0:T(8,128)(2,1)S(1)}, u32[]{:S(2)}, u32[]{:S(2)}) collective-permute-start(bf16[64,3072]{1,0:T(8,128)(2,1)S(1)} %get-tuple-element.74.refs_9_.refs_0_), channel_id=1, source_target_pairs={{0,1},{1,0},{2,3},{3,2},{4,5},{5,4},{6,7},{7,6},{8,9},{9,8},{10,11... | collective-permute-start | bytes 1179656 | tf_op jit(solution)/shard_map/ppermute | solution.py:41
  180.3 13.8 %collective-permute-start.25 = (bf16[64,3072]{1,0:T(8,128)(2,1)S(1)}, bf16[64,3072]{1,0:T(8,128)(2,1)S(1)}, u32[]{:S(2)}, u32[]{:S(2)}) collective-permute-start(bf16[64,3072]{1,0:T(8,128)(2,1)S(1)} %share_sums.11.refs_9_.refs_4_.refs_13_), channel_id=1, source_target_pairs={{0,1},{1,0},{2,3},{3,2},{4,5},{5,4},{6,7},{7,6},{8,9},{9,8},{10,11... | collective-permute-start | bytes 1179656 | tf_op jit(solution)/shard_map/ppermute | solution.py:41
  180.8 13.3 %collective-permute-start.22 = (bf16[64,3072]{1,0:T(8,128)(2,1)S(1)}, bf16[64,3072]{1,0:T(8,128)(2,1)S(1)}, u32[]{:S(2)}, u32[]{:S(2)}) collective-permute-start(bf16[64,3072]{1,0:T(8,128)(2,1)S(1)} %collective-permute-done.20.refs_1_.refs_10_), channel_id=1, source_target_pairs={{0,1},{1,0},{2,3},{3,2},{4,5},{5,4},{6,7},{7,6},{8,9},{9,8},{10,11... | collective-permute-start | bytes 1179656 | tf_op jit(solution)/shard_map/ppermute | solution.py:41
  187.6 6.6 %collective-permute-start.26 = (bf16[64,3072]{1,0:T(8,128)(2,1)S(1)}, bf16[64,3072]{1,0:T(8,128)(2,1)S(1)}, u32[]{:S(2)}, u32[]{:S(2)}) collective-permute-start(bf16[64,3072]{1,0:T(8,128)(2,1)S(1)} %collective-permute-done.24.refs_5_.refs_14_), channel_id=1, source_target_pairs={{0,1},{1,0},{2,3},{3,2},{4,5},{5,4},{6,7},{7,6},{8,9},{9,8},{10,11... | collective-permute-start | bytes 1179656 | tf_op jit(solution)/shard_map/ppermute | solution.py:41
  212.7 3.9 %collective-permute-start.28 = (f32[64,33]{1,0:T(8,128)S(1)}, f32[64,33]{1,0:T(8,128)S(1)}, u32[]{:S(2)}, u32[]{:S(2)}) collective-permute-start(f32[64,33]{1,0:T(8,128)S(1)} %relay.3), channel_id=1, source_target_pairs={{0,4},{4,0},{8,12},{12,8},{1,5},{5,1},{9,13},{13,9},{2,6},{6,2},{1... | collective-permute-start | bytes 25352 | tf_op jit(solution)/shard_map/ppermute | solution.py:41
  216.7 4.9 %collective-permute-start.29 = (f32[64,33]{1,0:T(8,128)S(1)}, f32[64,33]{1,0:T(8,128)S(1)}, u32[]{:S(2)}, u32[]{:S(2)}) collective-permute-start(f32[64,33]{1,0:T(8,128)S(1)} %add.226), channel_id=1, source_target_pairs={{0,8},{4,12},{8,0},{12,4},{1,9},{5,13},{9,1},{13,5},{2,10},{6,14},... | collective-permute-start | bytes 25352 | tf_op jit(solution)/shard_map/ppermute | solution.py:41
  219.4 20.8 %collective-permute-start.27 = (bf16[256,1536]{1,0:T(8,128)(2,1)}, bf16[256,1536]{1,0:T(8,128)(2,1)}, u32[]{:S(2)}, u32[]{:S(2)}) collective-permute-start(bf16[256,1536]{1,0:T(8,128)(2,1)} %copy-done.70), channel_id=1, source_target_pairs={{0,16},{16,0},{1,17},{17,1},{2,18},{18,2},{3,19},{19,3},{4,20},{20... | collective-permute-start | bytes 2359304 | tf_op jit(solution)/shard_map/ppermute | solution.py:41
  221.5 3.9 %collective-permute-start.30 = (f32[64,33]{1,0:T(8,128)S(1)}, f32[64,33]{1,0:T(8,128)S(1)}, u32[]{:S(2)}, u32[]{:S(2)}) collective-permute-start(f32[64,33]{1,0:T(8,128)S(1)} %add.227), channel_id=1, source_target_pairs={{0,2},{1,3},{2,0},{3,1},{4,6},{5,7},{6,4},{7,5},{8,10},{9,11},{10,... | collective-permute-start | bytes 25352 | tf_op jit(solution)/shard_map/ppermute | solution.py:41
  225.5 2.4 collective-permute-start.31
  226.3 30.7 %collective-permute-start.39 = (bf16[256,1536]{1,0:T(8,128)(2,1)}, bf16[256,1536]{1,0:T(8,128)(2,1)}, u32[]{:S(2)}, u32[]{:S(2)}) collective-permute-start(bf16[256,1536]{1,0:T(8,128)(2,1)} %copy-done.69), channel_id=1, source_target_pairs={{0,16},{16,0},{1,17},{17,1},{2,18},{18,2},{3,19},{19,3},{4,20},{20... | collective-permute-start | bytes 2359304 | tf_op jit(solution)/shard_map/ppermute | solution.py:41
  242.9 18.7 %collective-permute-start.33 = (bf16[128,1536]{1,0:T(8,128)(2,1)}, bf16[128,1536]{1,0:T(8,128)(2,1)}, u32[]{:S(2)}, u32[]{:S(2)}) collective-permute-start(bf16[128,1536]{1,0:T(8,128)(2,1)} %get-tuple-element.101.refs_11_), channel_id=1, source_target_pairs={{0,4},{4,0},{8,12},{12,8},{1,5},{5,1},{9,13},{13,9},{2,6},{6,2},{1... | collective-permute-start | bytes 1179656 | tf_op jit(solution)/shard_map/ppermute | solution.py:41
  251.7 9.7 %collective-permute-start.51 = (bf16[2,64,16]{2,1,0:T(8,128)(2,1)S(1)}, bf16[2,64,16]{2,1,0:T(8,128)(2,1)S(1)}, u32[]{:S(2)}, u32[]{:S(2)}) collective-permute-start(bf16[2,64,16]{2,1,0:T(8,128)(2,1)S(1)} %slice_select_fusion), channel_id=1, source_target_pairs={{0,2},{1,3},{2,0},{3,1},{4,6},{5,7},{6,4},{7,5},{8,10},{9,11},{10,... | collective-permute-start | bytes 12296 | tf_op jit(solution)/shard_map/ppermute | solution.py:41
  253.4 26.4 %collective-permute-start.32 = (bf16[256,1024]{1,0:T(8,128)(2,1)}, bf16[256,1024]{1,0:T(8,128)(2,1)}, u32[]{:S(2)}, u32[]{:S(2)}) collective-permute-start(bf16[256,1024]{1,0:T(8,128)(2,1)} %copy-done.71), channel_id=1, source_target_pairs={{0,16},{16,0},{1,17},{17,1},{2,18},{18,2},{3,19},{19,3},{4,20},{20... | collective-permute-start | bytes 1572872 | tf_op jit(solution)/shard_map/ppermute | solution.py:41
  259.8 15.9 %collective-permute-start.40 = (bf16[128,1536]{1,0:T(8,128)(2,1)}, bf16[128,1536]{1,0:T(8,128)(2,1)}, u32[]{:S(2)}, u32[]{:S(2)}) collective-permute-start(bf16[128,1536]{1,0:T(8,128)(2,1)} %get-tuple-element.98), channel_id=1, source_target_pairs={{0,4},{4,0},{8,12},{12,8},{1,5},{5,1},{9,13},{13,9},{2,6},{6,2},{1... | collective-permute-start | bytes 1179656 | tf_op jit(solution)/shard_map/ppermute | solution.py:41
  261.6 1.9 collective-permute-start.52
  263.0 12.3 %collective-permute-start.34 = (bf16[64,1536]{1,0:T(8,128)(2,1)S(1)}, bf16[64,1536]{1,0:T(8,128)(2,1)S(1)}, u32[]{:S(2)}, u32[]{:S(2)}) collective-permute-start(bf16[64,1536]{1,0:T(8,128)(2,1)S(1)} %get-tuple-element.106), channel_id=1, source_target_pairs={{0,8},{4,12},{8,0},{12,4},{1,9},{5,13},{9,1},{13,5},{2,10},{6,14},... | collective-permute-start | bytes 589832 | tf_op jit(solution)/shard_map/ppermute | solution.py:41
  275.7 13.5 %collective-permute-start.35 = (bf16[64,1536]{1,0:T(8,128)(2,1)S(1)}, bf16[64,1536]{1,0:T(8,128)(2,1)S(1)}, u32[]{:S(2)}, u32[]{:S(2)}) collective-permute-start(bf16[64,1536]{1,0:T(8,128)(2,1)S(1)} %get-tuple-element.83.refs_0_), channel_id=1, source_target_pairs={{0,8},{4,12},{8,0},{12,4},{1,9},{5,13},{9,1},{13,5},{2,10},{6,14},... | collective-permute-start | bytes 589832 | tf_op jit(solution)/shard_map/ppermute | solution.py:41
  276.9 16.6 %collective-permute-start.41 = (bf16[64,1536]{1,0:T(8,128)(2,1)S(1)}, bf16[64,1536]{1,0:T(8,128)(2,1)S(1)}, u32[]{:S(2)}, u32[]{:S(2)}) collective-permute-start(bf16[64,1536]{1,0:T(8,128)(2,1)S(1)} %get-tuple-element.104), channel_id=1, source_target_pairs={{0,8},{4,12},{8,0},{12,4},{1,9},{5,13},{9,1},{13,5},{2,10},{6,14},... | collective-permute-start | bytes 589832 | tf_op jit(solution)/shard_map/ppermute | solution.py:41
  290.4 13.5 %collective-permute-start.36 = (bf16[128,1024]{1,0:T(8,128)(2,1)S(1)}, bf16[128,1024]{1,0:T(8,128)(2,1)S(1)}, u32[]{:S(2)}, u32[]{:S(2)}) collective-permute-start(bf16[128,1024]{1,0:T(8,128)(2,1)S(1)} %get-tuple-element.102), channel_id=1, source_target_pairs={{0,4},{4,0},{8,12},{12,8},{1,5},{5,1},{9,13},{13,9},{2,6},{6,2},{1... | collective-permute-start | bytes 786440 | tf_op jit(solution)/shard_map/ppermute | solution.py:41
  291.4 16.6 %collective-permute-start.37 = (bf16[64,1536]{1,0:T(8,128)(2,1)S(1)}, bf16[64,1536]{1,0:T(8,128)(2,1)S(1)}, u32[]{:S(2)}, u32[]{:S(2)}) collective-permute-start(bf16[64,1536]{1,0:T(8,128)(2,1)S(1)} %collective-permute-done.35.refs_8_.refs_1_), channel_id=1, source_target_pairs={{0,4},{4,0},{8,12},{12,8},{1,5},{5,1},{9,13},{13,9},{2,6},{6,2},{1... | collective-permute-start | bytes 589832 | tf_op jit(solution)/shard_map/ppermute | solution.py:41
  292.5 19.8 %collective-permute-start.43 = (bf16[64,1536]{1,0:T(8,128)(2,1)S(1)}, bf16[64,1536]{1,0:T(8,128)(2,1)S(1)}, u32[]{:S(2)}, u32[]{:S(2)}) collective-permute-start(bf16[64,1536]{1,0:T(8,128)(2,1)S(1)} %get-tuple-element.83.refs_0_), channel_id=1, source_target_pairs={{0,4},{4,0},{8,12},{12,8},{1,5},{5,1},{9,13},{13,9},{2,6},{6,2},{1... | collective-permute-start | bytes 589832 | tf_op jit(solution)/shard_map/ppermute | solution.py:41
  293.8 18.5 %collective-permute-start.42 = (bf16[64,1536]{1,0:T(8,128)(2,1)S(1)}, bf16[64,1536]{1,0:T(8,128)(2,1)S(1)}, u32[]{:S(2)}, u32[]{:S(2)}) collective-permute-start(bf16[64,1536]{1,0:T(8,128)(2,1)S(1)} %get-tuple-element.88.refs_0_), channel_id=1, source_target_pairs={{0,8},{4,12},{8,0},{12,4},{1,9},{5,13},{9,1},{13,5},{2,10},{6,14},... | collective-permute-start | bytes 589832 | tf_op jit(solution)/shard_map/ppermute | solution.py:41
  308.0 8.5 %collective-permute-start.38 = (bf16[64,1024]{1,0:T(8,128)(2,1)S(1)}, bf16[64,1024]{1,0:T(8,128)(2,1)S(1)}, u32[]{:S(2)}, u32[]{:S(2)}) collective-permute-start(bf16[64,1024]{1,0:T(8,128)(2,1)S(1)} %get-tuple-element.85), channel_id=1, source_target_pairs={{0,8},{4,12},{8,0},{12,4},{1,9},{5,13},{9,1},{13,5},{2,10},{6,14},... | collective-permute-start | bytes 393224 | tf_op jit(solution)/shard_map/ppermute | solution.py:41
  310.1 16.5 %collective-permute-start.53 = (bf16[16,6656]{1,0:T(8,128)(2,1)S(1)}, bf16[16,6656]{1,0:T(8,128)(2,1)S(1)}, u32[]{:S(2)}, u32[]{:S(2)}) collective-permute-start(bf16[16,6656]{1,0:T(8,128)(2,1)S(1)} %convert_element_type.126), channel_id=1, source_target_pairs={{0,16},{16,0},{1,17},{17,1},{2,18},{18,2},{3,19},{19,3},{4,20},{20... | collective-permute-start | bytes 638984 | tf_op jit(solution)/shard_map/ppermute | solution.py:41
  311.6 5.6 %collective-permute-start.50 = (bf16[256,32]{1,0:T(8,128)(2,1)S(1)}, bf16[256,32]{1,0:T(8,128)(2,1)S(1)}, u32[]{:S(2)}, u32[]{:S(2)}) collective-permute-start(bf16[256,32]{1,0:T(8,128)(2,1)S(1)} %relay.4), channel_id=1, source_target_pairs={{0,16},{16,0},{1,17},{17,1},{2,18},{18,2},{3,19},{19,3},{4,20},{20... | collective-permute-start | bytes 49160 | tf_op jit(solution)/shard_map/ppermute | solution.py:41
  316.9 9.7 %collective-permute-start.44 = (bf16[80,1024]{1,0:T(8,128)(2,1)S(1)}, bf16[80,1024]{1,0:T(8,128)(2,1)S(1)}, u32[]{:S(2)}, u32[]{:S(2)}) collective-permute-start(bf16[80,1024]{1,0:T(8,128)(2,1)S(1)} %maximum_maximum_fusion.refs_0_), channel_id=1, source_target_pairs={{0,8},{4,12},{8,0},{12,4},{1,9},{5,13},{9,1},{13,5},{2,10},{6,14},... | collective-permute-start | bytes 491528 | tf_op jit(solution)/shard_map/ppermute | solution.py:41
  321.5 8.6 %collective-permute-start.45 = (bf16[80,1024]{1,0:T(8,128)(2,1)S(1)}, bf16[80,1024]{1,0:T(8,128)(2,1)S(1)}, u32[]{:S(2)}, u32[]{:S(2)}) collective-permute-start(bf16[80,1024]{1,0:T(8,128)(2,1)S(1)} %maximum_maximum_fusion.refs_0_), channel_id=1, source_target_pairs={{0,4},{4,0},{8,12},{12,8},{1,5},{5,1},{9,13},{13,9},{2,6},{6,2},{1... | collective-permute-start | bytes 491528 | tf_op jit(solution)/shard_map/ppermute | solution.py:41
  326.6 7.1 %collective-permute-start.46 = (bf16[80,1024]{1,0:T(8,128)(2,1)S(1)}, bf16[80,1024]{1,0:T(8,128)(2,1)S(1)}, u32[]{:S(2)}, u32[]{:S(2)}) collective-permute-start(bf16[80,1024]{1,0:T(8,128)(2,1)S(1)} %collective-permute-done.44.refs_1_), channel_id=1, source_target_pairs={{0,4},{4,0},{8,12},{12,8},{1,5},{5,1},{9,13},{13,9},{2,6},{6,2},{1... | collective-permute-start | bytes 491528 | tf_op jit(solution)/shard_map/ppermute | solution.py:41
  326.6 11.3 %collective-permute-start.47 = (bf16[64,1536]{1,0:T(8,128)(2,1)S(1)}, bf16[64,1536]{1,0:T(8,128)(2,1)S(1)}, u32[]{:S(2)}, u32[]{:S(2)}) collective-permute-start(bf16[64,1536]{1,0:T(8,128)(2,1)S(1)} %get-tuple-element.88.refs_0_), channel_id=1, source_target_pairs={{0,4},{4,0},{8,12},{12,8},{1,5},{5,1},{9,13},{13,9},{2,6},{6,2},{1... | collective-permute-start | bytes 589832 | tf_op jit(solution)/shard_map/ppermute | solution.py:41
  328.7 13.2 %collective-permute-start.48 = (bf16[64,1536]{1,0:T(8,128)(2,1)S(1)}, bf16[64,1536]{1,0:T(8,128)(2,1)S(1)}, u32[]{:S(2)}, u32[]{:S(2)}) collective-permute-start(bf16[64,1536]{1,0:T(8,128)(2,1)S(1)} %collective-permute-done.42.refs_8_.refs_1_), channel_id=1, source_target_pairs={{0,4},{4,0},{8,12},{12,8},{1,5},{5,1},{9,13},{13,9},{2,6},{6,2},{1... | collective-permute-start | bytes 589832 | tf_op jit(solution)/shard_map/ppermute | solution.py:41
  333.8 11.0 %collective-permute-start.49 = (f32[4,1024]{1,0:T(4,128)S(1)}, f32[4,1024]{1,0:T(4,128)S(1)}, u32[]{:S(2)}, u32[]{:S(2)}) collective-permute-start(f32[4,1024]{1,0:T(4,128)S(1)} %fusion.10), channel_id=1, source_target_pairs={{0,16},{16,0},{1,17},{17,1},{2,18},{18,2},{3,19},{19,3},{4,20},{20... | collective-permute-start | bytes 49160 | tf_op jit(solution)/shard_map/ppermute | solution.py:41
  (66 other events, 542.9 us)

commit v10 on v9

--- a/solution.py
+++ b/solution.py
@@ -553,27 +553,24 @@
             ]
             return total_of(sides[0], 0, half), total_of(sides[1], 0, half).astype(BF16)
 
-        first_steps = []
+        begun = []
         for j, ((first, n), base) in enumerate(zip(steps, bases)):
             wait = (products[-1],) if products else tuple(bases)
             if j == 2:
-                back = relay(back, (products[1],))
-                for bit in range(bits_of(ffn)):
-                    back = back + swap(back, "ffn", ffn, 1 << bit)
-                back = double(back, "hid", hid)
-                first_steps.append(halving_step([products[0], received[0]], 0))
-                wait += (first_steps[0][1], back)
+                keep, send = halving_step([products[0], relay(received[0], (products[1],))], 0)
+                begun = [keep, swap(send, "ffn", ffn, 1)]
+                wait += (send,)
             keep, send = backward_matmul(
                 grads[1], weights, chunks[1][0] * tile, first, n, width_tile, base=base, base_first=first,
                 after=wait,
             )
             products.append(keep)
             received.append(swap(send, "dp", dp, 1))
-        if len(steps) < 3:
-            for bit in range(bits_of(ffn)):
-                back = back + swap(back, "ffn", ffn, 1 << bit)
-            back = double(back, "hid", hid)
-        low = relay(low, (products[-1],))
+        back = relay(back, (products[-1], *begun[1:]))
+        for bit in range(bits_of(ffn)):
+            back = back + swap(back, "ffn", ffn, 1 << bit)
+        back = double(back, "hid", hid)
+        low = relay(low, (products[-1], received[-1]))
         low_mine = jnp.where(first_pair, low[:, :, :rank], low[:, :, rank:])
         low_mine = double(low_mine, "hid", hid, dim=1).reshape(2 * tokens, rank).T
         back_low = back[:, : 2 * rank].astype(BF16)
@@ -612,10 +609,10 @@
                 got = ordered(got, gathered[j - 2][1])
             parts = [products[j], got]
             for bit in range(bits_of(ffn)):
-                if bit == 0 and j < len(first_steps):
-                    keep, send = first_steps[j]
-                else:
-                    keep, send = halving_step(parts, bit)
+                if j == 0 and bit == 0 and begun:
+                    parts = begun
+                    continue
+                keep, send = halving_step(parts, bit)
                 if j == 2 and bit == 1:
                     send = ordered(send, gathered[0][-1])
                 parts = [keep, swap(send, "ffn", ffn, 1 << bit)]

time: 347 us -> 354 us (1.020)
  local copies, waits for them, and re-layouts: 23.2 us -> 47.4 us
  waiting for transfers between devices: 112 us -> 94.9 us
  starting transfers between devices: 55.5 us -> 48.9 us
  Pallas kernels: 122 us -> 127 us
    unnamed x154 -> x204, local copies, waits for them, and re-layouts: 19.9 us -> 39.2 us
    ppermute x54, waiting for transfers between devices: 112 us -> 94.9 us  [swap(): return lax.ppermute(x, axis, [(i, i ^ mask) for i in range(n)])]
    ppermute x54, starting transfers between devices: 55.5 us -> 48.9 us  [swap(): return lax.ppermute(x, axis, [(i, i ^ mask) for i in range(n)])]
  transfers between devices with their start and end apart: 54 -> 54, of which waited for: 26 -> 28; matrix products, arithmetic and copies ran while one was open for 6% -> 7% of each run, Pallas kernels for 25% -> 27%
where the time goes in v10:
time: 354 us; the launch traced here: 352 us
  Pallas kernels  127 us (36%)
  waiting for transfers between devices  94.9 us (27%)
  starting transfers between devices  48.9 us (14%)
  local copies, waits for them, and re-layouts  47.4 us (13%)
  other arithmetic  18.1 us (5%)
  blocking collectives  13.4 us (4%)
    ppermute x54, waiting for transfers between devices, swap(): return lax.ppermute(x, axis, [(i, i ^ mask) for i in range(n)])  94.9 us
    pallas_call x6, Pallas kernels, forward_matmul(): pl.pallas_call(kernel, grid=(stop - start,), in_specs=[RESIDENT, pl.Block...  54.6 us
    ppermute x54, starting transfers between devices, swap(): return lax.ppermute(x, axis, [(i, i ^ mask) for i in range(n)])  48.9 us
    pallas_call x6, Pallas kernels, backward_matmul(): pl.pallas_call(kernel, grid=(tiles,), in_specs=[pl.BlockSpec(g.shape, lam...  47.7 us
    unnamed x204, local copies, waits for them, and re-layouts  39.2 us
    psum x1, blocking collectives, local(): lax.psum((jnp.sum(rows * rows, axis=1), jnp.sum(steering * steering)), 'h...  7.37 us
  transfers between devices with their start and end apart: 54, of which 28 were waited for; matrix products, arithmetic and copies ran while one was open for 7% of the time, Pallas kernels for 27%

profile of v10, /device:TPU:0, one launch (start us, length us, event | category | flops | bytes accessed | tf_op | source)
XLA Modules:
  0.0 351.8 jit_solution(9623975567462853289)
XLA Ops:
  0.7 3.0 collective-permute-start
  5.0 2.1 fusion
  7.1 7.4 %all-reduce = (f32[256]{0:T(256)S(1)}, f32[]{:T(128)}) all-reduce(f32[256]{0:T(256)S(1)} %fusion, f32[]{:T(128)} %multiply_reduce_fusion), channel_id=1, replica_groups=mesh['dp'=2,'ffn'=4,'hid'=4] {'hid'}, use_global_device_ids=true, to_apply=%region_1.0 | all-reduce | flops 257 | bytes 2056 | tf_op jit(solution)/shard_map/psum | solution.py:425
  16.0 6.1 %psum.23 = f32[256]{0:T(256)S(1)} all-reduce(f32[256]{0:T(256)S(1)} %fusion.2), channel_id=1, replica_groups=mesh['dp'=2,'ffn'=4,'hid'=4] {'hid'}, use_global_device_ids=true, to_apply=%region_5.0 | all-reduce | flops 256 | bytes 2048 | tf_op jit(solution)/shard_map/psum | solution.py:432
  22.3 1.7 normalize.2
  24.0 14.6 %forward_matmul.6 = (f32[128,3584]{1,0:T(8,128)S(1)}, bf16[128,3584]{1,0:T(8,128)(2,1)S(1)}, f32[8,128]{1,0:T(8,128)}) custom-call(bf16[256,4096]{1,0:T(8,128)(2,1)S(1)} %get-tuple-element.50.x_ref.refs_0_, bf16[1,4096,6656]{2,1,0:T(8,128)(2,1)} %refs_8_.11), custom_call_target="tpu_custom_call" | custom-call | flops 75161928 | bytes 342097 | tf_op jit(solution)/shard_map/forward_matmul/pallas_call | solution.py:139
  38.6 2.5 collective-permute-done.2.refs_1_
  42.8 9.5 %collective-permute-done.1.stat_ref = f32[256,2]{1,0:T(8,128)S(1)} collective-permute-done((f32[256,2]{1,0:T(8,128)S(1)}, f32[256,2]{1,0:T(8,128)S(1)}, u32[]{:S(2)}, u32[]{:S(2)}) %collective-permute-start.1) | collective-permute-done | bytes 2080 | tf_op jit(solution)/shard_map/ppermute | solution.py:41
  52.3 3.4 normalize.3
  55.9 10.5 %forward_matmul.7 = (f32[128,3584]{1,0:T(8,128)S(1)}, bf16[128,3584]{1,0:T(8,128)(2,1)S(1)}, f32[8,128]{1,0:T(8,128)}) custom-call(bf16[256,4096]{1,0:T(8,128)(2,1)S(1)} %get-tuple-element.55.x_ref, bf16[1,4096,6656]{2,1,0:T(8,128)(2,1)} %refs_8_.11, bf16[64,3584]{1,0:T(8,128)(2,1)S(1)} %share_sums.6.refs_0_), custom_call_target="tpu_custom_call" | custom-call | flops 42949672 | bytes 204472 | tf_op jit(solution)/shard_map/forward_matmul/pallas_call | solution.py:139
  66.4 7.8 %forward_matmul.8 = (f32[128,3584]{1,0:T(8,128)S(1)}, bf16[128,3584]{1,0:T(8,128)(2,1)S(1)}, f32[8,128]{1,0:T(8,128)}) custom-call(bf16[256,4096]{1,0:T(8,128)(2,1)S(1)} %get-tuple-element.55.x_ref, bf16[1,4096,6656]{2,1,0:T(8,128)(2,1)} %refs_8_.11, f32[128,3584]{1,0:T(8,128)S(1)} %get-tuple-element.56.refs_0_, ...), custom_call_target="tpu_custom_call", output_to_operand_aliasing={{0}: (2, {}), {1}: (3, {})} | custom-call | flops 32212254 | bytes 158597 | tf_op jit(solution)/shard_map/forward_matmul/pallas_call | solution.py:139
  74.3 1.8 collective-permute-start.6
  76.1 2.7 collective-permute-done.6
  79.1 1.8 collective-permute-start.7
  80.9 7.0 %forward_matmul.9 = (f32[256,3072]{1,0:T(8,128)S(1)}, bf16[256,3072]{1,0:T(8,128)(2,1)S(1)}, f32[8,128]{1,0:T(8,128)S(1)}) custom-call(bf16[512,4096]{1,0:T(8,128)(2,1)S(1)} %get-tuple-element.54.x_ref.refs_1_, bf16[1,4096,6656]{2,1,0:T(8,128)(2,1)} %refs_8_.11, bf16[64,3584]{1,0:T(8,128)(2,1)S(1)} %share_sums.7.refs_0_), custom_call_target="tpu_custom_call" | custom-call | flops 42949672 | bytes 141557 | tf_op jit(solution)/shard_map/forward_matmul/pallas_call | solution.py:139
  88.0 3.3 collective-permute-done.7.refs_2_
  92.3 1.6 collective-permute-start.8
  94.0 2.2 copy-done.1
  98.6 9.5 %forward_matmul.10 = (f32[256,3072]{1,0:T(8,128)S(1)}, bf16[256,3072]{1,0:T(8,128)(2,1)S(1)}, f32[8,128]{1,0:T(8,128)S(1)}) custom-call(bf16[512,4096]{1,0:T(8,128)(2,1)S(1)} %copy-done.1, bf16[1,4096,6656]{2,1,0:T(8,128)(2,1)} %refs_8_.11, f32[256,3072]{1,0:T(8,128)S(1)} %get-tuple-element.62.refs_0_, ...), custom_call_target="tpu_custom_call", output_to_operand_aliasing={{0}: (2, {}), {1}: (3, {})} | custom-call | flops 64424508 | bytes 191365 | tf_op jit(solution)/shard_map/forward_matmul/pallas_call | solution.py:139
  109.3 3.1 gated_gradients.2
  113.0 1.5 collective-permute-start.10
  115.1 8.8 %collective-permute-done.10.refs_3_.refs_1_.refs_2_ = bf16[64,3584]{1,0:T(8,128)(2,1)S(1)} collective-permute-done((bf16[64,3584]{1,0:T(8,128)(2,1)S(1)}, bf16[64,3584]{1,0:T(8,128)(2,1)S(1)}, u32[]{:S(2)}, u32[]{:S(2)}) %collective-permute-start.10) | collective-permute-done | bytes 458784 | tf_op jit(solution)/shard_map/ppermute | solution.py:41
  125.2 5.2 %forward_matmul.11 = (f32[256,3072]{1,0:T(8,128)S(1)}, bf16[256,3072]{1,0:T(8,128)(2,1)S(1)}, f32[8,128]{1,0:T(8,128)}) custom-call(bf16[512,4096]{1,0:T(8,128)(2,1)S(1)} %copy-done.1, bf16[1,4096,6656]{2,1,0:T(8,128)(2,1)} %refs_8_.11, f32[256,3072]{1,0:T(8,128)S(1)} %get-tuple-element.65.refs_0_, ...), custom_call_target="tpu_custom_call", output_to_operand_aliasing={{0}: (2, {}), {1}: (3, {})} | custom-call | flops 21474836 | bytes 91750 | tf_op jit(solution)/shard_map/forward_matmul/pallas_call | solution.py:139
  131.6 11.7 %collective-permute-done.16.refs_5_.refs_6_ = bf16[64,3584]{1,0:T(8,128)(2,1)S(1)} collective-permute-done((bf16[64,3584]{1,0:T(8,128)(2,1)S(1)}, bf16[64,3584]{1,0:T(8,128)(2,1)S(1)}, u32[]{:S(2)}, u32[]{:S(2)}) %collective-permute-start.16) | collective-permute-done | bytes 458784 | tf_op jit(solution)/shard_map/ppermute | solution.py:41
  144.3 1.5 collective-permute-start.12
  145.8 9.0 %backward_matmul.6.refs_3_.refs_9_.refs_10_ = f32[512,1536]{1,0:T(8,128)S(1)} custom-call(bf16[64,3584]{1,0:T(8,128)(2,1)S(1)} %get-tuple-element.69.refs_0_.refs_1_, bf16[64,3584]{1,0:T(8,128)(2,1)S(1)} %collective-permute-done.10.refs_3_.refs_1_.refs_2_, bf16[64,3584]{1,0:T(8,128)(2,1)S(1)} %collective-permute-done.14.refs_2_.refs_3_, ...), custom_call_target="tpu_custom_call" | custom-call | flops 56371444 | bytes 178257 | tf_op jit(solution)/shard_map/backward_matmul/pallas_call | solution.py:298
  156.6 7.1 %collective-permute-done.12.refs_2_ = bf16[64,3072]{1,0:T(8,128)(2,1)S(1)} collective-permute-done((bf16[64,3072]{1,0:T(8,128)(2,1)S(1)}, bf16[64,3072]{1,0:T(8,128)(2,1)S(1)}, u32[]{:S(2)}, u32[]{:S(2)}) %collective-permute-start.12) | collective-permute-done | bytes 393248 | tf_op jit(solution)/shard_map/ppermute | solution.py:41
  163.7 2.7 collective-permute-done.19.refs_3_
  166.4 3.3 gated_gradients.3
  170.8 8.5 %backward_matmul.7.refs_1_.refs_11_.refs_9_ = f32[512,1536]{1,0:T(8,128)S(1)} custom-call(bf16[64,3584]{1,0:T(8,128)(2,1)S(1)} %get-tuple-element.69.refs_0_.refs_1_, bf16[64,3584]{1,0:T(8,128)(2,1)S(1)} %collective-permute-done.10.refs_3_.refs_1_.refs_2_, bf16[64,3584]{1,0:T(8,128)(2,1)S(1)} %collective-permute-done.14.refs_2_.refs_3_, ...), custom_call_target="tpu_custom_call" | custom-call | flops 56371444 | bytes 178257 | tf_op jit(solution)/shard_map/backward_matmul/pallas_call | solution.py:298
  179.5 1.6 collective-permute-start.24
  181.8 6.7 %collective-permute-done.24.refs_5_.refs_14_ = bf16[64,3072]{1,0:T(8,128)(2,1)S(1)} collective-permute-done((bf16[64,3072]{1,0:T(8,128)(2,1)S(1)}, bf16[64,3072]{1,0:T(8,128)(2,1)S(1)}, u32[]{:S(2)}, u32[]{:S(2)}) %collective-permute-start.24) | collective-permute-done | bytes 393248 | tf_op jit(solution)/shard_map/ppermute | solution.py:41
  188.5 6.4 %backward_matmul.8.refs_12_.refs_9_ = f32[512,1024]{1,0:T(8,128)S(1)} custom-call(bf16[64,3584]{1,0:T(8,128)(2,1)S(1)} %get-tuple-element.69.refs_0_.refs_1_, bf16[64,3584]{1,0:T(8,128)(2,1)S(1)} %collective-permute-done.10.refs_3_.refs_1_.refs_2_, bf16[64,3584]{1,0:T(8,128)(2,1)S(1)} %collective-permute-done.14.refs_2_.refs_3_, ...), custom_call_target="tpu_custom_call" | custom-call | flops 37580964 | bytes 131072 | tf_op jit(solution)/shard_map/backward_matmul/pallas_call | solution.py:298
  195.1 9.5 %backward_matmul.9 = (f32[256,1536]{1,0:T(8,128)S(1)}, bf16[256,1536]{1,0:T(8,128)(2,1)}) custom-call(bf16[64,3072]{1,0:T(8,128)(2,1)S(1)} %get-tuple-element.74.refs_9_.refs_0_, bf16[64,3072]{1,0:T(8,128)(2,1)S(1)} %collective-permute-done.20.refs_1_.refs_10_, bf16[64,3072]{1,0:T(8,128)(2,1)S(1)} %collective-permute-done.21.refs_2_.refs_11_, ...), custom_call_target="tpu_custom_call" | custom-call | flops 48318384 | bytes 188743 | tf_op jit(solution)/shard_map/backward_matmul/pallas_call | solution.py:298
  205.8 1.5 collective-permute-start.27
  215.7 8.3 %backward_matmul.10 = (f32[256,1536]{1,0:T(8,128)S(1)}, bf16[256,1536]{1,0:T(8,128)(2,1)}) custom-call(bf16[64,3072]{1,0:T(8,128)(2,1)S(1)} %copy-done.14, bf16[64,3072]{1,0:T(8,128)(2,1)S(1)} %copy-done.34, bf16[64,3072]{1,0:T(8,128)(2,1)S(1)} %copy-done.42, bf16[64,3072]{1,0:T(8,128)(2,1)S(1)} %copy-done.50, ...), custom_call_target="tpu_custom_call" | custom-call | flops 48318384 | bytes 188743 | tf_op jit(solution)/shard_map/backward_matmul/pallas_call | solution.py:298
  224.0 2.0 collective-permute-done.27.x_ref
  228.4 1.6 collective-permute-start.29
  230.0 1.5 collective-permute-start.39
  240.0 5.9 %backward_matmul.11 = (f32[256,1024]{1,0:T(8,128)S(1)}, bf16[256,1024]{1,0:T(8,128)(2,1)S(1)}) custom-call(bf16[64,3072]{1,0:T(8,128)(2,1)S(1)} %copy-done.15, bf16[64,3072]{1,0:T(8,128)(2,1)S(1)} %copy-done.35, bf16[64,3072]{1,0:T(8,128)(2,1)S(1)} %copy-done.43, bf16[64,3072]{1,0:T(8,128)(2,1)S(1)} %copy-done.51, ...), custom_call_target="tpu_custom_call" | custom-call | flops 32212254 | bytes 136314 | tf_op jit(solution)/shard_map/backward_matmul/pallas_call | solution.py:298
  247.7 2.2 collective-permute-done.31
  250.5 2.6 collective-permute-start.32
  256.6 1.5 collective-permute-start.33
  258.2 2.3 add_convert_fusion
  260.8 2.0 add_convert_fusion.4
  262.8 2.6 collective-permute-start.30
  268.6 1.5 collective-permute-start.51
  270.8 1.4 copy.75
  281.4 2.9 collective-permute-start.41
  297.3 2.0 collective-permute-start.37
  302.0 8.6 %collective-permute-done.36 = bf16[128,1024]{1,0:T(8,128)(2,1)S(1)} collective-permute-done((bf16[128,1024]{1,0:T(8,128)(2,1)S(1)}, bf16[128,1024]{1,0:T(8,128)(2,1)S(1)}, u32[]{:S(2)}, u32[]{:S(2)}) %collective-permute-start.36) | collective-permute-done | bytes 262176 | tf_op jit(solution)/shard_map/ppermute | solution.py:41
  310.7 4.2 %collective-permute-done.37.refs_10_.refs_3_ = bf16[64,1536]{1,0:T(8,128)(2,1)S(1)} collective-permute-done((bf16[64,1536]{1,0:T(8,128)(2,1)S(1)}, bf16[64,1536]{1,0:T(8,128)(2,1)S(1)}, u32[]{:S(2)}, u32[]{:S(2)}) %collective-permute-start.37) | collective-permute-done | bytes 196640 | tf_op jit(solution)/shard_map/ppermute | solution.py:41
  316.3 2.6 collective-permute-done.43.refs_9_.refs_2_
  319.0 3.8 %collective-permute-done.38.refs_1_ = bf16[64,1024]{1,0:T(8,128)(2,1)S(1)} collective-permute-done((bf16[64,1024]{1,0:T(8,128)(2,1)S(1)}, bf16[64,1024]{1,0:T(8,128)(2,1)S(1)}, u32[]{:S(2)}, u32[]{:S(2)}) %collective-permute-start.38) | collective-permute-done | bytes 131104 | tf_op jit(solution)/shard_map/ppermute | solution.py:41
  324.7 2.2 copy-done.2
  326.9 1.6 adapter_products.2
  328.5 2.5 collective-permute-start.45
  331.0 2.1 collective-permute-done.44.refs_1_
  333.1 2.1 collective-permute-start.47
  336.5 3.6 %collective-permute-done.46.refs_3_ = bf16[80,1024]{1,0:T(8,128)(2,1)S(1)} collective-permute-done((bf16[80,1024]{1,0:T(8,128)(2,1)S(1)}, bf16[80,1024]{1,0:T(8,128)(2,1)S(1)}, u32[]{:S(2)}, u32[]{:S(2)}) %collective-permute-start.46) | collective-permute-done | bytes 163872 | tf_op jit(solution)/shard_map/ppermute | solution.py:41
  340.2 1.7 collective-permute-start.49
  342.8 1.5 assemble.3.refs_4_
  344.4 4.0 %collective-permute-done.48.refs_3_ = bf16[64,1536]{1,0:T(8,128)(2,1)S(1)} collective-permute-done((bf16[64,1536]{1,0:T(8,128)(2,1)S(1)}, bf16[64,1536]{1,0:T(8,128)(2,1)S(1)}, u32[]{:S(2)}, u32[]{:S(2)}) %collective-permute-start.48) | collective-permute-done | bytes 196640 | tf_op jit(solution)/shard_map/ppermute | solution.py:41
  348.4 1.5 assemble.4.refs_4_
  (337 shorter events, 80.6 us)
Async XLA Ops:
  0.7 51.7 %collective-permute-start = (bf16[256,4096]{1,0:T(8,128)(2,1)}, bf16[256,4096]{1,0:T(8,128)(2,1)}, u32[]{:S(2)}, u32[]{:S(2)}) collective-permute-start(bf16[256,4096]{1,0:T(8,128)(2,1)} %x_ref.1), channel_id=1, source_target_pairs={{0,16},{16,0},{1,17},{17,1},{2,18},{18,2},{3,19},{19,3},{4,20},{20... | collective-permute-start | bytes 6291464 | tf_op jit(solution)/shard_map/ppermute | solution.py:41
  38.6 2.5 collective-permute-start.2
  41.3 25.1 %collective-permute-start.4 = (bf16[64,3584]{1,0:T(8,128)(2,1)S(1)}, bf16[64,3584]{1,0:T(8,128)(2,1)S(1)}, u32[]{:S(2)}, u32[]{:S(2)}) collective-permute-start(bf16[64,3584]{1,0:T(8,128)(2,1)S(1)} %share_sums.6.refs_0_), channel_id=1, source_target_pairs={{0,2},{1,3},{2,0},{3,1},{4,6},{5,7},{6,4},{7,5},{8,10},{9,11},{10,... | collective-permute-start | bytes 1376264 | tf_op jit(solution)/shard_map/ppermute | solution.py:41
  42.2 10.1 %collective-permute-start.1 = (f32[256,2]{1,0:T(8,128)S(1)}, f32[256,2]{1,0:T(8,128)S(1)}, u32[]{:S(2)}, u32[]{:S(2)}) collective-permute-start(f32[256,2]{1,0:T(8,128)S(1)} %copy.68.stat_ref), channel_id=1, source_target_pairs={{0,16},{16,0},{1,17},{17,1},{2,18},{18,2},{3,19},{19,3},{4,20},{20... | collective-permute-start | bytes 6152 | tf_op jit(solution)/shard_map/ppermute | solution.py:41
  55.8 25.2 %copy-start = (bf16[512,4096]{1,0:T(8,128)(2,1)}, bf16[512,4096]{1,0:T(8,128)(2,1)S(1)}, u32[]{:S(2)}) copy-start(bf16[512,4096]{1,0:T(8,128)(2,1)S(1)} %get-tuple-element.54.x_ref.refs_1_) | copy-start | bytes 12582916
  55.8 10.6 %collective-permute-start.3 = (f32[2,128,32]{2,1,0:T(8,128)S(1)}, f32[2,128,32]{2,1,0:T(8,128)S(1)}, u32[]{:S(2)}, u32[]{:S(2)}) collective-permute-start(f32[2,128,32]{2,1,0:T(8,128)S(1)} %pad_maximum_fusion), channel_id=1, source_target_pairs={{0,1},{1,0},{2,3},{3,2},{4,5},{5,4},{6,7},{7,6},{8,9},{9,8},{10,11... | collective-permute-start | bytes 98312 | tf_op jit(solution)/shard_map/ppermute | solution.py:41
  74.3 4.6 %collective-permute-start.5 = (bf16[128,3584]{1,0:T(8,128)(2,1)S(1)}, bf16[128,3584]{1,0:T(8,128)(2,1)S(1)}, u32[]{:S(2)}, u32[]{:S(2)}) collective-permute-start(bf16[128,3584]{1,0:T(8,128)(2,1)S(1)} %get-tuple-element.61), channel_id=1, source_target_pairs={{0,1},{1,0},{2,3},{3,2},{4,5},{5,4},{6,7},{7,6},{8,9},{9,8},{10,11... | collective-permute-start | bytes 2752520 | tf_op jit(solution)/shard_map/ppermute | solution.py:41
  74.3 4.5 %collective-permute-start.6 = (f32[2,64,32]{2,1,0:T(8,128)S(1)}, f32[2,64,32]{2,1,0:T(8,128)S(1)}, u32[]{:S(2)}, u32[]{:S(2)}) collective-permute-start(f32[2,64,32]{2,1,0:T(8,128)S(1)} %slice.68), channel_id=1, source_target_pairs={{0,2},{1,3},{2,0},{3,1},{4,6},{5,7},{6,4},{7,5},{8,10},{9,11},{10,... | collective-permute-start | bytes 49160 | tf_op jit(solution)/shard_map/ppermute | solution.py:41
  79.1 12.2 %collective-permute-start.7 = (bf16[64,3584]{1,0:T(8,128)(2,1)S(1)}, bf16[64,3584]{1,0:T(8,128)(2,1)S(1)}, u32[]{:S(2)}, u32[]{:S(2)}) collective-permute-start(bf16[64,3584]{1,0:T(8,128)(2,1)S(1)} %share_sums.7.refs_0_), channel_id=1, source_target_pairs={{0,2},{1,3},{2,0},{3,1},{4,6},{5,7},{6,4},{7,5},{8,10},{9,11},{10,... | collective-permute-start | bytes 1376264 | tf_op jit(solution)/shard_map/ppermute | solution.py:41
  92.3 16.9 %collective-permute-start.8 = (bf16[64,3584]{1,0:T(8,128)(2,1)}, bf16[64,3584]{1,0:T(8,128)(2,1)}, u32[]{:S(2)}, u32[]{:S(2)}) collective-permute-start(bf16[64,3584]{1,0:T(8,128)(2,1)} %share_sums.8.refs_3_), channel_id=1, source_target_pairs={{0,16},{16,0},{1,17},{17,1},{2,18},{18,2},{3,19},{19,3},{4,20},{20... | collective-permute-start | bytes 1376264 | tf_op jit(solution)/shard_map/ppermute | solution.py:41
  113.0 75.4 %copy-start.19 = (bf16[64,3584]{1,0:T(8,128)(2,1)}, bf16[64,3584]{1,0:T(8,128)(2,1)S(1)}, u32[]{:S(2)}) copy-start(bf16[64,3584]{1,0:T(8,128)(2,1)S(1)} %get-tuple-element.69.refs_0_.refs_1_) | copy-start | bytes 1376260
  113.0 10.9 %collective-permute-start.10 = (bf16[64,3584]{1,0:T(8,128)(2,1)S(1)}, bf16[64,3584]{1,0:T(8,128)(2,1)S(1)}, u32[]{:S(2)}, u32[]{:S(2)}) collective-permute-start(bf16[64,3584]{1,0:T(8,128)(2,1)S(1)} %get-tuple-element.69.refs_0_.refs_1_), channel_id=1, source_target_pairs={{0,2},{1,3},{2,0},{3,1},{4,6},{5,7},{6,4},{7,5},{8,10},{9,11},{10,... | collective-permute-start | bytes 1376264 | tf_op jit(solution)/shard_map/ppermute | solution.py:41
  114.6 10.6 %collective-permute-start.9 = (bf16[64,3584]{1,0:T(8,128)(2,1)S(1)}, bf16[64,3584]{1,0:T(8,128)(2,1)S(1)}, u32[]{:S(2)}, u32[]{:S(2)}) collective-permute-start(bf16[64,3584]{1,0:T(8,128)(2,1)S(1)} %get-tuple-element.68), channel_id=1, source_target_pairs={{0,16},{16,0},{1,17},{17,1},{2,18},{18,2},{3,19},{19,3},{4,20},{20... | collective-permute-start | bytes 1376264 | tf_op jit(solution)/shard_map/ppermute | solution.py:41
  123.9 64.5 %copy-start.9 = (bf16[64,3584]{1,0:T(8,128)(2,1)}, bf16[64,3584]{1,0:T(8,128)(2,1)S(1)}, u32[]{:S(2)}) copy-start(bf16[64,3584]{1,0:T(8,128)(2,1)S(1)} %collective-permute-done.10.refs_3_.refs_1_.refs_2_) | copy-start | bytes 1376260
  125.2 63.3 %copy-start.11 = (bf16[64,3584]{1,0:T(8,128)(2,1)}, bf16[64,3584]{1,0:T(8,128)(2,1)S(1)}, u32[]{:S(2)}) copy-start(bf16[64,3584]{1,0:T(8,128)(2,1)S(1)} %collective-permute-done.9.refs_2_.refs_4_.refs_5_) | copy-start | bytes 1376260
  130.3 12.9 %collective-permute-start.11 = (bf16[256,3072]{1,0:T(8,128)(2,1)S(1)}, bf16[256,3072]{1,0:T(8,128)(2,1)S(1)}, u32[]{:S(2)}, u32[]{:S(2)}) collective-permute-start(bf16[256,3072]{1,0:T(8,128)(2,1)S(1)} %get-tuple-element.71), channel_id=1, source_target_pairs={{0,1},{1,0},{2,3},{3,2},{4,5},{5,4},{6,7},{7,6},{8,9},{9,8},{10,11... | collective-permute-start | bytes 4718600 | tf_op jit(solution)/shard_map/ppermute | solution.py:41
  130.3 12.9 %collective-permute-start.16 = (bf16[64,3584]{1,0:T(8,128)(2,1)S(1)}, bf16[64,3584]{1,0:T(8,128)(2,1)S(1)}, u32[]{:S(2)}, u32[]{:S(2)}) collective-permute-start(bf16[64,3584]{1,0:T(8,128)(2,1)S(1)} %collective-permute-done.9.refs_2_.refs_4_.refs_5_), channel_id=1, source_target_pairs={{0,2},{1,3},{2,0},{3,1},{4,6},{5,7},{6,4},{7,5},{8,10},{9,11},{10,... | collective-permute-start | bytes 1376264 | tf_op jit(solution)/shard_map/ppermute | solution.py:41
  130.9 13.4 %collective-permute-start.14 = (bf16[64,3584]{1,0:T(8,128)(2,1)S(1)}, bf16[64,3584]{1,0:T(8,128)(2,1)S(1)}, u32[]{:S(2)}, u32[]{:S(2)}) collective-permute-start(bf16[64,3584]{1,0:T(8,128)(2,1)S(1)} %get-tuple-element.69.refs_0_.refs_1_), channel_id=1, source_target_pairs={{0,1},{1,0},{2,3},{3,2},{4,5},{5,4},{6,7},{7,6},{8,9},{9,8},{10,11... | collective-permute-start | bytes 1376264 | tf_op jit(solution)/shard_map/ppermute | solution.py:41
  131.1 14.7 %collective-permute-start.15 = (bf16[64,3584]{1,0:T(8,128)(2,1)S(1)}, bf16[64,3584]{1,0:T(8,128)(2,1)S(1)}, u32[]{:S(2)}, u32[]{:S(2)}) collective-permute-start(bf16[64,3584]{1,0:T(8,128)(2,1)S(1)} %collective-permute-done.10.refs_3_.refs_1_.refs_2_), channel_id=1, source_target_pairs={{0,1},{1,0},{2,3},{3,2},{4,5},{5,4},{6,7},{7,6},{8,9},{9,8},{10,11... | collective-permute-start | bytes 1376264 | tf_op jit(solution)/shard_map/ppermute | solution.py:41
  131.4 14.4 %collective-permute-start.17 = (bf16[64,3584]{1,0:T(8,128)(2,1)S(1)}, bf16[64,3584]{1,0:T(8,128)(2,1)S(1)}, u32[]{:S(2)}, u32[]{:S(2)}) collective-permute-start(bf16[64,3584]{1,0:T(8,128)(2,1)S(1)} %collective-permute-done.9.refs_2_.refs_4_.refs_5_), channel_id=1, source_target_pairs={{0,1},{1,0},{2,3},{3,2},{4,5},{5,4},{6,7},{7,6},{8,9},{9,8},{10,11... | collective-permute-start | bytes 1376264 | tf_op jit(solution)/shard_map/ppermute | solution.py:41
  143.3 45.2 %copy-start.21 = (bf16[64,3584]{1,0:T(8,128)(2,1)}, bf16[64,3584]{1,0:T(8,128)(2,1)S(1)}, u32[]{:S(2)}) copy-start(bf16[64,3584]{1,0:T(8,128)(2,1)S(1)} %collective-permute-done.16.refs_5_.refs_6_) | copy-start | bytes 1376260
  143.3 2.5 collective-permute-start.18
  143.7 12.0 %collective-permute-start.13 = (bf16[64,3072]{1,0:T(8,128)(2,1)S(1)}, bf16[64,3072]{1,0:T(8,128)(2,1)S(1)}, u32[]{:S(2)}, u32[]{:S(2)}) collective-permute-start(bf16[64,3072]{1,0:T(8,128)(2,1)S(1)} %get-tuple-element.73), channel_id=1, source_target_pairs={{0,2},{1,3},{2,0},{3,1},{4,6},{5,7},{6,4},{7,5},{8,10},{9,11},{10,... | collective-permute-start | bytes 1179656 | tf_op jit(solution)/shard_map/ppermute | solution.py:41
  144.3 44.2 %copy-start.23 = (bf16[64,3584]{1,0:T(8,128)(2,1)}, bf16[64,3584]{1,0:T(8,128)(2,1)S(1)}, u32[]{:S(2)}) copy-start(bf16[64,3584]{1,0:T(8,128)(2,1)S(1)} %collective-permute-done.14.refs_2_.refs_3_) | copy-start | bytes 1376260
  144.3 19.4 %collective-permute-start.12 = (bf16[64,3072]{1,0:T(8,128)(2,1)S(1)}, bf16[64,3072]{1,0:T(8,128)(2,1)S(1)}, u32[]{:S(2)}, u32[]{:S(2)}) collective-permute-start(bf16[64,3072]{1,0:T(8,128)(2,1)S(1)} %get-tuple-element.72.refs_9_), channel_id=1, source_target_pairs={{0,2},{1,3},{2,0},{3,1},{4,6},{5,7},{6,4},{7,5},{8,10},{9,11},{10,... | collective-permute-start | bytes 1179656 | tf_op jit(solution)/shard_map/ppermute | solution.py:41
  145.8 42.7 %copy-start.25 = (bf16[64,3584]{1,0:T(8,128)(2,1)}, bf16[64,3584]{1,0:T(8,128)(2,1)S(1)}, u32[]{:S(2)}) copy-start(bf16[64,3584]{1,0:T(8,128)(2,1)S(1)} %collective-permute-done.15.refs_3_.refs_4_) | copy-start | bytes 1376260
  145.8 42.7 %copy-start.27 = (bf16[64,3584]{1,0:T(8,128)(2,1)}, bf16[64,3584]{1,0:T(8,128)(2,1)S(1)}, u32[]{:S(2)}) copy-start(bf16[64,3584]{1,0:T(8,128)(2,1)S(1)} %collective-permute-done.17.refs_6_.refs_7_) | copy-start | bytes 1376260
  145.8 42.7 %copy-start.29 = (bf16[64,3584]{1,0:T(8,128)(2,1)}, bf16[64,3584]{1,0:T(8,128)(2,1)S(1)}, u32[]{:S(2)}) copy-start(bf16[64,3584]{1,0:T(8,128)(2,1)S(1)} %collective-permute-done.18.refs_7_.refs_8_) | copy-start | bytes 1376260
  156.0 10.4 %collective-permute-start.19 = (bf16[64,3072]{1,0:T(8,128)(2,1)S(1)}, bf16[64,3072]{1,0:T(8,128)(2,1)S(1)}, u32[]{:S(2)}, u32[]{:S(2)}) collective-permute-start(bf16[64,3072]{1,0:T(8,128)(2,1)S(1)} %share_sums.10), channel_id=1, source_target_pairs={{0,16},{16,0},{1,17},{17,1},{2,18},{18,2},{3,19},{19,3},{4,20},{20... | collective-permute-start | bytes 1179656 | tf_op jit(solution)/shard_map/ppermute | solution.py:41
  169.7 25.3 %copy-start.13 = (bf16[64,3072]{1,0:T(8,128)(2,1)}, bf16[64,3072]{1,0:T(8,128)(2,1)S(1)}, u32[]{:S(2)}) copy-start(bf16[64,3072]{1,0:T(8,128)(2,1)S(1)} %get-tuple-element.74.refs_9_.refs_0_) | copy-start | bytes 1179652
  169.7 9.6 %collective-permute-start.23 = (bf16[64,3072]{1,0:T(8,128)(2,1)S(1)}, bf16[64,3072]{1,0:T(8,128)(2,1)S(1)}, u32[]{:S(2)}, u32[]{:S(2)}) collective-permute-start(bf16[64,3072]{1,0:T(8,128)(2,1)S(1)} %get-tuple-element.75), channel_id=1, source_target_pairs={{0,16},{16,0},{1,17},{17,1},{2,18},{18,2},{3,19},{19,3},{4,20},{20... | collective-permute-start | bytes 1179656 | tf_op jit(solution)/shard_map/ppermute | solution.py:41
  170.4 11.3 %collective-permute-start.20 = (bf16[64,3072]{1,0:T(8,128)(2,1)S(1)}, bf16[64,3072]{1,0:T(8,128)(2,1)S(1)}, u32[]{:S(2)}, u32[]{:S(2)}) collective-permute-start(bf16[64,3072]{1,0:T(8,128)(2,1)S(1)} %get-tuple-element.74.refs_9_.refs_0_), channel_id=1, source_target_pairs={{0,2},{1,3},{2,0},{3,1},{4,6},{5,7},{6,4},{7,5},{8,10},{9,11},{10,... | collective-permute-start | bytes 1179656 | tf_op jit(solution)/shard_map/ppermute | solution.py:41
  179.5 8.9 %collective-permute-start.24 = (bf16[64,3072]{1,0:T(8,128)(2,1)S(1)}, bf16[64,3072]{1,0:T(8,128)(2,1)S(1)}, u32[]{:S(2)}, u32[]{:S(2)}) collective-permute-start(bf16[64,3072]{1,0:T(8,128)(2,1)S(1)} %share_sums.11.refs_9_.refs_4_.refs_13_), channel_id=1, source_target_pairs={{0,2},{1,3},{2,0},{3,1},{4,6},{5,7},{6,4},{7,5},{8,10},{9,11},{10,... | collective-permute-start | bytes 1179656 | tf_op jit(solution)/shard_map/ppermute | solution.py:41
  181.2 13.8 %collective-permute-start.21 = (bf16[64,3072]{1,0:T(8,128)(2,1)S(1)}, bf16[64,3072]{1,0:T(8,128)(2,1)S(1)}, u32[]{:S(2)}, u32[]{:S(2)}) collective-permute-start(bf16[64,3072]{1,0:T(8,128)(2,1)S(1)} %get-tuple-element.74.refs_9_.refs_0_), channel_id=1, source_target_pairs={{0,1},{1,0},{2,3},{3,2},{4,5},{5,4},{6,7},{7,6},{8,9},{9,8},{10,11... | collective-permute-start | bytes 1179656 | tf_op jit(solution)/shard_map/ppermute | solution.py:41
  181.2 13.8 %collective-permute-start.25 = (bf16[64,3072]{1,0:T(8,128)(2,1)S(1)}, bf16[64,3072]{1,0:T(8,128)(2,1)S(1)}, u32[]{:S(2)}, u32[]{:S(2)}) collective-permute-start(bf16[64,3072]{1,0:T(8,128)(2,1)S(1)} %share_sums.11.refs_9_.refs_4_.refs_13_), channel_id=1, source_target_pairs={{0,1},{1,0},{2,3},{3,2},{4,5},{5,4},{6,7},{7,6},{8,9},{9,8},{10,11... | collective-permute-start | bytes 1179656 | tf_op jit(solution)/shard_map/ppermute | solution.py:41
  181.7 13.3 %collective-permute-start.22 = (bf16[64,3072]{1,0:T(8,128)(2,1)S(1)}, bf16[64,3072]{1,0:T(8,128)(2,1)S(1)}, u32[]{:S(2)}, u32[]{:S(2)}) collective-permute-start(bf16[64,3072]{1,0:T(8,128)(2,1)S(1)} %collective-permute-done.20.refs_1_.refs_10_), channel_id=1, source_target_pairs={{0,1},{1,0},{2,3},{3,2},{4,5},{5,4},{6,7},{7,6},{8,9},{9,8},{10,11... | collective-permute-start | bytes 1179656 | tf_op jit(solution)/shard_map/ppermute | solution.py:41
  188.5 6.6 %collective-permute-start.26 = (bf16[64,3072]{1,0:T(8,128)(2,1)S(1)}, bf16[64,3072]{1,0:T(8,128)(2,1)S(1)}, u32[]{:S(2)}, u32[]{:S(2)}) collective-permute-start(bf16[64,3072]{1,0:T(8,128)(2,1)S(1)} %collective-permute-done.24.refs_5_.refs_14_), channel_id=1, source_target_pairs={{0,1},{1,0},{2,3},{3,2},{4,5},{5,4},{6,7},{7,6},{8,9},{9,8},{10,11... | collective-permute-start | bytes 1179656 | tf_op jit(solution)/shard_map/ppermute | solution.py:41
  205.8 20.2 %collective-permute-start.27 = (bf16[256,1536]{1,0:T(8,128)(2,1)}, bf16[256,1536]{1,0:T(8,128)(2,1)}, u32[]{:S(2)}, u32[]{:S(2)}) collective-permute-start(bf16[256,1536]{1,0:T(8,128)(2,1)} %get-tuple-element.78), channel_id=1, source_target_pairs={{0,16},{16,0},{1,17},{17,1},{2,18},{18,2},{3,19},{19,3},{4,20},{20... | collective-permute-start | bytes 2359304 | tf_op jit(solution)/shard_map/ppermute | solution.py:41
  228.4 17.5 %collective-permute-start.29 = (bf16[128,1536]{1,0:T(8,128)(2,1)}, bf16[128,1536]{1,0:T(8,128)(2,1)}, u32[]{:S(2)}, u32[]{:S(2)}) collective-permute-start(bf16[128,1536]{1,0:T(8,128)(2,1)} %get-tuple-element.101.refs_11_), channel_id=1, source_target_pairs={{0,4},{4,0},{8,12},{12,8},{1,5},{5,1},{9,13},{13,9},{2,6},{6,2},{1... | collective-permute-start | bytes 1179656 | tf_op jit(solution)/shard_map/ppermute | solution.py:41
  230.0 25.5 %collective-permute-start.39 = (bf16[256,1536]{1,0:T(8,128)(2,1)}, bf16[256,1536]{1,0:T(8,128)(2,1)}, u32[]{:S(2)}, u32[]{:S(2)}) collective-permute-start(bf16[256,1536]{1,0:T(8,128)(2,1)} %get-tuple-element.86), channel_id=1, source_target_pairs={{0,16},{16,0},{1,17},{17,1},{2,18},{18,2},{3,19},{19,3},{4,20},{20... | collective-permute-start | bytes 2359304 | tf_op jit(solution)/shard_map/ppermute | solution.py:41
  245.9 4.0 %collective-permute-start.31 = (f32[64,33]{1,0:T(8,128)S(1)}, f32[64,33]{1,0:T(8,128)S(1)}, u32[]{:S(2)}, u32[]{:S(2)}) collective-permute-start(f32[64,33]{1,0:T(8,128)S(1)} %relay.5), channel_id=1, source_target_pairs={{0,4},{4,0},{8,12},{12,8},{1,5},{5,1},{9,13},{13,9},{2,6},{6,2},{1... | collective-permute-start | bytes 25352 | tf_op jit(solution)/shard_map/ppermute | solution.py:41
  250.5 5.3 %collective-permute-start.32 = (f32[64,33]{1,0:T(8,128)}, f32[64,33]{1,0:T(8,128)}, u32[]{:S(2)}, u32[]{:S(2)}) collective-permute-start(f32[64,33]{1,0:T(8,128)} %add.233), channel_id=1, source_target_pairs={{0,8},{4,12},{8,0},{12,4},{1,9},{5,13},{9,1},{13,5},{2,10},{6,14},... | collective-permute-start | bytes 25352 | tf_op jit(solution)/shard_map/ppermute | solution.py:41
  255.0 12.1 %collective-permute-start.28 = (bf16[256,1024]{1,0:T(8,128)(2,1)}, bf16[256,1024]{1,0:T(8,128)(2,1)S(1)}, u32[]{:S(2)}, u32[]{:S(2)}) collective-permute-start(bf16[256,1024]{1,0:T(8,128)(2,1)} %copy-done.96), channel_id=1, source_target_pairs={{0,16},{16,0},{1,17},{17,1},{2,18},{18,2},{3,19},{19,3},{4,20},{20... | collective-permute-start | bytes 1572872 | tf_op jit(solution)/shard_map/ppermute | solution.py:41
  256.6 4.1 %collective-permute-start.33 = (f32[64,33]{1,0:T(8,128)S(1)}, f32[64,33]{1,0:T(8,128)S(1)}, u32[]{:S(2)}, u32[]{:S(2)}) collective-permute-start(f32[64,33]{1,0:T(8,128)S(1)} %add.234), channel_id=1, source_target_pairs={{0,2},{1,3},{2,0},{3,1},{4,6},{5,7},{6,4},{7,5},{8,10},{9,11},{10,... | collective-permute-start | bytes 25352 | tf_op jit(solution)/shard_map/ppermute | solution.py:41
  260.5 19.7 %collective-permute-start.40 = (bf16[128,1536]{1,0:T(8,128)(2,1)}, bf16[128,1536]{1,0:T(8,128)(2,1)}, u32[]{:S(2)}, u32[]{:S(2)}) collective-permute-start(bf16[128,1536]{1,0:T(8,128)(2,1)} %get-tuple-element.98), channel_id=1, source_target_pairs={{0,4},{4,0},{8,12},{12,8},{1,5},{5,1},{9,13},{13,9},{2,6},{6,2},{1... | collective-permute-start | bytes 1179656 | tf_op jit(solution)/shard_map/ppermute | solution.py:41
  260.7 4.7 %collective-permute-start.34 = (f32[128,33]{1,0:T(8,128)S(1)}, f32[128,33]{1,0:T(8,128)S(1)}, u32[]{:S(2)}, u32[]{:S(2)}) collective-permute-start(f32[128,33]{1,0:T(8,128)S(1)} %pad_maximum_fusion.2), channel_id=1, source_target_pairs={{0,1},{1,0},{2,3},{3,2},{4,5},{5,4},{6,7},{7,6},{8,9},{9,8},{10,11... | collective-permute-start | bytes 50696 | tf_op jit(solution)/shard_map/ppermute | solution.py:41
  262.8 12.7 %collective-permute-start.30 = (bf16[64,1536]{1,0:T(8,128)(2,1)}, bf16[64,1536]{1,0:T(8,128)(2,1)}, u32[]{:S(2)}, u32[]{:S(2)}) collective-permute-start(bf16[64,1536]{1,0:T(8,128)(2,1)} %get-tuple-element.106), channel_id=1, source_target_pairs={{0,8},{4,12},{8,0},{12,4},{1,9},{5,13},{9,1},{13,5},{2,10},{6,14},... | collective-permute-start | bytes 589832 | tf_op jit(solution)/shard_map/ppermute | solution.py:41
  268.6 4.2 %collective-permute-start.51 = (bf16[2,64,16]{2,1,0:T(8,128)(2,1)}, bf16[2,64,16]{2,1,0:T(8,128)(2,1)}, u32[]{:S(2)}, u32[]{:S(2)}) collective-permute-start(bf16[2,64,16]{2,1,0:T(8,128)(2,1)} %slice_select_fusion), channel_id=1, source_target_pairs={{0,2},{1,3},{2,0},{3,1},{4,6},{5,7},{6,4},{7,5},{8,10},{9,11},{10,... | collective-permute-start | bytes 12296 | tf_op jit(solution)/shard_map/ppermute | solution.py:41
  275.3 13.0 %collective-permute-start.52 = (bf16[2,128,16]{1,2,0:T(8,128)(2,1)S(1)}, bf16[2,128,16]{1,2,0:T(8,128)(2,1)S(1)}, u32[]{:S(2)}, u32[]{:S(2)}) collective-permute-start(bf16[2,128,16]{1,2,0:T(8,128)(2,1)S(1)} %pad_maximum_fusion.4), channel_id=1, source_target_pairs={{0,1},{1,0},{2,3},{3,2},{4,5},{5,4},{6,7},{7,6},{8,9},{9,8},{10,11... | collective-permute-start | bytes 24584 | tf_op jit(solution)/shard_map/ppermute | solution.py:41
  279.9 17.1 %collective-permute-start.35 = (bf16[64,1536]{1,0:T(8,128)(2,1)S(1)}, bf16[64,1536]{1,0:T(8,128)(2,1)S(1)}, u32[]{:S(2)}, u32[]{:S(2)}) collective-permute-start(bf16[64,1536]{1,0:T(8,128)(2,1)S(1)} %get-tuple-element.83.refs_0_), channel_id=1, source_target_pairs={{0,8},{4,12},{8,0},{12,4},{1,9},{5,13},{9,1},{13,5},{2,10},{6,14},... | collective-permute-start | bytes 589832 | tf_op jit(solution)/shard_map/ppermute | solution.py:41
  281.4 19.3 %collective-permute-start.41 = (bf16[64,1536]{1,0:T(8,128)(2,1)S(1)}, bf16[64,1536]{1,0:T(8,128)(2,1)S(1)}, u32[]{:S(2)}, u32[]{:S(2)}) collective-permute-start(bf16[64,1536]{1,0:T(8,128)(2,1)S(1)} %get-tuple-element.104), channel_id=1, source_target_pairs={{0,8},{4,12},{8,0},{12,4},{1,9},{5,13},{9,1},{13,5},{2,10},{6,14},... | collective-permute-start | bytes 589832 | tf_op jit(solution)/shard_map/ppermute | solution.py:41
  286.8 36.6 %collective-permute-start.50 = (bf16[256,32]{1,0:T(8,128)(2,1)}, bf16[256,32]{1,0:T(8,128)(2,1)}, u32[]{:S(2)}, u32[]{:S(2)}) collective-permute-start(bf16[256,32]{1,0:T(8,128)(2,1)} %relay.6), channel_id=1, source_target_pairs={{0,16},{16,0},{1,17},{17,1},{2,18},{18,2},{3,19},{19,3},{4,20},{20... | collective-permute-start | bytes 49160 | tf_op jit(solution)/shard_map/ppermute | solution.py:41
  297.2 13.5 %collective-permute-start.36 = (bf16[128,1024]{1,0:T(8,128)(2,1)S(1)}, bf16[128,1024]{1,0:T(8,128)(2,1)S(1)}, u32[]{:S(2)}, u32[]{:S(2)}) collective-permute-start(bf16[128,1024]{1,0:T(8,128)(2,1)S(1)} %get-tuple-element.102), channel_id=1, source_target_pairs={{0,4},{4,0},{8,12},{12,8},{1,5},{5,1},{9,13},{13,9},{2,6},{6,2},{1... | collective-permute-start | bytes 786440 | tf_op jit(solution)/shard_map/ppermute | solution.py:41
  297.3 17.6 %collective-permute-start.37 = (bf16[64,1536]{1,0:T(8,128)(2,1)S(1)}, bf16[64,1536]{1,0:T(8,128)(2,1)S(1)}, u32[]{:S(2)}, u32[]{:S(2)}) collective-permute-start(bf16[64,1536]{1,0:T(8,128)(2,1)S(1)} %collective-permute-done.35.refs_8_.refs_1_), channel_id=1, source_target_pairs={{0,4},{4,0},{8,12},{12,8},{1,5},{5,1},{9,13},{13,9},{2,6},{6,2},{1... | collective-permute-start | bytes 589832 | tf_op jit(solution)/shard_map/ppermute | solution.py:41
  299.3 19.6 %collective-permute-start.43 = (bf16[64,1536]{1,0:T(8,128)(2,1)S(1)}, bf16[64,1536]{1,0:T(8,128)(2,1)S(1)}, u32[]{:S(2)}, u32[]{:S(2)}) collective-permute-start(bf16[64,1536]{1,0:T(8,128)(2,1)S(1)} %get-tuple-element.83.refs_0_), channel_id=1, source_target_pairs={{0,4},{4,0},{8,12},{12,8},{1,5},{5,1},{9,13},{13,9},{2,6},{6,2},{1... | collective-permute-start | bytes 589832 | tf_op jit(solution)/shard_map/ppermute | solution.py:41
  301.0 17.9 %collective-permute-start.42 = (bf16[64,1536]{1,0:T(8,128)(2,1)S(1)}, bf16[64,1536]{1,0:T(8,128)(2,1)S(1)}, u32[]{:S(2)}, u32[]{:S(2)}) collective-permute-start(bf16[64,1536]{1,0:T(8,128)(2,1)S(1)} %get-tuple-element.88.refs_0_), channel_id=1, source_target_pairs={{0,8},{4,12},{8,0},{12,4},{1,9},{5,13},{9,1},{13,5},{2,10},{6,14},... | collective-permute-start | bytes 589832 | tf_op jit(solution)/shard_map/ppermute | solution.py:41
  314.9 7.9 %collective-permute-start.38 = (bf16[64,1024]{1,0:T(8,128)(2,1)S(1)}, bf16[64,1024]{1,0:T(8,128)(2,1)S(1)}, u32[]{:S(2)}, u32[]{:S(2)}) collective-permute-start(bf16[64,1024]{1,0:T(8,128)(2,1)S(1)} %get-tuple-element.85), channel_id=1, source_target_pairs={{0,8},{4,12},{8,0},{12,4},{1,9},{5,13},{9,1},{13,5},{2,10},{6,14},... | collective-permute-start | bytes 393224 | tf_op jit(solution)/shard_map/ppermute | solution.py:41
  314.9 18.1 %collective-permute-start.53 = (bf16[16,6656]{1,0:T(8,128)(2,1)S(1)}, bf16[16,6656]{1,0:T(8,128)(2,1)S(1)}, u32[]{:S(2)}, u32[]{:S(2)}) collective-permute-start(bf16[16,6656]{1,0:T(8,128)(2,1)S(1)} %convert_element_type.126), channel_id=1, source_target_pairs={{0,16},{16,0},{1,17},{17,1},{2,18},{18,2},{3,19},{19,3},{4,20},{20... | collective-permute-start | bytes 638984 | tf_op jit(solution)/shard_map/ppermute | solution.py:41
  323.1 9.9 %collective-permute-start.44 = (bf16[80,1024]{1,0:T(8,128)(2,1)S(1)}, bf16[80,1024]{1,0:T(8,128)(2,1)S(1)}, u32[]{:S(2)}, u32[]{:S(2)}) collective-permute-start(bf16[80,1024]{1,0:T(8,128)(2,1)S(1)} %maximum_maximum_fusion.refs_0_), channel_id=1, source_target_pairs={{0,8},{4,12},{8,0},{12,4},{1,9},{5,13},{9,1},{13,5},{2,10},{6,14},... | collective-permute-start | bytes 491528 | tf_op jit(solution)/shard_map/ppermute | solution.py:41
  328.5 8.0 %collective-permute-start.45 = (bf16[80,1024]{1,0:T(8,128)(2,1)S(1)}, bf16[80,1024]{1,0:T(8,128)(2,1)S(1)}, u32[]{:S(2)}, u32[]{:S(2)}) collective-permute-start(bf16[80,1024]{1,0:T(8,128)(2,1)S(1)} %maximum_maximum_fusion.refs_0_), channel_id=1, source_target_pairs={{0,4},{4,0},{8,12},{12,8},{1,5},{5,1},{9,13},{13,9},{2,6},{6,2},{1... | collective-permute-start | bytes 491528 | tf_op jit(solution)/shard_map/ppermute | solution.py:41
  333.0 7.1 %collective-permute-start.46 = (bf16[80,1024]{1,0:T(8,128)(2,1)S(1)}, bf16[80,1024]{1,0:T(8,128)(2,1)S(1)}, u32[]{:S(2)}, u32[]{:S(2)}) collective-permute-start(bf16[80,1024]{1,0:T(8,128)(2,1)S(1)} %collective-permute-done.44.refs_1_), channel_id=1, source_target_pairs={{0,4},{4,0},{8,12},{12,8},{1,5},{5,1},{9,13},{13,9},{2,6},{6,2},{1... | collective-permute-start | bytes 491528 | tf_op jit(solution)/shard_map/ppermute | solution.py:41
  333.1 11.3 %collective-permute-start.47 = (bf16[64,1536]{1,0:T(8,128)(2,1)S(1)}, bf16[64,1536]{1,0:T(8,128)(2,1)S(1)}, u32[]{:S(2)}, u32[]{:S(2)}) collective-permute-start(bf16[64,1536]{1,0:T(8,128)(2,1)S(1)} %get-tuple-element.88.refs_0_), channel_id=1, source_target_pairs={{0,4},{4,0},{8,12},{12,8},{1,5},{5,1},{9,13},{13,9},{2,6},{6,2},{1... | collective-permute-start | bytes 589832 | tf_op jit(solution)/shard_map/ppermute | solution.py:41
  335.2 13.2 %collective-permute-start.48 = (bf16[64,1536]{1,0:T(8,128)(2,1)S(1)}, bf16[64,1536]{1,0:T(8,128)(2,1)S(1)}, u32[]{:S(2)}, u32[]{:S(2)}) collective-permute-start(bf16[64,1536]{1,0:T(8,128)(2,1)S(1)} %collective-permute-done.42.refs_8_.refs_1_), channel_id=1, source_target_pairs={{0,4},{4,0},{8,12},{12,8},{1,5},{5,1},{9,13},{13,9},{2,6},{6,2},{1... | collective-permute-start | bytes 589832 | tf_op jit(solution)/shard_map/ppermute | solution.py:41
  340.2 11.0 %collective-permute-start.49 = (f32[4,1024]{1,0:T(4,128)S(1)}, f32[4,1024]{1,0:T(4,128)S(1)}, u32[]{:S(2)}, u32[]{:S(2)}) collective-permute-start(f32[4,1024]{1,0:T(4,128)S(1)} %fusion.10), channel_id=1, source_target_pairs={{0,16},{16,0},{1,17},{17,1},{2,18},{18,2},{3,19},{19,3},{4,20},{20... | collective-permute-start | bytes 49160 | tf_op jit(solution)/shard_map/ppermute | solution.py:41
  (91 other events, 666.5 us)
